TPU v7x, 32 devices: a whole 2x2x4 slice. The times are simulated.
32 devices in a mesh: row: 8 (over y, x, core), col: 4 (over z).
Axes of the slice: x: 2, y: 2, z: 4, core: 2. Of those that a mesh axis runs over, the one named last changes fastest.
Arguments:
- hidden: bfloat16 [64, 2048], P('row', 'col'), may hold values from -60 to 60
- queries: bfloat16 [64, 4096], P('row'), may hold values from -6 to 6
- new_kv: bfloat16 [64, 2, 2048], P('row'), may hold values from -12 to 12
- prompt_kv: bfloat16 [8, 2, 1024, 2048], P('row', None, 'col'), may hold values from -180 to 180
- suffix_kv: bfloat16 [64, 2, 128, 2048], P('row', None, 'col'), may hold values from -12 to 12
- lengths: int32 [64], P('row'), may hold values from 1 to 128, as said below
- w_out: bfloat16 [4096, 2048], P(None, 'col'), may hold values from -0.375 to 0.375
- moe_gain: bfloat16 [2048], P('col'), may hold values from 0.099609375 to 1.8984375
- w_router: bfloat16 [2048, 8], P('col'), may hold values from -0.5 to 0.5
- expert_weights: bfloat16 [8, 5632, 3, 2048], P(None, 'row', None, 'col'), may hold values from -0.25 to 0.25
- old_lines: int32 [8, 5632], replicated, may hold values from 0 to 5631, as said below
- new_lines: int32 [8, 5632], replicated, may hold values from 0 to 5631, as said below
- routes: int32 [64, 2], replicated, may hold values from 0 to 7, all different within a row
Outputs:
- layer_out: float32 [64, 2048], P('row', 'col')
- moved_weights: bfloat16 [8, 5632, 3, 2048], P(None, 'row', None, 'col')
Inputs may be any that keep to these rules, and one draw needn't show every extreme that they name: `lengths`: some sequence has all 128 slots filled. `old_lines`: each row is a permutation of the hidden units of one expert; stored lines [j * 704, (j + 1) * 704) lie on row index j. `new_lines`: each row is a permutation of the hidden units of one expert. Counting all experts together, exactly 704 of the lines that one row index holds under old_lines are held by each row index under new_lines. `routes`: the two experts of a token differ.
All inputs are finite; a program needn't handle non-finite values.
Results may differ from a plain program's by a relative error of at most 0.04.
Values may be sent and summed in bfloat16 or wider, within the bound.
No kernel may reach another device: no remote copies, remote signals or barrier semaphores. Data moves between devices by JAX's collectives and lax.ppermute only.
A program may use at most 128 MiB of HBM per device.

v0:
```python
import functools

import jax
import jax.numpy as jnp
from jax import lax
from jax.experimental import pallas as pl
from jax.experimental.pallas import tpu as pltpu
from jax.sharding import PartitionSpec as P

KVH = 16
HD = 128
REP = 2
TILE = 16
LANES = 128

norm_eps = 1e-06
neg_big = -1e30
VMEM_LIMIT = 48 * 1024 * 1024


def up_to(value, unit):
    return -(-value // unit) * unit


def iota(shape, axis):
    return lax.broadcasted_iota(jnp.int32, shape, axis)


def ones_where(mask):
    return jnp.where(mask, 1.0, 0.0).astype(jnp.bfloat16)


def params():
    return pltpu.CompilerParams(vmem_limit_bytes=VMEM_LIMIT)


def counting(shape, axis):
    return iota(shape, axis).astype(jnp.float32).astype(jnp.bfloat16)


def as_bf16(values):
    return values.astype(jnp.float32).astype(jnp.bfloat16)


def equal_ones(left, right):
    one = jnp.ones((), jnp.bfloat16)
    return jnp.where(left == right, one, jnp.zeros((), jnp.bfloat16))


def within(place, block):
    place = place - 256 * block
    return as_bf16(jnp.where((place >= 0) & (place < 256), place, -1))


def look_up(table_row, id_row, numbers, values):
    full = table_row.shape[1]
    ids = id_row.shape[1]
    high_count = up_to(-(-full // 64), 16)
    table_high = equal_ones(numbers[:high_count], as_bf16(table_row >> 6))
    low = as_bf16(table_row & 63)
    zero = jnp.zeros((), jnp.bfloat16)
    table_low = jnp.concatenate(
        [jnp.where(numbers[:64] == low, part, zero) for part in values], axis=0
    )
    square = lax.dot_general(
        table_low, table_high, (((1,), (1,)), ((), ())), preferred_element_type=jnp.float32
    )
    id_high = equal_ones(numbers[:high_count, :ids], as_bf16(id_row >> 6))
    spread = jnp.dot(square.astype(jnp.bfloat16), id_high, preferred_element_type=jnp.float32)
    wanted = iota((64, ids), 0) == (id_row & 63)
    return [
        jnp.sum(jnp.where(wanted, spread[64 * n : 64 * n + 64], 0.0), axis=0, keepdims=True)
        for n in range(len(values))
    ]


def numbers_for(full):
    return counting((max(up_to(-(-full // 64), 16), 64), full), 0)


def segment_plan(counts, experts, rows):
    starts = []
    running = jnp.zeros((rows, LANES), jnp.float32)
    for e in range(experts):
        starts.append(running)
        running = running + counts[e * rows : (e + 1) * rows]
    start = jnp.concatenate(starts, axis=0)
    lead = jnp.floor(start * (1.0 / TILE))
    tail = jnp.floor((start + counts + (TILE - 1.0)) * (1.0 / TILE))
    tiles = jnp.where(counts > 0.0, tail - lead, 0.0)
    pairs = experts * rows
    line = iota((pairs, pairs), 0)
    column = iota((pairs, pairs), 1)
    earlier = ones_where((line // rows == column // rows) & (column < line))
    base = jnp.dot(earlier, tiles.astype(jnp.bfloat16), preferred_element_type=jnp.float32)
    return start, lead, tiles, base


def write_plan(plan_ref, start, lead, tiles, base):
    shared = start - lead * TILE
    for n, part in enumerate((lead, tiles, base, shared)):
        plan_ref[n] = part.astype(jnp.int32)


def outgoing_kernel(lines, rows, new_ref, held_ref, stack_ref, plan_ref):
    experts = new_ref.shape[0]
    width = held_ref.shape[1]
    real = iota((1, width), 1) < lines
    hits = []
    full = new_ref.shape[1]
    numbers = numbers_for(full)
    slot = iota((64, full), 1).astype(jnp.float32)
    values = (jnp.floor((slot + 0.5) * (1.0 / lines)).astype(jnp.bfloat16),)
    for e in range(experts):
        (peer,) = look_up(new_ref[e : e + 1, :], held_ref[e : e + 1, :], numbers, values)
        peer = peer.astype(jnp.int32)
        hits.append(jnp.where((iota((rows, width), 0) == peer) & real, 1.0, 0.0))
    hits = jnp.concatenate(hits, axis=0)
    until = ones_where(iota((width, width), 0) <= iota((width, width), 1))
    ranks = jnp.dot(hits.astype(jnp.bfloat16), until, preferred_element_type=jnp.float32)
    counts = jnp.broadcast_to(jnp.sum(hits, axis=1, keepdims=True), (experts * rows, LANES))
    start, lead, tiles, base = segment_plan(counts, experts, rows)
    write_plan(plan_ref, start, lead, tiles, base)
    offset = (base * TILE + start - lead * TILE - 1.0)[:, :1]
    placed = hits * (ranks + offset)
    for e in range(experts):
        row = jnp.sum(placed[e * rows : (e + 1) * rows], axis=0, keepdims=True)
        stack_ref[e] = jnp.where(real, row, -1.0).astype(jnp.int32)


def incoming_kernel(lines, rows, old_ref, wanted_ref, stack_ref, plan_ref):
    experts = old_ref.shape[0]
    width = wanted_ref.shape[1]
    real = iota((1, width), 1) < lines
    held_at = []
    hits = []
    full = old_ref.shape[1]
    numbers = numbers_for(full)
    slot = iota((64, full), 1)
    values = (as_bf16(slot >> 7), as_bf16(slot & 127))
    for e in range(experts):
        high, low = look_up(old_ref[e : e + 1, :], wanted_ref[e : e + 1, :], numbers, values)
        slots = high * 128.0 + low
        held_at.append(jnp.where(real, slots, 1e9))
        peer = jnp.floor((slots + 0.5) * (1.0 / lines)).astype(jnp.int32)
        hits.append(jnp.where((iota((rows, width), 0) == peer) & real, 1.0, 0.0))
    hits = jnp.concatenate(hits, axis=0)
    counts = jnp.broadcast_to(jnp.sum(hits, axis=1, keepdims=True), (experts * rows, LANES))
    start, lead, tiles, base = segment_plan(counts, experts, rows)
    write_plan(plan_ref, start, lead, tiles, base)
    blank = jnp.zeros((LANES - experts, width), jnp.float32)
    columns = jnp.transpose(jnp.concatenate(held_at + [blank], axis=0))
    rows_out = []
    for e in range(experts):
        mine = slice(e * rows, (e + 1) * rows)
        before = jnp.where(columns[:, e : e + 1] < held_at[e], 1.0, 0.0)
        rank = jnp.sum(before, axis=0, keepdims=True)
        ahead = jnp.zeros((1, LANES), jnp.float32)
        firsts = []
        for r in range(rows):
            firsts.append(ahead)
            ahead = ahead + counts[e * rows + r : e * rows + r + 1]
        first = jnp.concatenate(firsts, axis=0)
        offset = (base[mine] * TILE + start[mine] - lead[mine] * TILE - first)[:, :1]
        rows_out.append(jnp.sum(hits[mine] * (rank + offset), axis=0, keepdims=True))
    stack_ref[...] = jnp.transpose(jnp.concatenate(rows_out + [blank], axis=0))


STRAIGHT = 8


def tile_at(index):
    return pl.ds(pl.multiple_of(index * TILE, TILE), TILE)


def pack_kernel(rows, plan_ref, place_ref, lines_ref, out_ref, stage_ref, number_ref):
    e = pl.program_id(0)
    pairs = pl.num_programs(0) * rows
    deep, _ = stage_ref.shape
    lines = lines_ref.shape[2]

    @pl.when(e == 0)
    def _():
        number_ref[...] = counting(number_ref.shape, 0)

    place = place_ref[0][:, :lines]
    source_lines = lines_ref[0, 0]
    for first in range(0, deep, 256):
        count = min(256, deep - first)
        onehot = equal_ones(number_ref[:count], within(place, first // 256))
        stage_ref[first : first + count] = jnp.dot(
            onehot, source_lines, preferred_element_type=jnp.float32
        ).astype(jnp.bfloat16)

    def one_peer(d, carry):
        k = e * rows + d
        lead = plan_ref[k]
        tiles = plan_ref[pairs + k]
        base = plan_ref[2 * pairs + k]
        shared = plan_ref[3 * pairs + k] > 0

        @pl.when(tiles > 0)
        def _():
            earlier = out_ref[d, tile_at(lead), :]
            for t in range(1, STRAIGHT):
                n = jnp.minimum(t, tiles - 1)
                out_ref[d, tile_at(lead + n), :] = stage_ref[tile_at(base + n), :]
            earlier = jnp.where(shared, earlier, jnp.zeros_like(earlier))
            out_ref[d, tile_at(lead), :] = earlier + stage_ref[tile_at(base), :]

        def put(t, c):
            out_ref[d, tile_at(lead + t), :] = stage_ref[tile_at(base + t), :]
            return c

        return lax.fori_loop(STRAIGHT, tiles, put, carry)

    lax.fori_loop(0, rows, one_peer, 0, unroll=rows <= 8)


def unpack_kernel(rows, plan_ref, place_ref, block_ref, *rest):
    out_ref, stage_ref, number_ref = rest[-3:]
    e = pl.program_id(0)
    pairs = pl.num_programs(0) * rows
    deep, _ = stage_ref.shape
    lines = out_ref.shape[2]

    @pl.when(e == 0)
    def _():
        stage_ref[...] = jnp.zeros_like(stage_ref)
        number_ref[...] = counting(number_ref.shape, 1)

    def one_peer(s, carry):
        k = e * rows + s
        lead = plan_ref[k]
        tiles = plan_ref[pairs + k]
        base = plan_ref[2 * pairs + k]

        @pl.when(tiles > 0)
        def _():
            for t in range(STRAIGHT):
                n = jnp.minimum(t, tiles - 1)
                stage_ref[tile_at(base + n), :] = block_ref[s, tile_at(lead + n), :]

        def put(t, c):
            stage_ref[tile_at(base + t), :] = block_ref[s, tile_at(lead + t), :]
            return c

        return lax.fori_loop(STRAIGHT, tiles, put, carry)

    lax.fori_loop(0, rows, one_peer, 0, unroll=rows <= 8)
    place = jnp.where(iota((lines, LANES), 1) == e, place_ref[:lines, :], 0.0)
    place = jnp.sum(place, axis=1, keepdims=True).astype(jnp.int32)
    onehot = jnp.concatenate(
        [equal_ones(number_ref[...], within(place, block)) for block in range(deep // 256)], axis=1
    )
    out_ref[0, 0] = jnp.dot(
        onehot, stage_ref[...], preferred_element_type=jnp.float32
    ).astype(jnp.bfloat16)


def call_plan(kernel, name, table, ids, lines, rows, transposed):
    experts, width = ids.shape
    stack = (
        jax.ShapeDtypeStruct((width, LANES), jnp.float32)
        if transposed
        else jax.ShapeDtypeStruct((experts, 1, width), jnp.int32)
    )
    stack, plan = pl.pallas_call(
        functools.partial(kernel, lines, rows),
        out_shape=(stack, jax.ShapeDtypeStruct((4, experts * rows, LANES), jnp.int32)),
        compiler_params=params(),
        cost_estimate=pl.CostEstimate(
            flops=20 * experts * table.shape[1] * 256,
            bytes_accessed=8 * table.size,
            transcendentals=0,
        ),
        name=name,
    )(table, ids)
    return stack, plan[:, :, 0].reshape(-1)


def pack(expert_lines, place, plan, piece, rows, block_rows, deep):
    experts, _, lines, _ = expert_lines.shape
    part, column, width = piece
    return pl.pallas_call(
        functools.partial(pack_kernel, rows),
        grid_spec=pltpu.PrefetchScalarGridSpec(
            num_scalar_prefetch=1,
            grid=(experts,),
            in_specs=[
                pl.BlockSpec((1, 1, place.shape[2]), lambda e, plan: (e, 0, 0)),
                pl.BlockSpec((1, 1, lines, width), lambda e, plan: (e, part, 0, column)),
            ],
            out_specs=pl.BlockSpec((rows, block_rows, width), lambda e, plan: (0, 0, 0)),
            scratch_shapes=[
                pltpu.VMEM((deep, width), jnp.bfloat16),
                pltpu.VMEM((256, lines), jnp.bfloat16),
            ],
        ),
        out_shape=jax.ShapeDtypeStruct((rows, block_rows, width), jnp.bfloat16),
        compiler_params=params(),
        cost_estimate=pl.CostEstimate(
            flops=2 * experts * deep * lines * width,
            bytes_accessed=4 * experts * lines * width,
            transcendentals=0,
        ),
        name="pack_lines",
    )(plan, place, expert_lines)


def unpack(arrived, place, plan, piece, shape, deep, previous):
    experts, _, lines, _ = shape
    part, column, width = piece
    rows, block_rows, _ = arrived.shape
    in_specs = [
        pl.BlockSpec(place.shape, lambda e, plan: (0, 0)),
        pl.BlockSpec((rows, block_rows, width), lambda e, plan: (0, 0, 0)),
    ]
    operands = [plan, place, arrived]
    aliases = {}
    if previous is not None:
        in_specs.append(pl.BlockSpec(memory_space=pl.ANY))
        operands.append(previous)
        aliases = {3: 0}
    return pl.pallas_call(
        functools.partial(unpack_kernel, rows),
        grid_spec=pltpu.PrefetchScalarGridSpec(
            num_scalar_prefetch=1,
            grid=(experts,),
            in_specs=in_specs,
            out_specs=pl.BlockSpec((1, 1, lines, width), lambda e, plan: (e, part, 0, column)),
            scratch_shapes=[
                pltpu.VMEM((deep, width), jnp.bfloat16),
                pltpu.VMEM((lines, 256), jnp.bfloat16),
            ],
        ),
        out_shape=jax.ShapeDtypeStruct(shape, jnp.bfloat16),
        input_output_aliases=aliases,
        compiler_params=params(),
        cost_estimate=pl.CostEstimate(
            flops=2 * experts * deep * lines * width,
            bytes_accessed=4 * experts * lines * width,
            transcendentals=0,
        ),
        name="unpack_lines",
    )(*operands)


def after_kernel(*refs):
    del refs


def after(values, signals):
    anywhere = pl.BlockSpec(memory_space=pl.ANY)
    return pl.pallas_call(
        after_kernel,
        in_specs=[anywhere] * (len(values) + len(signals)),
        out_specs=[anywhere] * len(values),
        out_shape=[jax.ShapeDtypeStruct(v.shape, v.dtype) for v in values],
        input_output_aliases={n: n for n in range(len(values))},
        name="after",
    )(*values, *signals)


def own_ids(table, lines, width):
    mine = lax.dynamic_slice_in_dim(table, lax.axis_index("row") * lines, lines, 1)
    return jnp.pad(mine, ((0, 0), (0, width - lines)), constant_values=-1)


def from_peer(block, axis, offset):
    size = lax.axis_size(axis)
    return lax.ppermute(block, axis, [(i, i ^ offset) for i in range(size)])


def bulk_pieces(parts, width):
    return [(part, 0, width) for part in range(parts)]


class Migration:
    def __init__(self, expert_lines, old_lines, new_lines):
        rows = lax.axis_size("row")
        experts, parts, lines, width = expert_lines.shape
        padded = up_to(lines, LANES)
        block_rows = up_to(experts * lines // rows, TILE)
        self.deep = up_to(lines + 2 * (TILE - 1) * rows, TILE)
        self.shape = expert_lines.shape
        self.pieces = bulk_pieces(parts, width)
        out_place, out_plan = call_plan(
            outgoing_kernel, "outgoing_plan", new_lines, own_ids(old_lines, lines, padded),
            lines, rows, False,
        )
        self.in_place, self.in_plan = call_plan(
            incoming_kernel, "incoming_plan", old_lines, own_ids(new_lines, lines, padded),
            lines, rows, True,
        )
        self.packed = [
            pack(expert_lines, out_place, out_plan, piece, rows, block_rows, self.deep)
            for piece in self.pieces
        ]
        self.arrived = []
        self.moved = None

    def send(self, signals=()):
        block = self.packed[len(self.arrived)]
        if signals:
            (block,) = after([block], signals)
        self.arrived.append(
            lax.all_to_all(block, "row", split_axis=0, concat_axis=0, tiled=True)
        )

    def receive(self, piece):
        self.moved = unpack(
            self.arrived[piece], self.in_place, self.in_plan, self.pieces[piece], self.shape,
            up_to(self.deep, 256), self.moved,
        )


def attend(queries, new_kv, prompt_kv, suffix_kv, lengths):
    seq_count = queries.shape[0]
    prompt_rows = prompt_kv.shape[2]
    suffix_rows = suffix_kv.shape[2]
    col_index = lax.axis_index("col")
    query_heads = queries.reshape(seq_count, KVH, REP, HD)
    prompt_keys = prompt_kv[0, 0].reshape(prompt_rows, KVH, HD)
    prompt_values = prompt_kv[0, 1].reshape(prompt_rows, KVH, HD)
    suffix_keys = suffix_kv[:, 0].reshape(seq_count, suffix_rows, KVH, HD)
    suffix_values = suffix_kv[:, 1].reshape(seq_count, suffix_rows, KVH, HD)
    own_keys = new_kv[:, 0].reshape(seq_count, KVH, HD)
    own_values = new_kv[:, 1].reshape(seq_count, KVH, HD)
    score_scale = HD ** (-0.5)
    prompt_scores = (
        jnp.einsum("skgd,pkd->skgp", query_heads, prompt_keys, preferred_element_type=jnp.float32)
        * score_scale
    )
    suffix_scores = (
        jnp.einsum("skgd,spkd->skgp", query_heads, suffix_keys, preferred_element_type=jnp.float32)
        * score_scale
    )
    own_scores = (
        jnp.einsum("skgd,skd->skg", query_heads, own_keys, preferred_element_type=jnp.float32)
        * score_scale
    )
    positions = col_index * suffix_rows + jnp.arange(suffix_rows, dtype=jnp.int32)
    live_slots = (positions[None, :] < lengths[:, None])[:, None, None, :]
    holder = col_index == 0
    suffix_scores = jnp.where(live_slots, suffix_scores, neg_big)
    own_scores = jnp.where(holder, own_scores, neg_big)
    highest = jnp.maximum(
        jnp.maximum(jnp.max(prompt_scores, axis=-1), jnp.max(suffix_scores, axis=-1)), own_scores
    )
    prompt_weights = jnp.exp(prompt_scores - highest[..., None])
    suffix_weights = jnp.where(live_slots, jnp.exp(suffix_scores - highest[..., None]), 0.0)
    own_weights = jnp.where(holder, jnp.exp(own_scores - highest), 0.0)
    totals = jnp.sum(prompt_weights, axis=-1) + jnp.sum(suffix_weights, axis=-1) + own_weights
    mixture = jnp.einsum(
        "skgp,pkd->skgd",
        prompt_weights.astype(jnp.bfloat16),
        prompt_values,
        preferred_element_type=jnp.float32,
    )
    mixture = mixture + jnp.einsum(
        "skgp,spkd->skgd",
        suffix_weights.astype(jnp.bfloat16),
        suffix_values,
        preferred_element_type=jnp.float32,
    )
    own_rounded = lax.optimization_barrier(own_weights.astype(jnp.bfloat16)).astype(jnp.float32)
    mixture = mixture + own_rounded[..., None] * own_values.astype(jnp.float32)[:, :, None, :]
    heads = KVH * REP
    bundle = jnp.concatenate(
        [
            mixture.reshape(seq_count, heads * HD),
            highest.reshape(seq_count, heads),
            totals.reshape(seq_count, heads),
            jnp.zeros((seq_count, LANES - 2 * heads), jnp.float32),
        ],
        axis=1,
    )
    bundles = [bundle] + [from_peer(bundle, "col", o) for o in range(1, lax.axis_size("col"))]
    every = jnp.stack(bundles)
    mixtures = every[:, :, : heads * HD].reshape(-1, seq_count, heads, HD)
    peaks = every[:, :, heads * HD : heads * HD + heads]
    sums = every[:, :, heads * HD + heads : heads * HD + 2 * heads]
    factors = jnp.exp(peaks - jnp.max(peaks, axis=0))
    total = jnp.sum(sums * factors, axis=0)
    mixed = jnp.sum(mixtures * factors[..., None], axis=0)
    return (mixed / total[..., None]).astype(jnp.bfloat16).reshape(seq_count, heads * HD)


def gate_up_kernel(me_ref, h_ref, gain_ref, router_ref, routes_ref, gate_ref, up_ref, out_ref, acc_ref):
    e = pl.program_id(0)
    tokens = h_ref.shape[0]
    lines = gate_ref.shape[2]
    padded = out_ref.shape[3]
    h = h_ref[...].astype(jnp.float32)
    scaled = (h * gain_ref[...].astype(jnp.float32)).astype(jnp.bfloat16)

    @pl.when(e == 0)
    def _():
        acc_ref[...] = jnp.zeros_like(acc_ref)

    against = (((1,), (1,)), ((), ()))
    gate = lax.dot_general(scaled, gate_ref[0, 0], against, preferred_element_type=jnp.float32)
    up = lax.dot_general(scaled, up_ref[0, 0], against, preferred_element_type=jnp.float32)
    for k in range(routes_ref.shape[1]):
        chosen = routes_ref[:, k : k + 1] == e
        acc_ref[2 * k, :, :lines] += jnp.where(chosen, gate, 0.0)
        acc_ref[2 * k + 1, :, :lines] += jnp.where(chosen, up, 0.0)

    @pl.when(e == pl.num_programs(0) - 1)
    def _():
        last = padded - LANES
        shift = lines - last
        experts = pl.num_programs(0)
        extra = jnp.dot(scaled, router_ref[...], preferred_element_type=jnp.float32)
        lane = iota((tokens, LANES), 1)
        square = jnp.sum(h * h, axis=1, keepdims=True)
        extra = jnp.where(lane == shift + experts, square, extra)
        high = extra.astype(jnp.bfloat16).astype(jnp.float32)
        low = extra - high
        acc_ref[0, :, last:] += jnp.where(lane >= shift, high, 0.0)
        acc_ref[1, :, last:] += jnp.where(lane >= shift, low, 0.0)
        peers, _, share, _ = out_ref.shape
        me = me_ref[0]
        for o in range(peers):
            begin = pl.multiple_of((me ^ o) * share, share)
            out_ref[o] = acc_ref[:, pl.ds(begin, share), :].astype(jnp.bfloat16)


def activate_kernel(lines, experts, model_width, routes_ref, *refs):
    out_ref = refs[-1]
    summed = refs[0][...].astype(jnp.float32)
    for ref in refs[1:-1]:
        summed = summed + ref[...].astype(jnp.float32)
    _, share, padded = summed.shape
    last = padded - LANES
    shift = lines - last
    extra = summed[0, :, last:] + summed[1, :, last:]
    lane = iota((share, LANES), 1)
    square = jnp.sum(jnp.where(lane == shift + experts, extra, 0.0), axis=1, keepdims=True)
    inverse_rms = lax.rsqrt(square / model_width + norm_eps)
    logits = []
    for k in range(out_ref.shape[0]):
        wanted = lane == routes_ref[:, k : k + 1] + shift
        logits.append(jnp.sum(jnp.where(wanted, extra, 0.0), axis=1, keepdims=True) * inverse_rms)
    peak = functools.reduce(jnp.maximum, logits)
    shares = [jnp.exp(v - peak) for v in logits]
    total = functools.reduce(jnp.add, shares)
    inside = iota((share, padded), 1) < lines
    for k in range(out_ref.shape[0]):
        gate = summed[2 * k] * inverse_rms
        up = summed[2 * k + 1] * inverse_rms
        act = gate / (1.0 + jnp.exp(-gate)) * up
        out_ref[k] = jnp.where(inside, act * (shares[k] / total), 0.0).astype(jnp.bfloat16)


def down_kernel(me_ref, routes_ref, *refs):
    down_ref, out_ref, act_ref = refs[-3:]
    chunks = refs[:-3]
    e = pl.program_id(0)
    topk, share, _ = chunks[0].shape
    lines = down_ref.shape[2]

    @pl.when(e == 0)
    def _():
        me = me_ref[0]
        out_ref[...] = jnp.zeros_like(out_ref)
        for o, chunk in enumerate(chunks):
            begin = pl.multiple_of((me ^ o) * share, share)
            act_ref[:, pl.ds(begin, share), :] = chunk[...]

    mine = jnp.zeros((act_ref.shape[1], lines), jnp.float32)
    for k in range(topk):
        chosen = routes_ref[:, k : k + 1] == e
        mine = mine + jnp.where(chosen, act_ref[k, :, :lines].astype(jnp.float32), 0.0)
    out_ref[...] += jnp.dot(
        mine.astype(jnp.bfloat16), down_ref[0, 0], preferred_element_type=jnp.float32
    )


def experts_part(h_mid, moe_gain, w_router, expert_lines, routes, migration):
    rows = lax.axis_size("row")
    cols = lax.axis_size("col")
    row_index = lax.axis_index("row")
    col_index = lax.axis_index("col")
    experts, _, lines, width = expert_lines.shape
    own, _ = h_mid.shape
    tokens = own * rows
    topk = routes.shape[1]
    share = tokens // cols
    padded = up_to(lines + experts + 1, LANES)
    shift = lines - (padded - LANES)
    me = col_index.astype(jnp.int32).reshape(1)

    order = row_index ^ jnp.arange(rows, dtype=jnp.int32)
    routes = routes.reshape(rows, own, topk)[order].reshape(tokens, topk)
    my_routes = lax.dynamic_slice_in_dim(routes, col_index * share, share, 0)
    router = jnp.pad(w_router, ((0, 0), (shift, LANES - shift - experts)))
    every_h = jnp.concatenate(
        [h_mid] + [from_peer(h_mid, "row", o) for o in range(1, rows)], axis=0
    )
    migration.send([every_h])
    part_spec = lambda part: pl.BlockSpec((1, 1, lines, width), lambda e, me: (e, part, 0, 0))
    whole = lambda a: pl.BlockSpec(a.shape, lambda e, me: (0,) * a.ndim)
    gain = moe_gain.reshape(1, width)
    partial = pl.pallas_call(
        gate_up_kernel,
        grid_spec=pltpu.PrefetchScalarGridSpec(
            num_scalar_prefetch=1,
            grid=(experts,),
            in_specs=[whole(every_h), whole(gain), whole(router), whole(routes)]
            + [part_spec(0), part_spec(1)],
            out_specs=pl.BlockSpec((cols, 2 * topk, share, padded), lambda e, me: (0, 0, 0, 0)),
            scratch_shapes=[pltpu.VMEM((2 * topk, tokens, padded), jnp.float32)],
        ),
        out_shape=jax.ShapeDtypeStruct((cols, 2 * topk, share, padded), jnp.bfloat16),
        compiler_params=params(),
        cost_estimate=pl.CostEstimate(
            flops=4 * experts * tokens * lines * width,
            bytes_accessed=4 * experts * lines * width,
            transcendentals=0,
        ),
        name="gate_up",
    )(me, every_h, gain, router, routes, expert_lines, expert_lines)
    gathered = [partial[0]] + [from_peer(partial[o], "col", o) for o in range(1, cols)]
    activated = pl.pallas_call(
        functools.partial(activate_kernel, lines, experts, width * cols),
        out_shape=jax.ShapeDtypeStruct((topk, share, padded), jnp.bfloat16),
        compiler_params=params(),
        name="activate",
    )(my_routes, *gathered)
    chunks = [activated] + [from_peer(activated, "col", o) for o in range(1, cols)]
    produced = pl.pallas_call(
        down_kernel,
        grid_spec=pltpu.PrefetchScalarGridSpec(
            num_scalar_prefetch=1,
            grid=(experts,),
            in_specs=[whole(routes)] + [whole(c) for c in chunks] + [part_spec(2)],
            out_specs=pl.BlockSpec((tokens, width), lambda e, me: (0, 0)),
            scratch_shapes=[pltpu.VMEM((topk, tokens, padded), jnp.bfloat16)],
        ),
        out_shape=jax.ShapeDtypeStruct((tokens, width), jnp.float32),
        compiler_params=params(),
        cost_estimate=pl.CostEstimate(
            flops=2 * experts * tokens * lines * width,
            bytes_accessed=2 * experts * lines * width,
            transcendentals=0,
        ),
        name="down",
    )(me, routes, *chunks, expert_lines)
    migration.receive(0)
    (produced,) = after([produced], [migration.moved])
    blocks = produced.reshape(rows, own, width)
    mixed = blocks[0]
    for o in range(1, rows):
        mixed = mixed + from_peer(blocks[o], "row", o)
    return mixed


def local(
    hidden,
    queries,
    new_kv,
    prompt_kv,
    suffix_kv,
    lengths,
    w_out,
    moe_gain,
    w_router,
    expert_weights,
    old_lines,
    new_lines,
    routes,
):
    expert_lines = jnp.transpose(expert_weights, (0, 2, 1, 3))
    migration = Migration(expert_lines, old_lines, new_lines)
    for _ in range(len(migration.pieces) - 2):
        migration.send()
    attended = attend(queries, new_kv, prompt_kv, suffix_kv, lengths)
    projected = jnp.dot(attended, w_out, preferred_element_type=jnp.float32)
    h_mid = (hidden.astype(jnp.float32) + projected).astype(jnp.bfloat16)
    (h_mid,) = after([h_mid], migration.packed)
    mixed = experts_part(h_mid, moe_gain, w_router, expert_lines, routes, migration)
    migration.send([mixed])
    for piece in range(1, len(migration.pieces)):
        migration.receive(piece)
    return (h_mid.astype(jnp.float32) + mixed, jnp.transpose(migration.moved, (0, 2, 1, 3)))


def solution(mesh):
    return jax.shard_map(
        local,
        mesh=mesh,
        in_specs=(
            P("row", "col"),
            P("row", None),
            P("row", None, None),
            P("row", None, "col", None),
            P("row", None, "col", None),
            P("row"),
            P(None, "col"),
            P("col"),
            P("col", None),
            P(None, "row", None, "col"),
            P(),
            P(),
            P(),
        ),
        out_specs=(P("row", "col"), P(None, "row", None, "col")),
        check_vma=False,
    )
```

profile of v0, /device:TPU:0, one launch (start us, length us, event | category | flops | bytes accessed | tf_op | source)
XLA Modules:
  0.0 265.5 jit_solution(12367617812972121739)
XLA Ops:
  2.4 6.1 %outgoing_plan.1 = (s32[8,1,768]{2,1,0:T(1,128)S(1)}, s32[4,64,128]{2,1,0:T(8,128)S(1)}) custom-call(s32[8,5632]{1,0:T(8,128)S(1)} %copy-done.6, s32[8,768]{1,0:T(8,128)S(1)} %pad.11.held_ref), custom_call_target="tpu_custom_call" | custom-call | flops 230686720 | bytes 360448 | tf_op jit(solution)/shard_map/outgoing_plan/pallas_call | solution.py:268
  8.7 11.9 %pack_lines.3.refs_1_ = bf16[8,704,512]{2,1,0:T(8,128)(2,1)S(1)} custom-call(s32[256]{0:T(256)S(1)} %reshape_squeeze.27.plan_ref, s32[8,1,768]{2,1,0:T(1,128)S(1)} %get-tuple-element.7.place_ref, bf16[8,3,704,512]{3,2,1,0:T(8,128)(2,1)} %bitcast.83), custom_call_target="tpu_custom_call" | custom-call | flops 5444206592 | bytes 11534336 | tf_op jit(solution)/shard_map/pack_lines/pallas_call | solution.py:285
  20.7 2.5 copy-done.2
  23.2 5.2 %all-to-all-start = ((bf16[8,704,512]{2,1,0:T(8,128)(2,1)}), bf16[8,704,512]{2,1,0:T(8,128)(2,1)}, u32[]{:S(2)}, u32[]{:S(2)}) async-start(bf16[8,704,512]{2,1,0:T(8,128)(2,1)} %copy-done.2), calls=%async_computation | async-start | bytes 11534336 | tf_op jit(solution)/shard_map/all_to_all | solution.py:408
  30.6 1.7 fusion.34
  34.8 3.2 %fusion.38 = (f32[8,16,2]{2,1,0:T(8,128)}, f32[8,16,2,32]{3,2,1,0:T(2,128)}) fusion(bf16[8,32,16,128]{3,2,1,0:T(8,128)(2,1)} %bitcast.107, bf16[8,16,2,128]{3,0,2,1:T(8,128)(2,1)} %bitcast.112, pred[8,32]{1,0:T(8,128)(4,1)S(1)} %broadcast_compare_fusion), kind=kOutput, calls=%fused_computation.77 | convolution fusion | flops 2121472 | bytes 1148160 | tf_op jit(solution)/shard_map/skgd,spkd->skgp/dot_general | solution.py:436
  38.0 1.8 fusion.17
  47.5 4.8 %collective-permute-start.2 = (f32[8,4224]{1,0:T(8,128)S(1)}, f32[8,4224]{1,0:T(8,128)S(1)}, u32[]{:S(2)}, u32[]{:S(2)}) collective-permute-start(f32[8,4224]{1,0:T(8,128)S(1)} %concatenate.6), channel_id=1, source_target_pairs={{0,3},{1,2},{2,1},{3,0},{4,7},{5,6},{6,5},{7,4},{8,11},{9,10},{10,... | collective-permute-start | bytes 405512 | tf_op jit(solution)/shard_map/ppermute | solution.py:372
  52.9 11.9 %pack_lines.4.refs_2_.refs_0_ = bf16[8,704,512]{2,1,0:T(8,128)(2,1)S(1)} custom-call(s32[256]{0:T(256)S(1)} %reshape_squeeze.27.plan_ref, s32[8,1,768]{2,1,0:T(1,128)S(1)} %get-tuple-element.7.place_ref, bf16[8,3,704,512]{3,2,1,0:T(8,128)(2,1)} %bitcast.84), custom_call_target="tpu_custom_call" | custom-call | flops 5444206592 | bytes 11534336 | tf_op jit(solution)/shard_map/pack_lines/pallas_call | solution.py:285
  64.9 2.5 copy-done.1
  67.4 11.9 %pack_lines.5.refs_3_.refs_0_ = bf16[8,704,512]{2,1,0:T(8,128)(2,1)S(1)} custom-call(s32[256]{0:T(256)S(1)} %reshape_squeeze.27.plan_ref, s32[8,1,768]{2,1,0:T(1,128)S(1)} %get-tuple-element.7.place_ref, bf16[8,3,704,512]{3,2,1,0:T(8,128)(2,1)} %bitcast.85), custom_call_target="tpu_custom_call" | custom-call | flops 5444206592 | bytes 11534336 | tf_op jit(solution)/shard_map/pack_lines/pallas_call | solution.py:285
  79.3 2.5 copy-done
  82.3 3.5 %fusion.4.refs_0_ = bf16[8,512]{1,0:T(8,128)(2,1)} fusion(bf16[4096,512]{1,0:T(8,128)(2,1)} %param.19, f32[8,4096]{1,0:T(8,128)S(1)} %fusion.8, f32[8,32]{0,1:T(8,128)S(1)} %copy.127, bf16[8,512]{1,0:T(8,128)(2,1)S(1)} %copy-done.9), kind=kOutput, calls=%fused_computation.9 | convolution fusion | flops 33632256 | bytes 4342784 | tf_op jit(solution)/shard_map/dot_general | solution.py:680
  86.5 1.7 collective-permute-start.4
  88.4 1.7 collective-permute-start.6
  90.1 2.5 collective-permute-start.8
  95.2 2.9 %collective-permute-done.9 = bf16[8,512]{1,0:T(8,128)(2,1)S(1)} collective-permute-done((bf16[8,512]{1,0:T(8,128)(2,1)}, bf16[8,512]{1,0:T(8,128)(2,1)S(1)}, u32[]{:S(2)}, u32[]{:S(2)}) %collective-permute-start.9) | collective-permute-done | bytes 8224 | tf_op jit(solution)/shard_map/ppermute | solution.py:372
  98.8 5.1 %all-to-all-start.2 = ((bf16[8,704,512]{2,1,0:T(8,128)(2,1)}), bf16[8,704,512]{2,1,0:T(8,128)(2,1)}, u32[]{:S(2)}, u32[]{:S(2)}) async-start(bf16[8,704,512]{2,1,0:T(8,128)(2,1)} %after.7), calls=%async_computation.2 | async-start | bytes 11534336 | tf_op jit(solution)/shard_map/all_to_all | solution.py:408
  105.8 9.8 %incoming_plan.1 = (f32[768,128]{1,0:T(8,128)S(1)}, s32[4,64,128]{2,1,0:T(8,128)S(1)}) custom-call(s32[8,5632]{1,0:T(8,128)S(1)} %copy-done.7, s32[8,768]{1,0:T(8,128)S(1)} %pad.13.wanted_ref), custom_call_target="tpu_custom_call" | custom-call | flops 230686720 | bytes 360448 | tf_op jit(solution)/shard_map/incoming_plan/pallas_call | solution.py:268
  115.6 8.8 %gate_up.1 = bf16[4,4,16,768]{3,2,1,0:T(8,128)(2,1)S(1)} custom-call(s32[1]{0:T(128)} %bitcast.20.me_ref, bf16[64,512]{1,0:T(8,128)(2,1)S(1)} %copy-done.5, bf16[1,512]{1,0:T(2,128)(2,1)S(1)} %reshape.114.gain_ref, bf16[512,128]{1,0:T(8,128)(2,1)S(1)} %pad.12.router_ref, s32[64,2]{1,0:T(8,128)S(1)} %bitcast.80, bf16[8,3,704,512]{3,2,1,0:T(8,128)(2,1)} %bitcast.86, ...), custom_call_target="tpu_custom_call" | custom-call | flops 738197504 | bytes 11534336 | tf_op jit(solution)/shard_map/gate_up/pallas_call | solution.py:606
  124.5 2.4 collective-permute-start.10
  126.9 2.5 collective-permute-start.11
  130.0 7.5 %collective-permute-done.11.refs_2_ = bf16[4,16,768]{2,1,0:T(8,128)(2,1)S(1)} collective-permute-done((bf16[4,16,768]{2,1,0:T(8,128)(2,1)S(1)}, bf16[4,16,768]{2,1,0:T(8,128)(2,1)S(1)}, u32[]{:S(2)}, u32[]{:S(2)}) %collective-permute-start.11) | collective-permute-done | bytes 98336 | tf_op jit(solution)/shard_map/ppermute | solution.py:372
  137.7 1.8 collective-permute-start.13
  142.4 3.0 %collective-permute-done.14.refs_2_ = bf16[2,16,768]{2,1,0:T(8,128)(2,1)S(1)} collective-permute-done((bf16[2,16,768]{2,1,0:T(8,128)(2,1)S(1)}, bf16[2,16,768]{2,1,0:T(8,128)(2,1)S(1)}, u32[]{:S(2)}, u32[]{:S(2)}) %collective-permute-start.14) | collective-permute-done | bytes 49184 | tf_op jit(solution)/shard_map/ppermute | solution.py:372
  146.8 6.1 %down.1.refs_0_ = f32[64,512]{1,0:T(8,128)S(1)} custom-call(s32[1]{0:T(128)} %bitcast.20.me_ref, s32[64,2]{1,0:T(8,128)S(1)} %bitcast.82, bf16[2,16,768]{2,1,0:T(8,128)(2,1)S(1)} %activate.1.refs_0_, bf16[2,16,768]{2,1,0:T(8,128)(2,1)S(1)} %collective-permute-done.13.refs_1_, bf16[2,16,768]{2,1,0:T(8,128)(2,1)S(1)} %collective-permute-done.14.refs_2_, ...), custom_call_target="tpu_custom_call" | custom-call | flops 369098752 | bytes 5767168 | tf_op jit(solution)/shard_map/down/pallas_call | solution.py:633
  153.6 14.9 %unpack_lines.3.refs_1_.rest_0_ = bf16[8,3,704,512]{3,2,1,0:T(8,128)(2,1)} custom-call(s32[256]{0:T(256)S(1)} %reshape_squeeze.28.plan_ref, f32[768,128]{1,0:T(8,128)S(1)} %get-tuple-element.9.place_ref, bf16[8,704,512]{2,1,0:T(8,128)(2,1)} %all-to-all-done.block_ref), custom_call_target="tpu_custom_call" | custom-call | flops 5905580032 | bytes 11534336 | tf_op jit(solution)/shard_map/unpack_lines/pallas_call | solution.py:325
  169.5 2.5 collective-permute-start.21
  179.9 5.0 %all-to-all-start.1 = ((bf16[8,704,512]{2,1,0:T(8,128)(2,1)}), bf16[8,704,512]{2,1,0:T(8,128)(2,1)}, u32[]{:S(2)}, u32[]{:S(2)}) async-start(bf16[8,704,512]{2,1,0:T(8,128)(2,1)} %after.6), calls=%async_computation.1 | async-start | bytes 11534336 | tf_op jit(solution)/shard_map/all_to_all | solution.py:408
  184.9 14.9 %unpack_lines.4.rest_0_ = bf16[8,3,704,512]{3,2,1,0:T(8,128)(2,1)} custom-call(s32[256]{0:T(256)S(1)} %reshape_squeeze.28.plan_ref, f32[768,128]{1,0:T(8,128)S(1)} %get-tuple-element.9.place_ref, bf16[8,704,512]{2,1,0:T(8,128)(2,1)} %all-to-all-done.2.block_ref, bf16[8,3,704,512]{3,2,1,0:T(8,128)(2,1)} %unpack_lines.3.refs_1_.rest_0_), custom_call_target="tpu_custom_call", output_to_operand_aliasing={{}: (3, {})} | custom-call | flops 5905580032 | bytes 11534336 | tf_op jit(solution)/shard_map/unpack_lines/pallas_call | solution.py:325
  199.8 50.8 %all-to-all-done.1.block_ref = bf16[8,704,512]{2,1,0:T(8,128)(2,1)} async-done(((bf16[8,704,512]{2,1,0:T(8,128)(2,1)}), bf16[8,704,512]{2,1,0:T(8,128)(2,1)}, u32[]{:S(2)}, u32[]{:S(2)}) %all-to-all-start.1) | async-done | bytes 5767200 | tf_op jit(solution)/shard_map/all_to_all | solution.py:408
  250.6 14.9 %unpack_lines.5 = bf16[8,3,704,512]{3,2,1,0:T(8,128)(2,1)} custom-call(s32[256]{0:T(256)S(1)} %reshape_squeeze.28.plan_ref, f32[768,128]{1,0:T(8,128)S(1)} %get-tuple-element.9.place_ref, bf16[8,704,512]{2,1,0:T(8,128)(2,1)} %all-to-all-done.1.block_ref, bf16[8,3,704,512]{3,2,1,0:T(8,128)(2,1)} %unpack_lines.4.rest_0_), custom_call_target="tpu_custom_call", output_to_operand_aliasing={{}: (3, {})} | custom-call | flops 5905580032 | bytes 11534336 | tf_op jit(solution)/shard_map/unpack_lines/pallas_call | solution.py:325
  (127 shorter events, 36.0 us)
Async XLA Ops:
  23.2 75.6 %all-to-all-start = ((bf16[8,704,512]{2,1,0:T(8,128)(2,1)}), bf16[8,704,512]{2,1,0:T(8,128)(2,1)}, u32[]{:S(2)}, u32[]{:S(2)}) async-start(bf16[8,704,512]{2,1,0:T(8,128)(2,1)} %copy-done.2), calls=%async_computation | async-start | bytes 11534336 | tf_op jit(solution)/shard_map/all_to_all | solution.py:408
  47.5 34.3 %collective-permute-start.2 = (f32[8,4224]{1,0:T(8,128)S(1)}, f32[8,4224]{1,0:T(8,128)S(1)}, u32[]{:S(2)}, u32[]{:S(2)}) collective-permute-start(f32[8,4224]{1,0:T(8,128)S(1)} %concatenate.6), channel_id=1, source_target_pairs={{0,3},{1,2},{2,1},{3,0},{4,7},{5,6},{6,5},{7,4},{8,11},{9,10},{10,... | collective-permute-start | bytes 405512 | tf_op jit(solution)/shard_map/ppermute | solution.py:372
  52.3 29.5 %collective-permute-start.1 = (f32[8,4224]{1,0:T(8,128)S(1)}, f32[8,4224]{1,0:T(8,128)S(1)}, u32[]{:S(2)}, u32[]{:S(2)}) collective-permute-start(f32[8,4224]{1,0:T(8,128)S(1)} %concatenate.6), channel_id=1, source_target_pairs={{0,2},{1,3},{2,0},{3,1},{4,6},{5,7},{6,4},{7,5},{8,10},{9,11},{10,... | collective-permute-start | bytes 405512 | tf_op jit(solution)/shard_map/ppermute | solution.py:372
  52.3 29.5 %collective-permute-start = (f32[8,4224]{1,0:T(8,128)S(1)}, f32[8,4224]{1,0:T(8,128)S(1)}, u32[]{:S(2)}, u32[]{:S(2)}) collective-permute-start(f32[8,4224]{1,0:T(8,128)S(1)} %concatenate.6), channel_id=1, source_target_pairs={{0,1},{1,0},{2,3},{3,2},{4,5},{5,4},{6,7},{7,6},{8,9},{9,8},{10,11... | collective-permute-start | bytes 405512 | tf_op jit(solution)/shard_map/ppermute | solution.py:372
  67.4 15.0 %copy-start.9 = (bf16[8,512]{1,0:T(8,128)(2,1)S(1)}, bf16[8,512]{1,0:T(8,128)(2,1)}, u32[]{:S(2)}) copy-start(bf16[8,512]{1,0:T(8,128)(2,1)} %param.13) | copy-start | bytes 24580
  85.8 4.3 %collective-permute-start.3 = (bf16[8,512]{1,0:T(8,128)(2,1)}, bf16[8,512]{1,0:T(8,128)(2,1)S(1)}, u32[]{:S(2)}, u32[]{:S(2)}) collective-permute-start(bf16[8,512]{1,0:T(8,128)(2,1)} %after.4), channel_id=1, source_target_pairs={{0,4},{4,0},{8,12},{12,8},{16,20},{20,16},{24,28},{28,24},{1,5},{5... | collective-permute-start | bytes 24584 | tf_op jit(solution)/shard_map/ppermute | solution.py:372
  86.5 7.4 %collective-permute-start.4 = (bf16[8,512]{1,0:T(8,128)(2,1)}, bf16[8,512]{1,0:T(8,128)(2,1)S(1)}, u32[]{:S(2)}, u32[]{:S(2)}) collective-permute-start(bf16[8,512]{1,0:T(8,128)(2,1)} %after.4), channel_id=1, source_target_pairs={{0,8},{4,12},{8,0},{12,4},{16,24},{20,28},{24,16},{28,20},{1,9},{5... | collective-permute-start | bytes 24584 | tf_op jit(solution)/shard_map/ppermute | solution.py:372
  88.2 6.1 %collective-permute-start.5 = (bf16[8,512]{1,0:T(8,128)(2,1)}, bf16[8,512]{1,0:T(8,128)(2,1)S(1)}, u32[]{:S(2)}, u32[]{:S(2)}) collective-permute-start(bf16[8,512]{1,0:T(8,128)(2,1)} %after.4), channel_id=1, source_target_pairs={{0,12},{4,8},{8,4},{12,0},{16,28},{20,24},{24,20},{28,16},{1,13},{... | collective-permute-start | bytes 24584 | tf_op jit(solution)/shard_map/ppermute | solution.py:372
  88.4 6.0 %collective-permute-start.6 = (bf16[8,512]{1,0:T(8,128)(2,1)}, bf16[8,512]{1,0:T(8,128)(2,1)S(1)}, u32[]{:S(2)}, u32[]{:S(2)}) collective-permute-start(bf16[8,512]{1,0:T(8,128)(2,1)} %after.4), channel_id=1, source_target_pairs={{0,16},{4,20},{8,24},{12,28},{16,0},{20,4},{24,8},{28,12},{1,17},{... | collective-permute-start | bytes 24584 | tf_op jit(solution)/shard_map/ppermute | solution.py:372
  90.1 4.9 %collective-permute-start.7 = (bf16[8,512]{1,0:T(8,128)(2,1)}, bf16[8,512]{1,0:T(8,128)(2,1)S(1)}, u32[]{:S(2)}, u32[]{:S(2)}) collective-permute-start(bf16[8,512]{1,0:T(8,128)(2,1)} %after.4), channel_id=1, source_target_pairs={{0,20},{4,16},{8,28},{12,24},{16,4},{20,0},{24,12},{28,8},{1,21},{... | collective-permute-start | bytes 24584 | tf_op jit(solution)/shard_map/ppermute | solution.py:372
  90.1 5.1 %collective-permute-start.8 = (bf16[8,512]{1,0:T(8,128)(2,1)}, bf16[8,512]{1,0:T(8,128)(2,1)S(1)}, u32[]{:S(2)}, u32[]{:S(2)}) collective-permute-start(bf16[8,512]{1,0:T(8,128)(2,1)} %after.4), channel_id=1, source_target_pairs={{0,24},{4,28},{8,16},{12,20},{16,8},{20,12},{24,0},{28,4},{1,25},{... | collective-permute-start | bytes 24584 | tf_op jit(solution)/shard_map/ppermute | solution.py:372
  93.9 4.2 %collective-permute-start.9 = (bf16[8,512]{1,0:T(8,128)(2,1)}, bf16[8,512]{1,0:T(8,128)(2,1)S(1)}, u32[]{:S(2)}, u32[]{:S(2)}) collective-permute-start(bf16[8,512]{1,0:T(8,128)(2,1)} %after.4), channel_id=1, source_target_pairs={{0,28},{4,24},{8,20},{12,16},{16,12},{20,8},{24,4},{28,0},{1,29},{... | collective-permute-start | bytes 24584 | tf_op jit(solution)/shard_map/ppermute | solution.py:372
  98.7 5.9 %copy-start.12 = (bf16[512]{0:T(512)(128)(2,1)S(1)}, bf16[512]{0:T(512)(128)(2,1)}, u32[]{:S(2)}) copy-start(bf16[512]{0:T(512)(128)(2,1)} %param.20) | copy-start | bytes 3076
  98.7 5.9 %copy-start.10 = (bf16[512,8]{0,1:T(8,128)(2,1)S(1)}, bf16[512,8]{0,1:T(8,128)(2,1)}, u32[]{:S(2)}) copy-start(bf16[512,8]{0,1:T(8,128)(2,1)} %param.21) | copy-start | bytes 24580
  98.7 7.1 %copy-start.7 = (s32[8,5632]{1,0:T(8,128)S(1)}, s32[8,5632]{1,0:T(8,128)}, u32[]{:S(2)}) copy-start(s32[8,5632]{1,0:T(8,128)} %old_ref.1) | copy-start | bytes 540676
  98.7 16.9 %copy-start.5 = (bf16[64,512]{1,0:T(8,128)(2,1)S(1)}, bf16[64,512]{1,0:T(8,128)(2,1)}, u32[]{:S(2)}) copy-start(bf16[64,512]{1,0:T(8,128)(2,1)} %copy-done.4) | copy-start | bytes 196612
  98.8 81.1 %all-to-all-start.2 = ((bf16[8,704,512]{2,1,0:T(8,128)(2,1)}), bf16[8,704,512]{2,1,0:T(8,128)(2,1)}, u32[]{:S(2)}, u32[]{:S(2)}) async-start(bf16[8,704,512]{2,1,0:T(8,128)(2,1)} %after.7), calls=%async_computation.2 | async-start | bytes 11534336 | tf_op jit(solution)/shard_map/all_to_all | solution.py:408
  124.5 5.5 %collective-permute-start.10 = (bf16[4,16,768]{2,1,0:T(8,128)(2,1)S(1)}, bf16[4,16,768]{2,1,0:T(8,128)(2,1)S(1)}, u32[]{:S(2)}, u32[]{:S(2)}) collective-permute-start(bf16[4,16,768]{2,1,0:T(8,128)(2,1)S(1)} %get-tuple-element.22), channel_id=1, source_target_pairs={{0,1},{1,0},{2,3},{3,2},{4,5},{5,4},{6,7},{7,6},{8,9},{9,8},{10,11... | collective-permute-start | bytes 294920 | tf_op jit(solution)/shard_map/ppermute | solution.py:372
  126.9 10.7 %collective-permute-start.11 = (bf16[4,16,768]{2,1,0:T(8,128)(2,1)S(1)}, bf16[4,16,768]{2,1,0:T(8,128)(2,1)S(1)}, u32[]{:S(2)}, u32[]{:S(2)}) collective-permute-start(bf16[4,16,768]{2,1,0:T(8,128)(2,1)S(1)} %get-tuple-element.21), channel_id=1, source_target_pairs={{0,2},{1,3},{2,0},{3,1},{4,6},{5,7},{6,4},{7,5},{8,10},{9,11},{10,... | collective-permute-start | bytes 294920 | tf_op jit(solution)/shard_map/ppermute | solution.py:372
  129.4 8.2 %collective-permute-start.12 = (bf16[4,16,768]{2,1,0:T(8,128)(2,1)S(1)}, bf16[4,16,768]{2,1,0:T(8,128)(2,1)S(1)}, u32[]{:S(2)}, u32[]{:S(2)}) collective-permute-start(bf16[4,16,768]{2,1,0:T(8,128)(2,1)S(1)} %get-tuple-element.20), channel_id=1, source_target_pairs={{0,3},{1,2},{2,1},{3,0},{4,7},{5,6},{6,5},{7,4},{8,11},{9,10},{10,... | collective-permute-start | bytes 294920 | tf_op jit(solution)/shard_map/ppermute | solution.py:372
  137.7 4.7 %collective-permute-start.13 = (bf16[2,16,768]{2,1,0:T(8,128)(2,1)S(1)}, bf16[2,16,768]{2,1,0:T(8,128)(2,1)S(1)}, u32[]{:S(2)}, u32[]{:S(2)}) collective-permute-start(bf16[2,16,768]{2,1,0:T(8,128)(2,1)S(1)} %activate.1.refs_0_), channel_id=1, source_target_pairs={{0,1},{1,0},{2,3},{3,2},{4,5},{5,4},{6,7},{7,6},{8,9},{9,8},{10,11... | collective-permute-start | bytes 147464 | tf_op jit(solution)/shard_map/ppermute | solution.py:372
  139.5 5.9 %collective-permute-start.14 = (bf16[2,16,768]{2,1,0:T(8,128)(2,1)S(1)}, bf16[2,16,768]{2,1,0:T(8,128)(2,1)S(1)}, u32[]{:S(2)}, u32[]{:S(2)}) collective-permute-start(bf16[2,16,768]{2,1,0:T(8,128)(2,1)S(1)} %activate.1.refs_0_), channel_id=1, source_target_pairs={{0,2},{1,3},{2,0},{3,1},{4,6},{5,7},{6,4},{7,5},{8,10},{9,11},{10,... | collective-permute-start | bytes 147464 | tf_op jit(solution)/shard_map/ppermute | solution.py:372
  140.9 5.9 %collective-permute-start.15 = (bf16[2,16,768]{2,1,0:T(8,128)(2,1)S(1)}, bf16[2,16,768]{2,1,0:T(8,128)(2,1)S(1)}, u32[]{:S(2)}, u32[]{:S(2)}) collective-permute-start(bf16[2,16,768]{2,1,0:T(8,128)(2,1)S(1)} %activate.1.refs_0_), channel_id=1, source_target_pairs={{0,3},{1,2},{2,1},{3,0},{4,7},{5,6},{6,5},{7,4},{8,11},{9,10},{10,... | collective-permute-start | bytes 147464 | tf_op jit(solution)/shard_map/ppermute | solution.py:372
  168.5 10.0 %copy-start.8 = (bf16[8,512]{1,0:T(8,128)(2,1)S(1)}, bf16[8,512]{1,0:T(8,128)(2,1)}, u32[]{:S(2)}) copy-start(bf16[8,512]{1,0:T(8,128)(2,1)} %after.4) | copy-start | bytes 24580
  169.3 5.3 %collective-permute-start.22 = (f32[8,512]{1,0:T(8,128)S(1)}, f32[8,512]{1,0:T(8,128)S(1)}, u32[]{:S(2)}, u32[]{:S(2)}) collective-permute-start(f32[8,512]{1,0:T(8,128)S(1)} %get-tuple-element.25), channel_id=1, source_target_pairs={{0,28},{4,24},{8,20},{12,16},{16,12},{20,8},{24,4},{28,0},{1,29},{... | collective-permute-start | bytes 49160 | tf_op jit(solution)/shard_map/ppermute | solution.py:372
  169.5 6.1 %collective-permute-start.21 = (f32[8,512]{1,0:T(8,128)S(1)}, f32[8,512]{1,0:T(8,128)S(1)}, u32[]{:S(2)}, u32[]{:S(2)}) collective-permute-start(f32[8,512]{1,0:T(8,128)S(1)} %get-tuple-element.26), channel_id=1, source_target_pairs={{0,24},{4,28},{8,16},{12,20},{16,8},{20,12},{24,0},{28,4},{1,25},{... | collective-permute-start | bytes 49160 | tf_op jit(solution)/shard_map/ppermute | solution.py:372
  172.1 3.6 %collective-permute-start.20 = (f32[8,512]{1,0:T(8,128)S(1)}, f32[8,512]{1,0:T(8,128)S(1)}, u32[]{:S(2)}, u32[]{:S(2)}) collective-permute-start(f32[8,512]{1,0:T(8,128)S(1)} %get-tuple-element.27), channel_id=1, source_target_pairs={{0,20},{4,16},{8,28},{12,24},{16,4},{20,0},{24,12},{28,8},{1,21},{... | collective-permute-start | bytes 49160 | tf_op jit(solution)/shard_map/ppermute | solution.py:372
  173.5 3.7 %collective-permute-start.19 = (f32[8,512]{1,0:T(8,128)S(1)}, f32[8,512]{1,0:T(8,128)S(1)}, u32[]{:S(2)}, u32[]{:S(2)}) collective-permute-start(f32[8,512]{1,0:T(8,128)S(1)} %get-tuple-element.28), channel_id=1, source_target_pairs={{0,16},{4,20},{8,24},{12,28},{16,0},{20,4},{24,8},{28,12},{1,17},{... | collective-permute-start | bytes 49160 | tf_op jit(solution)/shard_map/ppermute | solution.py:372
  173.8 3.4 %collective-permute-start.18 = (f32[8,512]{1,0:T(8,128)S(1)}, f32[8,512]{1,0:T(8,128)S(1)}, u32[]{:S(2)}, u32[]{:S(2)}) collective-permute-start(f32[8,512]{1,0:T(8,128)S(1)} %get-tuple-element.29), channel_id=1, source_target_pairs={{0,12},{4,8},{8,4},{12,0},{16,28},{20,24},{24,20},{28,16},{1,13},{... | collective-permute-start | bytes 49160 | tf_op jit(solution)/shard_map/ppermute | solution.py:372
  174.7 3.9 %collective-permute-start.17 = (f32[8,512]{1,0:T(8,128)S(1)}, f32[8,512]{1,0:T(8,128)S(1)}, u32[]{:S(2)}, u32[]{:S(2)}) collective-permute-start(f32[8,512]{1,0:T(8,128)S(1)} %get-tuple-element.30), channel_id=1, source_target_pairs={{0,8},{4,12},{8,0},{12,4},{16,24},{20,28},{24,16},{28,20},{1,9},{5... | collective-permute-start | bytes 49160 | tf_op jit(solution)/shard_map/ppermute | solution.py:372
  175.6 2.9 %collective-permute-start.16 = (f32[8,512]{1,0:T(8,128)S(1)}, f32[8,512]{1,0:T(8,128)S(1)}, u32[]{:S(2)}, u32[]{:S(2)}) collective-permute-start(f32[8,512]{1,0:T(8,128)S(1)} %get-tuple-element.24), channel_id=1, source_target_pairs={{0,4},{4,0},{8,12},{12,8},{16,20},{20,16},{24,28},{28,24},{1,5},{5... | collective-permute-start | bytes 49160 | tf_op jit(solution)/shard_map/ppermute | solution.py:372
  179.9 70.7 %all-to-all-start.1 = ((bf16[8,704,512]{2,1,0:T(8,128)(2,1)}), bf16[8,704,512]{2,1,0:T(8,128)(2,1)}, u32[]{:S(2)}, u32[]{:S(2)}) async-start(bf16[8,704,512]{2,1,0:T(8,128)(2,1)} %after.6), calls=%async_computation.1 | async-start | bytes 11534336 | tf_op jit(solution)/shard_map/all_to_all | solution.py:408
  (8 other events, 19.5 us)
where the time goes:
time: 267 us; the launch traced here: 266 us
  Pallas kernels  112 us (42%)
  waiting for transfers between devices  71.1 us (27%)
  starting transfers between devices  42.9 us (16%)
  local copies, waits for them, and re-layouts  23.1 us (9%)
  matrix products  11.5 us (4%)
  other arithmetic  4.28 us (2%)
    all_to_all x3, waiting for transfers between devices, send(): lax.all_to_all(block, 'row', split_axis=0, concat_axis=0, tiled=True)  50.8 us
    pallas_call x3, Pallas kernels, unpack(): pl.pallas_call(functools.partial(unpack_kernel, rows), grid_spec=pltpu.Pr...  44.8 us
    pallas_call x3, Pallas kernels, pack(): pl.pallas_call(functools.partial(pack_kernel, rows), grid_spec=pltpu.Pref...  35.8 us
    ppermute x23, starting transfers between devices, from_peer(): return lax.ppermute(block, axis, [(i, i ^ offset) for i in range(size)])  27.7 us
    ppermute x23, waiting for transfers between devices, from_peer(): return lax.ppermute(block, axis, [(i, i ^ offset) for i in range(size)])  20.3 us
    pallas_call x2, Pallas kernels, call_plan(): pl.pallas_call(functools.partial(kernel, lines, rows), out_shape=(stack,...  15.9 us
    all_to_all x3, starting transfers between devices, send(): lax.all_to_all(block, 'row', split_axis=0, concat_axis=0, tiled=True)  15.2 us
    unnamed x40, local copies, waits for them, and re-layouts  13.1 us
  transfers between devices with their start and end apart: 26, of which 12 were waited for; matrix products, arithmetic and copies ran while one was open for 11% of the time, Pallas kernels for 30%

commit v1 on v0

--- a/solution.py
+++ b/solution.py
@@ -44,7 +44,7 @@
 
 def equal_ones(left, right):
     one = jnp.ones((), jnp.bfloat16)
-    return jnp.where(left == right, one, jnp.zeros((), jnp.bfloat16))
+    return jnp.maximum(one - jnp.abs(left - right), jnp.zeros((), jnp.bfloat16))
 
 
 def within(place, block):
@@ -85,7 +85,7 @@
         starts.append(running)
         running = running + counts[e * rows : (e + 1) * rows]
     start = jnp.concatenate(starts, axis=0)
-    lead = jnp.floor(start * (1.0 / TILE))
+    lead = jnp.where(counts > 0.0, jnp.floor(start * (1.0 / TILE)), 0.0)
     tail = jnp.floor((start + counts + (TILE - 1.0)) * (1.0 / TILE))
     tiles = jnp.where(counts > 0.0, tail - lead, 0.0)
     pairs = experts * rows
@@ -173,89 +173,114 @@
     return pl.ds(pl.multiple_of(index * TILE, TILE), TILE)
 
 
-def pack_kernel(rows, plan_ref, place_ref, lines_ref, out_ref, stage_ref, number_ref):
-    e = pl.program_id(0)
-    pairs = pl.num_programs(0) * rows
-    deep, _ = stage_ref.shape
+def pack_kernel(rows, span, plan_ref, place_ref, lines_ref, out_ref, packed_ref, number_ref, sem, *stages):
+    step = pl.program_id(0)
+    pairs = pl.num_programs(0) * span * rows
+    deep, _ = stages[0].shape
     lines = lines_ref.shape[2]
 
-    @pl.when(e == 0)
+    @pl.when(step == 0)
     def _():
         number_ref[...] = counting(number_ref.shape, 0)
 
-    place = place_ref[0][:, :lines]
-    source_lines = lines_ref[0, 0]
-    for first in range(0, deep, 256):
-        count = min(256, deep - first)
-        onehot = equal_ones(number_ref[:count], within(place, first // 256))
-        stage_ref[first : first + count] = jnp.dot(
-            onehot, source_lines, preferred_element_type=jnp.float32
+    def entry(n, j, d):
+        return plan_ref[n * pairs + (step * span + j) * rows + d]
+
+    for j, stage_ref in enumerate(stages):
+        place = place_ref[j][:, :lines]
+        source_lines = lines_ref[j, 0]
+        for first in range(0, deep, 256):
+            count = min(256, deep - first)
+            onehot = equal_ones(number_ref[:count], within(place, first // 256))
+            stage_ref[first : first + count] = jnp.dot(
+                onehot, source_lines, preferred_element_type=jnp.float32
+            ).astype(jnp.bfloat16)
+
+        def one_peer(d, most, j=j, stage_ref=stage_ref):
+            lead, tiles, base = entry(0, j, d), entry(1, j, d), entry(2, j, d)
+            shared = entry(3, j, d) > 0
+            earlier = packed_ref[d, tile_at(lead), :]
+            for t in range(1, STRAIGHT):
+                n = jnp.maximum(jnp.minimum(t, tiles - 1), 0)
+                packed_ref[d, tile_at(lead + n), :] = stage_ref[tile_at(base + n), :]
+            kept = jnp.where(shared | (tiles == 0), earlier, jnp.zeros_like(earlier))
+            fresh = stage_ref[tile_at(base), :]
+            fresh = jnp.where(tiles == 0, jnp.zeros_like(fresh), fresh)
+            packed_ref[d, tile_at(lead), :] = kept + fresh
+            return jnp.maximum(most, tiles)
+
+        most = lax.fori_loop(0, rows, one_peer, 0, unroll=rows <= 8)
+
+        @pl.when(most > STRAIGHT)
+        def _(j=j, stage_ref=stage_ref):
+            def long_peer(d, carry):
+                lead, tiles, base = entry(0, j, d), entry(1, j, d), entry(2, j, d)
+
+                def put(t, c):
+                    packed_ref[d, tile_at(lead + t), :] = stage_ref[tile_at(base + t), :]
+                    return c
+
+                return lax.fori_loop(STRAIGHT, tiles, put, carry)
+
+            lax.fori_loop(0, rows, long_peer, 0)
+
+    @pl.when(step == pl.num_programs(0) - 1)
+    def _():
+        copy = pltpu.make_async_copy(packed_ref, out_ref, sem)
+        copy.start()
+        copy.wait()
+
+
+def unpack_kernel(rows, span, stage_count, plan_ref, place_ref, block_ref, *rest):
+    stages = rest[-stage_count:]
+    out_ref, number_ref = rest[-stage_count - 2 : -stage_count]
+    step = pl.program_id(0)
+    pairs = pl.num_programs(0) * span * rows
+    deep, _ = stages[0].shape
+    lines = out_ref.shape[2]
+
+    @pl.when(step == 0)
+    def _():
+        for stage_ref in stages:
+            stage_ref[...] = jnp.zeros_like(stage_ref)
+        number_ref[...] = counting(number_ref.shape, 1)
+
+    def entry(n, j, d):
+        return plan_ref[n * pairs + (step * span + j) * rows + d]
+
+    for j, stage_ref in enumerate(stages):
+
+        def one_peer(s, most, j=j, stage_ref=stage_ref):
+            lead, tiles, base = entry(0, j, s), entry(1, j, s), entry(2, j, s)
+            for t in range(STRAIGHT):
+                n = jnp.maximum(jnp.minimum(t, tiles - 1), 0)
+                stage_ref[tile_at(base + n), :] = block_ref[s, tile_at(lead + n), :]
+            return jnp.maximum(most, tiles)
+
+        most = lax.fori_loop(0, rows, one_peer, 0, unroll=rows <= 8)
+
+        @pl.when(most > STRAIGHT)
+        def _(j=j, stage_ref=stage_ref):
+            def long_peer(s, carry):
+                lead, tiles, base = entry(0, j, s), entry(1, j, s), entry(2, j, s)
+
+                def put(t, c):
+                    stage_ref[tile_at(base + t), :] = block_ref[s, tile_at(lead + t), :]
+                    return c
+
+                return lax.fori_loop(STRAIGHT, tiles, put, carry)
+
+            lax.fori_loop(0, rows, long_peer, 0)
+
+    for j, stage_ref in enumerate(stages):
+        place = jnp.where(iota((lines, LANES), 1) == step * span + j, place_ref[:lines, :], 0.0)
+        place = jnp.sum(place, axis=1, keepdims=True).astype(jnp.int32)
+        onehot = jnp.concatenate(
+            [equal_ones(number_ref[...], within(place, n)) for n in range(deep // 256)], axis=1
+        )
+        out_ref[j, 0] = jnp.dot(
+            onehot, stage_ref[...], preferred_element_type=jnp.float32
         ).astype(jnp.bfloat16)
-
-    def one_peer(d, carry):
-        k = e * rows + d
-        lead = plan_ref[k]
-        tiles = plan_ref[pairs + k]
-        base = plan_ref[2 * pairs + k]
-        shared = plan_ref[3 * pairs + k] > 0
-
-        @pl.when(tiles > 0)
-        def _():
-            earlier = out_ref[d, tile_at(lead), :]
-            for t in range(1, STRAIGHT):
-                n = jnp.minimum(t, tiles - 1)
-                out_ref[d, tile_at(lead + n), :] = stage_ref[tile_at(base + n), :]
-            earlier = jnp.where(shared, earlier, jnp.zeros_like(earlier))
-            out_ref[d, tile_at(lead), :] = earlier + stage_ref[tile_at(base), :]
-
-        def put(t, c):
-            out_ref[d, tile_at(lead + t), :] = stage_ref[tile_at(base + t), :]
-            return c
-
-        return lax.fori_loop(STRAIGHT, tiles, put, carry)
-
-    lax.fori_loop(0, rows, one_peer, 0, unroll=rows <= 8)
-
-
-def unpack_kernel(rows, plan_ref, place_ref, block_ref, *rest):
-    out_ref, stage_ref, number_ref = rest[-3:]
-    e = pl.program_id(0)
-    pairs = pl.num_programs(0) * rows
-    deep, _ = stage_ref.shape
-    lines = out_ref.shape[2]
-
-    @pl.when(e == 0)
-    def _():
-        stage_ref[...] = jnp.zeros_like(stage_ref)
-        number_ref[...] = counting(number_ref.shape, 1)
-
-    def one_peer(s, carry):
-        k = e * rows + s
-        lead = plan_ref[k]
-        tiles = plan_ref[pairs + k]
-        base = plan_ref[2 * pairs + k]
-
-        @pl.when(tiles > 0)
-        def _():
-            for t in range(STRAIGHT):
-                n = jnp.minimum(t, tiles - 1)
-                stage_ref[tile_at(base + n), :] = block_ref[s, tile_at(lead + n), :]
-
-        def put(t, c):
-            stage_ref[tile_at(base + t), :] = block_ref[s, tile_at(lead + t), :]
-            return c
-
-        return lax.fori_loop(STRAIGHT, tiles, put, carry)
-
-    lax.fori_loop(0, rows, one_peer, 0, unroll=rows <= 8)
-    place = jnp.where(iota((lines, LANES), 1) == e, place_ref[:lines, :], 0.0)
-    place = jnp.sum(place, axis=1, keepdims=True).astype(jnp.int32)
-    onehot = jnp.concatenate(
-        [equal_ones(number_ref[...], within(place, block)) for block in range(deep // 256)], axis=1
-    )
-    out_ref[0, 0] = jnp.dot(
-        onehot, stage_ref[...], preferred_element_type=jnp.float32
-    ).astype(jnp.bfloat16)
 
 
 def call_plan(kernel, name, table, ids, lines, rows, transposed):
@@ -282,20 +307,23 @@
 def pack(expert_lines, place, plan, piece, rows, block_rows, deep):
     experts, _, lines, _ = expert_lines.shape
     part, column, width = piece
+    span = 2 - experts % 2
     return pl.pallas_call(
-        functools.partial(pack_kernel, rows),
+        functools.partial(pack_kernel, rows, span),
         grid_spec=pltpu.PrefetchScalarGridSpec(
             num_scalar_prefetch=1,
-            grid=(experts,),
+            grid=(experts // span,),
             in_specs=[
-                pl.BlockSpec((1, 1, place.shape[2]), lambda e, plan: (e, 0, 0)),
-                pl.BlockSpec((1, 1, lines, width), lambda e, plan: (e, part, 0, column)),
+                pl.BlockSpec((span, 1, place.shape[2]), lambda e, plan: (e, 0, 0)),
+                pl.BlockSpec((span, 1, lines, width), lambda e, plan: (e, part, 0, column)),
             ],
-            out_specs=pl.BlockSpec((rows, block_rows, width), lambda e, plan: (0, 0, 0)),
+            out_specs=pl.BlockSpec(memory_space=pltpu.HBM),
             scratch_shapes=[
-                pltpu.VMEM((deep, width), jnp.bfloat16),
+                pltpu.VMEM((rows, block_rows, width), jnp.bfloat16),
                 pltpu.VMEM((256, lines), jnp.bfloat16),
-            ],
+                pltpu.SemaphoreType.DMA(()),
+            ]
+            + [pltpu.VMEM((deep, width), jnp.bfloat16)] * span,
         ),
         out_shape=jax.ShapeDtypeStruct((rows, block_rows, width), jnp.bfloat16),
         compiler_params=params(),
@@ -312,6 +340,7 @@
     experts, _, lines, _ = shape
     part, column, width = piece
     rows, block_rows, _ = arrived.shape
+    span = 2 - experts % 2
     in_specs = [
         pl.BlockSpec(place.shape, lambda e, plan: (0, 0)),
         pl.BlockSpec((rows, block_rows, width), lambda e, plan: (0, 0, 0)),
@@ -323,16 +352,14 @@
         operands.append(previous)
         aliases = {3: 0}
     return pl.pallas_call(
-        functools.partial(unpack_kernel, rows),
+        functools.partial(unpack_kernel, rows, span, span),
         grid_spec=pltpu.PrefetchScalarGridSpec(
             num_scalar_prefetch=1,
-            grid=(experts,),
+            grid=(experts // span,),
             in_specs=in_specs,
-            out_specs=pl.BlockSpec((1, 1, lines, width), lambda e, plan: (e, part, 0, column)),
-            scratch_shapes=[
-                pltpu.VMEM((deep, width), jnp.bfloat16),
-                pltpu.VMEM((lines, 256), jnp.bfloat16),
-            ],
+            out_specs=pl.BlockSpec((span, 1, lines, width), lambda e, plan: (e, part, 0, column)),
+            scratch_shapes=[pltpu.VMEM((lines, 256), jnp.bfloat16)]
+            + [pltpu.VMEM((deep, width), jnp.bfloat16)] * span,
         ),
         out_shape=jax.ShapeDtypeStruct(shape, jnp.bfloat16),
         input_output_aliases=aliases,
@@ -382,7 +409,7 @@
         experts, parts, lines, width = expert_lines.shape
         padded = up_to(lines, LANES)
         block_rows = up_to(experts * lines // rows, TILE)
-        self.deep = up_to(lines + 2 * (TILE - 1) * rows, TILE)
+        self.deep = up_to(lines + 2 * (TILE - 1) * rows, TILE) + TILE
         self.shape = expert_lines.shape
         self.pieces = bulk_pieces(parts, width)
         out_place, out_plan = call_plan(
@@ -592,13 +619,14 @@
     shift = lines - (padded - LANES)
     me = col_index.astype(jnp.int32).reshape(1)
 
-    order = row_index ^ jnp.arange(rows, dtype=jnp.int32)
+    order = row_index ^ jnp.array(sorted(range(rows), key=lambda o: (o % 2, o)), jnp.int32)
     routes = routes.reshape(rows, own, topk)[order].reshape(tokens, topk)
     my_routes = lax.dynamic_slice_in_dim(routes, col_index * share, share, 0)
     router = jnp.pad(w_router, ((0, 0), (shift, LANES - shift - experts)))
-    every_h = jnp.concatenate(
-        [h_mid] + [from_peer(h_mid, "row", o) for o in range(1, rows)], axis=0
-    )
+    same_core = jnp.concatenate(
+        [h_mid] + [from_peer(h_mid, "row", o) for o in range(2, rows, 2)], axis=0
+    )
+    every_h = jnp.concatenate([same_core, from_peer(same_core, "row", 1)], axis=0)
     migration.send([every_h])
     part_spec = lambda part: pl.BlockSpec((1, 1, lines, width), lambda e, me: (e, part, 0, 0))
     whole = lambda a: pl.BlockSpec(a.shape, lambda e, me: (0,) * a.ndim)
@@ -648,12 +676,12 @@
         ),
         name="down",
     )(me, routes, *chunks, expert_lines)
-    migration.receive(0)
-    (produced,) = after([produced], [migration.moved])
-    blocks = produced.reshape(rows, own, width)
+    half = tokens // 2
+    both_cores = produced[:half] + from_peer(produced[half:], "row", 1)
+    blocks = both_cores.reshape(rows // 2, own, width)
     mixed = blocks[0]
-    for o in range(1, rows):
-        mixed = mixed + from_peer(blocks[o], "row", o)
+    for n in range(1, rows // 2):
+        mixed = mixed + from_peer(blocks[n], "row", 2 * n)
     return mixed
 
 
@@ -682,7 +710,7 @@
     (h_mid,) = after([h_mid], migration.packed)
     mixed = experts_part(h_mid, moe_gain, w_router, expert_lines, routes, migration)
     migration.send([mixed])
-    for piece in range(1, len(migration.pieces)):
+    for piece in range(len(migration.pieces)):
         migration.receive(piece)
     return (h_mid.astype(jnp.float32) + mixed, jnp.transpose(migration.moved, (0, 2, 1, 3)))
 

time: 267 us -> 256 us (0.959)
  starting transfers between devices: 42.9 us -> 37.1 us
  waiting for transfers between devices: 71.1 us -> 76.8 us
  Pallas kernels: 112 us -> 108 us
  matrix products: 11.5 us -> 8.03 us
  local copies, waits for them, and re-layouts: 23.1 us -> 19.7 us
    ppermute x23 -> x17, waiting for transfers between devices: 20.3 us -> 50.1 us  [from_peer(): return lax.ppermute(block, axis, [(i, i ^ offset) for i in range(size)])]
    all_to_all x3, waiting for transfers between devices: 50.8 us -> 26.6 us  [send(): lax.all_to_all(block, 'row', split_axis=0, concat_axis=0, tiled=True)]
    ppermute x23 -> x17, starting transfers between devices: 27.7 us -> 21.9 us  [from_peer(): return lax.ppermute(block, axis, [(i, i ^ offset) for i in range(size)])]
    pallas_call x6, Pallas kernels: 80.6 us -> 77.3 us  [the longest x3 42.2 us: unpack(): pl.pallas_call(functools.partial(unpack_kernel, rows, span, span), grid_s...]
    unnamed x40 -> x41, local copies, waits for them, and re-layouts: 13.1 us -> 11.5 us
  transfers between devices with their start and end apart: 26 -> 20, of which waited for: 12 -> 10; matrix products, arithmetic and copies ran while one was open for 11% -> 8% of each run, Pallas kernels for 30% -> 30%
where the time goes in v1:
time: 256 us; the launch traced here: 254 us
  Pallas kernels  108 us (42%)
  waiting for transfers between devices  76.8 us (30%)
  starting transfers between devices  37.1 us (14%)
  local copies, waits for them, and re-layouts  19.7 us (8%)
  matrix products  8.03 us (3%)
  other arithmetic  3.44 us (1%)
    ppermute x17, waiting for transfers between devices, from_peer(): return lax.ppermute(block, axis, [(i, i ^ offset) for i in range(size)])  50.1 us
    pallas_call x3, Pallas kernels, unpack(): pl.pallas_call(functools.partial(unpack_kernel, rows, span, span), grid_s...  42.2 us
    pallas_call x3, Pallas kernels, pack(): pl.pallas_call(functools.partial(pack_kernel, rows, span), grid_spec=pltp...  35 us
    all_to_all x3, waiting for transfers between devices, send(): lax.all_to_all(block, 'row', split_axis=0, concat_axis=0, tiled=True)  26.6 us
    ppermute x17, starting transfers between devices, from_peer(): return lax.ppermute(block, axis, [(i, i ^ offset) for i in range(size)])  21.9 us
    pallas_call x2, Pallas kernels, call_plan(): pl.pallas_call(functools.partial(kernel, lines, rows), out_shape=(stack,...  15.9 us
    all_to_all x3, starting transfers between devices, send(): lax.all_to_all(block, 'row', split_axis=0, concat_axis=0, tiled=True)  15.2 us
    unnamed x41, local copies, waits for them, and re-layouts  11.5 us
  transfers between devices with their start and end apart: 20, of which 10 were waited for; matrix products, arithmetic and copies ran while one was open for 8% of the time, Pallas kernels for 30%

profile of v1, /device:TPU:0, one launch (start us, length us, event | category | flops | bytes accessed | tf_op | source)
XLA Modules:
  0.0 254.3 jit_solution(10999070677066694235)
XLA Ops:
  2.4 6.1 %outgoing_plan.1 = (s32[8,1,768]{2,1,0:T(1,128)S(1)}, s32[4,64,128]{2,1,0:T(8,128)S(1)}) custom-call(s32[8,5632]{1,0:T(8,128)S(1)} %copy-done.5, s32[8,768]{1,0:T(8,128)S(1)} %pad.11.held_ref), custom_call_target="tpu_custom_call" | custom-call | flops 230686720 | bytes 360448 | tf_op jit(solution)/shard_map/outgoing_plan/pallas_call | solution.py:293
  8.7 11.7 %pack_lines.3.refs_1_ = bf16[8,704,512]{2,1,0:T(8,128)(2,1)S(1)} custom-call(s32[256]{0:T(256)S(1)} %reshape_squeeze.27.plan_ref, s32[8,1,768]{2,1,0:T(1,128)S(1)} %get-tuple-element.7.place_ref, bf16[8,3,704,512]{3,2,1,0:T(8,128)(2,1)} %bitcast.81), custom_call_target="tpu_custom_call" | custom-call | flops 5536481280 | bytes 11534336 | tf_op jit(solution)/shard_map/pack_lines/pallas_call | solution.py:311
  20.4 2.5 copy-done.2
  22.9 5.3 %all-to-all-start.2 = ((bf16[8,704,512]{2,1,0:T(8,128)(2,1)}), bf16[8,704,512]{2,1,0:T(8,128)(2,1)}, u32[]{:S(2)}, u32[]{:S(2)}) async-start(bf16[8,704,512]{2,1,0:T(8,128)(2,1)} %copy-done.2), calls=%async_computation.2 | async-start | bytes 11534336 | tf_op jit(solution)/shard_map/all_to_all | solution.py:435
  29.4 1.7 fusion.30
  32.2 1.7 fusion.29
  41.1 4.8 %collective-permute-start.2 = (f32[8,4224]{1,0:T(8,128)S(1)}, f32[8,4224]{1,0:T(8,128)S(1)}, u32[]{:S(2)}, u32[]{:S(2)}) collective-permute-start(f32[8,4224]{1,0:T(8,128)S(1)} %concatenate.10), channel_id=1, source_target_pairs={{0,3},{1,2},{2,1},{3,0},{4,7},{5,6},{6,5},{7,4},{8,11},{9,10},{10,... | collective-permute-start | bytes 405512 | tf_op jit(solution)/shard_map/ppermute | solution.py:399
  46.5 11.7 %pack_lines.5.refs_3_.refs_0_ = bf16[8,704,512]{2,1,0:T(8,128)(2,1)S(1)} custom-call(s32[256]{0:T(256)S(1)} %reshape_squeeze.27.plan_ref, s32[8,1,768]{2,1,0:T(1,128)S(1)} %get-tuple-element.7.place_ref, bf16[8,3,704,512]{3,2,1,0:T(8,128)(2,1)} %bitcast.82), custom_call_target="tpu_custom_call" | custom-call | flops 5536481280 | bytes 11534336 | tf_op jit(solution)/shard_map/pack_lines/pallas_call | solution.py:311
  58.2 2.5 copy-done
  60.7 11.7 %pack_lines.4.refs_2_.refs_0_ = bf16[8,704,512]{2,1,0:T(8,128)(2,1)S(1)} custom-call(s32[256]{0:T(256)S(1)} %reshape_squeeze.27.plan_ref, s32[8,1,768]{2,1,0:T(1,128)S(1)} %get-tuple-element.7.place_ref, bf16[8,3,704,512]{3,2,1,0:T(8,128)(2,1)} %bitcast.83), custom_call_target="tpu_custom_call" | custom-call | flops 5536481280 | bytes 11534336 | tf_op jit(solution)/shard_map/pack_lines/pallas_call | solution.py:311
  72.4 2.5 copy-done.1
  75.5 3.5 %fusion.4.refs_0_ = bf16[8,512]{1,0:T(8,128)(2,1)} fusion(bf16[4096,512]{1,0:T(8,128)(2,1)} %param.20, f32[8,4096]{1,0:T(8,128)S(1)} %fusion.8, f32[8,32]{0,1:T(8,128)S(1)} %copy.127, bf16[8,512]{1,0:T(8,128)(2,1)S(1)} %copy-done.10), kind=kOutput, calls=%fused_computation.9 | convolution fusion | flops 33632256 | bytes 4342784 | tf_op jit(solution)/shard_map/dot_general | solution.py:708
  78.9 2.6 %collective-permute-start.5 = (bf16[8,512]{1,0:T(8,128)(2,1)}, bf16[8,512]{1,0:T(8,128)(2,1)S(1)}, u32[]{:S(2)}, u32[]{:S(2)}) collective-permute-start(bf16[8,512]{1,0:T(8,128)(2,1)} %after.3), channel_id=1, source_target_pairs={{0,24},{4,28},{8,16},{12,20},{16,8},{20,12},{24,0},{28,4},{1,25},{... | collective-permute-start | bytes 24584 | tf_op jit(solution)/shard_map/ppermute | solution.py:399
  83.2 11.7 %collective-permute-done.5 = bf16[8,512]{1,0:T(8,128)(2,1)S(1)} collective-permute-done((bf16[8,512]{1,0:T(8,128)(2,1)}, bf16[8,512]{1,0:T(8,128)(2,1)S(1)}, u32[]{:S(2)}, u32[]{:S(2)}) %collective-permute-start.5) | collective-permute-done | bytes 8224 | tf_op jit(solution)/shard_map/ppermute | solution.py:399
  97.4 4.8 %all-to-all-start.1 = ((bf16[8,704,512]{2,1,0:T(8,128)(2,1)}), bf16[8,704,512]{2,1,0:T(8,128)(2,1)}, u32[]{:S(2)}, u32[]{:S(2)}) async-start(bf16[8,704,512]{2,1,0:T(8,128)(2,1)} %after.5), calls=%async_computation.1 | async-start | bytes 11534336 | tf_op jit(solution)/shard_map/all_to_all | solution.py:435
  103.4 8.8 %gate_up.1 = bf16[4,4,16,768]{3,2,1,0:T(8,128)(2,1)S(1)} custom-call(s32[1]{0:T(128)} %bitcast.20.me_ref, bf16[64,512]{1,0:T(8,128)(2,1)S(1)} %copy-done.4, bf16[1,512]{1,0:T(2,128)(2,1)S(1)} %reshape.90.gain_ref, bf16[512,128]{1,0:T(8,128)(2,1)S(1)} %pad.12.router_ref, s32[64,2]{1,0:T(8,128)S(1)} %bitcast.78, bf16[8,3,704,512]{3,2,1,0:T(8,128)(2,1)} %bitcast.84, ...), custom_call_target="tpu_custom_call" | custom-call | flops 738197504 | bytes 11534336 | tf_op jit(solution)/shard_map/gate_up/pallas_call | solution.py:634
  112.2 4.3 %collective-permute-start.9 = (bf16[4,16,768]{2,1,0:T(8,128)(2,1)S(1)}, bf16[4,16,768]{2,1,0:T(8,128)(2,1)S(1)}, u32[]{:S(2)}, u32[]{:S(2)}) collective-permute-start(bf16[4,16,768]{2,1,0:T(8,128)(2,1)S(1)} %get-tuple-element.20), channel_id=1, source_target_pairs={{0,3},{1,2},{2,1},{3,0},{4,7},{5,6},{6,5},{7,4},{8,11},{9,10},{10,... | collective-permute-start | bytes 294920 | tf_op jit(solution)/shard_map/ppermute | solution.py:399
  117.1 3.1 %collective-permute-done.9.refs_3_ = bf16[4,16,768]{2,1,0:T(8,128)(2,1)S(1)} collective-permute-done((bf16[4,16,768]{2,1,0:T(8,128)(2,1)S(1)}, bf16[4,16,768]{2,1,0:T(8,128)(2,1)S(1)}, u32[]{:S(2)}, u32[]{:S(2)}) %collective-permute-start.9) | collective-permute-done | bytes 98336 | tf_op jit(solution)/shard_map/ppermute | solution.py:399
  120.2 5.0 %collective-permute-done.8.refs_2_ = bf16[4,16,768]{2,1,0:T(8,128)(2,1)S(1)} collective-permute-done((bf16[4,16,768]{2,1,0:T(8,128)(2,1)S(1)}, bf16[4,16,768]{2,1,0:T(8,128)(2,1)S(1)}, u32[]{:S(2)}, u32[]{:S(2)}) %collective-permute-start.8) | collective-permute-done | bytes 98336 | tf_op jit(solution)/shard_map/ppermute | solution.py:399
  125.5 2.5 collective-permute-start.12
  128.0 1.9 collective-permute-start.10
  129.9 1.5 collective-permute-done.12.refs_3_
  131.4 1.6 collective-permute-done.11.refs_2_
  133.0 6.1 %down.1 = f32[64,512]{1,0:T(8,128)S(1)} custom-call(s32[1]{0:T(128)} %bitcast.20.me_ref, s32[64,2]{1,0:T(8,128)S(1)} %bitcast.80, bf16[2,16,768]{2,1,0:T(8,128)(2,1)S(1)} %activate.1.refs_0_, bf16[2,16,768]{2,1,0:T(8,128)(2,1)S(1)} %collective-permute-done.10.refs_1_, bf16[2,16,768]{2,1,0:T(8,128)(2,1)S(1)} %collective-permute-done.11.refs_2_, ...), custom_call_target="tpu_custom_call" | custom-call | flops 369098752 | bytes 5767168 | tf_op jit(solution)/shard_map/down/pallas_call | solution.py:661
  140.5 1.7 collective-permute-start.14
  144.1 23.7 %collective-permute-done.14 = f32[8,512]{1,0:T(8,128)S(1)} collective-permute-done((f32[8,512]{1,0:T(8,128)S(1)}, f32[8,512]{1,0:T(8,128)S(1)}, u32[]{:S(2)}, u32[]{:S(2)}) %collective-permute-start.14) | collective-permute-done | bytes 16416 | tf_op jit(solution)/shard_map/ppermute | solution.py:399
  169.5 5.1 %all-to-all-start = ((bf16[8,704,512]{2,1,0:T(8,128)(2,1)}), bf16[8,704,512]{2,1,0:T(8,128)(2,1)}, u32[]{:S(2)}, u32[]{:S(2)}) async-start(bf16[8,704,512]{2,1,0:T(8,128)(2,1)} %after.4), calls=%async_computation | async-start | bytes 11534336 | tf_op jit(solution)/shard_map/all_to_all | solution.py:435
  175.4 9.8 %incoming_plan.1 = (f32[768,128]{1,0:T(8,128)S(1)}, s32[4,64,128]{2,1,0:T(8,128)S(1)}) custom-call(s32[8,5632]{1,0:T(8,128)S(1)} %copy-done.6, s32[8,768]{1,0:T(8,128)S(1)} %pad.13.wanted_ref), custom_call_target="tpu_custom_call" | custom-call | flops 230686720 | bytes 360448 | tf_op jit(solution)/shard_map/incoming_plan/pallas_call | solution.py:293
  185.5 14.0 %unpack_lines.3.rest_0_ = bf16[8,3,704,512]{3,2,1,0:T(8,128)(2,1)} custom-call(s32[256]{0:T(256)S(1)} %reshape_squeeze.28.plan_ref, f32[768,128]{1,0:T(8,128)S(1)} %get-tuple-element.9.place_ref, bf16[8,704,512]{2,1,0:T(8,128)(2,1)} %all-to-all-done.2.block_ref), custom_call_target="tpu_custom_call" | custom-call | flops 5905580032 | bytes 11534336 | tf_op jit(solution)/shard_map/unpack_lines/pallas_call | solution.py:354
  199.5 14.2 %unpack_lines.4.rest_0_ = bf16[8,3,704,512]{3,2,1,0:T(8,128)(2,1)} custom-call(s32[256]{0:T(256)S(1)} %reshape_squeeze.28.plan_ref, f32[768,128]{1,0:T(8,128)S(1)} %get-tuple-element.9.place_ref, bf16[8,704,512]{2,1,0:T(8,128)(2,1)} %all-to-all-done.1.block_ref, bf16[8,3,704,512]{3,2,1,0:T(8,128)(2,1)} %unpack_lines.3.rest_0_), custom_call_target="tpu_custom_call", output_to_operand_aliasing={{}: (3, {})} | custom-call | flops 5905580032 | bytes 11534336 | tf_op jit(solution)/shard_map/unpack_lines/pallas_call | solution.py:354
  213.7 26.6 %all-to-all-done.block_ref = bf16[8,704,512]{2,1,0:T(8,128)(2,1)} async-done(((bf16[8,704,512]{2,1,0:T(8,128)(2,1)}), bf16[8,704,512]{2,1,0:T(8,128)(2,1)}, u32[]{:S(2)}, u32[]{:S(2)}) %all-to-all-start) | async-done | bytes 5767200 | tf_op jit(solution)/shard_map/all_to_all | solution.py:435
  240.3 14.0 %unpack_lines.5 = bf16[8,3,704,512]{3,2,1,0:T(8,128)(2,1)} custom-call(s32[256]{0:T(256)S(1)} %reshape_squeeze.28.plan_ref, f32[768,128]{1,0:T(8,128)S(1)} %get-tuple-element.9.place_ref, bf16[8,704,512]{2,1,0:T(8,128)(2,1)} %all-to-all-done.block_ref, bf16[8,3,704,512]{3,2,1,0:T(8,128)(2,1)} %unpack_lines.4.rest_0_), custom_call_target="tpu_custom_call", output_to_operand_aliasing={{}: (3, {})} | custom-call | flops 5905580032 | bytes 11534336 | tf_op jit(solution)/shard_map/unpack_lines/pallas_call | solution.py:354
  (118 shorter events, 24.6 us)
Async XLA Ops:
  20.4 2.5 copy-start.2
  22.9 5.3 %copy-start.9 = (bf16[8,2,2048]{2,1,0:T(2,128)(2,1)S(1)}, bf16[8,2,2048]{2,1,0:T(2,128)(2,1)}, u32[]{:S(2)}) copy-start(bf16[8,2,2048]{2,1,0:T(2,128)(2,1)} %param.16) | copy-start | bytes 196612
  22.9 5.4 %copy-start.8 = (bf16[8,4096]{1,0:T(8,128)(2,1)S(1)}, bf16[8,4096]{1,0:T(8,128)(2,1)}, u32[]{:S(2)}) copy-start(bf16[8,4096]{1,0:T(8,128)(2,1)} %param.15) | copy-start | bytes 196612
  22.9 74.5 %all-to-all-start.2 = ((bf16[8,704,512]{2,1,0:T(8,128)(2,1)}), bf16[8,704,512]{2,1,0:T(8,128)(2,1)}, u32[]{:S(2)}, u32[]{:S(2)}) async-start(bf16[8,704,512]{2,1,0:T(8,128)(2,1)} %copy-done.2), calls=%async_computation.2 | async-start | bytes 11534336 | tf_op jit(solution)/shard_map/all_to_all | solution.py:435
  31.1 3.0 %copy-start.14 = (s32[8]{0:T(128)S(1)}, s32[8]{0:T(128)}, u32[]{:S(2)}) copy-start(s32[8]{0:T(128)} %param.19) | copy-start | bytes 100
  41.1 33.8 %collective-permute-start.2 = (f32[8,4224]{1,0:T(8,128)S(1)}, f32[8,4224]{1,0:T(8,128)S(1)}, u32[]{:S(2)}, u32[]{:S(2)}) collective-permute-start(f32[8,4224]{1,0:T(8,128)S(1)} %concatenate.10), channel_id=1, source_target_pairs={{0,3},{1,2},{2,1},{3,0},{4,7},{5,6},{6,5},{7,4},{8,11},{9,10},{10,... | collective-permute-start | bytes 405512 | tf_op jit(solution)/shard_map/ppermute | solution.py:399
  45.9 29.0 %collective-permute-start.1 = (f32[8,4224]{1,0:T(8,128)S(1)}, f32[8,4224]{1,0:T(8,128)S(1)}, u32[]{:S(2)}, u32[]{:S(2)}) collective-permute-start(f32[8,4224]{1,0:T(8,128)S(1)} %concatenate.10), channel_id=1, source_target_pairs={{0,2},{1,3},{2,0},{3,1},{4,6},{5,7},{6,4},{7,5},{8,10},{9,11},{10,... | collective-permute-start | bytes 405512 | tf_op jit(solution)/shard_map/ppermute | solution.py:399
  45.9 29.0 %collective-permute-start = (f32[8,4224]{1,0:T(8,128)S(1)}, f32[8,4224]{1,0:T(8,128)S(1)}, u32[]{:S(2)}, u32[]{:S(2)}) collective-permute-start(f32[8,4224]{1,0:T(8,128)S(1)} %concatenate.10), channel_id=1, source_target_pairs={{0,1},{1,0},{2,3},{3,2},{4,5},{5,4},{6,7},{7,6},{8,9},{9,8},{10,11... | collective-permute-start | bytes 405512 | tf_op jit(solution)/shard_map/ppermute | solution.py:399
  60.7 14.7 %copy-start.10 = (bf16[8,512]{1,0:T(8,128)(2,1)S(1)}, bf16[8,512]{1,0:T(8,128)(2,1)}, u32[]{:S(2)}) copy-start(bf16[8,512]{1,0:T(8,128)(2,1)} %param.14) | copy-start | bytes 24580
  78.9 15.9 %collective-permute-start.5 = (bf16[8,512]{1,0:T(8,128)(2,1)}, bf16[8,512]{1,0:T(8,128)(2,1)S(1)}, u32[]{:S(2)}, u32[]{:S(2)}) collective-permute-start(bf16[8,512]{1,0:T(8,128)(2,1)} %after.3), channel_id=1, source_target_pairs={{0,24},{4,28},{8,16},{12,20},{16,8},{20,12},{24,0},{28,4},{1,25},{... | collective-permute-start | bytes 24584 | tf_op jit(solution)/shard_map/ppermute | solution.py:399
  81.6 13.3 %collective-permute-start.4 = (bf16[8,512]{1,0:T(8,128)(2,1)}, bf16[8,512]{1,0:T(8,128)(2,1)S(1)}, u32[]{:S(2)}, u32[]{:S(2)}) collective-permute-start(bf16[8,512]{1,0:T(8,128)(2,1)} %after.3), channel_id=1, source_target_pairs={{0,16},{4,20},{8,24},{12,28},{16,0},{20,4},{24,8},{28,12},{1,17},{... | collective-permute-start | bytes 24584 | tf_op jit(solution)/shard_map/ppermute | solution.py:399
  82.1 12.7 %collective-permute-start.3 = (bf16[8,512]{1,0:T(8,128)(2,1)}, bf16[8,512]{1,0:T(8,128)(2,1)S(1)}, u32[]{:S(2)}, u32[]{:S(2)}) collective-permute-start(bf16[8,512]{1,0:T(8,128)(2,1)} %after.3), channel_id=1, source_target_pairs={{0,8},{4,12},{8,0},{12,4},{16,24},{20,28},{24,16},{28,20},{1,9},{5... | collective-permute-start | bytes 24584 | tf_op jit(solution)/shard_map/ppermute | solution.py:399
  95.6 1.2 collective-permute-start.6
  97.4 4.9 %copy-start.12 = (bf16[512]{0:T(512)(128)(2,1)S(1)}, bf16[512]{0:T(512)(128)(2,1)}, u32[]{:S(2)}) copy-start(bf16[512]{0:T(512)(128)(2,1)} %param.21) | copy-start | bytes 3076
  97.4 4.9 %copy-start.13 = (s32[64,2]{0,1:T(2,128)S(1)}, s32[64,2]{0,1:T(2,128)}, u32[]{:S(2)}) copy-start(s32[64,2]{0,1:T(2,128)} %param.26) | copy-start | bytes 1540
  97.4 5.0 %copy-start.15 = (s32[8]{0:T(128)S(1)}, s32[8]{0:T(128)}, u32[]{:S(2)}) copy-start(s32[8]{0:T(128)} %constant.41.clone) | copy-start | bytes 100
  97.4 5.7 %copy-start.11 = (bf16[512,8]{0,1:T(8,128)(2,1)S(1)}, bf16[512,8]{0,1:T(8,128)(2,1)}, u32[]{:S(2)}) copy-start(bf16[512,8]{0,1:T(8,128)(2,1)} %param.22) | copy-start | bytes 24580
  97.4 6.0 %copy-start.4 = (bf16[64,512]{1,0:T(8,128)(2,1)S(1)}, bf16[64,512]{1,0:T(8,128)(2,1)}, u32[]{:S(2)}) copy-start(bf16[64,512]{1,0:T(8,128)(2,1)} %copy-done.3) | copy-start | bytes 196612
  97.4 72.1 %all-to-all-start.1 = ((bf16[8,704,512]{2,1,0:T(8,128)(2,1)}), bf16[8,704,512]{2,1,0:T(8,128)(2,1)}, u32[]{:S(2)}, u32[]{:S(2)}) async-start(bf16[8,704,512]{2,1,0:T(8,128)(2,1)} %after.5), calls=%async_computation.1 | async-start | bytes 11534336 | tf_op jit(solution)/shard_map/all_to_all | solution.py:435
  112.2 8.0 %collective-permute-start.9 = (bf16[4,16,768]{2,1,0:T(8,128)(2,1)S(1)}, bf16[4,16,768]{2,1,0:T(8,128)(2,1)S(1)}, u32[]{:S(2)}, u32[]{:S(2)}) collective-permute-start(bf16[4,16,768]{2,1,0:T(8,128)(2,1)S(1)} %get-tuple-element.20), channel_id=1, source_target_pairs={{0,3},{1,2},{2,1},{3,0},{4,7},{5,6},{6,5},{7,4},{8,11},{9,10},{10,... | collective-permute-start | bytes 294920 | tf_op jit(solution)/shard_map/ppermute | solution.py:399
  116.5 8.8 %collective-permute-start.8 = (bf16[4,16,768]{2,1,0:T(8,128)(2,1)S(1)}, bf16[4,16,768]{2,1,0:T(8,128)(2,1)S(1)}, u32[]{:S(2)}, u32[]{:S(2)}) collective-permute-start(bf16[4,16,768]{2,1,0:T(8,128)(2,1)S(1)} %get-tuple-element.21), channel_id=1, source_target_pairs={{0,2},{1,3},{2,0},{3,1},{4,6},{5,7},{6,4},{7,5},{8,10},{9,11},{10,... | collective-permute-start | bytes 294920 | tf_op jit(solution)/shard_map/ppermute | solution.py:399
  116.5 8.8 %collective-permute-start.7 = (bf16[4,16,768]{2,1,0:T(8,128)(2,1)S(1)}, bf16[4,16,768]{2,1,0:T(8,128)(2,1)S(1)}, u32[]{:S(2)}, u32[]{:S(2)}) collective-permute-start(bf16[4,16,768]{2,1,0:T(8,128)(2,1)S(1)} %get-tuple-element.22), channel_id=1, source_target_pairs={{0,1},{1,0},{2,3},{3,2},{4,5},{5,4},{6,7},{7,6},{8,9},{9,8},{10,11... | collective-permute-start | bytes 294920 | tf_op jit(solution)/shard_map/ppermute | solution.py:399
  125.5 43.4 %copy-start.7 = (bf16[8,512]{1,0:T(8,128)(2,1)S(1)}, bf16[8,512]{1,0:T(8,128)(2,1)}, u32[]{:S(2)}) copy-start(bf16[8,512]{1,0:T(8,128)(2,1)} %after.3) | copy-start | bytes 24580
  125.5 6.0 %collective-permute-start.12 = (bf16[2,16,768]{2,1,0:T(8,128)(2,1)S(1)}, bf16[2,16,768]{2,1,0:T(8,128)(2,1)S(1)}, u32[]{:S(2)}, u32[]{:S(2)}) collective-permute-start(bf16[2,16,768]{2,1,0:T(8,128)(2,1)S(1)} %activate.1.refs_0_), channel_id=1, source_target_pairs={{0,3},{1,2},{2,1},{3,0},{4,7},{5,6},{6,5},{7,4},{8,11},{9,10},{10,... | collective-permute-start | bytes 147464 | tf_op jit(solution)/shard_map/ppermute | solution.py:399
  128.0 5.0 %collective-permute-start.11 = (bf16[2,16,768]{2,1,0:T(8,128)(2,1)S(1)}, bf16[2,16,768]{2,1,0:T(8,128)(2,1)S(1)}, u32[]{:S(2)}, u32[]{:S(2)}) collective-permute-start(bf16[2,16,768]{2,1,0:T(8,128)(2,1)S(1)} %activate.1.refs_0_), channel_id=1, source_target_pairs={{0,2},{1,3},{2,0},{3,1},{4,6},{5,7},{6,4},{7,5},{8,10},{9,11},{10,... | collective-permute-start | bytes 147464 | tf_op jit(solution)/shard_map/ppermute | solution.py:399
  128.0 5.0 %collective-permute-start.10 = (bf16[2,16,768]{2,1,0:T(8,128)(2,1)S(1)}, bf16[2,16,768]{2,1,0:T(8,128)(2,1)S(1)}, u32[]{:S(2)}, u32[]{:S(2)}) collective-permute-start(bf16[2,16,768]{2,1,0:T(8,128)(2,1)S(1)} %activate.1.refs_0_), channel_id=1, source_target_pairs={{0,1},{1,0},{2,3},{3,2},{4,5},{5,4},{6,7},{7,6},{8,9},{9,8},{10,11... | collective-permute-start | bytes 147464 | tf_op jit(solution)/shard_map/ppermute | solution.py:399
  139.2 1.3 collective-permute-start.13
  140.5 27.2 %collective-permute-start.14 = (f32[8,512]{1,0:T(8,128)S(1)}, f32[8,512]{1,0:T(8,128)S(1)}, u32[]{:S(2)}, u32[]{:S(2)}) collective-permute-start(f32[8,512]{1,0:T(8,128)S(1)} %get-tuple-element.24), channel_id=1, source_target_pairs={{0,8},{4,12},{8,0},{12,4},{16,24},{20,28},{24,16},{28,20},{1,9},{5... | collective-permute-start | bytes 49160 | tf_op jit(solution)/shard_map/ppermute | solution.py:399
  142.2 26.6 %collective-permute-start.16 = (f32[8,512]{1,0:T(8,128)S(1)}, f32[8,512]{1,0:T(8,128)S(1)}, u32[]{:S(2)}, u32[]{:S(2)}) collective-permute-start(f32[8,512]{1,0:T(8,128)S(1)} %get-tuple-element.25), channel_id=1, source_target_pairs={{0,24},{4,28},{8,16},{12,20},{16,8},{20,12},{24,0},{28,4},{1,25},{... | collective-permute-start | bytes 49160 | tf_op jit(solution)/shard_map/ppermute | solution.py:399
  143.7 25.1 %collective-permute-start.15 = (f32[8,512]{1,0:T(8,128)S(1)}, f32[8,512]{1,0:T(8,128)S(1)}, u32[]{:S(2)}, u32[]{:S(2)}) collective-permute-start(f32[8,512]{1,0:T(8,128)S(1)} %get-tuple-element.26), channel_id=1, source_target_pairs={{0,16},{4,20},{8,24},{12,28},{16,0},{20,4},{24,8},{28,12},{1,17},{... | collective-permute-start | bytes 49160 | tf_op jit(solution)/shard_map/ppermute | solution.py:399
  169.5 5.9 %copy-start.6 = (s32[8,5632]{1,0:T(8,128)S(1)}, s32[8,5632]{1,0:T(8,128)}, u32[]{:S(2)}) copy-start(s32[8,5632]{1,0:T(8,128)} %old_ref.1) | copy-start | bytes 540676
  169.5 70.8 %all-to-all-start = ((bf16[8,704,512]{2,1,0:T(8,128)(2,1)}), bf16[8,704,512]{2,1,0:T(8,128)(2,1)}, u32[]{:S(2)}, u32[]{:S(2)}) async-start(bf16[8,704,512]{2,1,0:T(8,128)(2,1)} %after.4), calls=%async_computation | async-start | bytes 11534336 | tf_op jit(solution)/shard_map/all_to_all | solution.py:435
  (4 other events, 6.6 us)

commit v2 on v1

--- a/solution.py
+++ b/solution.py
@@ -16,6 +16,7 @@
 norm_eps = 1e-06
 neg_big = -1e30
 VMEM_LIMIT = 48 * 1024 * 1024
+PACK_LIMIT = 61 * 1024 * 1024
 
 
 def up_to(value, unit):
@@ -94,12 +95,6 @@
     earlier = ones_where((line // rows == column // rows) & (column < line))
     base = jnp.dot(earlier, tiles.astype(jnp.bfloat16), preferred_element_type=jnp.float32)
     return start, lead, tiles, base
-
-
-def write_plan(plan_ref, start, lead, tiles, base):
-    shared = start - lead * TILE
-    for n, part in enumerate((lead, tiles, base, shared)):
-        plan_ref[n] = part.astype(jnp.int32)
 
 
 def outgoing_kernel(lines, rows, new_ref, held_ref, stack_ref, plan_ref):
@@ -120,7 +115,8 @@
     ranks = jnp.dot(hits.astype(jnp.bfloat16), until, preferred_element_type=jnp.float32)
     counts = jnp.broadcast_to(jnp.sum(hits, axis=1, keepdims=True), (experts * rows, LANES))
     start, lead, tiles, base = segment_plan(counts, experts, rows)
-    write_plan(plan_ref, start, lead, tiles, base)
+    for n, part in enumerate((lead, tiles, base, start - lead * TILE)):
+        plan_ref[n] = part.astype(jnp.int32)
     offset = (base * TILE + start - lead * TILE - 1.0)[:, :1]
     placed = hits * (ranks + offset)
     for e in range(experts):
@@ -128,7 +124,7 @@
         stack_ref[e] = jnp.where(real, row, -1.0).astype(jnp.int32)
 
 
-def incoming_kernel(lines, rows, old_ref, wanted_ref, stack_ref, plan_ref):
+def incoming_kernel(lines, rows, block_tiles, slot, old_ref, wanted_ref, stack_ref, plan_ref):
     experts = old_ref.shape[0]
     width = wanted_ref.shape[1]
     real = iota((1, width), 1) < lines
@@ -136,8 +132,8 @@
     hits = []
     full = old_ref.shape[1]
     numbers = numbers_for(full)
-    slot = iota((64, full), 1)
-    values = (as_bf16(slot >> 7), as_bf16(slot & 127))
+    at = iota((64, full), 1)
+    values = (as_bf16(at >> 7), as_bf16(at & 127))
     for e in range(experts):
         high, low = look_up(old_ref[e : e + 1, :], wanted_ref[e : e + 1, :], numbers, values)
         slots = high * 128.0 + low
@@ -147,7 +143,19 @@
     hits = jnp.concatenate(hits, axis=0)
     counts = jnp.broadcast_to(jnp.sum(hits, axis=1, keepdims=True), (experts * rows, LANES))
     start, lead, tiles, base = segment_plan(counts, experts, rows)
-    write_plan(plan_ref, start, lead, tiles, base)
+    line = iota((experts * rows, LANES), 0)
+    peer = (line % rows).astype(jnp.float32)
+    longest = [
+        jnp.max(tiles[e * rows : (e + 1) * rows], axis=0, keepdims=True) for e in range(experts)
+    ]
+    longest = jnp.concatenate(
+        [jnp.broadcast_to(most, (rows, LANES)) for most in longest], axis=0
+    )
+    slotted = longest <= slot
+    lead = jnp.where(slotted, jnp.minimum(lead, float(block_tiles - slot)), lead)
+    base = jnp.where(slotted, peer * slot, base)
+    for n, part in enumerate((lead, tiles, base, jnp.where(slotted, 1.0, 0.0))):
+        plan_ref[n] = part.astype(jnp.int32)
     blank = jnp.zeros((LANES - experts, width), jnp.float32)
     columns = jnp.transpose(jnp.concatenate(held_at + [blank], axis=0))
     rows_out = []
@@ -163,7 +171,12 @@
         first = jnp.concatenate(firsts, axis=0)
         offset = (base[mine] * TILE + start[mine] - lead[mine] * TILE - first)[:, :1]
         rows_out.append(jnp.sum(hits[mine] * (rank + offset), axis=0, keepdims=True))
-    stack_ref[...] = jnp.transpose(jnp.concatenate(rows_out + [blank], axis=0))
+    places = jnp.transpose(jnp.concatenate(rows_out + [blank], axis=0))
+    for e in range(experts):
+        place = jnp.broadcast_to(places[:lines, e : e + 1], (lines, LANES))
+        block = jnp.floor(place * (1.0 / 256.0))
+        stack_ref[e, 0] = (place - 256.0 * block).astype(jnp.bfloat16)
+        stack_ref[e, 1] = block.astype(jnp.bfloat16)
 
 
 STRAIGHT = 8
@@ -174,12 +187,13 @@
 
 
 def pack_kernel(rows, span, plan_ref, place_ref, lines_ref, out_ref, packed_ref, number_ref, sem, *stages):
-    step = pl.program_id(0)
-    pairs = pl.num_programs(0) * span * rows
+    part = pl.program_id(0)
+    step = pl.program_id(1)
+    pairs = pl.num_programs(1) * span * rows
     deep, _ = stages[0].shape
     lines = lines_ref.shape[2]
 
-    @pl.when(step == 0)
+    @pl.when((part == 0) & (step == 0))
     def _():
         number_ref[...] = counting(number_ref.shape, 0)
 
@@ -224,98 +238,114 @@
 
             lax.fori_loop(0, rows, long_peer, 0)
 
-    @pl.when(step == pl.num_programs(0) - 1)
-    def _():
-        copy = pltpu.make_async_copy(packed_ref, out_ref, sem)
+    @pl.when(step == pl.num_programs(1) - 1)
+    def _():
+        copy = pltpu.make_async_copy(packed_ref, out_ref.at[:, part], sem)
         copy.start()
         copy.wait()
 
 
-def unpack_kernel(rows, span, stage_count, plan_ref, place_ref, block_ref, *rest):
-    stages = rest[-stage_count:]
-    out_ref, number_ref = rest[-stage_count - 2 : -stage_count]
-    step = pl.program_id(0)
-    pairs = pl.num_programs(0) * span * rows
-    deep, _ = stages[0].shape
+def unpack_kernel(slot, plan_ref, place_ref, block_ref, *rest):
+    out_ref, stage_ref, sems = rest[-3:]
+    experts = pl.num_programs(1)
+    rows = block_ref.shape[0]
+    pairs = experts * rows
+    _, deep, _ = stage_ref.shape
     lines = out_ref.shape[2]
+    step = pl.program_id(0) * experts + pl.program_id(1)
+    steps = pl.num_programs(0) * experts
+
+    def entry(n, e, s):
+        return plan_ref[n * pairs + e * rows + s]
+
+    def slotted(e):
+        return entry(3, e, 0) > 0
+
+    def slot_copy(at, s):
+        part, e, buffer = at // experts, at % experts, at % 2
+        there = pl.ds(pl.multiple_of(entry(0, e, s) * TILE, TILE), slot * TILE)
+        return pltpu.make_async_copy(
+            block_ref.at[s, part, there],
+            stage_ref.at[buffer, pl.ds(s * slot * TILE, slot * TILE)],
+            sems.at[buffer, s],
+        )
+
+    def begin(at):
+        @pl.when(slotted(at % experts))
+        def _():
+            for s in range(rows):
+                slot_copy(at, s).start()
 
     @pl.when(step == 0)
     def _():
-        for stage_ref in stages:
-            stage_ref[...] = jnp.zeros_like(stage_ref)
-        number_ref[...] = counting(number_ref.shape, 1)
-
-    def entry(n, j, d):
-        return plan_ref[n * pairs + (step * span + j) * rows + d]
-
-    for j, stage_ref in enumerate(stages):
-
-        def one_peer(s, most, j=j, stage_ref=stage_ref):
-            lead, tiles, base = entry(0, j, s), entry(1, j, s), entry(2, j, s)
-            for t in range(STRAIGHT):
-                n = jnp.maximum(jnp.minimum(t, tiles - 1), 0)
-                stage_ref[tile_at(base + n), :] = block_ref[s, tile_at(lead + n), :]
-            return jnp.maximum(most, tiles)
-
-        most = lax.fori_loop(0, rows, one_peer, 0, unroll=rows <= 8)
-
-        @pl.when(most > STRAIGHT)
-        def _(j=j, stage_ref=stage_ref):
-            def long_peer(s, carry):
-                lead, tiles, base = entry(0, j, s), entry(1, j, s), entry(2, j, s)
-
-                def put(t, c):
-                    stage_ref[tile_at(base + t), :] = block_ref[s, tile_at(lead + t), :]
-                    return c
-
-                return lax.fori_loop(STRAIGHT, tiles, put, carry)
-
-            lax.fori_loop(0, rows, long_peer, 0)
-
-    for j, stage_ref in enumerate(stages):
-        place = jnp.where(iota((lines, LANES), 1) == step * span + j, place_ref[:lines, :], 0.0)
-        place = jnp.sum(place, axis=1, keepdims=True).astype(jnp.int32)
-        onehot = jnp.concatenate(
-            [equal_ones(number_ref[...], within(place, n)) for n in range(deep // 256)], axis=1
-        )
-        out_ref[j, 0] = jnp.dot(
-            onehot, stage_ref[...], preferred_element_type=jnp.float32
-        ).astype(jnp.bfloat16)
-
-
-def call_plan(kernel, name, table, ids, lines, rows, transposed):
-    experts, width = ids.shape
-    stack = (
-        jax.ShapeDtypeStruct((width, LANES), jnp.float32)
-        if transposed
-        else jax.ShapeDtypeStruct((experts, 1, width), jnp.int32)
-    )
-    stack, plan = pl.pallas_call(
-        functools.partial(kernel, lines, rows),
-        out_shape=(stack, jax.ShapeDtypeStruct((4, experts * rows, LANES), jnp.int32)),
+        stage_ref[...] = jnp.zeros_like(stage_ref)
+        begin(step)
+
+    @pl.when(step + 1 < steps)
+    def _():
+        begin(step + 1)
+
+    part, e, buffer = pl.program_id(0), pl.program_id(1), step % 2
+
+    @pl.when(slotted(e))
+    def _():
+        for s in range(rows):
+            slot_copy(step, s).wait()
+
+    @pl.when(jnp.logical_not(slotted(e)))
+    def _():
+        def one_peer(s, carry):
+            def put(t, c):
+                copy = pltpu.make_async_copy(
+                    block_ref.at[s, part, tile_at(entry(0, e, s) + t)],
+                    stage_ref.at[buffer, tile_at(entry(2, e, s) + t)],
+                    sems.at[buffer, 0],
+                )
+                copy.start()
+                copy.wait()
+                return c
+
+            return lax.fori_loop(0, entry(1, e, s), put, carry)
+
+        lax.fori_loop(0, rows, one_peer, 0)
+
+    within_block, block = place_ref[0, 0], place_ref[0, 1]
+    lane = counting((lines, LANES), 1)
+    pieces = []
+    for first in range(0, deep, LANES):
+        away = jnp.abs(block - jnp.asarray(first // 256, jnp.bfloat16))
+        place = within_block + away * jnp.asarray(512, jnp.bfloat16)
+        pieces.append(equal_ones(lane + jnp.asarray(first % 256, jnp.bfloat16), place))
+    onehot = jnp.concatenate(pieces, axis=1)
+    out_ref[0, 0] = jnp.dot(
+        onehot, stage_ref[buffer], preferred_element_type=jnp.float32
+    ).astype(jnp.bfloat16)
+
+
+def call_plan(kernel, name, table, ids, pairs, place):
+    return pl.pallas_call(
+        kernel,
+        out_shape=(place, jax.ShapeDtypeStruct((4, pairs, LANES), jnp.int32)),
         compiler_params=params(),
         cost_estimate=pl.CostEstimate(
-            flops=20 * experts * table.shape[1] * 256,
-            bytes_accessed=8 * table.size,
-            transcendentals=0,
+            flops=20 * table.size * 256, bytes_accessed=8 * table.size, transcendentals=0
         ),
         name=name,
     )(table, ids)
-    return stack, plan[:, :, 0].reshape(-1)
 
 
 def pack(expert_lines, place, plan, piece, rows, block_rows, deep):
-    experts, _, lines, _ = expert_lines.shape
-    part, column, width = piece
+    experts, _, lines, width = expert_lines.shape
+    first, count = piece
     span = 2 - experts % 2
     return pl.pallas_call(
         functools.partial(pack_kernel, rows, span),
         grid_spec=pltpu.PrefetchScalarGridSpec(
             num_scalar_prefetch=1,
-            grid=(experts // span,),
+            grid=(count, experts // span),
             in_specs=[
-                pl.BlockSpec((span, 1, place.shape[2]), lambda e, plan: (e, 0, 0)),
-                pl.BlockSpec((span, 1, lines, width), lambda e, plan: (e, part, 0, column)),
+                pl.BlockSpec((span, 1, place.shape[2]), lambda p, e, plan: (e, 0, 0)),
+                pl.BlockSpec((span, 1, lines, width), lambda p, e, plan: (e, first + p, 0, 0)),
             ],
             out_specs=pl.BlockSpec(memory_space=pltpu.HBM),
             scratch_shapes=[
@@ -325,25 +355,24 @@
             ]
             + [pltpu.VMEM((deep, width), jnp.bfloat16)] * span,
         ),
-        out_shape=jax.ShapeDtypeStruct((rows, block_rows, width), jnp.bfloat16),
-        compiler_params=params(),
+        out_shape=jax.ShapeDtypeStruct((rows, count, block_rows, width), jnp.bfloat16),
+        compiler_params=pltpu.CompilerParams(vmem_limit_bytes=PACK_LIMIT),
         cost_estimate=pl.CostEstimate(
-            flops=2 * experts * deep * lines * width,
-            bytes_accessed=4 * experts * lines * width,
+            flops=2 * count * experts * deep * lines * width,
+            bytes_accessed=4 * count * experts * lines * width,
             transcendentals=0,
         ),
         name="pack_lines",
     )(plan, place, expert_lines)
 
 
-def unpack(arrived, place, plan, piece, shape, deep, previous):
-    experts, _, lines, _ = shape
-    part, column, width = piece
-    rows, block_rows, _ = arrived.shape
-    span = 2 - experts % 2
+def unpack(arrived, place, plan, piece, shape, deep, slot, previous):
+    experts, _, lines, width = shape
+    first, count = piece
+    rows = arrived.shape[0]
     in_specs = [
-        pl.BlockSpec(place.shape, lambda e, plan: (0, 0)),
-        pl.BlockSpec((rows, block_rows, width), lambda e, plan: (0, 0, 0)),
+        pl.BlockSpec((1, 2, lines, LANES), lambda p, e, plan: (e, 0, 0, 0)),
+        pl.BlockSpec(memory_space=pl.ANY),
     ]
     operands = [plan, place, arrived]
     aliases = {}
@@ -352,21 +381,23 @@
         operands.append(previous)
         aliases = {3: 0}
     return pl.pallas_call(
-        functools.partial(unpack_kernel, rows, span, span),
+        functools.partial(unpack_kernel, slot),
         grid_spec=pltpu.PrefetchScalarGridSpec(
             num_scalar_prefetch=1,
-            grid=(experts // span,),
+            grid=(count, experts),
             in_specs=in_specs,
-            out_specs=pl.BlockSpec((span, 1, lines, width), lambda e, plan: (e, part, 0, column)),
-            scratch_shapes=[pltpu.VMEM((lines, 256), jnp.bfloat16)]
-            + [pltpu.VMEM((deep, width), jnp.bfloat16)] * span,
+            out_specs=pl.BlockSpec((1, 1, lines, width), lambda p, e, plan: (e, first + p, 0, 0)),
+            scratch_shapes=[
+                pltpu.VMEM((2, deep, width), jnp.bfloat16),
+                pltpu.SemaphoreType.DMA((2, rows)),
+            ],
         ),
         out_shape=jax.ShapeDtypeStruct(shape, jnp.bfloat16),
         input_output_aliases=aliases,
         compiler_params=params(),
         cost_estimate=pl.CostEstimate(
-            flops=2 * experts * deep * lines * width,
-            bytes_accessed=4 * experts * lines * width,
+            flops=2 * count * experts * deep * lines * width,
+            bytes_accessed=4 * count * experts * lines * width,
             transcendentals=0,
         ),
         name="unpack_lines",
@@ -385,6 +416,7 @@
         out_specs=[anywhere] * len(values),
         out_shape=[jax.ShapeDtypeStruct(v.shape, v.dtype) for v in values],
         input_output_aliases={n: n for n in range(len(values))},
+        compiler_params=pltpu.CompilerParams(vmem_limit_bytes=PACK_LIMIT),
         name="after",
     )(*values, *signals)
 
@@ -397,10 +429,6 @@
 def from_peer(block, axis, offset):
     size = lax.axis_size(axis)
     return lax.ppermute(block, axis, [(i, i ^ offset) for i in range(size)])
-
-
-def bulk_pieces(parts, width):
-    return [(part, 0, width) for part in range(parts)]
 
 
 class Migration:
@@ -409,19 +437,27 @@
         experts, parts, lines, width = expert_lines.shape
         padded = up_to(lines, LANES)
         block_rows = up_to(experts * lines // rows, TILE)
-        self.deep = up_to(lines + 2 * (TILE - 1) * rows, TILE) + TILE
+        pairs = experts * rows
+        compact = up_to(lines + 2 * (TILE - 1) * rows, TILE) + TILE
+        self.slot = min(STRAIGHT, block_rows // TILE)
+        self.deep = up_to(max(compact, rows * self.slot * TILE), 256)
         self.shape = expert_lines.shape
-        self.pieces = bulk_pieces(parts, width)
+        self.pieces = [(0, 1), (1, parts - 1)]
         out_place, out_plan = call_plan(
-            outgoing_kernel, "outgoing_plan", new_lines, own_ids(old_lines, lines, padded),
-            lines, rows, False,
+            functools.partial(outgoing_kernel, lines, rows), "outgoing_plan",
+            new_lines, own_ids(old_lines, lines, padded), pairs,
+            jax.ShapeDtypeStruct((experts, 1, padded), jnp.int32),
         )
-        self.in_place, self.in_plan = call_plan(
-            incoming_kernel, "incoming_plan", old_lines, own_ids(new_lines, lines, padded),
-            lines, rows, True,
+        self.in_place, in_plan = call_plan(
+            functools.partial(incoming_kernel, lines, rows, block_rows // TILE, self.slot),
+            "incoming_plan",
+            old_lines, own_ids(new_lines, lines, padded), pairs,
+            jax.ShapeDtypeStruct((experts, 2, lines, LANES), jnp.bfloat16),
         )
+        out_plan = out_plan[:, :, 0].reshape(-1)
+        self.in_plan = in_plan[:, :, 0].reshape(-1)
         self.packed = [
-            pack(expert_lines, out_place, out_plan, piece, rows, block_rows, self.deep)
+            pack(expert_lines, out_place, out_plan, piece, rows, block_rows, compact)
             for piece in self.pieces
         ]
         self.arrived = []
@@ -438,7 +474,7 @@
     def receive(self, piece):
         self.moved = unpack(
             self.arrived[piece], self.in_place, self.in_plan, self.pieces[piece], self.shape,
-            up_to(self.deep, 256), self.moved,
+            self.deep, self.slot, self.moved,
         )
 
 
@@ -676,6 +712,8 @@
         ),
         name="down",
     )(me, routes, *chunks, expert_lines)
+    migration.receive(0)
+    (produced,) = after([produced], [migration.moved])
     half = tokens // 2
     both_cores = produced[:half] + from_peer(produced[half:], "row", 1)
     blocks = both_cores.reshape(rows // 2, own, width)
@@ -702,16 +740,13 @@
 ):
     expert_lines = jnp.transpose(expert_weights, (0, 2, 1, 3))
     migration = Migration(expert_lines, old_lines, new_lines)
-    for _ in range(len(migration.pieces) - 2):
-        migration.send()
+    migration.send()
     attended = attend(queries, new_kv, prompt_kv, suffix_kv, lengths)
     projected = jnp.dot(attended, w_out, preferred_element_type=jnp.float32)
     h_mid = (hidden.astype(jnp.float32) + projected).astype(jnp.bfloat16)
     (h_mid,) = after([h_mid], migration.packed)
     mixed = experts_part(h_mid, moe_gain, w_router, expert_lines, routes, migration)
-    migration.send([mixed])
-    for piece in range(len(migration.pieces)):
-        migration.receive(piece)
+    migration.receive(1)
     return (h_mid.astype(jnp.float32) + mixed, jnp.transpose(migration.moved, (0, 2, 1, 3)))
 
 

time: 256 us -> 257 us (level)
  waiting for transfers between devices: 76.8 us -> 84.8 us
  starting transfers between devices: 37.1 us -> 32.7 us
  local copies, waits for them, and re-layouts: 19.7 us -> 15.8 us
    ppermute x17, waiting for transfers between devices: 50.1 us -> 84.8 us  [from_peer(): return lax.ppermute(block, axis, [(i, i ^ offset) for i in range(size)])]
    all_to_all x3 -> x2, waiting for transfers between devices: 26.6 us -> 0.01 us  [send(): lax.all_to_all(block, 'row', split_axis=0, concat_axis=0, tiled=True)]
    pallas_call x5 -> x4, Pallas kernels: 58.1 us -> 51.2 us  [the longest x2 34.5 us: unpack(): pl.pallas_call(functools.partial(unpack_kernel, slot), grid_spec=pltpu.Pr...]
    unnamed x41, local copies, waits for them, and re-layouts: 11.5 us -> 6.24 us
    pallas_call x3 -> x2, Pallas kernels: 35 us -> 39.9 us  [pack(): pl.pallas_call(functools.partial(pack_kernel, rows, span), grid_spec=pltp...]
    all_to_all x3 -> x2, starting transfers between devices: 15.2 us -> 10.8 us  [send(): lax.all_to_all(block, 'row', split_axis=0, concat_axis=0, tiled=True)]
  transfers between devices with their start and end apart: 20 -> 19, of which waited for: 10 -> 10; matrix products, arithmetic and copies ran while one was open for 8% -> 10% of each run, Pallas kernels for 30% -> 25%
where the time goes in v2:
time: 257 us; the launch traced here: 255 us
  Pallas kernels  106 us (41%)
  waiting for transfers between devices  84.8 us (33%)
  starting transfers between devices  32.7 us (13%)
  local copies, waits for them, and re-layouts  15.8 us (6%)
  matrix products  8.45 us (3%)
  other arithmetic  5.59 us (2%)
    ppermute x17, waiting for transfers between devices, from_peer(): return lax.ppermute(block, axis, [(i, i ^ offset) for i in range(size)])  84.8 us
    pallas_call x2, Pallas kernels, pack(): pl.pallas_call(functools.partial(pack_kernel, rows, span), grid_spec=pltp...  39.9 us
    pallas_call x2, Pallas kernels, unpack(): pl.pallas_call(functools.partial(unpack_kernel, slot), grid_spec=pltpu.Pr...  34.5 us
    ppermute x17, starting transfers between devices, from_peer(): return lax.ppermute(block, axis, [(i, i ^ offset) for i in range(size)])  21.9 us
    pallas_call x2, Pallas kernels, call_plan(): pl.pallas_call(kernel, out_shape=(place, jax.ShapeDtypeStruct((4, pairs,...  16.8 us
    all_to_all x2, starting transfers between devices, send(): lax.all_to_all(block, 'row', split_axis=0, concat_axis=0, tiled=True)  10.8 us
    pallas_call x1, Pallas kernels, experts_part(): pl.pallas_call(gate_up_kernel, grid_spec=pltpu.PrefetchScalarGridSpec(num...  8.76 us
    unnamed x41, local copies, waits for them, and re-layouts  6.24 us
  transfers between devices with their start and end apart: 19, of which 10 were waited for; matrix products, arithmetic and copies ran while one was open for 10% of the time, Pallas kernels for 25%

profile of v2, /device:TPU:0, one launch (start us, length us, event | category | flops | bytes accessed | tf_op | source)
XLA Modules:
  0.0 254.8 jit_solution(8883362081079070810)
XLA Ops:
  2.4 6.1 %outgoing_plan.1 = (s32[8,1,768]{2,1,0:T(1,128)S(1)}, s32[4,64,128]{2,1,0:T(8,128)S(1)}) custom-call(s32[8,5632]{1,0:T(8,128)S(1)} %copy-done.4, s32[8,768]{1,0:T(8,128)S(1)} %pad.11.held_ref), custom_call_target="tpu_custom_call" | custom-call | flops 230686720 | bytes 360448 | tf_op jit(solution)/shard_map/outgoing_plan/pallas_call | solution.py:326
  9.9 14.1 %pack_lines.2.refs_1_ = bf16[8,1,704,512]{3,2,1,0:T(8,128)(2,1)} custom-call(s32[256]{0:T(256)} %reshape_squeeze.27.plan_ref, s32[8,1,768]{2,1,0:T(1,128)} %copy-done.3, bf16[8,3,704,512]{3,2,1,0:T(8,128)(2,1)} %bitcast.81), custom_call_target="tpu_custom_call" | custom-call | flops 5536481280 | bytes 11534336 | tf_op jit(solution)/shard_map/pack_lines/pallas_call | solution.py:341
  23.9 5.2 %all-to-all-start = ((bf16[8,1,704,512]{3,2,1,0:T(8,128)(2,1)}), bf16[8,1,704,512]{3,2,1,0:T(8,128)(2,1)}, u32[]{:S(2)}, u32[]{:S(2)}) async-start(bf16[8,1,704,512]{3,2,1,0:T(8,128)(2,1)} %pack_lines.2.refs_1_), calls=%async_computation | async-start | bytes 11534336 | tf_op jit(solution)/shard_map/all_to_all | solution.py:471
  29.1 1.7 fusion.30
  31.9 1.7 fusion.29
  33.9 1.2 copy.145
  35.6 2.0 fusion.33
  38.4 1.2 fusion.32
  44.8 4.8 %collective-permute-start.2 = (f32[8,4224]{1,0:T(8,128)S(1)}, f32[8,4224]{1,0:T(8,128)S(1)}, u32[]{:S(2)}, u32[]{:S(2)}) collective-permute-start(f32[8,4224]{1,0:T(8,128)S(1)} %concatenate.10), channel_id=1, source_target_pairs={{0,3},{1,2},{2,1},{3,0},{4,7},{5,6},{6,5},{7,4},{8,11},{9,10},{10,... | collective-permute-start | bytes 405512 | tf_op jit(solution)/shard_map/ppermute | solution.py:431
  50.2 25.9 %pack_lines.3.refs_2_.refs_0_ = bf16[8,2,704,512]{3,2,1,0:T(8,128)(2,1)} custom-call(s32[256]{0:T(256)} %reshape_squeeze.27.plan_ref, s32[8,1,768]{2,1,0:T(1,128)} %copy-done.3, bf16[8,3,704,512]{3,2,1,0:T(8,128)(2,1)} %bitcast.82), custom_call_target="tpu_custom_call" | custom-call | flops 11072962560 | bytes 23068672 | tf_op jit(solution)/shard_map/pack_lines/pallas_call | solution.py:341
  76.7 3.5 %fusion.4.refs_0_ = bf16[8,512]{1,0:T(8,128)(2,1)} fusion(bf16[4096,512]{1,0:T(8,128)(2,1)} %param.20, f32[8,4096]{1,0:T(8,128)S(1)} %fusion.8, f32[8,32]{0,1:T(8,128)S(1)} %copy.126, bf16[8,512]{1,0:T(8,128)(2,1)S(1)} %copy-done.9), kind=kOutput, calls=%fused_computation.9 | convolution fusion | flops 33632256 | bytes 4342784 | tf_op jit(solution)/shard_map/dot_general | solution.py:745
  80.2 1.7 collective-permute-start.3
  81.9 1.5 collective-permute-start.4
  84.4 10.4 %collective-permute-done.3 = bf16[8,512]{1,0:T(8,128)(2,1)S(1)} collective-permute-done((bf16[8,512]{1,0:T(8,128)(2,1)}, bf16[8,512]{1,0:T(8,128)(2,1)S(1)}, u32[]{:S(2)}, u32[]{:S(2)}) %collective-permute-start.3) | collective-permute-done | bytes 8224 | tf_op jit(solution)/shard_map/ppermute | solution.py:431
  96.5 1.2 collective-permute-done.6
  98.3 5.6 %all-to-all-start.1 = ((bf16[8,2,704,512]{3,2,1,0:T(8,128)(2,1)}), bf16[8,2,704,512]{3,2,1,0:T(8,128)(2,1)}, u32[]{:S(2)}, u32[]{:S(2)}) async-start(bf16[8,2,704,512]{3,2,1,0:T(8,128)(2,1)} %after.5), calls=%async_computation.1 | async-start | bytes 23068672 | tf_op jit(solution)/shard_map/all_to_all | solution.py:471
  105.9 10.7 %incoming_plan.1 = (bf16[8,2,704,128]{3,2,1,0:T(8,128)(2,1)S(1)}, s32[4,64,128]{2,1,0:T(8,128)S(1)}) custom-call(s32[8,5632]{1,0:T(8,128)S(1)} %copy-done.5, s32[8,768]{1,0:T(8,128)S(1)} %pad.13.wanted_ref), custom_call_target="tpu_custom_call" | custom-call | flops 230686720 | bytes 360448 | tf_op jit(solution)/shard_map/incoming_plan/pallas_call | solution.py:326
  116.6 8.8 %gate_up.1 = bf16[4,4,16,768]{3,2,1,0:T(8,128)(2,1)S(1)} custom-call(s32[1]{0:T(128)} %bitcast.20.me_ref, bf16[64,512]{1,0:T(8,128)(2,1)S(1)} %copy-done.2, bf16[1,512]{1,0:T(2,128)(2,1)S(1)} %reshape.90.gain_ref, bf16[512,128]{1,0:T(8,128)(2,1)S(1)} %pad.12.router_ref, s32[64,2]{1,0:T(8,128)S(1)} %bitcast.78, bf16[8,3,704,512]{3,2,1,0:T(8,128)(2,1)} %bitcast.83, ...), custom_call_target="tpu_custom_call" | custom-call | flops 738197504 | bytes 11534336 | tf_op jit(solution)/shard_map/gate_up/pallas_call | solution.py:670
  125.4 2.3 collective-permute-start.7
  127.7 2.6 %collective-permute-start.8 = (bf16[4,16,768]{2,1,0:T(8,128)(2,1)S(1)}, bf16[4,16,768]{2,1,0:T(8,128)(2,1)S(1)}, u32[]{:S(2)}, u32[]{:S(2)}) collective-permute-start(bf16[4,16,768]{2,1,0:T(8,128)(2,1)S(1)} %get-tuple-element.19), channel_id=1, source_target_pairs={{0,2},{1,3},{2,0},{3,1},{4,6},{5,7},{6,4},{7,5},{8,10},{9,11},{10,... | collective-permute-start | bytes 294920 | tf_op jit(solution)/shard_map/ppermute | solution.py:431
  130.8 7.6 %collective-permute-done.8.refs_2_ = bf16[4,16,768]{2,1,0:T(8,128)(2,1)S(1)} collective-permute-done((bf16[4,16,768]{2,1,0:T(8,128)(2,1)S(1)}, bf16[4,16,768]{2,1,0:T(8,128)(2,1)S(1)}, u32[]{:S(2)}, u32[]{:S(2)}) %collective-permute-start.8) | collective-permute-done | bytes 98336 | tf_op jit(solution)/shard_map/ppermute | solution.py:431
  138.6 1.8 collective-permute-start.10
  140.4 1.4 collective-permute-start.11
  141.8 1.2 collective-permute-start.12
  143.2 3.1 %collective-permute-done.11.refs_2_ = bf16[2,16,768]{2,1,0:T(8,128)(2,1)S(1)} collective-permute-done((bf16[2,16,768]{2,1,0:T(8,128)(2,1)S(1)}, bf16[2,16,768]{2,1,0:T(8,128)(2,1)S(1)}, u32[]{:S(2)}, u32[]{:S(2)}) %collective-permute-start.11) | collective-permute-done | bytes 49184 | tf_op jit(solution)/shard_map/ppermute | solution.py:431
  146.3 1.4 collective-permute-done.12.refs_3_
  147.7 6.1 %down.1.refs_0_ = f32[64,512]{1,0:T(8,128)S(1)} custom-call(s32[1]{0:T(128)} %bitcast.20.me_ref, s32[64,2]{1,0:T(8,128)S(1)} %bitcast.80, bf16[2,16,768]{2,1,0:T(8,128)(2,1)S(1)} %activate.1.refs_0_, bf16[2,16,768]{2,1,0:T(8,128)(2,1)S(1)} %collective-permute-done.10.refs_1_, bf16[2,16,768]{2,1,0:T(8,128)(2,1)S(1)} %collective-permute-done.11.refs_2_, ...), custom_call_target="tpu_custom_call" | custom-call | flops 369098752 | bytes 5767168 | tf_op jit(solution)/shard_map/down/pallas_call | solution.py:697
  154.5 12.3 %unpack_lines.2.refs_1_.rest_0_ = bf16[8,3,704,512]{3,2,1,0:T(8,128)(2,1)} custom-call(s32[256]{0:T(256)S(1)} %reshape_squeeze.28.plan_ref, bf16[8,2,704,128]{3,2,1,0:T(8,128)(2,1)S(1)} %get-tuple-element.9.place_ref, bf16[8,1,704,512]{3,2,1,0:T(8,128)(2,1)} %all-to-all-done.block_ref), custom_call_target="tpu_custom_call" | custom-call | flops 5905580032 | bytes 11534336 | tf_op jit(solution)/shard_map/unpack_lines/pallas_call | solution.py:383
  167.7 1.3 collective-permute-done.13
  169.8 2.7 %collective-permute-start.16 = (f32[8,512]{1,0:T(8,128)S(1)}, f32[8,512]{1,0:T(8,128)S(1)}, u32[]{:S(2)}, u32[]{:S(2)}) collective-permute-start(f32[8,512]{1,0:T(8,128)S(1)} %get-tuple-element.23), channel_id=1, source_target_pairs={{0,24},{4,28},{8,16},{12,20},{16,8},{20,12},{24,0},{28,4},{1,25},{... | collective-permute-start | bytes 49160 | tf_op jit(solution)/shard_map/ppermute | solution.py:431
  173.4 58.5 %collective-permute-done.16 = f32[8,512]{1,0:T(8,128)S(1)} collective-permute-done((f32[8,512]{1,0:T(8,128)S(1)}, f32[8,512]{1,0:T(8,128)S(1)}, u32[]{:S(2)}, u32[]{:S(2)}) %collective-permute-start.16) | collective-permute-done | bytes 16416 | tf_op jit(solution)/shard_map/ppermute | solution.py:431
  232.5 22.1 %unpack_lines.3 = bf16[8,3,704,512]{3,2,1,0:T(8,128)(2,1)} custom-call(s32[256]{0:T(256)S(1)} %reshape_squeeze.28.plan_ref, bf16[8,2,704,128]{3,2,1,0:T(8,128)(2,1)S(1)} %get-tuple-element.9.place_ref, bf16[8,2,704,512]{3,2,1,0:T(8,128)(2,1)} %all-to-all-done.1.block_ref, ...), custom_call_target="tpu_custom_call", output_to_operand_aliasing={{}: (3, {})} | custom-call | flops 11811160064 | bytes 23068672 | tf_op jit(solution)/shard_map/unpack_lines/pallas_call | solution.py:383
  (114 shorter events, 22.1 us)
Async XLA Ops:
  1.5 0.9 copy-start.4
  23.9 74.4 %all-to-all-start = ((bf16[8,1,704,512]{3,2,1,0:T(8,128)(2,1)}), bf16[8,1,704,512]{3,2,1,0:T(8,128)(2,1)}, u32[]{:S(2)}, u32[]{:S(2)}) async-start(bf16[8,1,704,512]{3,2,1,0:T(8,128)(2,1)} %pack_lines.2.refs_1_), calls=%async_computation | async-start | bytes 11534336 | tf_op jit(solution)/shard_map/all_to_all | solution.py:471
  31.9 3.2 %copy-start.7 = (bf16[8,4096]{1,0:T(8,128)(2,1)S(1)}, bf16[8,4096]{1,0:T(8,128)(2,1)}, u32[]{:S(2)}) copy-start(bf16[8,4096]{1,0:T(8,128)(2,1)} %param.15) | copy-start | bytes 196612
  31.9 3.2 %copy-start.8 = (bf16[8,2,2048]{2,1,0:T(2,128)(2,1)S(1)}, bf16[8,2,2048]{2,1,0:T(2,128)(2,1)}, u32[]{:S(2)}) copy-start(bf16[8,2,2048]{2,1,0:T(2,128)(2,1)} %param.16) | copy-start | bytes 196612
  31.9 3.7 %copy-start.14 = (s32[8]{0:T(128)S(1)}, s32[8]{0:T(128)}, u32[]{:S(2)}) copy-start(s32[8]{0:T(128)} %param.19) | copy-start | bytes 100
  35.6 2.8 %copy-start.11 = (pred[8,32]{1,0:T(8,128)(4,1)}, pred[8,32]{1,0:T(8,128)(4,1)S(1)}, u32[]{:S(2)}) copy-start(pred[8,32]{1,0:T(8,128)(4,1)S(1)} %broadcast_compare_fusion) | copy-start | bytes 772
  44.8 31.9 %copy-start.9 = (bf16[8,512]{1,0:T(8,128)(2,1)S(1)}, bf16[8,512]{1,0:T(8,128)(2,1)}, u32[]{:S(2)}) copy-start(bf16[8,512]{1,0:T(8,128)(2,1)} %param.14) | copy-start | bytes 24580
  44.8 31.4 %collective-permute-start.2 = (f32[8,4224]{1,0:T(8,128)S(1)}, f32[8,4224]{1,0:T(8,128)S(1)}, u32[]{:S(2)}, u32[]{:S(2)}) collective-permute-start(f32[8,4224]{1,0:T(8,128)S(1)} %concatenate.10), channel_id=1, source_target_pairs={{0,3},{1,2},{2,1},{3,0},{4,7},{5,6},{6,5},{7,4},{8,11},{9,10},{10,... | collective-permute-start | bytes 405512 | tf_op jit(solution)/shard_map/ppermute | solution.py:431
  49.6 26.6 %collective-permute-start.1 = (f32[8,4224]{1,0:T(8,128)S(1)}, f32[8,4224]{1,0:T(8,128)S(1)}, u32[]{:S(2)}, u32[]{:S(2)}) collective-permute-start(f32[8,4224]{1,0:T(8,128)S(1)} %concatenate.10), channel_id=1, source_target_pairs={{0,2},{1,3},{2,0},{3,1},{4,6},{5,7},{6,4},{7,5},{8,10},{9,11},{10,... | collective-permute-start | bytes 405512 | tf_op jit(solution)/shard_map/ppermute | solution.py:431
  49.6 26.6 %collective-permute-start = (f32[8,4224]{1,0:T(8,128)S(1)}, f32[8,4224]{1,0:T(8,128)S(1)}, u32[]{:S(2)}, u32[]{:S(2)}) collective-permute-start(f32[8,4224]{1,0:T(8,128)S(1)} %concatenate.10), channel_id=1, source_target_pairs={{0,1},{1,0},{2,3},{3,2},{4,5},{5,4},{6,7},{7,6},{8,9},{9,8},{10,11... | collective-permute-start | bytes 405512 | tf_op jit(solution)/shard_map/ppermute | solution.py:431
  80.2 14.6 %collective-permute-start.3 = (bf16[8,512]{1,0:T(8,128)(2,1)}, bf16[8,512]{1,0:T(8,128)(2,1)S(1)}, u32[]{:S(2)}, u32[]{:S(2)}) collective-permute-start(bf16[8,512]{1,0:T(8,128)(2,1)} %after.3), channel_id=1, source_target_pairs={{0,8},{4,12},{8,0},{12,4},{16,24},{20,28},{24,16},{28,20},{1,9},{5... | collective-permute-start | bytes 24584 | tf_op jit(solution)/shard_map/ppermute | solution.py:431
  81.9 13.3 %collective-permute-start.4 = (bf16[8,512]{1,0:T(8,128)(2,1)}, bf16[8,512]{1,0:T(8,128)(2,1)S(1)}, u32[]{:S(2)}, u32[]{:S(2)}) collective-permute-start(bf16[8,512]{1,0:T(8,128)(2,1)} %after.3), channel_id=1, source_target_pairs={{0,16},{4,20},{8,24},{12,28},{16,0},{20,4},{24,8},{28,12},{1,17},{... | collective-permute-start | bytes 24584 | tf_op jit(solution)/shard_map/ppermute | solution.py:431
  83.4 12.4 %collective-permute-start.5 = (bf16[8,512]{1,0:T(8,128)(2,1)}, bf16[8,512]{1,0:T(8,128)(2,1)S(1)}, u32[]{:S(2)}, u32[]{:S(2)}) collective-permute-start(bf16[8,512]{1,0:T(8,128)(2,1)} %after.3), channel_id=1, source_target_pairs={{0,24},{4,28},{8,16},{12,20},{16,8},{20,12},{24,0},{28,4},{1,25},{... | collective-permute-start | bytes 24584 | tf_op jit(solution)/shard_map/ppermute | solution.py:431
  96.4 1.2 collective-permute-start.6
  98.3 5.7 %copy-start.12 = (s32[64,2]{0,1:T(2,128)S(1)}, s32[64,2]{0,1:T(2,128)}, u32[]{:S(2)}) copy-start(s32[64,2]{0,1:T(2,128)} %param.26) | copy-start | bytes 1540
  98.3 5.8 %copy-start.15 = (s32[8]{0:T(128)S(1)}, s32[8]{0:T(128)}, u32[]{:S(2)}) copy-start(s32[8]{0:T(128)} %constant.41.clone) | copy-start | bytes 100
  98.3 6.5 %copy-start.13 = (bf16[512]{0:T(512)(128)(2,1)S(1)}, bf16[512]{0:T(512)(128)(2,1)}, u32[]{:S(2)}) copy-start(bf16[512]{0:T(512)(128)(2,1)} %param.21) | copy-start | bytes 3076
  98.3 6.5 %copy-start.10 = (bf16[512,8]{0,1:T(8,128)(2,1)S(1)}, bf16[512,8]{0,1:T(8,128)(2,1)}, u32[]{:S(2)}) copy-start(bf16[512,8]{0,1:T(8,128)(2,1)} %param.22) | copy-start | bytes 24580
  98.3 7.6 %copy-start.5 = (s32[8,5632]{1,0:T(8,128)S(1)}, s32[8,5632]{1,0:T(8,128)}, u32[]{:S(2)}) copy-start(s32[8,5632]{1,0:T(8,128)} %old_ref.1) | copy-start | bytes 540676
  98.3 18.3 %copy-start.2 = (bf16[64,512]{1,0:T(8,128)(2,1)S(1)}, bf16[64,512]{1,0:T(8,128)(2,1)}, u32[]{:S(2)}) copy-start(bf16[64,512]{1,0:T(8,128)(2,1)} %copy-done.1) | copy-start | bytes 196612
  98.3 134.2 %all-to-all-start.1 = ((bf16[8,2,704,512]{3,2,1,0:T(8,128)(2,1)}), bf16[8,2,704,512]{3,2,1,0:T(8,128)(2,1)}, u32[]{:S(2)}, u32[]{:S(2)}) async-start(bf16[8,2,704,512]{3,2,1,0:T(8,128)(2,1)} %after.5), calls=%async_computation.1 | async-start | bytes 23068672 | tf_op jit(solution)/shard_map/all_to_all | solution.py:471
  125.4 5.4 %collective-permute-start.7 = (bf16[4,16,768]{2,1,0:T(8,128)(2,1)S(1)}, bf16[4,16,768]{2,1,0:T(8,128)(2,1)S(1)}, u32[]{:S(2)}, u32[]{:S(2)}) collective-permute-start(bf16[4,16,768]{2,1,0:T(8,128)(2,1)S(1)} %get-tuple-element.20), channel_id=1, source_target_pairs={{0,1},{1,0},{2,3},{3,2},{4,5},{5,4},{6,7},{7,6},{8,9},{9,8},{10,11... | collective-permute-start | bytes 294920 | tf_op jit(solution)/shard_map/ppermute | solution.py:431
  127.7 10.7 %collective-permute-start.8 = (bf16[4,16,768]{2,1,0:T(8,128)(2,1)S(1)}, bf16[4,16,768]{2,1,0:T(8,128)(2,1)S(1)}, u32[]{:S(2)}, u32[]{:S(2)}) collective-permute-start(bf16[4,16,768]{2,1,0:T(8,128)(2,1)S(1)} %get-tuple-element.19), channel_id=1, source_target_pairs={{0,2},{1,3},{2,0},{3,1},{4,6},{5,7},{6,4},{7,5},{8,10},{9,11},{10,... | collective-permute-start | bytes 294920 | tf_op jit(solution)/shard_map/ppermute | solution.py:431
  130.3 8.1 %collective-permute-start.9 = (bf16[4,16,768]{2,1,0:T(8,128)(2,1)S(1)}, bf16[4,16,768]{2,1,0:T(8,128)(2,1)S(1)}, u32[]{:S(2)}, u32[]{:S(2)}) collective-permute-start(bf16[4,16,768]{2,1,0:T(8,128)(2,1)S(1)} %get-tuple-element.18), channel_id=1, source_target_pairs={{0,3},{1,2},{2,1},{3,0},{4,7},{5,6},{6,5},{7,4},{8,11},{9,10},{10,... | collective-permute-start | bytes 294920 | tf_op jit(solution)/shard_map/ppermute | solution.py:431
  138.6 4.7 %collective-permute-start.10 = (bf16[2,16,768]{2,1,0:T(8,128)(2,1)S(1)}, bf16[2,16,768]{2,1,0:T(8,128)(2,1)S(1)}, u32[]{:S(2)}, u32[]{:S(2)}) collective-permute-start(bf16[2,16,768]{2,1,0:T(8,128)(2,1)S(1)} %activate.1.refs_0_), channel_id=1, source_target_pairs={{0,1},{1,0},{2,3},{3,2},{4,5},{5,4},{6,7},{7,6},{8,9},{9,8},{10,11... | collective-permute-start | bytes 147464 | tf_op jit(solution)/shard_map/ppermute | solution.py:431
  140.4 5.9 %collective-permute-start.11 = (bf16[2,16,768]{2,1,0:T(8,128)(2,1)S(1)}, bf16[2,16,768]{2,1,0:T(8,128)(2,1)S(1)}, u32[]{:S(2)}, u32[]{:S(2)}) collective-permute-start(bf16[2,16,768]{2,1,0:T(8,128)(2,1)S(1)} %activate.1.refs_0_), channel_id=1, source_target_pairs={{0,2},{1,3},{2,0},{3,1},{4,6},{5,7},{6,4},{7,5},{8,10},{9,11},{10,... | collective-permute-start | bytes 147464 | tf_op jit(solution)/shard_map/ppermute | solution.py:431
  141.8 5.9 %collective-permute-start.12 = (bf16[2,16,768]{2,1,0:T(8,128)(2,1)S(1)}, bf16[2,16,768]{2,1,0:T(8,128)(2,1)S(1)}, u32[]{:S(2)}, u32[]{:S(2)}) collective-permute-start(bf16[2,16,768]{2,1,0:T(8,128)(2,1)S(1)} %activate.1.refs_0_), channel_id=1, source_target_pairs={{0,3},{1,2},{2,1},{3,0},{4,7},{5,6},{6,5},{7,4},{8,11},{9,10},{10,... | collective-permute-start | bytes 147464 | tf_op jit(solution)/shard_map/ppermute | solution.py:431
  166.8 65.1 %copy-start.6 = (bf16[8,512]{1,0:T(8,128)(2,1)S(1)}, bf16[8,512]{1,0:T(8,128)(2,1)}, u32[]{:S(2)}) copy-start(bf16[8,512]{1,0:T(8,128)(2,1)} %after.3) | copy-start | bytes 24580
  167.7 1.3 collective-permute-start.13
  169.8 62.1 %collective-permute-start.16 = (f32[8,512]{1,0:T(8,128)S(1)}, f32[8,512]{1,0:T(8,128)S(1)}, u32[]{:S(2)}, u32[]{:S(2)}) collective-permute-start(f32[8,512]{1,0:T(8,128)S(1)} %get-tuple-element.23), channel_id=1, source_target_pairs={{0,24},{4,28},{8,16},{12,20},{16,8},{20,12},{24,0},{28,4},{1,25},{... | collective-permute-start | bytes 49160 | tf_op jit(solution)/shard_map/ppermute | solution.py:431
  172.5 59.4 %collective-permute-start.15 = (f32[8,512]{1,0:T(8,128)S(1)}, f32[8,512]{1,0:T(8,128)S(1)}, u32[]{:S(2)}, u32[]{:S(2)}) collective-permute-start(f32[8,512]{1,0:T(8,128)S(1)} %get-tuple-element.24), channel_id=1, source_target_pairs={{0,16},{4,20},{8,24},{12,28},{16,0},{20,4},{24,8},{28,12},{1,17},{... | collective-permute-start | bytes 49160 | tf_op jit(solution)/shard_map/ppermute | solution.py:431
  173.0 58.9 %collective-permute-start.14 = (f32[8,512]{1,0:T(8,128)S(1)}, f32[8,512]{1,0:T(8,128)S(1)}, u32[]{:S(2)}, u32[]{:S(2)}) collective-permute-start(f32[8,512]{1,0:T(8,128)S(1)} %get-tuple-element.22), channel_id=1, source_target_pairs={{0,8},{4,12},{8,0},{12,4},{16,24},{20,28},{24,16},{28,20},{1,9},{5... | collective-permute-start | bytes 49160 | tf_op jit(solution)/shard_map/ppermute | solution.py:431
  (3 other events, 1.9 us)

commit v3 on v2

--- a/solution.py
+++ b/solution.py
@@ -200,15 +200,29 @@
     def entry(n, j, d):
         return plan_ref[n * pairs + (step * span + j) * rows + d]
 
+    usual = min(deep, up_to(lines + rows * TILE, TILE))
+
+    def move(j, begin, end):
+        place = place_ref[j][:, :lines]
+        onehot = [
+            equal_ones(number_ref[: min(256, end - row)], within(place - begin, (row - begin) // 256))
+            for row in range(begin, end, 256)
+        ]
+        stages[j][begin:end] = jnp.dot(
+            jnp.concatenate(onehot, axis=0), lines_ref[j, 0], preferred_element_type=jnp.float32
+        ).astype(jnp.bfloat16)
+
+    for j in range(span):
+        move(j, 0, usual)
+    if usual < deep:
+        for j in range(span):
+            used = entry(1, j, rows - 1) + entry(2, j, rows - 1)
+
+            @pl.when(used * TILE > usual)
+            def _(j=j):
+                move(j, usual, deep)
+
     for j, stage_ref in enumerate(stages):
-        place = place_ref[j][:, :lines]
-        source_lines = lines_ref[j, 0]
-        for first in range(0, deep, 256):
-            count = min(256, deep - first)
-            onehot = equal_ones(number_ref[:count], within(place, first // 256))
-            stage_ref[first : first + count] = jnp.dot(
-                onehot, source_lines, preferred_element_type=jnp.float32
-            ).astype(jnp.bfloat16)
 
         def one_peer(d, most, j=j, stage_ref=stage_ref):
             lead, tiles, base = entry(0, j, d), entry(1, j, d), entry(2, j, d)
@@ -247,13 +261,13 @@
 
 def unpack_kernel(slot, plan_ref, place_ref, block_ref, *rest):
     out_ref, stage_ref, sems = rest[-3:]
-    experts = pl.num_programs(1)
-    rows = block_ref.shape[0]
+    experts = pl.num_programs(0)
+    rows, count, _, width = block_ref.shape
     pairs = experts * rows
     _, deep, _ = stage_ref.shape
     lines = out_ref.shape[2]
-    step = pl.program_id(0) * experts + pl.program_id(1)
-    steps = pl.num_programs(0) * experts
+    e = pl.program_id(0)
+    buffer = e % 2
 
     def entry(n, e, s):
         return plan_ref[n * pairs + e * rows + s]
@@ -261,48 +275,52 @@
     def slotted(e):
         return entry(3, e, 0) > 0
 
-    def slot_copy(at, s):
-        part, e, buffer = at // experts, at % experts, at % 2
-        there = pl.ds(pl.multiple_of(entry(0, e, s) * TILE, TILE), slot * TILE)
-        return pltpu.make_async_copy(
-            block_ref.at[s, part, there],
-            stage_ref.at[buffer, pl.ds(s * slot * TILE, slot * TILE)],
-            sems.at[buffer, s],
-        )
-
-    def begin(at):
-        @pl.when(slotted(at % experts))
+    def columns(part):
+        return pl.ds(part * width, width)
+
+    def slot_copies(e):
+        for s in range(rows):
+            there = pl.ds(pl.multiple_of(entry(0, e, s) * TILE, TILE), slot * TILE)
+            here = pl.ds(s * slot * TILE, slot * TILE)
+            for part in range(count):
+                yield pltpu.make_async_copy(
+                    block_ref.at[s, part, there],
+                    stage_ref.at[e % 2, here, columns(part)],
+                    sems.at[e % 2, s * count + part],
+                )
+
+    def begin(e):
+        @pl.when(slotted(e))
         def _():
-            for s in range(rows):
-                slot_copy(at, s).start()
-
-    @pl.when(step == 0)
+            for copy in slot_copies(e):
+                copy.start()
+
+    @pl.when(e == 0)
     def _():
         stage_ref[...] = jnp.zeros_like(stage_ref)
-        begin(step)
-
-    @pl.when(step + 1 < steps)
-    def _():
-        begin(step + 1)
-
-    part, e, buffer = pl.program_id(0), pl.program_id(1), step % 2
+        begin(e)
+
+    @pl.when(e + 1 < experts)
+    def _():
+        begin(e + 1)
 
     @pl.when(slotted(e))
     def _():
-        for s in range(rows):
-            slot_copy(step, s).wait()
+        for copy in slot_copies(e):
+            copy.wait()
 
     @pl.when(jnp.logical_not(slotted(e)))
     def _():
         def one_peer(s, carry):
             def put(t, c):
-                copy = pltpu.make_async_copy(
-                    block_ref.at[s, part, tile_at(entry(0, e, s) + t)],
-                    stage_ref.at[buffer, tile_at(entry(2, e, s) + t)],
-                    sems.at[buffer, 0],
-                )
-                copy.start()
-                copy.wait()
+                for part in range(count):
+                    copy = pltpu.make_async_copy(
+                        block_ref.at[s, part, tile_at(entry(0, e, s) + t)],
+                        stage_ref.at[buffer, tile_at(entry(2, e, s) + t), columns(part)],
+                        sems.at[buffer, part],
+                    )
+                    copy.start()
+                    copy.wait()
                 return c
 
             return lax.fori_loop(0, entry(1, e, s), put, carry)
@@ -317,9 +335,11 @@
         place = within_block + away * jnp.asarray(512, jnp.bfloat16)
         pieces.append(equal_ones(lane + jnp.asarray(first % 256, jnp.bfloat16), place))
     onehot = jnp.concatenate(pieces, axis=1)
-    out_ref[0, 0] = jnp.dot(
+    moved = jnp.dot(
         onehot, stage_ref[buffer], preferred_element_type=jnp.float32
     ).astype(jnp.bfloat16)
+    for part in range(count):
+        out_ref[0, part] = moved[:, part * width : (part + 1) * width]
 
 
 def call_plan(kernel, name, table, ids, pairs, place):
@@ -371,7 +391,7 @@
     first, count = piece
     rows = arrived.shape[0]
     in_specs = [
-        pl.BlockSpec((1, 2, lines, LANES), lambda p, e, plan: (e, 0, 0, 0)),
+        pl.BlockSpec((1, 2, lines, LANES), lambda e, plan: (e, 0, 0, 0)),
         pl.BlockSpec(memory_space=pl.ANY),
     ]
     operands = [plan, place, arrived]
@@ -384,12 +404,12 @@
         functools.partial(unpack_kernel, slot),
         grid_spec=pltpu.PrefetchScalarGridSpec(
             num_scalar_prefetch=1,
-            grid=(count, experts),
+            grid=(experts,),
             in_specs=in_specs,
-            out_specs=pl.BlockSpec((1, 1, lines, width), lambda p, e, plan: (e, first + p, 0, 0)),
+            out_specs=pl.BlockSpec((1, count, lines, width), lambda e, plan: (e, first // count, 0, 0)),
             scratch_shapes=[
-                pltpu.VMEM((2, deep, width), jnp.bfloat16),
-                pltpu.SemaphoreType.DMA((2, rows)),
+                pltpu.VMEM((2, deep, count * width), jnp.bfloat16),
+                pltpu.SemaphoreType.DMA((2, rows * count)),
             ],
         ),
         out_shape=jax.ShapeDtypeStruct(shape, jnp.bfloat16),
@@ -442,7 +462,7 @@
         self.slot = min(STRAIGHT, block_rows // TILE)
         self.deep = up_to(max(compact, rows * self.slot * TILE), 256)
         self.shape = expert_lines.shape
-        self.pieces = [(0, 1), (1, parts - 1)]
+        self.pieces = [(parts - 1, 1), (0, parts - 1)]
         out_place, out_plan = call_plan(
             functools.partial(outgoing_kernel, lines, rows), "outgoing_plan",
             new_lines, own_ids(old_lines, lines, padded), pairs,

time: 257 us -> 252 us (0.981)
  Pallas kernels: 106 us -> 99.1 us
    pallas_call x2, Pallas kernels: 34.5 us -> 30.9 us  [unpack(): pl.pallas_call(functools.partial(unpack_kernel, slot), grid_spec=pltpu.Pr...]
    pallas_call x2, Pallas kernels: 39.9 us -> 36.4 us  [pack(): pl.pallas_call(functools.partial(pack_kernel, rows, span), grid_spec=pltp...]
where the time goes in v3:
time: 252 us; the launch traced here: 250 us
  Pallas kernels  99.1 us (39%)
  waiting for transfers between devices  87.2 us (35%)
  starting transfers between devices  32.7 us (13%)
  local copies, waits for them, and re-layouts  15.8 us (6%)
  matrix products  8.45 us (3%)
  other arithmetic  5.59 us (2%)
    ppermute x17, waiting for transfers between devices, from_peer(): return lax.ppermute(block, axis, [(i, i ^ offset) for i in range(size)])  87.1 us
    pallas_call x2, Pallas kernels, pack(): pl.pallas_call(functools.partial(pack_kernel, rows, span), grid_spec=pltp...  36.4 us
    pallas_call x2, Pallas kernels, unpack(): pl.pallas_call(functools.partial(unpack_kernel, slot), grid_spec=pltpu.Pr...  30.9 us
    ppermute x17, starting transfers between devices, from_peer(): return lax.ppermute(block, axis, [(i, i ^ offset) for i in range(size)])  21.9 us
    pallas_call x2, Pallas kernels, call_plan(): pl.pallas_call(kernel, out_shape=(place, jax.ShapeDtypeStruct((4, pairs,...  16.8 us
    all_to_all x2, starting transfers between devices, send(): lax.all_to_all(block, 'row', split_axis=0, concat_axis=0, tiled=True)  10.8 us
    pallas_call x1, Pallas kernels, experts_part(): pl.pallas_call(gate_up_kernel, grid_spec=pltpu.PrefetchScalarGridSpec(num...  8.76 us
    unnamed x41, local copies, waits for them, and re-layouts  6.24 us
  transfers between devices with their start and end apart: 19, of which 10 were waited for; matrix products, arithmetic and copies ran while one was open for 10% of the time, Pallas kernels for 25%

profile of v3, /device:TPU:0, one launch (start us, length us, event | category | flops | bytes accessed | tf_op | source)
XLA Modules:
  0.0 250.1 jit_solution(9960904581601462649)
XLA Ops:
  2.4 6.1 %outgoing_plan.1 = (s32[8,1,768]{2,1,0:T(1,128)S(1)}, s32[4,64,128]{2,1,0:T(8,128)S(1)}) custom-call(s32[8,5632]{1,0:T(8,128)S(1)} %copy-done.4, s32[8,768]{1,0:T(8,128)S(1)} %pad.11.held_ref), custom_call_target="tpu_custom_call" | custom-call | flops 230686720 | bytes 360448 | tf_op jit(solution)/shard_map/outgoing_plan/pallas_call | solution.py:346
  9.9 12.9 %pack_lines.2.refs_1_ = bf16[8,1,704,512]{3,2,1,0:T(8,128)(2,1)} custom-call(s32[256]{0:T(256)} %reshape_squeeze.27.plan_ref, s32[8,1,768]{2,1,0:T(1,128)} %copy-done.3, bf16[8,3,704,512]{3,2,1,0:T(8,128)(2,1)} %bitcast.81), custom_call_target="tpu_custom_call" | custom-call | flops 5536481280 | bytes 11534336 | tf_op jit(solution)/shard_map/pack_lines/pallas_call | solution.py:361
  22.7 5.2 %all-to-all-start = ((bf16[8,1,704,512]{3,2,1,0:T(8,128)(2,1)}), bf16[8,1,704,512]{3,2,1,0:T(8,128)(2,1)}, u32[]{:S(2)}, u32[]{:S(2)}) async-start(bf16[8,1,704,512]{3,2,1,0:T(8,128)(2,1)} %pack_lines.2.refs_1_), calls=%async_computation | async-start | bytes 11534336 | tf_op jit(solution)/shard_map/all_to_all | solution.py:491
  27.9 1.7 fusion.30
  30.7 1.7 fusion.29
  32.7 1.2 copy.145
  34.5 2.0 fusion.33
  37.2 1.2 fusion.32
  43.6 4.8 %collective-permute-start.2 = (f32[8,4224]{1,0:T(8,128)S(1)}, f32[8,4224]{1,0:T(8,128)S(1)}, u32[]{:S(2)}, u32[]{:S(2)}) collective-permute-start(f32[8,4224]{1,0:T(8,128)S(1)} %concatenate.10), channel_id=1, source_target_pairs={{0,3},{1,2},{2,1},{3,0},{4,7},{5,6},{6,5},{7,4},{8,11},{9,10},{10,... | collective-permute-start | bytes 405512 | tf_op jit(solution)/shard_map/ppermute | solution.py:451
  49.0 23.6 %pack_lines.3.refs_2_.refs_0_ = bf16[8,2,704,512]{3,2,1,0:T(8,128)(2,1)} custom-call(s32[256]{0:T(256)} %reshape_squeeze.27.plan_ref, s32[8,1,768]{2,1,0:T(1,128)} %copy-done.3, bf16[8,3,704,512]{3,2,1,0:T(8,128)(2,1)} %bitcast.82), custom_call_target="tpu_custom_call" | custom-call | flops 11072962560 | bytes 23068672 | tf_op jit(solution)/shard_map/pack_lines/pallas_call | solution.py:361
  73.2 3.5 %fusion.4.refs_0_ = bf16[8,512]{1,0:T(8,128)(2,1)} fusion(bf16[4096,512]{1,0:T(8,128)(2,1)} %param.20, f32[8,4096]{1,0:T(8,128)S(1)} %fusion.8, f32[8,32]{0,1:T(8,128)S(1)} %copy.126, bf16[8,512]{1,0:T(8,128)(2,1)S(1)} %copy-done.9), kind=kOutput, calls=%fused_computation.9 | convolution fusion | flops 33632256 | bytes 4342784 | tf_op jit(solution)/shard_map/dot_general | solution.py:765
  76.7 1.7 collective-permute-start.3
  78.4 1.5 collective-permute-start.4
  80.9 12.7 %collective-permute-done.3 = bf16[8,512]{1,0:T(8,128)(2,1)S(1)} collective-permute-done((bf16[8,512]{1,0:T(8,128)(2,1)}, bf16[8,512]{1,0:T(8,128)(2,1)S(1)}, u32[]{:S(2)}, u32[]{:S(2)}) %collective-permute-start.3) | collective-permute-done | bytes 8224 | tf_op jit(solution)/shard_map/ppermute | solution.py:451
  95.3 1.2 collective-permute-done.6
  97.1 5.6 %all-to-all-start.1 = ((bf16[8,2,704,512]{3,2,1,0:T(8,128)(2,1)}), bf16[8,2,704,512]{3,2,1,0:T(8,128)(2,1)}, u32[]{:S(2)}, u32[]{:S(2)}) async-start(bf16[8,2,704,512]{3,2,1,0:T(8,128)(2,1)} %after.5), calls=%async_computation.1 | async-start | bytes 23068672 | tf_op jit(solution)/shard_map/all_to_all | solution.py:491
  104.7 10.7 %incoming_plan.1 = (bf16[8,2,704,128]{3,2,1,0:T(8,128)(2,1)S(1)}, s32[4,64,128]{2,1,0:T(8,128)S(1)}) custom-call(s32[8,5632]{1,0:T(8,128)S(1)} %copy-done.5, s32[8,768]{1,0:T(8,128)S(1)} %pad.13.wanted_ref), custom_call_target="tpu_custom_call" | custom-call | flops 230686720 | bytes 360448 | tf_op jit(solution)/shard_map/incoming_plan/pallas_call | solution.py:346
  115.4 8.8 %gate_up.1 = bf16[4,4,16,768]{3,2,1,0:T(8,128)(2,1)S(1)} custom-call(s32[1]{0:T(128)} %bitcast.20.me_ref, bf16[64,512]{1,0:T(8,128)(2,1)S(1)} %copy-done.2, bf16[1,512]{1,0:T(2,128)(2,1)S(1)} %reshape.90.gain_ref, bf16[512,128]{1,0:T(8,128)(2,1)S(1)} %pad.12.router_ref, s32[64,2]{1,0:T(8,128)S(1)} %bitcast.78, bf16[8,3,704,512]{3,2,1,0:T(8,128)(2,1)} %bitcast.83, ...), custom_call_target="tpu_custom_call" | custom-call | flops 738197504 | bytes 11534336 | tf_op jit(solution)/shard_map/gate_up/pallas_call | solution.py:690
  124.2 2.3 collective-permute-start.7
  126.5 2.6 %collective-permute-start.8 = (bf16[4,16,768]{2,1,0:T(8,128)(2,1)S(1)}, bf16[4,16,768]{2,1,0:T(8,128)(2,1)S(1)}, u32[]{:S(2)}, u32[]{:S(2)}) collective-permute-start(bf16[4,16,768]{2,1,0:T(8,128)(2,1)S(1)} %get-tuple-element.19), channel_id=1, source_target_pairs={{0,2},{1,3},{2,0},{3,1},{4,6},{5,7},{6,4},{7,5},{8,10},{9,11},{10,... | collective-permute-start | bytes 294920 | tf_op jit(solution)/shard_map/ppermute | solution.py:451
  129.6 7.6 %collective-permute-done.8.refs_2_ = bf16[4,16,768]{2,1,0:T(8,128)(2,1)S(1)} collective-permute-done((bf16[4,16,768]{2,1,0:T(8,128)(2,1)S(1)}, bf16[4,16,768]{2,1,0:T(8,128)(2,1)S(1)}, u32[]{:S(2)}, u32[]{:S(2)}) %collective-permute-start.8) | collective-permute-done | bytes 98336 | tf_op jit(solution)/shard_map/ppermute | solution.py:451
  137.4 1.8 collective-permute-start.10
  139.2 1.4 collective-permute-start.11
  140.6 1.2 collective-permute-start.12
  142.1 3.1 %collective-permute-done.11.refs_2_ = bf16[2,16,768]{2,1,0:T(8,128)(2,1)S(1)} collective-permute-done((bf16[2,16,768]{2,1,0:T(8,128)(2,1)S(1)}, bf16[2,16,768]{2,1,0:T(8,128)(2,1)S(1)}, u32[]{:S(2)}, u32[]{:S(2)}) %collective-permute-start.11) | collective-permute-done | bytes 49184 | tf_op jit(solution)/shard_map/ppermute | solution.py:451
  145.1 1.4 collective-permute-done.12.refs_3_
  146.5 6.1 %down.1.refs_0_ = f32[64,512]{1,0:T(8,128)S(1)} custom-call(s32[1]{0:T(128)} %bitcast.20.me_ref, s32[64,2]{1,0:T(8,128)S(1)} %bitcast.80, bf16[2,16,768]{2,1,0:T(8,128)(2,1)S(1)} %activate.1.refs_0_, bf16[2,16,768]{2,1,0:T(8,128)(2,1)S(1)} %collective-permute-done.10.refs_1_, bf16[2,16,768]{2,1,0:T(8,128)(2,1)S(1)} %collective-permute-done.11.refs_2_, ...), custom_call_target="tpu_custom_call" | custom-call | flops 369098752 | bytes 5767168 | tf_op jit(solution)/shard_map/down/pallas_call | solution.py:717
  153.3 12.3 %unpack_lines.2.refs_1_.rest_0_ = bf16[8,3,704,512]{3,2,1,0:T(8,128)(2,1)} custom-call(s32[256]{0:T(256)S(1)} %reshape_squeeze.28.plan_ref, bf16[8,2,704,128]{3,2,1,0:T(8,128)(2,1)S(1)} %get-tuple-element.9.place_ref, bf16[8,1,704,512]{3,2,1,0:T(8,128)(2,1)} %all-to-all-done.block_ref), custom_call_target="tpu_custom_call" | custom-call | flops 5905580032 | bytes 11534336 | tf_op jit(solution)/shard_map/unpack_lines/pallas_call | solution.py:403
  166.5 1.3 collective-permute-done.13
  168.6 2.7 %collective-permute-start.16 = (f32[8,512]{1,0:T(8,128)S(1)}, f32[8,512]{1,0:T(8,128)S(1)}, u32[]{:S(2)}, u32[]{:S(2)}) collective-permute-start(f32[8,512]{1,0:T(8,128)S(1)} %get-tuple-element.23), channel_id=1, source_target_pairs={{0,24},{4,28},{8,16},{12,20},{16,8},{20,12},{24,0},{28,4},{1,25},{... | collective-permute-start | bytes 49160 | tf_op jit(solution)/shard_map/ppermute | solution.py:451
  172.2 58.5 %collective-permute-done.16 = f32[8,512]{1,0:T(8,128)S(1)} collective-permute-done((f32[8,512]{1,0:T(8,128)S(1)}, f32[8,512]{1,0:T(8,128)S(1)}, u32[]{:S(2)}, u32[]{:S(2)}) %collective-permute-start.16) | collective-permute-done | bytes 16416 | tf_op jit(solution)/shard_map/ppermute | solution.py:451
  231.3 18.5 %unpack_lines.3 = bf16[8,3,704,512]{3,2,1,0:T(8,128)(2,1)} custom-call(s32[256]{0:T(256)S(1)} %reshape_squeeze.28.plan_ref, bf16[8,2,704,128]{3,2,1,0:T(8,128)(2,1)S(1)} %get-tuple-element.9.place_ref, bf16[8,2,704,512]{3,2,1,0:T(8,128)(2,1)} %all-to-all-done.1.block_ref, ...), custom_call_target="tpu_custom_call", output_to_operand_aliasing={{}: (3, {})} | custom-call | flops 11811160064 | bytes 23068672 | tf_op jit(solution)/shard_map/unpack_lines/pallas_call | solution.py:403
  (114 shorter events, 22.1 us)
Async XLA Ops:
  1.5 0.9 copy-start.4
  22.7 74.4 %all-to-all-start = ((bf16[8,1,704,512]{3,2,1,0:T(8,128)(2,1)}), bf16[8,1,704,512]{3,2,1,0:T(8,128)(2,1)}, u32[]{:S(2)}, u32[]{:S(2)}) async-start(bf16[8,1,704,512]{3,2,1,0:T(8,128)(2,1)} %pack_lines.2.refs_1_), calls=%async_computation | async-start | bytes 11534336 | tf_op jit(solution)/shard_map/all_to_all | solution.py:491
  30.7 3.2 %copy-start.7 = (bf16[8,4096]{1,0:T(8,128)(2,1)S(1)}, bf16[8,4096]{1,0:T(8,128)(2,1)}, u32[]{:S(2)}) copy-start(bf16[8,4096]{1,0:T(8,128)(2,1)} %param.15) | copy-start | bytes 196612
  30.7 3.2 %copy-start.8 = (bf16[8,2,2048]{2,1,0:T(2,128)(2,1)S(1)}, bf16[8,2,2048]{2,1,0:T(2,128)(2,1)}, u32[]{:S(2)}) copy-start(bf16[8,2,2048]{2,1,0:T(2,128)(2,1)} %param.16) | copy-start | bytes 196612
  30.7 3.7 %copy-start.14 = (s32[8]{0:T(128)S(1)}, s32[8]{0:T(128)}, u32[]{:S(2)}) copy-start(s32[8]{0:T(128)} %param.19) | copy-start | bytes 100
  34.4 2.8 %copy-start.11 = (pred[8,32]{1,0:T(8,128)(4,1)}, pred[8,32]{1,0:T(8,128)(4,1)S(1)}, u32[]{:S(2)}) copy-start(pred[8,32]{1,0:T(8,128)(4,1)S(1)} %broadcast_compare_fusion) | copy-start | bytes 772
  43.6 29.6 %copy-start.9 = (bf16[8,512]{1,0:T(8,128)(2,1)S(1)}, bf16[8,512]{1,0:T(8,128)(2,1)}, u32[]{:S(2)}) copy-start(bf16[8,512]{1,0:T(8,128)(2,1)} %param.14) | copy-start | bytes 24580
  43.6 29.0 %collective-permute-start.2 = (f32[8,4224]{1,0:T(8,128)S(1)}, f32[8,4224]{1,0:T(8,128)S(1)}, u32[]{:S(2)}, u32[]{:S(2)}) collective-permute-start(f32[8,4224]{1,0:T(8,128)S(1)} %concatenate.10), channel_id=1, source_target_pairs={{0,3},{1,2},{2,1},{3,0},{4,7},{5,6},{6,5},{7,4},{8,11},{9,10},{10,... | collective-permute-start | bytes 405512 | tf_op jit(solution)/shard_map/ppermute | solution.py:451
  48.4 24.2 %collective-permute-start.1 = (f32[8,4224]{1,0:T(8,128)S(1)}, f32[8,4224]{1,0:T(8,128)S(1)}, u32[]{:S(2)}, u32[]{:S(2)}) collective-permute-start(f32[8,4224]{1,0:T(8,128)S(1)} %concatenate.10), channel_id=1, source_target_pairs={{0,2},{1,3},{2,0},{3,1},{4,6},{5,7},{6,4},{7,5},{8,10},{9,11},{10,... | collective-permute-start | bytes 405512 | tf_op jit(solution)/shard_map/ppermute | solution.py:451
  48.4 24.2 %collective-permute-start = (f32[8,4224]{1,0:T(8,128)S(1)}, f32[8,4224]{1,0:T(8,128)S(1)}, u32[]{:S(2)}, u32[]{:S(2)}) collective-permute-start(f32[8,4224]{1,0:T(8,128)S(1)} %concatenate.10), channel_id=1, source_target_pairs={{0,1},{1,0},{2,3},{3,2},{4,5},{5,4},{6,7},{7,6},{8,9},{9,8},{10,11... | collective-permute-start | bytes 405512 | tf_op jit(solution)/shard_map/ppermute | solution.py:451
  76.7 16.9 %collective-permute-start.3 = (bf16[8,512]{1,0:T(8,128)(2,1)}, bf16[8,512]{1,0:T(8,128)(2,1)S(1)}, u32[]{:S(2)}, u32[]{:S(2)}) collective-permute-start(bf16[8,512]{1,0:T(8,128)(2,1)} %after.3), channel_id=1, source_target_pairs={{0,8},{4,12},{8,0},{12,4},{16,24},{20,28},{24,16},{28,20},{1,9},{5... | collective-permute-start | bytes 24584 | tf_op jit(solution)/shard_map/ppermute | solution.py:451
  78.4 15.6 %collective-permute-start.4 = (bf16[8,512]{1,0:T(8,128)(2,1)}, bf16[8,512]{1,0:T(8,128)(2,1)S(1)}, u32[]{:S(2)}, u32[]{:S(2)}) collective-permute-start(bf16[8,512]{1,0:T(8,128)(2,1)} %after.3), channel_id=1, source_target_pairs={{0,16},{4,20},{8,24},{12,28},{16,0},{20,4},{24,8},{28,12},{1,17},{... | collective-permute-start | bytes 24584 | tf_op jit(solution)/shard_map/ppermute | solution.py:451
  79.8 14.7 %collective-permute-start.5 = (bf16[8,512]{1,0:T(8,128)(2,1)}, bf16[8,512]{1,0:T(8,128)(2,1)S(1)}, u32[]{:S(2)}, u32[]{:S(2)}) collective-permute-start(bf16[8,512]{1,0:T(8,128)(2,1)} %after.3), channel_id=1, source_target_pairs={{0,24},{4,28},{8,16},{12,20},{16,8},{20,12},{24,0},{28,4},{1,25},{... | collective-permute-start | bytes 24584 | tf_op jit(solution)/shard_map/ppermute | solution.py:451
  95.2 1.2 collective-permute-start.6
  97.1 5.7 %copy-start.12 = (s32[64,2]{0,1:T(2,128)S(1)}, s32[64,2]{0,1:T(2,128)}, u32[]{:S(2)}) copy-start(s32[64,2]{0,1:T(2,128)} %param.26) | copy-start | bytes 1540
  97.1 5.8 %copy-start.15 = (s32[8]{0:T(128)S(1)}, s32[8]{0:T(128)}, u32[]{:S(2)}) copy-start(s32[8]{0:T(128)} %constant.41.clone) | copy-start | bytes 100
  97.1 6.5 %copy-start.13 = (bf16[512]{0:T(512)(128)(2,1)S(1)}, bf16[512]{0:T(512)(128)(2,1)}, u32[]{:S(2)}) copy-start(bf16[512]{0:T(512)(128)(2,1)} %param.21) | copy-start | bytes 3076
  97.1 6.5 %copy-start.10 = (bf16[512,8]{0,1:T(8,128)(2,1)S(1)}, bf16[512,8]{0,1:T(8,128)(2,1)}, u32[]{:S(2)}) copy-start(bf16[512,8]{0,1:T(8,128)(2,1)} %param.22) | copy-start | bytes 24580
  97.1 7.6 %copy-start.5 = (s32[8,5632]{1,0:T(8,128)S(1)}, s32[8,5632]{1,0:T(8,128)}, u32[]{:S(2)}) copy-start(s32[8,5632]{1,0:T(8,128)} %old_ref.1) | copy-start | bytes 540676
  97.1 18.3 %copy-start.2 = (bf16[64,512]{1,0:T(8,128)(2,1)S(1)}, bf16[64,512]{1,0:T(8,128)(2,1)}, u32[]{:S(2)}) copy-start(bf16[64,512]{1,0:T(8,128)(2,1)} %copy-done.1) | copy-start | bytes 196612
  97.1 134.2 %all-to-all-start.1 = ((bf16[8,2,704,512]{3,2,1,0:T(8,128)(2,1)}), bf16[8,2,704,512]{3,2,1,0:T(8,128)(2,1)}, u32[]{:S(2)}, u32[]{:S(2)}) async-start(bf16[8,2,704,512]{3,2,1,0:T(8,128)(2,1)} %after.5), calls=%async_computation.1 | async-start | bytes 23068672 | tf_op jit(solution)/shard_map/all_to_all | solution.py:491
  124.2 5.4 %collective-permute-start.7 = (bf16[4,16,768]{2,1,0:T(8,128)(2,1)S(1)}, bf16[4,16,768]{2,1,0:T(8,128)(2,1)S(1)}, u32[]{:S(2)}, u32[]{:S(2)}) collective-permute-start(bf16[4,16,768]{2,1,0:T(8,128)(2,1)S(1)} %get-tuple-element.20), channel_id=1, source_target_pairs={{0,1},{1,0},{2,3},{3,2},{4,5},{5,4},{6,7},{7,6},{8,9},{9,8},{10,11... | collective-permute-start | bytes 294920 | tf_op jit(solution)/shard_map/ppermute | solution.py:451
  126.5 10.7 %collective-permute-start.8 = (bf16[4,16,768]{2,1,0:T(8,128)(2,1)S(1)}, bf16[4,16,768]{2,1,0:T(8,128)(2,1)S(1)}, u32[]{:S(2)}, u32[]{:S(2)}) collective-permute-start(bf16[4,16,768]{2,1,0:T(8,128)(2,1)S(1)} %get-tuple-element.19), channel_id=1, source_target_pairs={{0,2},{1,3},{2,0},{3,1},{4,6},{5,7},{6,4},{7,5},{8,10},{9,11},{10,... | collective-permute-start | bytes 294920 | tf_op jit(solution)/shard_map/ppermute | solution.py:451
  129.1 8.1 %collective-permute-start.9 = (bf16[4,16,768]{2,1,0:T(8,128)(2,1)S(1)}, bf16[4,16,768]{2,1,0:T(8,128)(2,1)S(1)}, u32[]{:S(2)}, u32[]{:S(2)}) collective-permute-start(bf16[4,16,768]{2,1,0:T(8,128)(2,1)S(1)} %get-tuple-element.18), channel_id=1, source_target_pairs={{0,3},{1,2},{2,1},{3,0},{4,7},{5,6},{6,5},{7,4},{8,11},{9,10},{10,... | collective-permute-start | bytes 294920 | tf_op jit(solution)/shard_map/ppermute | solution.py:451
  137.4 4.7 %collective-permute-start.10 = (bf16[2,16,768]{2,1,0:T(8,128)(2,1)S(1)}, bf16[2,16,768]{2,1,0:T(8,128)(2,1)S(1)}, u32[]{:S(2)}, u32[]{:S(2)}) collective-permute-start(bf16[2,16,768]{2,1,0:T(8,128)(2,1)S(1)} %activate.1.refs_0_), channel_id=1, source_target_pairs={{0,1},{1,0},{2,3},{3,2},{4,5},{5,4},{6,7},{7,6},{8,9},{9,8},{10,11... | collective-permute-start | bytes 147464 | tf_op jit(solution)/shard_map/ppermute | solution.py:451
  139.2 5.9 %collective-permute-start.11 = (bf16[2,16,768]{2,1,0:T(8,128)(2,1)S(1)}, bf16[2,16,768]{2,1,0:T(8,128)(2,1)S(1)}, u32[]{:S(2)}, u32[]{:S(2)}) collective-permute-start(bf16[2,16,768]{2,1,0:T(8,128)(2,1)S(1)} %activate.1.refs_0_), channel_id=1, source_target_pairs={{0,2},{1,3},{2,0},{3,1},{4,6},{5,7},{6,4},{7,5},{8,10},{9,11},{10,... | collective-permute-start | bytes 147464 | tf_op jit(solution)/shard_map/ppermute | solution.py:451
  140.6 5.9 %collective-permute-start.12 = (bf16[2,16,768]{2,1,0:T(8,128)(2,1)S(1)}, bf16[2,16,768]{2,1,0:T(8,128)(2,1)S(1)}, u32[]{:S(2)}, u32[]{:S(2)}) collective-permute-start(bf16[2,16,768]{2,1,0:T(8,128)(2,1)S(1)} %activate.1.refs_0_), channel_id=1, source_target_pairs={{0,3},{1,2},{2,1},{3,0},{4,7},{5,6},{6,5},{7,4},{8,11},{9,10},{10,... | collective-permute-start | bytes 147464 | tf_op jit(solution)/shard_map/ppermute | solution.py:451
  165.6 65.1 %copy-start.6 = (bf16[8,512]{1,0:T(8,128)(2,1)S(1)}, bf16[8,512]{1,0:T(8,128)(2,1)}, u32[]{:S(2)}) copy-start(bf16[8,512]{1,0:T(8,128)(2,1)} %after.3) | copy-start | bytes 24580
  166.5 1.3 collective-permute-start.13
  168.6 62.1 %collective-permute-start.16 = (f32[8,512]{1,0:T(8,128)S(1)}, f32[8,512]{1,0:T(8,128)S(1)}, u32[]{:S(2)}, u32[]{:S(2)}) collective-permute-start(f32[8,512]{1,0:T(8,128)S(1)} %get-tuple-element.23), channel_id=1, source_target_pairs={{0,24},{4,28},{8,16},{12,20},{16,8},{20,12},{24,0},{28,4},{1,25},{... | collective-permute-start | bytes 49160 | tf_op jit(solution)/shard_map/ppermute | solution.py:451
  171.3 59.4 %collective-permute-start.15 = (f32[8,512]{1,0:T(8,128)S(1)}, f32[8,512]{1,0:T(8,128)S(1)}, u32[]{:S(2)}, u32[]{:S(2)}) collective-permute-start(f32[8,512]{1,0:T(8,128)S(1)} %get-tuple-element.24), channel_id=1, source_target_pairs={{0,16},{4,20},{8,24},{12,28},{16,0},{20,4},{24,8},{28,12},{1,17},{... | collective-permute-start | bytes 49160 | tf_op jit(solution)/shard_map/ppermute | solution.py:451
  171.8 58.9 %collective-permute-start.14 = (f32[8,512]{1,0:T(8,128)S(1)}, f32[8,512]{1,0:T(8,128)S(1)}, u32[]{:S(2)}, u32[]{:S(2)}) collective-permute-start(f32[8,512]{1,0:T(8,128)S(1)} %get-tuple-element.22), channel_id=1, source_target_pairs={{0,8},{4,12},{8,0},{12,4},{16,24},{20,28},{24,16},{28,20},{1,9},{5... | collective-permute-start | bytes 49160 | tf_op jit(solution)/shard_map/ppermute | solution.py:451
  (3 other events, 1.9 us)

commit v4 on v3

--- a/solution.py
+++ b/solution.py
@@ -86,7 +86,7 @@
         starts.append(running)
         running = running + counts[e * rows : (e + 1) * rows]
     start = jnp.concatenate(starts, axis=0)
-    lead = jnp.where(counts > 0.0, jnp.floor(start * (1.0 / TILE)), 0.0)
+    lead = jnp.floor(start * (1.0 / TILE))
     tail = jnp.floor((start + counts + (TILE - 1.0)) * (1.0 / TILE))
     tiles = jnp.where(counts > 0.0, tail - lead, 0.0)
     pairs = experts * rows
@@ -95,6 +95,14 @@
     earlier = ones_where((line // rows == column // rows) & (column < line))
     base = jnp.dot(earlier, tiles.astype(jnp.bfloat16), preferred_element_type=jnp.float32)
     return start, lead, tiles, base
+
+
+def write_plan(plan_ref, parts):
+    for n, part in enumerate(parts):
+        short = -part.shape[0] % LANES
+        if short:
+            part = jnp.concatenate([part, jnp.zeros((short, LANES), jnp.float32)], axis=0)
+        plan_ref[n : n + 1, :] = jnp.transpose(part)[:1].astype(jnp.int32)
 
 
 def outgoing_kernel(lines, rows, new_ref, held_ref, stack_ref, plan_ref):
@@ -115,8 +123,7 @@
     ranks = jnp.dot(hits.astype(jnp.bfloat16), until, preferred_element_type=jnp.float32)
     counts = jnp.broadcast_to(jnp.sum(hits, axis=1, keepdims=True), (experts * rows, LANES))
     start, lead, tiles, base = segment_plan(counts, experts, rows)
-    for n, part in enumerate((lead, tiles, base, start - lead * TILE)):
-        plan_ref[n] = part.astype(jnp.int32)
+    write_plan(plan_ref, (lead, tiles, base, start - lead * TILE))
     offset = (base * TILE + start - lead * TILE - 1.0)[:, :1]
     placed = hits * (ranks + offset)
     for e in range(experts):
@@ -154,8 +161,7 @@
     slotted = longest <= slot
     lead = jnp.where(slotted, jnp.minimum(lead, float(block_tiles - slot)), lead)
     base = jnp.where(slotted, peer * slot, base)
-    for n, part in enumerate((lead, tiles, base, jnp.where(slotted, 1.0, 0.0))):
-        plan_ref[n] = part.astype(jnp.int32)
+    write_plan(plan_ref, (lead, tiles, base, jnp.where(slotted, 1.0, 0.0)))
     blank = jnp.zeros((LANES - experts, width), jnp.float32)
     columns = jnp.transpose(jnp.concatenate(held_at + [blank], axis=0))
     rows_out = []
@@ -189,8 +195,7 @@
 def pack_kernel(rows, span, plan_ref, place_ref, lines_ref, out_ref, packed_ref, number_ref, sem, *stages):
     part = pl.program_id(0)
     step = pl.program_id(1)
-    pairs = pl.num_programs(1) * span * rows
-    deep, _ = stages[0].shape
+    deep = stages[0].shape[0] - STRAIGHT * TILE
     lines = lines_ref.shape[2]
 
     @pl.when((part == 0) & (step == 0))
@@ -198,7 +203,7 @@
         number_ref[...] = counting(number_ref.shape, 0)
 
     def entry(n, j, d):
-        return plan_ref[n * pairs + (step * span + j) * rows + d]
+        return plan_ref[n, (step * span + j) * rows + d]
 
     usual = min(deep, up_to(lines + rows * TILE, TILE))
 
@@ -226,15 +231,14 @@
 
         def one_peer(d, most, j=j, stage_ref=stage_ref):
             lead, tiles, base = entry(0, j, d), entry(1, j, d), entry(2, j, d)
-            shared = entry(3, j, d) > 0
-            earlier = packed_ref[d, tile_at(lead), :]
-            for t in range(1, STRAIGHT):
-                n = jnp.maximum(jnp.minimum(t, tiles - 1), 0)
-                packed_ref[d, tile_at(lead + n), :] = stage_ref[tile_at(base + n), :]
-            kept = jnp.where(shared | (tiles == 0), earlier, jnp.zeros_like(earlier))
-            fresh = stage_ref[tile_at(base), :]
-            fresh = jnp.where(tiles == 0, jnp.zeros_like(fresh), fresh)
-            packed_ref[d, tile_at(lead), :] = kept + fresh
+            there = pl.multiple_of(lead * TILE, TILE)
+            here = pl.multiple_of(base * TILE, TILE)
+            earlier = packed_ref[d, pl.ds(there, TILE), :]
+            fresh = stage_ref[pl.ds(here, STRAIGHT * TILE), :]
+            packed_ref[d, pl.ds(there + TILE, (STRAIGHT - 1) * TILE), :] = fresh[TILE:]
+            kept = jnp.where(entry(3, j, d) > 0, earlier, jnp.zeros_like(earlier))
+            added = jnp.where(tiles > 0, fresh[:TILE], jnp.zeros_like(earlier))
+            packed_ref[d, pl.ds(there, TILE), :] = kept + added
             return jnp.maximum(most, tiles)
 
         most = lax.fori_loop(0, rows, one_peer, 0, unroll=rows <= 8)
@@ -254,23 +258,24 @@
 
     @pl.when(step == pl.num_programs(1) - 1)
     def _():
-        copy = pltpu.make_async_copy(packed_ref, out_ref.at[:, part], sem)
+        full = packed_ref.at[:, pl.ds(0, out_ref.shape[2])]
+        copy = pltpu.make_async_copy(full, out_ref.at[:, part], sem)
         copy.start()
         copy.wait()
 
 
-def unpack_kernel(slot, plan_ref, place_ref, block_ref, *rest):
-    out_ref, stage_ref, sems = rest[-3:]
+def unpack_kernel(slot, makes, plan_ref, place_ref, block_ref, *rest):
+    stage_ref, sems = rest[-2:]
+    out_ref = rest[-4] if makes else rest[-3]
     experts = pl.num_programs(0)
     rows, count, _, width = block_ref.shape
-    pairs = experts * rows
     _, deep, _ = stage_ref.shape
     lines = out_ref.shape[2]
     e = pl.program_id(0)
     buffer = e % 2
 
     def entry(n, e, s):
-        return plan_ref[n * pairs + e * rows + s]
+        return plan_ref[n, e * rows + s]
 
     def slotted(e):
         return entry(3, e, 0) > 0
@@ -327,16 +332,20 @@
 
         lax.fori_loop(0, rows, one_peer, 0)
 
-    within_block, block = place_ref[0, 0], place_ref[0, 1]
-    lane = counting((lines, LANES), 1)
-    pieces = []
-    for first in range(0, deep, LANES):
-        away = jnp.abs(block - jnp.asarray(first // 256, jnp.bfloat16))
-        place = within_block + away * jnp.asarray(512, jnp.bfloat16)
-        pieces.append(equal_ones(lane + jnp.asarray(first % 256, jnp.bfloat16), place))
-    onehot = jnp.concatenate(pieces, axis=1)
+    if makes:
+        onehot_ref = rest[-3]
+        within_block, block = place_ref[0, 0], place_ref[0, 1]
+        lane = counting((lines, LANES), 1)
+        for first in range(0, deep, LANES):
+            away = jnp.abs(block - jnp.asarray(first // 256, jnp.bfloat16))
+            place = within_block + away * jnp.asarray(512, jnp.bfloat16)
+            onehot_ref[0, :, first : first + LANES] = equal_ones(
+                lane + jnp.asarray(first % 256, jnp.bfloat16), place
+            )
+    else:
+        onehot_ref = place_ref
     moved = jnp.dot(
-        onehot, stage_ref[buffer], preferred_element_type=jnp.float32
+        onehot_ref[0], stage_ref[buffer], preferred_element_type=jnp.float32
     ).astype(jnp.bfloat16)
     for part in range(count):
         out_ref[0, part] = moved[:, part * width : (part + 1) * width]
@@ -345,7 +354,7 @@
 def call_plan(kernel, name, table, ids, pairs, place):
     return pl.pallas_call(
         kernel,
-        out_shape=(place, jax.ShapeDtypeStruct((4, pairs, LANES), jnp.int32)),
+        out_shape=(place, jax.ShapeDtypeStruct((4, up_to(pairs, LANES)), jnp.int32)),
         compiler_params=params(),
         cost_estimate=pl.CostEstimate(
             flops=20 * table.size * 256, bytes_accessed=8 * table.size, transcendentals=0
@@ -369,11 +378,11 @@
             ],
             out_specs=pl.BlockSpec(memory_space=pltpu.HBM),
             scratch_shapes=[
-                pltpu.VMEM((rows, block_rows, width), jnp.bfloat16),
+                pltpu.VMEM((rows, block_rows + STRAIGHT * TILE, width), jnp.bfloat16),
                 pltpu.VMEM((256, lines), jnp.bfloat16),
                 pltpu.SemaphoreType.DMA(()),
             ]
-            + [pltpu.VMEM((deep, width), jnp.bfloat16)] * span,
+            + [pltpu.VMEM((deep + STRAIGHT * TILE, width), jnp.bfloat16)] * span,
         ),
         out_shape=jax.ShapeDtypeStruct((rows, count, block_rows, width), jnp.bfloat16),
         compiler_params=pltpu.CompilerParams(vmem_limit_bytes=PACK_LIMIT),
@@ -390,8 +399,11 @@
     experts, _, lines, width = shape
     first, count = piece
     rows = arrived.shape[0]
+    makes = previous is None
+    onehot_spec = pl.BlockSpec((1, lines, deep), lambda e, plan: (e, 0, 0))
+    place_spec = pl.BlockSpec((1, 2, lines, LANES), lambda e, plan: (e, 0, 0, 0))
     in_specs = [
-        pl.BlockSpec((1, 2, lines, LANES), lambda e, plan: (e, 0, 0, 0)),
+        place_spec if makes else onehot_spec,
         pl.BlockSpec(memory_space=pl.ANY),
     ]
     operands = [plan, place, arrived]
@@ -401,18 +413,22 @@
         operands.append(previous)
         aliases = {3: 0}
     return pl.pallas_call(
-        functools.partial(unpack_kernel, slot),
+        functools.partial(unpack_kernel, slot, makes),
         grid_spec=pltpu.PrefetchScalarGridSpec(
             num_scalar_prefetch=1,
             grid=(experts,),
             in_specs=in_specs,
-            out_specs=pl.BlockSpec((1, count, lines, width), lambda e, plan: (e, first // count, 0, 0)),
+            out_specs=[
+                pl.BlockSpec((1, count, lines, width), lambda e, plan: (e, first // count, 0, 0))
+            ]
+            + [onehot_spec] * makes,
             scratch_shapes=[
                 pltpu.VMEM((2, deep, count * width), jnp.bfloat16),
                 pltpu.SemaphoreType.DMA((2, rows * count)),
             ],
         ),
-        out_shape=jax.ShapeDtypeStruct(shape, jnp.bfloat16),
+        out_shape=[jax.ShapeDtypeStruct(shape, jnp.bfloat16)]
+        + [jax.ShapeDtypeStruct((experts, lines, deep), jnp.bfloat16)] * makes,
         input_output_aliases=aliases,
         compiler_params=params(),
         cost_estimate=pl.CostEstimate(
@@ -458,7 +474,7 @@
         padded = up_to(lines, LANES)
         block_rows = up_to(experts * lines // rows, TILE)
         pairs = experts * rows
-        compact = up_to(lines + 2 * (TILE - 1) * rows, TILE) + TILE
+        compact = up_to(lines + 2 * (TILE - 1) * rows, TILE)
         self.slot = min(STRAIGHT, block_rows // TILE)
         self.deep = up_to(max(compact, rows * self.slot * TILE), 256)
         self.shape = expert_lines.shape
@@ -468,14 +484,12 @@
             new_lines, own_ids(old_lines, lines, padded), pairs,
             jax.ShapeDtypeStruct((experts, 1, padded), jnp.int32),
         )
-        self.in_place, in_plan = call_plan(
+        self.in_place, self.in_plan = call_plan(
             functools.partial(incoming_kernel, lines, rows, block_rows // TILE, self.slot),
             "incoming_plan",
             old_lines, own_ids(new_lines, lines, padded), pairs,
             jax.ShapeDtypeStruct((experts, 2, lines, LANES), jnp.bfloat16),
         )
-        out_plan = out_plan[:, :, 0].reshape(-1)
-        self.in_plan = in_plan[:, :, 0].reshape(-1)
         self.packed = [
             pack(expert_lines, out_place, out_plan, piece, rows, block_rows, compact)
             for piece in self.pieces
@@ -492,10 +506,12 @@
         )
 
     def receive(self, piece):
-        self.moved = unpack(
+        self.moved, *onehots = unpack(
             self.arrived[piece], self.in_place, self.in_plan, self.pieces[piece], self.shape,
             self.deep, self.slot, self.moved,
         )
+        if onehots:
+            (self.in_place,) = onehots
 
 
 def attend(queries, new_kv, prompt_kv, suffix_kv, lengths):

time: 252 us -> 253 us (level)
    pallas_call x4, Pallas kernels: 47.6 us -> 52.8 us  [the longest x2 35.9 us: unpack(): pl.pallas_call(functools.partial(unpack_kernel, slot, makes), grid_spec=p...]
    pallas_call x2, Pallas kernels: 36.4 us -> 32.8 us  [pack(): pl.pallas_call(functools.partial(pack_kernel, rows, span), grid_spec=pltp...]
    unnamed x41 -> x43, local copies, waits for them, and re-layouts: 6.24 us -> 6.79 us
  transfers between devices with their start and end apart: 19 -> 19, of which waited for: 10 -> 7; matrix products, arithmetic and copies ran while one was open for 10% -> 10% of each run, Pallas kernels for 25% -> 25%
where the time goes in v4:
time: 253 us; the launch traced here: 251 us
  Pallas kernels  101 us (40%)
  waiting for transfers between devices  87.3 us (35%)
  starting transfers between devices  32.7 us (13%)
  local copies, waits for them, and re-layouts  15.3 us (6%)
  matrix products  8.46 us (3%)
  other arithmetic  5.59 us (2%)
    ppermute x17, waiting for transfers between devices, from_peer(): return lax.ppermute(block, axis, [(i, i ^ offset) for i in range(size)])  87.3 us
    pallas_call x2, Pallas kernels, unpack(): pl.pallas_call(functools.partial(unpack_kernel, slot, makes), grid_spec=p...  35.9 us
    pallas_call x2, Pallas kernels, pack(): pl.pallas_call(functools.partial(pack_kernel, rows, span), grid_spec=pltp...  32.8 us
    ppermute x17, starting transfers between devices, from_peer(): return lax.ppermute(block, axis, [(i, i ^ offset) for i in range(size)])  21.9 us
    pallas_call x2, Pallas kernels, call_plan(): pl.pallas_call(kernel, out_shape=(place, jax.ShapeDtypeStruct((4, up_to(p...  16.9 us
    all_to_all x2, starting transfers between devices, send(): lax.all_to_all(block, 'row', split_axis=0, concat_axis=0, tiled=True)  10.8 us
    pallas_call x1, Pallas kernels, experts_part(): pl.pallas_call(gate_up_kernel, grid_spec=pltpu.PrefetchScalarGridSpec(num...  8.8 us
    unnamed x43, local copies, waits for them, and re-layouts  6.79 us
  transfers between devices with their start and end apart: 19, of which 7 were waited for; matrix products, arithmetic and copies ran while one was open for 10% of the time, Pallas kernels for 25%

profile of v4, /device:TPU:0, one launch (start us, length us, event | category | flops | bytes accessed | tf_op | source)
XLA Modules:
  0.0 251.4 jit_solution(17534280752996141689)
XLA Ops:
  2.4 6.1 %outgoing_plan.1 = (s32[8,1,768]{2,1,0:T(1,128)S(1)}, s32[4,128]{1,0:T(4,128)S(1)}) custom-call(s32[8,5632]{1,0:T(8,128)S(1)} %copy-done.4, s32[8,768]{1,0:T(8,128)S(1)} %pad.11.held_ref), custom_call_target="tpu_custom_call" | custom-call | flops 230686720 | bytes 360448 | tf_op jit(solution)/shard_map/outgoing_plan/pallas_call | solution.py:355
  9.6 11.7 %pack_lines.2.refs_1_ = bf16[8,1,704,512]{3,2,1,0:T(8,128)(2,1)} custom-call(s32[4,128]{1,0:T(4,128)} %copy-done.6, s32[8,1,768]{2,1,0:T(1,128)} %copy-done.3, bf16[8,3,704,512]{3,2,1,0:T(8,128)(2,1)} %bitcast.81), custom_call_target="tpu_custom_call" | custom-call | flops 5444206592 | bytes 11534336 | tf_op jit(solution)/shard_map/pack_lines/pallas_call | solution.py:370
  21.3 5.2 %all-to-all-start = ((bf16[8,1,704,512]{3,2,1,0:T(8,128)(2,1)}), bf16[8,1,704,512]{3,2,1,0:T(8,128)(2,1)}, u32[]{:S(2)}, u32[]{:S(2)}) async-start(bf16[8,1,704,512]{3,2,1,0:T(8,128)(2,1)} %pack_lines.2.refs_1_), calls=%async_computation | async-start | bytes 11534336 | tf_op jit(solution)/shard_map/all_to_all | solution.py:505
  26.5 1.7 fusion.30
  29.3 1.7 fusion.29
  31.2 1.2 copy.145
  33.0 2.0 fusion.33
  35.7 1.2 fusion.32
  38.9 1.1 fusion.25
  40.5 1.1 fusion.5
  42.1 4.8 %collective-permute-start.2 = (f32[8,4224]{1,0:T(8,128)S(1)}, f32[8,4224]{1,0:T(8,128)S(1)}, u32[]{:S(2)}, u32[]{:S(2)}) collective-permute-start(f32[8,4224]{1,0:T(8,128)S(1)} %concatenate.10), channel_id=1, source_target_pairs={{0,3},{1,2},{2,1},{3,0},{4,7},{5,6},{6,5},{7,4},{8,11},{9,10},{10,... | collective-permute-start | bytes 405512 | tf_op jit(solution)/shard_map/ppermute | solution.py:467
  47.6 21.2 %pack_lines.3.refs_2_.refs_0_ = bf16[8,2,704,512]{3,2,1,0:T(8,128)(2,1)} custom-call(s32[4,128]{1,0:T(4,128)} %copy-done.6, s32[8,1,768]{2,1,0:T(1,128)} %copy-done.3, bf16[8,3,704,512]{3,2,1,0:T(8,128)(2,1)} %bitcast.82), custom_call_target="tpu_custom_call" | custom-call | flops 10888413184 | bytes 23068672 | tf_op jit(solution)/shard_map/pack_lines/pallas_call | solution.py:370
  69.3 3.5 %fusion.4.refs_0_ = bf16[8,512]{1,0:T(8,128)(2,1)} fusion(bf16[4096,512]{1,0:T(8,128)(2,1)} %param.20, f32[8,4096]{1,0:T(8,128)S(1)} %fusion.8, f32[8,32]{0,1:T(8,128)S(1)} %copy.126, bf16[8,512]{1,0:T(8,128)(2,1)S(1)} %copy-done.10), kind=kOutput, calls=%fused_computation.9 | convolution fusion | flops 33632256 | bytes 4342784 | tf_op jit(solution)/shard_map/dot_general | solution.py:781
  72.8 1.7 collective-permute-start.3
  74.5 1.5 collective-permute-start.4
  77.0 15.1 %collective-permute-done.3 = bf16[8,512]{1,0:T(8,128)(2,1)S(1)} collective-permute-done((bf16[8,512]{1,0:T(8,128)(2,1)}, bf16[8,512]{1,0:T(8,128)(2,1)S(1)}, u32[]{:S(2)}, u32[]{:S(2)}) %collective-permute-start.3) | collective-permute-done | bytes 8224 | tf_op jit(solution)/shard_map/ppermute | solution.py:467
  93.9 1.2 collective-permute-done.6
  95.7 5.6 %all-to-all-start.1 = ((bf16[8,2,704,512]{3,2,1,0:T(8,128)(2,1)}), bf16[8,2,704,512]{3,2,1,0:T(8,128)(2,1)}, u32[]{:S(2)}, u32[]{:S(2)}) async-start(bf16[8,2,704,512]{3,2,1,0:T(8,128)(2,1)} %after.5), calls=%async_computation.1 | async-start | bytes 23068672 | tf_op jit(solution)/shard_map/all_to_all | solution.py:505
  102.5 8.8 %gate_up.1 = bf16[4,4,16,768]{3,2,1,0:T(8,128)(2,1)S(1)} custom-call(s32[1]{0:T(128)} %bitcast.20.me_ref, bf16[64,512]{1,0:T(8,128)(2,1)S(1)} %copy-done.2, bf16[1,512]{1,0:T(2,128)(2,1)S(1)} %reshape.90.gain_ref, bf16[512,128]{1,0:T(8,128)(2,1)S(1)} %pad.12.router_ref, s32[64,2]{1,0:T(8,128)S(1)} %bitcast.78, bf16[8,3,704,512]{3,2,1,0:T(8,128)(2,1)} %bitcast.83, ...), custom_call_target="tpu_custom_call" | custom-call | flops 738197504 | bytes 11534336 | tf_op jit(solution)/shard_map/gate_up/pallas_call | solution.py:706
  111.3 2.3 collective-permute-start.7
  113.6 2.6 %collective-permute-start.8 = (bf16[4,16,768]{2,1,0:T(8,128)(2,1)S(1)}, bf16[4,16,768]{2,1,0:T(8,128)(2,1)S(1)}, u32[]{:S(2)}, u32[]{:S(2)}) collective-permute-start(bf16[4,16,768]{2,1,0:T(8,128)(2,1)S(1)} %get-tuple-element.23), channel_id=1, source_target_pairs={{0,2},{1,3},{2,0},{3,1},{4,6},{5,7},{6,4},{7,5},{8,10},{9,11},{10,... | collective-permute-start | bytes 294920 | tf_op jit(solution)/shard_map/ppermute | solution.py:467
  116.7 7.5 %collective-permute-done.8.refs_2_ = bf16[4,16,768]{2,1,0:T(8,128)(2,1)S(1)} collective-permute-done((bf16[4,16,768]{2,1,0:T(8,128)(2,1)S(1)}, bf16[4,16,768]{2,1,0:T(8,128)(2,1)S(1)}, u32[]{:S(2)}, u32[]{:S(2)}) %collective-permute-start.8) | collective-permute-done | bytes 98336 | tf_op jit(solution)/shard_map/ppermute | solution.py:467
  124.4 1.8 collective-permute-start.10
  126.2 1.4 collective-permute-start.11
  127.6 1.2 collective-permute-start.12
  129.7 10.8 %incoming_plan.1 = (bf16[8,2,704,128]{3,2,1,0:T(8,128)(2,1)S(1)}, s32[4,128]{1,0:T(4,128)S(1)}) custom-call(s32[8,5632]{1,0:T(8,128)S(1)} %copy-done.5, s32[8,768]{1,0:T(8,128)S(1)} %pad.13.wanted_ref), custom_call_target="tpu_custom_call" | custom-call | flops 230686720 | bytes 360448 | tf_op jit(solution)/shard_map/incoming_plan/pallas_call | solution.py:355
  140.5 6.1 %down.1.refs_0_ = f32[64,512]{1,0:T(8,128)S(1)} custom-call(s32[1]{0:T(128)} %bitcast.20.me_ref, s32[64,2]{1,0:T(8,128)S(1)} %bitcast.80, bf16[2,16,768]{2,1,0:T(8,128)(2,1)S(1)} %activate.1.refs_0_, bf16[2,16,768]{2,1,0:T(8,128)(2,1)S(1)} %collective-permute-done.10.refs_1_, bf16[2,16,768]{2,1,0:T(8,128)(2,1)S(1)} %collective-permute-done.11.refs_2_, ...), custom_call_target="tpu_custom_call" | custom-call | flops 369098752 | bytes 5767168 | tf_op jit(solution)/shard_map/down/pallas_call | solution.py:733
  147.3 14.7 %unpack_lines.2 = (bf16[8,3,704,512]{3,2,1,0:T(8,128)(2,1)}, bf16[8,704,1024]{2,1,0:T(8,128)(2,1)}) custom-call(s32[4,128]{1,0:T(4,128)S(1)} %get-tuple-element.10.plan_ref, bf16[8,2,704,128]{3,2,1,0:T(8,128)(2,1)S(1)} %get-tuple-element.11.place_ref, bf16[8,1,704,512]{3,2,1,0:T(8,128)(2,1)} %all-to-all-done.block_ref), custom_call_target="tpu_custom_call" | custom-call | flops 5905580032 | bytes 11534336 | tf_op jit(solution)/shard_map/unpack_lines/pallas_call | solution.py:415
  162.9 1.3 collective-permute-done.13
  165.0 2.7 %collective-permute-start.16 = (f32[8,512]{1,0:T(8,128)S(1)}, f32[8,512]{1,0:T(8,128)S(1)}, u32[]{:S(2)}, u32[]{:S(2)}) collective-permute-start(f32[8,512]{1,0:T(8,128)S(1)} %get-tuple-element.27), channel_id=1, source_target_pairs={{0,24},{4,28},{8,16},{12,20},{16,8},{20,12},{24,0},{28,4},{1,25},{... | collective-permute-start | bytes 49160 | tf_op jit(solution)/shard_map/ppermute | solution.py:467
  168.5 60.8 %collective-permute-done.16 = f32[8,512]{1,0:T(8,128)S(1)} collective-permute-done((f32[8,512]{1,0:T(8,128)S(1)}, f32[8,512]{1,0:T(8,128)S(1)}, u32[]{:S(2)}, u32[]{:S(2)}) %collective-permute-start.16) | collective-permute-done | bytes 16416 | tf_op jit(solution)/shard_map/ppermute | solution.py:467
  229.9 21.3 %unpack_lines.3 = bf16[8,3,704,512]{3,2,1,0:T(8,128)(2,1)} custom-call(s32[4,128]{1,0:T(4,128)S(1)} %get-tuple-element.10.plan_ref, bf16[8,704,1024]{2,1,0:T(8,128)(2,1)} %get-tuple-element.13.place_ref, bf16[8,2,704,512]{3,2,1,0:T(8,128)(2,1)} %all-to-all-done.1.block_ref, ...), custom_call_target="tpu_custom_call", output_to_operand_aliasing={{}: (3, {})} | custom-call | flops 11811160064 | bytes 23068672 | tf_op jit(solution)/shard_map/unpack_lines/pallas_call | solution.py:415
  (112 shorter events, 19.5 us)
Async XLA Ops:
  1.5 0.9 copy-start.4
  21.3 74.4 %all-to-all-start = ((bf16[8,1,704,512]{3,2,1,0:T(8,128)(2,1)}), bf16[8,1,704,512]{3,2,1,0:T(8,128)(2,1)}, u32[]{:S(2)}, u32[]{:S(2)}) async-start(bf16[8,1,704,512]{3,2,1,0:T(8,128)(2,1)} %pack_lines.2.refs_1_), calls=%async_computation | async-start | bytes 11534336 | tf_op jit(solution)/shard_map/all_to_all | solution.py:505
  28.7 3.7 %copy-start.8 = (bf16[8,4096]{1,0:T(8,128)(2,1)S(1)}, bf16[8,4096]{1,0:T(8,128)(2,1)}, u32[]{:S(2)}) copy-start(bf16[8,4096]{1,0:T(8,128)(2,1)} %param.15) | copy-start | bytes 196612
  28.7 3.7 %copy-start.9 = (bf16[8,2,2048]{2,1,0:T(2,128)(2,1)S(1)}, bf16[8,2,2048]{2,1,0:T(2,128)(2,1)}, u32[]{:S(2)}) copy-start(bf16[8,2,2048]{2,1,0:T(2,128)(2,1)} %param.16) | copy-start | bytes 196612
  28.7 4.2 %copy-start.15 = (s32[8]{0:T(128)S(1)}, s32[8]{0:T(128)}, u32[]{:S(2)}) copy-start(s32[8]{0:T(128)} %param.19) | copy-start | bytes 100
  33.0 2.8 %copy-start.12 = (pred[8,32]{1,0:T(8,128)(4,1)}, pred[8,32]{1,0:T(8,128)(4,1)S(1)}, u32[]{:S(2)}) copy-start(pred[8,32]{1,0:T(8,128)(4,1)S(1)} %broadcast_compare_fusion) | copy-start | bytes 772
  42.1 27.2 %copy-start.10 = (bf16[8,512]{1,0:T(8,128)(2,1)S(1)}, bf16[8,512]{1,0:T(8,128)(2,1)}, u32[]{:S(2)}) copy-start(bf16[8,512]{1,0:T(8,128)(2,1)} %param.14) | copy-start | bytes 24580
  42.1 26.7 %collective-permute-start.2 = (f32[8,4224]{1,0:T(8,128)S(1)}, f32[8,4224]{1,0:T(8,128)S(1)}, u32[]{:S(2)}, u32[]{:S(2)}) collective-permute-start(f32[8,4224]{1,0:T(8,128)S(1)} %concatenate.10), channel_id=1, source_target_pairs={{0,3},{1,2},{2,1},{3,0},{4,7},{5,6},{6,5},{7,4},{8,11},{9,10},{10,... | collective-permute-start | bytes 405512 | tf_op jit(solution)/shard_map/ppermute | solution.py:467
  47.0 21.8 %collective-permute-start.1 = (f32[8,4224]{1,0:T(8,128)S(1)}, f32[8,4224]{1,0:T(8,128)S(1)}, u32[]{:S(2)}, u32[]{:S(2)}) collective-permute-start(f32[8,4224]{1,0:T(8,128)S(1)} %concatenate.10), channel_id=1, source_target_pairs={{0,2},{1,3},{2,0},{3,1},{4,6},{5,7},{6,4},{7,5},{8,10},{9,11},{10,... | collective-permute-start | bytes 405512 | tf_op jit(solution)/shard_map/ppermute | solution.py:467
  47.0 21.8 %collective-permute-start = (f32[8,4224]{1,0:T(8,128)S(1)}, f32[8,4224]{1,0:T(8,128)S(1)}, u32[]{:S(2)}, u32[]{:S(2)}) collective-permute-start(f32[8,4224]{1,0:T(8,128)S(1)} %concatenate.10), channel_id=1, source_target_pairs={{0,1},{1,0},{2,3},{3,2},{4,5},{5,4},{6,7},{7,6},{8,9},{9,8},{10,11... | collective-permute-start | bytes 405512 | tf_op jit(solution)/shard_map/ppermute | solution.py:467
  72.8 19.3 %collective-permute-start.3 = (bf16[8,512]{1,0:T(8,128)(2,1)}, bf16[8,512]{1,0:T(8,128)(2,1)S(1)}, u32[]{:S(2)}, u32[]{:S(2)}) collective-permute-start(bf16[8,512]{1,0:T(8,128)(2,1)} %after.3), channel_id=1, source_target_pairs={{0,8},{4,12},{8,0},{12,4},{16,24},{20,28},{24,16},{28,20},{1,9},{5... | collective-permute-start | bytes 24584 | tf_op jit(solution)/shard_map/ppermute | solution.py:467
  74.5 17.6 %collective-permute-start.4 = (bf16[8,512]{1,0:T(8,128)(2,1)}, bf16[8,512]{1,0:T(8,128)(2,1)S(1)}, u32[]{:S(2)}, u32[]{:S(2)}) collective-permute-start(bf16[8,512]{1,0:T(8,128)(2,1)} %after.3), channel_id=1, source_target_pairs={{0,16},{4,20},{8,24},{12,28},{16,0},{20,4},{24,8},{28,12},{1,17},{... | collective-permute-start | bytes 24584 | tf_op jit(solution)/shard_map/ppermute | solution.py:467
  76.0 17.1 %collective-permute-start.5 = (bf16[8,512]{1,0:T(8,128)(2,1)}, bf16[8,512]{1,0:T(8,128)(2,1)S(1)}, u32[]{:S(2)}, u32[]{:S(2)}) collective-permute-start(bf16[8,512]{1,0:T(8,128)(2,1)} %after.3), channel_id=1, source_target_pairs={{0,24},{4,28},{8,16},{12,20},{16,8},{20,12},{24,0},{28,4},{1,25},{... | collective-permute-start | bytes 24584 | tf_op jit(solution)/shard_map/ppermute | solution.py:467
  93.8 1.2 collective-permute-start.6
  95.7 5.7 %copy-start.13 = (s32[64,2]{0,1:T(2,128)S(1)}, s32[64,2]{0,1:T(2,128)}, u32[]{:S(2)}) copy-start(s32[64,2]{0,1:T(2,128)} %param.26) | copy-start | bytes 1540
  95.7 5.8 %copy-start.16 = (s32[8]{0:T(128)S(1)}, s32[8]{0:T(128)}, u32[]{:S(2)}) copy-start(s32[8]{0:T(128)} %constant.41.clone) | copy-start | bytes 100
  95.7 6.5 %copy-start.14 = (bf16[512]{0:T(512)(128)(2,1)S(1)}, bf16[512]{0:T(512)(128)(2,1)}, u32[]{:S(2)}) copy-start(bf16[512]{0:T(512)(128)(2,1)} %param.21) | copy-start | bytes 3076
  95.7 6.5 %copy-start.11 = (bf16[512,8]{0,1:T(8,128)(2,1)S(1)}, bf16[512,8]{0,1:T(8,128)(2,1)}, u32[]{:S(2)}) copy-start(bf16[512,8]{0,1:T(8,128)(2,1)} %param.22) | copy-start | bytes 24580
  95.7 6.8 %copy-start.2 = (bf16[64,512]{1,0:T(8,128)(2,1)S(1)}, bf16[64,512]{1,0:T(8,128)(2,1)}, u32[]{:S(2)}) copy-start(bf16[64,512]{1,0:T(8,128)(2,1)} %copy-done.1) | copy-start | bytes 196612
  95.7 134.2 %all-to-all-start.1 = ((bf16[8,2,704,512]{3,2,1,0:T(8,128)(2,1)}), bf16[8,2,704,512]{3,2,1,0:T(8,128)(2,1)}, u32[]{:S(2)}, u32[]{:S(2)}) async-start(bf16[8,2,704,512]{3,2,1,0:T(8,128)(2,1)} %after.5), calls=%async_computation.1 | async-start | bytes 23068672 | tf_op jit(solution)/shard_map/all_to_all | solution.py:505
  102.5 27.2 %copy-start.5 = (s32[8,5632]{1,0:T(8,128)S(1)}, s32[8,5632]{1,0:T(8,128)}, u32[]{:S(2)}) copy-start(s32[8,5632]{1,0:T(8,128)} %old_ref.1) | copy-start | bytes 540676
  111.3 5.4 %collective-permute-start.7 = (bf16[4,16,768]{2,1,0:T(8,128)(2,1)S(1)}, bf16[4,16,768]{2,1,0:T(8,128)(2,1)S(1)}, u32[]{:S(2)}, u32[]{:S(2)}) collective-permute-start(bf16[4,16,768]{2,1,0:T(8,128)(2,1)S(1)} %get-tuple-element.24), channel_id=1, source_target_pairs={{0,1},{1,0},{2,3},{3,2},{4,5},{5,4},{6,7},{7,6},{8,9},{9,8},{10,11... | collective-permute-start | bytes 294920 | tf_op jit(solution)/shard_map/ppermute | solution.py:467
  113.6 10.7 %collective-permute-start.8 = (bf16[4,16,768]{2,1,0:T(8,128)(2,1)S(1)}, bf16[4,16,768]{2,1,0:T(8,128)(2,1)S(1)}, u32[]{:S(2)}, u32[]{:S(2)}) collective-permute-start(bf16[4,16,768]{2,1,0:T(8,128)(2,1)S(1)} %get-tuple-element.23), channel_id=1, source_target_pairs={{0,2},{1,3},{2,0},{3,1},{4,6},{5,7},{6,4},{7,5},{8,10},{9,11},{10,... | collective-permute-start | bytes 294920 | tf_op jit(solution)/shard_map/ppermute | solution.py:467
  116.2 8.0 %collective-permute-start.9 = (bf16[4,16,768]{2,1,0:T(8,128)(2,1)S(1)}, bf16[4,16,768]{2,1,0:T(8,128)(2,1)S(1)}, u32[]{:S(2)}, u32[]{:S(2)}) collective-permute-start(bf16[4,16,768]{2,1,0:T(8,128)(2,1)S(1)} %get-tuple-element.22), channel_id=1, source_target_pairs={{0,3},{1,2},{2,1},{3,0},{4,7},{5,6},{6,5},{7,4},{8,11},{9,10},{10,... | collective-permute-start | bytes 294920 | tf_op jit(solution)/shard_map/ppermute | solution.py:467
  124.4 16.1 %collective-permute-start.10 = (bf16[2,16,768]{2,1,0:T(8,128)(2,1)S(1)}, bf16[2,16,768]{2,1,0:T(8,128)(2,1)S(1)}, u32[]{:S(2)}, u32[]{:S(2)}) collective-permute-start(bf16[2,16,768]{2,1,0:T(8,128)(2,1)S(1)} %activate.1.refs_0_), channel_id=1, source_target_pairs={{0,1},{1,0},{2,3},{3,2},{4,5},{5,4},{6,7},{7,6},{8,9},{9,8},{10,11... | collective-permute-start | bytes 147464 | tf_op jit(solution)/shard_map/ppermute | solution.py:467
  126.2 14.3 %collective-permute-start.11 = (bf16[2,16,768]{2,1,0:T(8,128)(2,1)S(1)}, bf16[2,16,768]{2,1,0:T(8,128)(2,1)S(1)}, u32[]{:S(2)}, u32[]{:S(2)}) collective-permute-start(bf16[2,16,768]{2,1,0:T(8,128)(2,1)S(1)} %activate.1.refs_0_), channel_id=1, source_target_pairs={{0,2},{1,3},{2,0},{3,1},{4,6},{5,7},{6,4},{7,5},{8,10},{9,11},{10,... | collective-permute-start | bytes 147464 | tf_op jit(solution)/shard_map/ppermute | solution.py:467
  127.6 12.9 %collective-permute-start.12 = (bf16[2,16,768]{2,1,0:T(8,128)(2,1)S(1)}, bf16[2,16,768]{2,1,0:T(8,128)(2,1)S(1)}, u32[]{:S(2)}, u32[]{:S(2)}) collective-permute-start(bf16[2,16,768]{2,1,0:T(8,128)(2,1)S(1)} %activate.1.refs_0_), channel_id=1, source_target_pairs={{0,3},{1,2},{2,1},{3,0},{4,7},{5,6},{6,5},{7,4},{8,11},{9,10},{10,... | collective-permute-start | bytes 147464 | tf_op jit(solution)/shard_map/ppermute | solution.py:467
  162.0 67.3 %copy-start.7 = (bf16[8,512]{1,0:T(8,128)(2,1)S(1)}, bf16[8,512]{1,0:T(8,128)(2,1)}, u32[]{:S(2)}) copy-start(bf16[8,512]{1,0:T(8,128)(2,1)} %after.3) | copy-start | bytes 24580
  162.8 1.3 collective-permute-start.13
  165.0 64.3 %collective-permute-start.16 = (f32[8,512]{1,0:T(8,128)S(1)}, f32[8,512]{1,0:T(8,128)S(1)}, u32[]{:S(2)}, u32[]{:S(2)}) collective-permute-start(f32[8,512]{1,0:T(8,128)S(1)} %get-tuple-element.27), channel_id=1, source_target_pairs={{0,24},{4,28},{8,16},{12,20},{16,8},{20,12},{24,0},{28,4},{1,25},{... | collective-permute-start | bytes 49160 | tf_op jit(solution)/shard_map/ppermute | solution.py:467
  167.6 61.7 %collective-permute-start.15 = (f32[8,512]{1,0:T(8,128)S(1)}, f32[8,512]{1,0:T(8,128)S(1)}, u32[]{:S(2)}, u32[]{:S(2)}) collective-permute-start(f32[8,512]{1,0:T(8,128)S(1)} %get-tuple-element.28), channel_id=1, source_target_pairs={{0,16},{4,20},{8,24},{12,28},{16,0},{20,4},{24,8},{28,12},{1,17},{... | collective-permute-start | bytes 49160 | tf_op jit(solution)/shard_map/ppermute | solution.py:467
  168.2 61.1 %collective-permute-start.14 = (f32[8,512]{1,0:T(8,128)S(1)}, f32[8,512]{1,0:T(8,128)S(1)}, u32[]{:S(2)}, u32[]{:S(2)}) collective-permute-start(f32[8,512]{1,0:T(8,128)S(1)} %get-tuple-element.26), channel_id=1, source_target_pairs={{0,8},{4,12},{8,0},{12,4},{16,24},{20,28},{24,16},{28,20},{1,9},{5... | collective-permute-start | bytes 49160 | tf_op jit(solution)/shard_map/ppermute | solution.py:467
  (4 other events, 2.4 us)

commit v5 on v4

--- a/solution.py
+++ b/solution.py
@@ -17,6 +17,7 @@
 neg_big = -1e30
 VMEM_LIMIT = 48 * 1024 * 1024
 PACK_LIMIT = 61 * 1024 * 1024
+UNPACK_LIMIT = 24 * 1024 * 1024
 
 
 def up_to(value, unit):
@@ -53,26 +54,54 @@
     return as_bf16(jnp.where((place >= 0) & (place < 256), place, -1))
 
 
-def look_up(table_row, id_row, numbers, values):
-    full = table_row.shape[1]
-    ids = id_row.shape[1]
+def look_up(table_rows, id_rows, numbers, values):
+    full = table_rows[0].shape[1]
+    ids = id_rows[0].shape[1]
     high_count = up_to(-(-full // 64), 16)
-    table_high = equal_ones(numbers[:high_count], as_bf16(table_row >> 6))
-    low = as_bf16(table_row & 63)
     zero = jnp.zeros((), jnp.bfloat16)
-    table_low = jnp.concatenate(
-        [jnp.where(numbers[:64] == low, part, zero) for part in values], axis=0
-    )
+    highs = [equal_ones(numbers[:high_count], as_bf16(row >> 6)) for row in table_rows]
+    lows = []
+    for row in table_rows:
+        hit = numbers[:64] == as_bf16(row & 63)
+        lows += [jnp.where(hit, part, zero) for part in values]
     square = lax.dot_general(
-        table_low, table_high, (((1,), (1,)), ((), ())), preferred_element_type=jnp.float32
-    )
-    id_high = equal_ones(numbers[:high_count, :ids], as_bf16(id_row >> 6))
-    spread = jnp.dot(square.astype(jnp.bfloat16), id_high, preferred_element_type=jnp.float32)
-    wanted = iota((64, ids), 0) == (id_row & 63)
-    return [
-        jnp.sum(jnp.where(wanted, spread[64 * n : 64 * n + 64], 0.0), axis=0, keepdims=True)
-        for n in range(len(values))
-    ]
+        jnp.concatenate(highs, axis=0),
+        jnp.concatenate(lows, axis=0),
+        (((1,), (1,)), ((), ())),
+        preferred_element_type=jnp.float32,
+    )
+    wide = 64 * len(values)
+    found = []
+    for n, row in enumerate(id_rows):
+        block = square[n * high_count : (n + 1) * high_count, n * wide : (n + 1) * wide]
+        id_high = equal_ones(numbers[:high_count, :ids], as_bf16(row >> 6))
+        spread = lax.dot_general(
+            block.astype(jnp.bfloat16), id_high, (((0,), (0,)), ((), ())),
+            preferred_element_type=jnp.float32,
+        )
+        wanted = iota((64, ids), 0) == (row & 63)
+        found.append(
+            [
+                jnp.sum(jnp.where(wanted, spread[64 * m : 64 * m + 64], 0.0), axis=0, keepdims=True)
+                for m in range(len(values))
+            ]
+        )
+    return found
+
+
+def look_up_all(table_ref, id_ref, numbers, values):
+    experts = table_ref.shape[0]
+    group = 4 // len(values)
+    found = []
+    for first in range(0, experts, group):
+        members = range(first, min(first + group, experts))
+        found += look_up(
+            [table_ref[e : e + 1, :] for e in members],
+            [id_ref[e : e + 1, :] for e in members],
+            numbers,
+            values,
+        )
+    return found
 
 
 def numbers_for(full):
@@ -114,8 +143,7 @@
     numbers = numbers_for(full)
     slot = iota((64, full), 1).astype(jnp.float32)
     values = (jnp.floor((slot + 0.5) * (1.0 / lines)).astype(jnp.bfloat16),)
-    for e in range(experts):
-        (peer,) = look_up(new_ref[e : e + 1, :], held_ref[e : e + 1, :], numbers, values)
+    for (peer,) in look_up_all(new_ref, held_ref, numbers, values):
         peer = peer.astype(jnp.int32)
         hits.append(jnp.where((iota((rows, width), 0) == peer) & real, 1.0, 0.0))
     hits = jnp.concatenate(hits, axis=0)
@@ -141,8 +169,7 @@
     numbers = numbers_for(full)
     at = iota((64, full), 1)
     values = (as_bf16(at >> 7), as_bf16(at & 127))
-    for e in range(experts):
-        high, low = look_up(old_ref[e : e + 1, :], wanted_ref[e : e + 1, :], numbers, values)
+    for high, low in look_up_all(old_ref, wanted_ref, numbers, values):
         slots = high * 128.0 + low
         held_at.append(jnp.where(real, slots, 1e9))
         peer = jnp.floor((slots + 0.5) * (1.0 / lines)).astype(jnp.int32)
@@ -186,13 +213,14 @@
 
 
 STRAIGHT = 8
+SLOT = 7
 
 
 def tile_at(index):
     return pl.ds(pl.multiple_of(index * TILE, TILE), TILE)
 
 
-def pack_kernel(rows, span, plan_ref, place_ref, lines_ref, out_ref, packed_ref, number_ref, sem, *stages):
+def pack_kernel(rows, span, plan_ref, place_ref, lines_ref, out_ref, packed_ref, number_ref, sems, *stages):
     part = pl.program_id(0)
     step = pl.program_id(1)
     deep = stages[0].shape[0] - STRAIGHT * TILE
@@ -258,10 +286,16 @@
 
     @pl.when(step == pl.num_programs(1) - 1)
     def _():
-        full = packed_ref.at[:, pl.ds(0, out_ref.shape[2])]
-        copy = pltpu.make_async_copy(full, out_ref.at[:, part], sem)
-        copy.start()
-        copy.wait()
+        copies = [
+            pltpu.make_async_copy(
+                packed_ref.at[d, pl.ds(0, out_ref.shape[2])], out_ref.at[d, part], sems.at[d]
+            )
+            for d in range(rows)
+        ]
+        for copy in copies:
+            copy.start()
+        for copy in copies:
+            copy.wait()
 
 
 def unpack_kernel(slot, makes, plan_ref, place_ref, block_ref, *rest):
@@ -380,7 +414,7 @@
             scratch_shapes=[
                 pltpu.VMEM((rows, block_rows + STRAIGHT * TILE, width), jnp.bfloat16),
                 pltpu.VMEM((256, lines), jnp.bfloat16),
-                pltpu.SemaphoreType.DMA(()),
+                pltpu.SemaphoreType.DMA((rows,)),
             ]
             + [pltpu.VMEM((deep + STRAIGHT * TILE, width), jnp.bfloat16)] * span,
         ),
@@ -430,7 +464,7 @@
         out_shape=[jax.ShapeDtypeStruct(shape, jnp.bfloat16)]
         + [jax.ShapeDtypeStruct((experts, lines, deep), jnp.bfloat16)] * makes,
         input_output_aliases=aliases,
-        compiler_params=params(),
+        compiler_params=pltpu.CompilerParams(vmem_limit_bytes=UNPACK_LIMIT),
         cost_estimate=pl.CostEstimate(
             flops=2 * count * experts * deep * lines * width,
             bytes_accessed=4 * count * experts * lines * width,
@@ -475,7 +509,7 @@
         block_rows = up_to(experts * lines // rows, TILE)
         pairs = experts * rows
         compact = up_to(lines + 2 * (TILE - 1) * rows, TILE)
-        self.slot = min(STRAIGHT, block_rows // TILE)
+        self.slot = min(SLOT, block_rows // TILE)
         self.deep = up_to(max(compact, rows * self.slot * TILE), 256)
         self.shape = expert_lines.shape
         self.pieces = [(parts - 1, 1), (0, parts - 1)]

time: 253 us -> 254 us (level)
  local copies, waits for them, and re-layouts: 15.3 us -> 23.1 us
  Pallas kernels: 101 us -> 95.2 us
    unnamed x43 -> x47, local copies, waits for them, and re-layouts: 6.79 us -> 14.6 us
    pallas_call x2, Pallas kernels: 35.9 us -> 30.6 us  [unpack(): pl.pallas_call(functools.partial(unpack_kernel, slot, makes), grid_spec=p...]
  transfers between devices with their start and end apart: 19 -> 19, of which waited for: 7 -> 7; matrix products, arithmetic and copies ran while one was open for 10% -> 10% of each run, Pallas kernels for 25% -> 24%
where the time goes in v5:
time: 254 us; the launch traced here: 252 us
  Pallas kernels  95.2 us (37%)
  waiting for transfers between devices  86.2 us (34%)
  starting transfers between devices  32.6 us (13%)
  local copies, waits for them, and re-layouts  23.1 us (9%)
  matrix products  8.45 us (3%)
  other arithmetic  5.58 us (2%)
    ppermute x17, waiting for transfers between devices, from_peer(): return lax.ppermute(block, axis, [(i, i ^ offset) for i in range(size)])  86.2 us
    pallas_call x2, Pallas kernels, pack(): pl.pallas_call(functools.partial(pack_kernel, rows, span), grid_spec=pltp...  32.9 us
    pallas_call x2, Pallas kernels, unpack(): pl.pallas_call(functools.partial(unpack_kernel, slot, makes), grid_spec=p...  30.6 us
    ppermute x17, starting transfers between devices, from_peer(): return lax.ppermute(block, axis, [(i, i ^ offset) for i in range(size)])  21.8 us
    pallas_call x2, Pallas kernels, call_plan(): pl.pallas_call(kernel, out_shape=(place, jax.ShapeDtypeStruct((4, up_to(p...  16.6 us
    unnamed x47, local copies, waits for them, and re-layouts  14.6 us
    all_to_all x2, starting transfers between devices, send(): lax.all_to_all(block, 'row', split_axis=0, concat_axis=0, tiled=True)  10.8 us
    pallas_call x1, Pallas kernels, experts_part(): pl.pallas_call(gate_up_kernel, grid_spec=pltpu.PrefetchScalarGridSpec(num...  8.8 us
  transfers between devices with their start and end apart: 19, of which 7 were waited for; matrix products, arithmetic and copies ran while one was open for 10% of the time, Pallas kernels for 24%

profile of v5, /device:TPU:0, one launch (start us, length us, event | category | flops | bytes accessed | tf_op | source)
XLA Modules:
  0.0 252.4 jit_solution(16968856174273700316)
XLA Ops:
  2.4 5.7 %outgoing_plan.1 = (s32[8,1,768]{2,1,0:T(1,128)S(1)}, s32[4,128]{1,0:T(4,128)S(1)}) custom-call(s32[8,5632]{1,0:T(8,128)S(1)} %copy-done.6, s32[8,768]{1,0:T(8,128)S(1)} %pad.11.held_ref), custom_call_target="tpu_custom_call" | custom-call | flops 230686720 | bytes 360448 | tf_op jit(solution)/shard_map/outgoing_plan/pallas_call | solution.py:389
  9.3 11.7 %pack_lines.2.refs_1_ = bf16[8,1,704,512]{3,2,1,0:T(8,128)(2,1)} custom-call(s32[4,128]{1,0:T(4,128)} %copy-done.8, s32[8,1,768]{2,1,0:T(1,128)} %copy-done.5, bf16[8,3,704,512]{3,2,1,0:T(8,128)(2,1)} %bitcast.81), custom_call_target="tpu_custom_call" | custom-call | flops 5444206592 | bytes 11534336 | tf_op jit(solution)/shard_map/pack_lines/pallas_call | solution.py:404
  21.1 5.2 %all-to-all-start = ((bf16[8,1,704,512]{3,2,1,0:T(8,128)(2,1)}), bf16[8,1,704,512]{3,2,1,0:T(8,128)(2,1)}, u32[]{:S(2)}, u32[]{:S(2)}) async-start(bf16[8,1,704,512]{3,2,1,0:T(8,128)(2,1)} %pack_lines.2.refs_1_), calls=%async_computation | async-start | bytes 11534336 | tf_op jit(solution)/shard_map/all_to_all | solution.py:539
  26.2 1.7 fusion.30
  29.0 1.7 fusion.29
  30.9 1.2 copy.145
  32.7 2.0 fusion.33
  35.5 1.2 fusion.32
  41.8 4.8 %collective-permute-start.2 = (f32[8,4224]{1,0:T(8,128)S(1)}, f32[8,4224]{1,0:T(8,128)S(1)}, u32[]{:S(2)}, u32[]{:S(2)}) collective-permute-start(f32[8,4224]{1,0:T(8,128)S(1)} %concatenate.10), channel_id=1, source_target_pairs={{0,3},{1,2},{2,1},{3,0},{4,7},{5,6},{6,5},{7,4},{8,11},{9,10},{10,... | collective-permute-start | bytes 405512 | tf_op jit(solution)/shard_map/ppermute | solution.py:501
  47.3 21.2 %pack_lines.3.refs_2_.refs_0_ = bf16[8,2,704,512]{3,2,1,0:T(8,128)(2,1)} custom-call(s32[4,128]{1,0:T(4,128)} %copy-done.8, s32[8,1,768]{2,1,0:T(1,128)} %copy-done.5, bf16[8,3,704,512]{3,2,1,0:T(8,128)(2,1)} %bitcast.82), custom_call_target="tpu_custom_call" | custom-call | flops 10888413184 | bytes 23068672 | tf_op jit(solution)/shard_map/pack_lines/pallas_call | solution.py:404
  69.0 3.5 %fusion.4.refs_0_ = bf16[8,512]{1,0:T(8,128)(2,1)} fusion(bf16[4096,512]{1,0:T(8,128)(2,1)} %param.20, f32[8,4096]{1,0:T(8,128)S(1)} %fusion.8, f32[8,32]{0,1:T(8,128)S(1)} %copy.126, bf16[8,512]{1,0:T(8,128)(2,1)S(1)} %copy-done.12), kind=kOutput, calls=%fused_computation.9 | convolution fusion | flops 33632256 | bytes 4342784 | tf_op jit(solution)/shard_map/dot_general | solution.py:815
  72.5 1.7 collective-permute-start.3
  74.2 1.5 collective-permute-start.4
  76.7 15.2 %collective-permute-done.3 = bf16[8,512]{1,0:T(8,128)(2,1)S(1)} collective-permute-done((bf16[8,512]{1,0:T(8,128)(2,1)}, bf16[8,512]{1,0:T(8,128)(2,1)S(1)}, u32[]{:S(2)}, u32[]{:S(2)}) %collective-permute-start.3) | collective-permute-done | bytes 8224 | tf_op jit(solution)/shard_map/ppermute | solution.py:501
  93.6 1.2 collective-permute-done.6
  95.4 5.6 %all-to-all-start.1 = ((bf16[8,2,704,512]{3,2,1,0:T(8,128)(2,1)}), bf16[8,2,704,512]{3,2,1,0:T(8,128)(2,1)}, u32[]{:S(2)}, u32[]{:S(2)}) async-start(bf16[8,2,704,512]{3,2,1,0:T(8,128)(2,1)} %after.5), calls=%async_computation.1 | async-start | bytes 23068672 | tf_op jit(solution)/shard_map/all_to_all | solution.py:539
  102.2 8.8 %gate_up.1 = bf16[4,4,16,768]{3,2,1,0:T(8,128)(2,1)S(1)} custom-call(s32[1]{0:T(128)} %bitcast.20.me_ref, bf16[64,512]{1,0:T(8,128)(2,1)S(1)} %copy-done.4, bf16[1,512]{1,0:T(2,128)(2,1)S(1)} %reshape.90.gain_ref, bf16[512,128]{1,0:T(8,128)(2,1)S(1)} %pad.12.router_ref, s32[64,2]{1,0:T(8,128)S(1)} %bitcast.78, bf16[8,3,704,512]{3,2,1,0:T(8,128)(2,1)} %bitcast.83, ...), custom_call_target="tpu_custom_call" | custom-call | flops 738197504 | bytes 11534336 | tf_op jit(solution)/shard_map/gate_up/pallas_call | solution.py:740
  111.0 2.2 collective-permute-start.7
  113.3 2.6 %collective-permute-start.8 = (bf16[4,16,768]{2,1,0:T(8,128)(2,1)S(1)}, bf16[4,16,768]{2,1,0:T(8,128)(2,1)S(1)}, u32[]{:S(2)}, u32[]{:S(2)}) collective-permute-start(bf16[4,16,768]{2,1,0:T(8,128)(2,1)S(1)} %get-tuple-element.23), channel_id=1, source_target_pairs={{0,2},{1,3},{2,0},{3,1},{4,6},{5,7},{6,4},{7,5},{8,10},{9,11},{10,... | collective-permute-start | bytes 294920 | tf_op jit(solution)/shard_map/ppermute | solution.py:501
  116.4 7.6 %collective-permute-done.8.refs_2_ = bf16[4,16,768]{2,1,0:T(8,128)(2,1)S(1)} collective-permute-done((bf16[4,16,768]{2,1,0:T(8,128)(2,1)S(1)}, bf16[4,16,768]{2,1,0:T(8,128)(2,1)S(1)}, u32[]{:S(2)}, u32[]{:S(2)}) %collective-permute-start.8) | collective-permute-done | bytes 98336 | tf_op jit(solution)/shard_map/ppermute | solution.py:501
  124.1 1.8 collective-permute-start.10
  125.9 1.4 collective-permute-start.11
  127.3 1.2 collective-permute-start.12
  129.4 10.8 %incoming_plan.1 = (bf16[8,2,704,128]{3,2,1,0:T(8,128)(2,1)S(1)}, s32[4,128]{1,0:T(4,128)S(1)}) custom-call(s32[8,5632]{1,0:T(8,128)S(1)} %copy-done.7, s32[8,768]{1,0:T(8,128)S(1)} %pad.13.wanted_ref), custom_call_target="tpu_custom_call" | custom-call | flops 230686720 | bytes 360448 | tf_op jit(solution)/shard_map/incoming_plan/pallas_call | solution.py:389
  140.2 6.1 %down.1.refs_0_ = f32[64,512]{1,0:T(8,128)S(1)} custom-call(s32[1]{0:T(128)} %bitcast.20.me_ref, s32[64,2]{1,0:T(8,128)S(1)} %bitcast.80, bf16[2,16,768]{2,1,0:T(8,128)(2,1)S(1)} %activate.1.refs_0_, bf16[2,16,768]{2,1,0:T(8,128)(2,1)S(1)} %collective-permute-done.10.refs_1_, bf16[2,16,768]{2,1,0:T(8,128)(2,1)S(1)} %collective-permute-done.11.refs_2_, ...), custom_call_target="tpu_custom_call" | custom-call | flops 369098752 | bytes 5767168 | tf_op jit(solution)/shard_map/down/pallas_call | solution.py:767
  146.4 12.3 %unpack_lines.2 = (bf16[8,3,704,512]{3,2,1,0:T(8,128)(2,1)}, bf16[8,704,1024]{2,1,0:T(8,128)(2,1)S(1)}) custom-call(s32[4,128]{1,0:T(4,128)S(1)} %get-tuple-element.10.plan_ref, bf16[8,2,704,128]{3,2,1,0:T(8,128)(2,1)S(1)} %get-tuple-element.11.place_ref, bf16[8,1,704,512]{3,2,1,0:T(8,128)(2,1)} %all-to-all-done.block_ref), custom_call_target="tpu_custom_call" | custom-call | flops 5905580032 | bytes 11534336 | tf_op jit(solution)/shard_map/unpack_lines/pallas_call | solution.py:449
  158.7 4.2 %copy-done = bf16[8,704,1024]{2,1,0:T(8,128)(2,1)} copy-done((bf16[8,704,1024]{2,1,0:T(8,128)(2,1)}, bf16[8,704,1024]{2,1,0:T(8,128)(2,1)S(1)}, u32[]{:S(2)}) %copy-start) | copy-done | bytes 11534360
  163.8 1.3 collective-permute-done.13
  165.9 2.7 %collective-permute-start.16 = (f32[8,512]{1,0:T(8,128)S(1)}, f32[8,512]{1,0:T(8,128)S(1)}, u32[]{:S(2)}, u32[]{:S(2)}) collective-permute-start(f32[8,512]{1,0:T(8,128)S(1)} %get-tuple-element.27), channel_id=1, source_target_pairs={{0,24},{4,28},{8,16},{12,20},{16,8},{20,12},{24,0},{28,4},{1,25},{... | collective-permute-start | bytes 49160 | tf_op jit(solution)/shard_map/ppermute | solution.py:501
  169.4 59.6 %collective-permute-done.16 = f32[8,512]{1,0:T(8,128)S(1)} collective-permute-done((f32[8,512]{1,0:T(8,128)S(1)}, f32[8,512]{1,0:T(8,128)S(1)}, u32[]{:S(2)}, u32[]{:S(2)}) %collective-permute-start.16) | collective-permute-done | bytes 16416 | tf_op jit(solution)/shard_map/ppermute | solution.py:501
  229.7 4.3 %copy-done.1 = bf16[8,704,1024]{2,1,0:T(8,128)(2,1)S(1)} copy-done((bf16[8,704,1024]{2,1,0:T(8,128)(2,1)S(1)}, bf16[8,704,1024]{2,1,0:T(8,128)(2,1)}, u32[]{:S(2)}) %copy-start.1) | copy-done | bytes 11534360
  233.9 18.3 %unpack_lines.3 = bf16[8,3,704,512]{3,2,1,0:T(8,128)(2,1)} custom-call(s32[4,128]{1,0:T(4,128)S(1)} %get-tuple-element.10.plan_ref, bf16[8,704,1024]{2,1,0:T(8,128)(2,1)S(1)} %copy-done.1, bf16[8,2,704,512]{3,2,1,0:T(8,128)(2,1)} %all-to-all-done.1.block_ref, bf16[8,3,704,512]{3,2,1,0:T(8,128)(2,1)} %get-tuple-element.12.refs_1_.rest_0_), custom_call_target="tpu_custom_call", output_to_operand_aliasing={{}: (3, {})} | custom-call | flops 11811160064 | bytes 23068672 | tf_op jit(solution)/shard_map/unpack_lines/pallas_call | solution.py:449
  (116 shorter events, 20.9 us)
Async XLA Ops:
  21.1 74.4 %all-to-all-start = ((bf16[8,1,704,512]{3,2,1,0:T(8,128)(2,1)}), bf16[8,1,704,512]{3,2,1,0:T(8,128)(2,1)}, u32[]{:S(2)}, u32[]{:S(2)}) async-start(bf16[8,1,704,512]{3,2,1,0:T(8,128)(2,1)} %pack_lines.2.refs_1_), calls=%async_computation | async-start | bytes 11534336 | tf_op jit(solution)/shard_map/all_to_all | solution.py:539
  28.4 3.7 %copy-start.10 = (bf16[8,4096]{1,0:T(8,128)(2,1)S(1)}, bf16[8,4096]{1,0:T(8,128)(2,1)}, u32[]{:S(2)}) copy-start(bf16[8,4096]{1,0:T(8,128)(2,1)} %param.15) | copy-start | bytes 196612
  28.5 4.2 %copy-start.17 = (s32[8]{0:T(128)S(1)}, s32[8]{0:T(128)}, u32[]{:S(2)}) copy-start(s32[8]{0:T(128)} %param.19) | copy-start | bytes 100
  41.8 27.2 %copy-start.12 = (bf16[8,512]{1,0:T(8,128)(2,1)S(1)}, bf16[8,512]{1,0:T(8,128)(2,1)}, u32[]{:S(2)}) copy-start(bf16[8,512]{1,0:T(8,128)(2,1)} %param.14) | copy-start | bytes 24580
  41.8 26.6 %collective-permute-start.2 = (f32[8,4224]{1,0:T(8,128)S(1)}, f32[8,4224]{1,0:T(8,128)S(1)}, u32[]{:S(2)}, u32[]{:S(2)}) collective-permute-start(f32[8,4224]{1,0:T(8,128)S(1)} %concatenate.10), channel_id=1, source_target_pairs={{0,3},{1,2},{2,1},{3,0},{4,7},{5,6},{6,5},{7,4},{8,11},{9,10},{10,... | collective-permute-start | bytes 405512 | tf_op jit(solution)/shard_map/ppermute | solution.py:501
  46.6 21.8 %collective-permute-start.1 = (f32[8,4224]{1,0:T(8,128)S(1)}, f32[8,4224]{1,0:T(8,128)S(1)}, u32[]{:S(2)}, u32[]{:S(2)}) collective-permute-start(f32[8,4224]{1,0:T(8,128)S(1)} %concatenate.10), channel_id=1, source_target_pairs={{0,2},{1,3},{2,0},{3,1},{4,6},{5,7},{6,4},{7,5},{8,10},{9,11},{10,... | collective-permute-start | bytes 405512 | tf_op jit(solution)/shard_map/ppermute | solution.py:501
  46.6 21.8 %collective-permute-start = (f32[8,4224]{1,0:T(8,128)S(1)}, f32[8,4224]{1,0:T(8,128)S(1)}, u32[]{:S(2)}, u32[]{:S(2)}) collective-permute-start(f32[8,4224]{1,0:T(8,128)S(1)} %concatenate.10), channel_id=1, source_target_pairs={{0,1},{1,0},{2,3},{3,2},{4,5},{5,4},{6,7},{7,6},{8,9},{9,8},{10,11... | collective-permute-start | bytes 405512 | tf_op jit(solution)/shard_map/ppermute | solution.py:501
  72.5 19.4 %collective-permute-start.3 = (bf16[8,512]{1,0:T(8,128)(2,1)}, bf16[8,512]{1,0:T(8,128)(2,1)S(1)}, u32[]{:S(2)}, u32[]{:S(2)}) collective-permute-start(bf16[8,512]{1,0:T(8,128)(2,1)} %after.3), channel_id=1, source_target_pairs={{0,8},{4,12},{8,0},{12,4},{16,24},{20,28},{24,16},{28,20},{1,9},{5... | collective-permute-start | bytes 24584 | tf_op jit(solution)/shard_map/ppermute | solution.py:501
  74.2 17.7 %collective-permute-start.4 = (bf16[8,512]{1,0:T(8,128)(2,1)}, bf16[8,512]{1,0:T(8,128)(2,1)S(1)}, u32[]{:S(2)}, u32[]{:S(2)}) collective-permute-start(bf16[8,512]{1,0:T(8,128)(2,1)} %after.3), channel_id=1, source_target_pairs={{0,16},{4,20},{8,24},{12,28},{16,0},{20,4},{24,8},{28,12},{1,17},{... | collective-permute-start | bytes 24584 | tf_op jit(solution)/shard_map/ppermute | solution.py:501
  75.7 17.1 %collective-permute-start.5 = (bf16[8,512]{1,0:T(8,128)(2,1)}, bf16[8,512]{1,0:T(8,128)(2,1)S(1)}, u32[]{:S(2)}, u32[]{:S(2)}) collective-permute-start(bf16[8,512]{1,0:T(8,128)(2,1)} %after.3), channel_id=1, source_target_pairs={{0,24},{4,28},{8,16},{12,20},{16,8},{20,12},{24,0},{28,4},{1,25},{... | collective-permute-start | bytes 24584 | tf_op jit(solution)/shard_map/ppermute | solution.py:501
  93.6 1.2 collective-permute-start.6
  95.4 5.7 %copy-start.15 = (s32[64,2]{0,1:T(2,128)S(1)}, s32[64,2]{0,1:T(2,128)}, u32[]{:S(2)}) copy-start(s32[64,2]{0,1:T(2,128)} %param.26) | copy-start | bytes 1540
  95.4 5.8 %copy-start.18 = (s32[8]{0:T(128)S(1)}, s32[8]{0:T(128)}, u32[]{:S(2)}) copy-start(s32[8]{0:T(128)} %constant.41.clone) | copy-start | bytes 100
  95.4 6.5 %copy-start.16 = (bf16[512]{0:T(512)(128)(2,1)S(1)}, bf16[512]{0:T(512)(128)(2,1)}, u32[]{:S(2)}) copy-start(bf16[512]{0:T(512)(128)(2,1)} %param.21) | copy-start | bytes 3076
  95.4 6.5 %copy-start.13 = (bf16[512,8]{0,1:T(8,128)(2,1)S(1)}, bf16[512,8]{0,1:T(8,128)(2,1)}, u32[]{:S(2)}) copy-start(bf16[512,8]{0,1:T(8,128)(2,1)} %param.22) | copy-start | bytes 24580
  95.4 6.8 %copy-start.4 = (bf16[64,512]{1,0:T(8,128)(2,1)S(1)}, bf16[64,512]{1,0:T(8,128)(2,1)}, u32[]{:S(2)}) copy-start(bf16[64,512]{1,0:T(8,128)(2,1)} %copy-done.3) | copy-start | bytes 196612
  95.4 134.2 %all-to-all-start.1 = ((bf16[8,2,704,512]{3,2,1,0:T(8,128)(2,1)}), bf16[8,2,704,512]{3,2,1,0:T(8,128)(2,1)}, u32[]{:S(2)}, u32[]{:S(2)}) async-start(bf16[8,2,704,512]{3,2,1,0:T(8,128)(2,1)} %after.5), calls=%async_computation.1 | async-start | bytes 23068672 | tf_op jit(solution)/shard_map/all_to_all | solution.py:539
  102.2 27.2 %copy-start.7 = (s32[8,5632]{1,0:T(8,128)S(1)}, s32[8,5632]{1,0:T(8,128)}, u32[]{:S(2)}) copy-start(s32[8,5632]{1,0:T(8,128)} %old_ref.1) | copy-start | bytes 540676
  111.0 5.3 %collective-permute-start.7 = (bf16[4,16,768]{2,1,0:T(8,128)(2,1)S(1)}, bf16[4,16,768]{2,1,0:T(8,128)(2,1)S(1)}, u32[]{:S(2)}, u32[]{:S(2)}) collective-permute-start(bf16[4,16,768]{2,1,0:T(8,128)(2,1)S(1)} %get-tuple-element.24), channel_id=1, source_target_pairs={{0,1},{1,0},{2,3},{3,2},{4,5},{5,4},{6,7},{7,6},{8,9},{9,8},{10,11... | collective-permute-start | bytes 294920 | tf_op jit(solution)/shard_map/ppermute | solution.py:501
  113.3 10.7 %collective-permute-start.8 = (bf16[4,16,768]{2,1,0:T(8,128)(2,1)S(1)}, bf16[4,16,768]{2,1,0:T(8,128)(2,1)S(1)}, u32[]{:S(2)}, u32[]{:S(2)}) collective-permute-start(bf16[4,16,768]{2,1,0:T(8,128)(2,1)S(1)} %get-tuple-element.23), channel_id=1, source_target_pairs={{0,2},{1,3},{2,0},{3,1},{4,6},{5,7},{6,4},{7,5},{8,10},{9,11},{10,... | collective-permute-start | bytes 294920 | tf_op jit(solution)/shard_map/ppermute | solution.py:501
  115.9 8.0 %collective-permute-start.9 = (bf16[4,16,768]{2,1,0:T(8,128)(2,1)S(1)}, bf16[4,16,768]{2,1,0:T(8,128)(2,1)S(1)}, u32[]{:S(2)}, u32[]{:S(2)}) collective-permute-start(bf16[4,16,768]{2,1,0:T(8,128)(2,1)S(1)} %get-tuple-element.22), channel_id=1, source_target_pairs={{0,3},{1,2},{2,1},{3,0},{4,7},{5,6},{6,5},{7,4},{8,11},{9,10},{10,... | collective-permute-start | bytes 294920 | tf_op jit(solution)/shard_map/ppermute | solution.py:501
  124.1 16.1 %collective-permute-start.10 = (bf16[2,16,768]{2,1,0:T(8,128)(2,1)S(1)}, bf16[2,16,768]{2,1,0:T(8,128)(2,1)S(1)}, u32[]{:S(2)}, u32[]{:S(2)}) collective-permute-start(bf16[2,16,768]{2,1,0:T(8,128)(2,1)S(1)} %activate.1.refs_0_), channel_id=1, source_target_pairs={{0,1},{1,0},{2,3},{3,2},{4,5},{5,4},{6,7},{7,6},{8,9},{9,8},{10,11... | collective-permute-start | bytes 147464 | tf_op jit(solution)/shard_map/ppermute | solution.py:501
  125.9 14.3 %collective-permute-start.11 = (bf16[2,16,768]{2,1,0:T(8,128)(2,1)S(1)}, bf16[2,16,768]{2,1,0:T(8,128)(2,1)S(1)}, u32[]{:S(2)}, u32[]{:S(2)}) collective-permute-start(bf16[2,16,768]{2,1,0:T(8,128)(2,1)S(1)} %activate.1.refs_0_), channel_id=1, source_target_pairs={{0,2},{1,3},{2,0},{3,1},{4,6},{5,7},{6,4},{7,5},{8,10},{9,11},{10,... | collective-permute-start | bytes 147464 | tf_op jit(solution)/shard_map/ppermute | solution.py:501
  127.3 12.9 %collective-permute-start.12 = (bf16[2,16,768]{2,1,0:T(8,128)(2,1)S(1)}, bf16[2,16,768]{2,1,0:T(8,128)(2,1)S(1)}, u32[]{:S(2)}, u32[]{:S(2)}) collective-permute-start(bf16[2,16,768]{2,1,0:T(8,128)(2,1)S(1)} %activate.1.refs_0_), channel_id=1, source_target_pairs={{0,3},{1,2},{2,1},{3,0},{4,7},{5,6},{6,5},{7,4},{8,11},{9,10},{10,... | collective-permute-start | bytes 147464 | tf_op jit(solution)/shard_map/ppermute | solution.py:501
  146.4 12.3 %copy-start.2 = (f32[64,512]{1,0:T(8,128)}, f32[64,512]{1,0:T(8,128)S(1)}, u32[]{:S(2)}) copy-start(f32[64,512]{1,0:T(8,128)S(1)} %down.1.refs_0_) | copy-start | bytes 393220
  158.7 4.2 %copy-start = (bf16[8,704,1024]{2,1,0:T(8,128)(2,1)}, bf16[8,704,1024]{2,1,0:T(8,128)(2,1)S(1)}, u32[]{:S(2)}) copy-start(bf16[8,704,1024]{2,1,0:T(8,128)(2,1)S(1)} %get-tuple-element.13.place_ref) | copy-start | bytes 34603012
  162.9 66.1 %copy-start.9 = (bf16[8,512]{1,0:T(8,128)(2,1)S(1)}, bf16[8,512]{1,0:T(8,128)(2,1)}, u32[]{:S(2)}) copy-start(bf16[8,512]{1,0:T(8,128)(2,1)} %after.3) | copy-start | bytes 24580
  163.8 1.3 collective-permute-start.13
  165.9 63.1 %collective-permute-start.16 = (f32[8,512]{1,0:T(8,128)S(1)}, f32[8,512]{1,0:T(8,128)S(1)}, u32[]{:S(2)}, u32[]{:S(2)}) collective-permute-start(f32[8,512]{1,0:T(8,128)S(1)} %get-tuple-element.27), channel_id=1, source_target_pairs={{0,24},{4,28},{8,16},{12,20},{16,8},{20,12},{24,0},{28,4},{1,25},{... | collective-permute-start | bytes 49160 | tf_op jit(solution)/shard_map/ppermute | solution.py:501
  168.5 60.5 %collective-permute-start.15 = (f32[8,512]{1,0:T(8,128)S(1)}, f32[8,512]{1,0:T(8,128)S(1)}, u32[]{:S(2)}, u32[]{:S(2)}) collective-permute-start(f32[8,512]{1,0:T(8,128)S(1)} %get-tuple-element.28), channel_id=1, source_target_pairs={{0,16},{4,20},{8,24},{12,28},{16,0},{20,4},{24,8},{28,12},{1,17},{... | collective-permute-start | bytes 49160 | tf_op jit(solution)/shard_map/ppermute | solution.py:501
  169.1 59.9 %collective-permute-start.14 = (f32[8,512]{1,0:T(8,128)S(1)}, f32[8,512]{1,0:T(8,128)S(1)}, u32[]{:S(2)}, u32[]{:S(2)}) collective-permute-start(f32[8,512]{1,0:T(8,128)S(1)} %get-tuple-element.26), channel_id=1, source_target_pairs={{0,8},{4,12},{8,0},{12,4},{16,24},{20,28},{24,16},{28,20},{1,9},{5... | collective-permute-start | bytes 49160 | tf_op jit(solution)/shard_map/ppermute | solution.py:501
  229.7 4.3 %copy-start.1 = (bf16[8,704,1024]{2,1,0:T(8,128)(2,1)S(1)}, bf16[8,704,1024]{2,1,0:T(8,128)(2,1)}, u32[]{:S(2)}) copy-start(bf16[8,704,1024]{2,1,0:T(8,128)(2,1)} %copy-done) | copy-start | bytes 34603012
  (6 other events, 9.2 us)

commit v6 on v5

--- a/solution.py
+++ b/solution.py
@@ -17,7 +17,6 @@
 neg_big = -1e30
 VMEM_LIMIT = 48 * 1024 * 1024
 PACK_LIMIT = 61 * 1024 * 1024
-UNPACK_LIMIT = 24 * 1024 * 1024
 
 
 def up_to(value, unit):
@@ -298,15 +297,14 @@
             copy.wait()
 
 
-def unpack_kernel(slot, makes, plan_ref, place_ref, block_ref, *rest):
-    stage_ref, sems = rest[-2:]
-    out_ref = rest[-4] if makes else rest[-3]
-    experts = pl.num_programs(0)
+def unpack_kernel(slot, span, plan_ref, place_ref, block_ref, *rest):
+    out_ref, stage_ref, sems = rest[-3:]
+    step = pl.program_id(0)
+    steps = pl.num_programs(0)
     rows, count, _, width = block_ref.shape
-    _, deep, _ = stage_ref.shape
+    deep = stage_ref.shape[3]
     lines = out_ref.shape[2]
-    e = pl.program_id(0)
-    buffer = e % 2
+    buffer = step % 2
 
     def entry(n, e, s):
         return plan_ref[n, e * rows + s]
@@ -314,75 +312,68 @@
     def slotted(e):
         return entry(3, e, 0) > 0
 
-    def columns(part):
-        return pl.ds(part * width, width)
-
-    def slot_copies(e):
-        for s in range(rows):
-            there = pl.ds(pl.multiple_of(entry(0, e, s) * TILE, TILE), slot * TILE)
-            here = pl.ds(s * slot * TILE, slot * TILE)
-            for part in range(count):
-                yield pltpu.make_async_copy(
-                    block_ref.at[s, part, there],
-                    stage_ref.at[e % 2, here, columns(part)],
-                    sems.at[e % 2, s * count + part],
-                )
-
-    def begin(e):
-        @pl.when(slotted(e))
-        def _():
-            for copy in slot_copies(e):
-                copy.start()
-
-    @pl.when(e == 0)
+    def begin(step):
+        for j in range(span):
+            e = step * span + j
+
+            @pl.when(slotted(e))
+            def _(e=e, j=j):
+                for s in range(rows):
+                    there = pl.ds(pl.multiple_of(entry(0, e, s) * TILE, TILE), slot * TILE)
+                    here = pl.ds(s * slot * TILE, slot * TILE)
+                    pltpu.make_async_copy(
+                        block_ref.at[s, :, there],
+                        stage_ref.at[step % 2, j, :, here],
+                        sems.at[step % 2, j],
+                    ).start()
+
+    @pl.when(step == 0)
     def _():
         stage_ref[...] = jnp.zeros_like(stage_ref)
-        begin(e)
-
-    @pl.when(e + 1 < experts)
+        begin(step)
+
+    @pl.when(step + 1 < steps)
     def _():
-        begin(e + 1)
-
-    @pl.when(slotted(e))
-    def _():
-        for copy in slot_copies(e):
-            copy.wait()
-
-    @pl.when(jnp.logical_not(slotted(e)))
-    def _():
-        def one_peer(s, carry):
-            def put(t, c):
-                for part in range(count):
+        begin(step + 1)
+
+    for j in range(span):
+        e = step * span + j
+
+        @pl.when(slotted(e))
+        def _(j=j):
+            all_slots = stage_ref.at[buffer, j, :, pl.ds(0, rows * slot * TILE)]
+            pltpu.make_async_copy(all_slots, all_slots, sems.at[buffer, j]).wait()
+
+        @pl.when(jnp.logical_not(slotted(e)))
+        def _(e=e, j=j):
+            def one_peer(s, carry):
+                def put(t, c):
                     copy = pltpu.make_async_copy(
-                        block_ref.at[s, part, tile_at(entry(0, e, s) + t)],
-                        stage_ref.at[buffer, tile_at(entry(2, e, s) + t), columns(part)],
-                        sems.at[buffer, part],
+                        block_ref.at[s, :, tile_at(entry(0, e, s) + t)],
+                        stage_ref.at[buffer, j, :, tile_at(entry(2, e, s) + t)],
+                        sems.at[buffer, j],
                     )
                     copy.start()
                     copy.wait()
-                return c
-
-            return lax.fori_loop(0, entry(1, e, s), put, carry)
-
-        lax.fori_loop(0, rows, one_peer, 0)
-
-    if makes:
-        onehot_ref = rest[-3]
-        within_block, block = place_ref[0, 0], place_ref[0, 1]
-        lane = counting((lines, LANES), 1)
+                    return c
+
+                return lax.fori_loop(0, entry(1, e, s), put, carry)
+
+            lax.fori_loop(0, rows, one_peer, 0)
+
+    lane = counting((lines, LANES), 1)
+    for j in range(span):
+        within_block, block = place_ref[j, 0], place_ref[j, 1]
+        pieces = []
         for first in range(0, deep, LANES):
             away = jnp.abs(block - jnp.asarray(first // 256, jnp.bfloat16))
             place = within_block + away * jnp.asarray(512, jnp.bfloat16)
-            onehot_ref[0, :, first : first + LANES] = equal_ones(
-                lane + jnp.asarray(first % 256, jnp.bfloat16), place
-            )
-    else:
-        onehot_ref = place_ref
-    moved = jnp.dot(
-        onehot_ref[0], stage_ref[buffer], preferred_element_type=jnp.float32
-    ).astype(jnp.bfloat16)
-    for part in range(count):
-        out_ref[0, part] = moved[:, part * width : (part + 1) * width]
+            pieces.append(equal_ones(lane + jnp.asarray(first % 256, jnp.bfloat16), place))
+        onehot = jnp.concatenate(pieces, axis=1)
+        for part in range(count):
+            out_ref[j, part] = jnp.dot(
+                onehot, stage_ref[buffer, j, part], preferred_element_type=jnp.float32
+            ).astype(jnp.bfloat16)
 
 
 def call_plan(kernel, name, table, ids, pairs, place):
@@ -432,12 +423,9 @@
 def unpack(arrived, place, plan, piece, shape, deep, slot, previous):
     experts, _, lines, width = shape
     first, count = piece
-    rows = arrived.shape[0]
-    makes = previous is None
-    onehot_spec = pl.BlockSpec((1, lines, deep), lambda e, plan: (e, 0, 0))
-    place_spec = pl.BlockSpec((1, 2, lines, LANES), lambda e, plan: (e, 0, 0, 0))
+    span = 2 - experts % 2
     in_specs = [
-        place_spec if makes else onehot_spec,
+        pl.BlockSpec((span, 2, lines, LANES), lambda e, plan: (e, 0, 0, 0)),
         pl.BlockSpec(memory_space=pl.ANY),
     ]
     operands = [plan, place, arrived]
@@ -447,24 +435,22 @@
         operands.append(previous)
         aliases = {3: 0}
     return pl.pallas_call(
-        functools.partial(unpack_kernel, slot, makes),
+        functools.partial(unpack_kernel, slot, span),
         grid_spec=pltpu.PrefetchScalarGridSpec(
             num_scalar_prefetch=1,
-            grid=(experts,),
+            grid=(experts // span,),
             in_specs=in_specs,
-            out_specs=[
-                pl.BlockSpec((1, count, lines, width), lambda e, plan: (e, first // count, 0, 0))
-            ]
-            + [onehot_spec] * makes,
+            out_specs=pl.BlockSpec(
+                (span, count, lines, width), lambda e, plan: (e, first // count, 0, 0)
+            ),
             scratch_shapes=[
-                pltpu.VMEM((2, deep, count * width), jnp.bfloat16),
-                pltpu.SemaphoreType.DMA((2, rows * count)),
+                pltpu.VMEM((2, span, count, deep, width), jnp.bfloat16),
+                pltpu.SemaphoreType.DMA((2, span)),
             ],
         ),
-        out_shape=[jax.ShapeDtypeStruct(shape, jnp.bfloat16)]
-        + [jax.ShapeDtypeStruct((experts, lines, deep), jnp.bfloat16)] * makes,
+        out_shape=jax.ShapeDtypeStruct(shape, jnp.bfloat16),
         input_output_aliases=aliases,
-        compiler_params=pltpu.CompilerParams(vmem_limit_bytes=UNPACK_LIMIT),
+        compiler_params=params(),
         cost_estimate=pl.CostEstimate(
             flops=2 * count * experts * deep * lines * width,
             bytes_accessed=4 * count * experts * lines * width,
@@ -540,12 +526,10 @@
         )
 
     def receive(self, piece):
-        self.moved, *onehots = unpack(
+        self.moved = unpack(
             self.arrived[piece], self.in_place, self.in_plan, self.pieces[piece], self.shape,
             self.deep, self.slot, self.moved,
         )
-        if onehots:
-            (self.in_place,) = onehots
 
 
 def attend(queries, new_kv, prompt_kv, suffix_kv, lengths):
@@ -733,7 +717,7 @@
         [h_mid] + [from_peer(h_mid, "row", o) for o in range(2, rows, 2)], axis=0
     )
     every_h = jnp.concatenate([same_core, from_peer(same_core, "row", 1)], axis=0)
-    migration.send([every_h])
+    migration.send([same_core])
     part_spec = lambda part: pl.BlockSpec((1, 1, lines, width), lambda e, me: (e, part, 0, 0))
     whole = lambda a: pl.BlockSpec(a.shape, lambda e, me: (0,) * a.ndim)
     gain = moe_gain.reshape(1, width)

time: 254 us -> 248 us (0.976)
  local copies, waits for them, and re-layouts: 23.1 us -> 15.4 us
  waiting for transfers between devices: 86.2 us -> 88.8 us
    unnamed x47 -> x49, local copies, waits for them, and re-layouts: 14.6 us -> 8.98 us
    ppermute x17, waiting for transfers between devices: 86.2 us -> 88.8 us  [from_peer(): return lax.ppermute(block, axis, [(i, i ^ offset) for i in range(size)])]
  transfers between devices with their start and end apart: 19 -> 19, of which waited for: 7 -> 8; matrix products, arithmetic and copies ran while one was open for 10% -> 10% of each run, Pallas kernels for 24% -> 24%
where the time goes in v6:
time: 248 us; the launch traced here: 247 us
  Pallas kernels  93.4 us (38%)
  waiting for transfers between devices  88.8 us (36%)
  starting transfers between devices  33 us (13%)
  local copies, waits for them, and re-layouts  15.4 us (6%)
  matrix products  8.48 us (3%)
  other arithmetic  6.18 us (2%)
    ppermute x17, waiting for transfers between devices, from_peer(): return lax.ppermute(block, axis, [(i, i ^ offset) for i in range(size)])  88.8 us
    pallas_call x2, Pallas kernels, pack(): pl.pallas_call(functools.partial(pack_kernel, rows, span), grid_spec=pltp...  33 us
    pallas_call x2, Pallas kernels, unpack(): pl.pallas_call(functools.partial(unpack_kernel, slot, span), grid_spec=pl...  28.7 us
    ppermute x17, starting transfers between devices, from_peer(): return lax.ppermute(block, axis, [(i, i ^ offset) for i in range(size)])  22.1 us
    pallas_call x2, Pallas kernels, call_plan(): pl.pallas_call(kernel, out_shape=(place, jax.ShapeDtypeStruct((4, up_to(p...  16.6 us
    all_to_all x2, starting transfers between devices, send(): lax.all_to_all(block, 'row', split_axis=0, concat_axis=0, tiled=True)  10.9 us
    unnamed x49, local copies, waits for them, and re-layouts  8.98 us
    pallas_call x1, Pallas kernels, experts_part(): pl.pallas_call(gate_up_kernel, grid_spec=pltpu.PrefetchScalarGridSpec(num...  8.79 us
  transfers between devices with their start and end apart: 19, of which 8 were waited for; matrix products, arithmetic and copies ran while one was open for 10% of the time, Pallas kernels for 24%

profile of v6, /device:TPU:0, one launch (start us, length us, event | category | flops | bytes accessed | tf_op | source)
XLA Modules:
  0.0 246.6 jit_solution(16513236247647711335)
XLA Ops:
  2.4 5.7 %outgoing_plan.1 = (s32[8,1,768]{2,1,0:T(1,128)S(1)}, s32[4,128]{1,0:T(4,128)S(1)}) custom-call(s32[8,5632]{1,0:T(8,128)S(1)} %copy-done.2, s32[8,768]{1,0:T(8,128)S(1)} %pad.11.held_ref), custom_call_target="tpu_custom_call" | custom-call | flops 230686720 | bytes 360448 | tf_op jit(solution)/shard_map/outgoing_plan/pallas_call | solution.py:380
  9.3 11.8 %pack_lines.2.refs_1_ = bf16[8,1,704,512]{3,2,1,0:T(8,128)(2,1)} custom-call(s32[4,128]{1,0:T(4,128)} %copy-done.4, s32[8,1,768]{2,1,0:T(1,128)} %copy-done.1, bf16[8,3,704,512]{3,2,1,0:T(8,128)(2,1)} %bitcast.81), custom_call_target="tpu_custom_call" | custom-call | flops 5444206592 | bytes 11534336 | tf_op jit(solution)/shard_map/pack_lines/pallas_call | solution.py:395
  21.1 5.3 %all-to-all-start = ((bf16[8,1,704,512]{3,2,1,0:T(8,128)(2,1)}), bf16[8,1,704,512]{3,2,1,0:T(8,128)(2,1)}, u32[]{:S(2)}, u32[]{:S(2)}) async-start(bf16[8,1,704,512]{3,2,1,0:T(8,128)(2,1)} %pack_lines.2.refs_1_), calls=%async_computation | async-start | bytes 11534336 | tf_op jit(solution)/shard_map/all_to_all | solution.py:525
  28.9 1.3 copy.144
  30.2 1.5 copy.143
  31.7 1.2 copy.146
  32.9 1.2 copy.145
  34.4 2.0 fusion.33
  37.2 1.2 fusion.32
  43.5 4.8 %collective-permute-start.2 = (f32[8,4224]{1,0:T(8,128)S(1)}, f32[8,4224]{1,0:T(8,128)S(1)}, u32[]{:S(2)}, u32[]{:S(2)}) collective-permute-start(f32[8,4224]{1,0:T(8,128)S(1)} %concatenate.10), channel_id=1, source_target_pairs={{0,3},{1,2},{2,1},{3,0},{4,7},{5,6},{6,5},{7,4},{8,11},{9,10},{10,... | collective-permute-start | bytes 405512 | tf_op jit(solution)/shard_map/ppermute | solution.py:487
  49.0 21.2 %pack_lines.3.refs_2_.refs_0_ = bf16[8,2,704,512]{3,2,1,0:T(8,128)(2,1)} custom-call(s32[4,128]{1,0:T(4,128)} %copy-done.4, s32[8,1,768]{2,1,0:T(1,128)} %copy-done.1, bf16[8,3,704,512]{3,2,1,0:T(8,128)(2,1)} %bitcast.82), custom_call_target="tpu_custom_call" | custom-call | flops 10888413184 | bytes 23068672 | tf_op jit(solution)/shard_map/pack_lines/pallas_call | solution.py:395
  70.7 3.5 %fusion.4.refs_0_ = bf16[8,512]{1,0:T(8,128)(2,1)} fusion(bf16[4096,512]{1,0:T(8,128)(2,1)} %param.20, f32[8,4096]{1,0:T(8,128)S(1)} %fusion.8, f32[8,32]{0,1:T(8,128)S(1)} %copy.126, bf16[8,512]{1,0:T(8,128)(2,1)S(1)} %copy-done.13), kind=kOutput, calls=%fused_computation.9 | convolution fusion | flops 33632256 | bytes 4342784 | tf_op jit(solution)/shard_map/dot_general | solution.py:799
  74.2 1.7 collective-permute-start.3
  75.9 1.5 collective-permute-start.4
  77.7 14.3 %collective-permute-done.3 = bf16[8,512]{1,0:T(8,128)(2,1)S(1)} collective-permute-done((bf16[8,512]{1,0:T(8,128)(2,1)}, bf16[8,512]{1,0:T(8,128)(2,1)S(1)}, u32[]{:S(2)}, u32[]{:S(2)}) %collective-permute-start.3) | collective-permute-done | bytes 8224 | tf_op jit(solution)/shard_map/ppermute | solution.py:487
  93.0 1.3 pad_maximum_fusion.1.refs_1_
  94.4 5.6 %all-to-all-start.1 = ((bf16[8,2,704,512]{3,2,1,0:T(8,128)(2,1)}), bf16[8,2,704,512]{3,2,1,0:T(8,128)(2,1)}, u32[]{:S(2)}, u32[]{:S(2)}) async-start(bf16[8,2,704,512]{3,2,1,0:T(8,128)(2,1)} %after.5), calls=%async_computation.1 | async-start | bytes 23068672 | tf_op jit(solution)/shard_map/all_to_all | solution.py:525
  101.4 1.5 collective-permute-done.6
  102.9 8.8 %gate_up.1 = bf16[4,4,16,768]{3,2,1,0:T(8,128)(2,1)S(1)} custom-call(s32[1]{0:T(128)} %bitcast.20.me_ref, bf16[64,512]{1,0:T(8,128)(2,1)S(1)} %constant_dynamic-update-slice_fusion.h_ref, bf16[1,512]{1,0:T(2,128)(2,1)S(1)} %reshape.90.gain_ref, bf16[512,128]{1,0:T(8,128)(2,1)S(1)} %pad.12.router_ref, s32[64,2]{1,0:T(8,128)S(1)} %bitcast.78, ...), custom_call_target="tpu_custom_call" | custom-call | flops 738197504 | bytes 11534336 | tf_op jit(solution)/shard_map/gate_up/pallas_call | solution.py:724
  111.7 2.3 collective-permute-start.7
  114.0 2.6 %collective-permute-start.8 = (bf16[4,16,768]{2,1,0:T(8,128)(2,1)S(1)}, bf16[4,16,768]{2,1,0:T(8,128)(2,1)S(1)}, u32[]{:S(2)}, u32[]{:S(2)}) collective-permute-start(bf16[4,16,768]{2,1,0:T(8,128)(2,1)S(1)} %get-tuple-element.19), channel_id=1, source_target_pairs={{0,2},{1,3},{2,0},{3,1},{4,6},{5,7},{6,4},{7,5},{8,10},{9,11},{10,... | collective-permute-start | bytes 294920 | tf_op jit(solution)/shard_map/ppermute | solution.py:487
  117.3 7.4 %collective-permute-done.8.refs_2_ = bf16[4,16,768]{2,1,0:T(8,128)(2,1)S(1)} collective-permute-done((bf16[4,16,768]{2,1,0:T(8,128)(2,1)S(1)}, bf16[4,16,768]{2,1,0:T(8,128)(2,1)S(1)}, u32[]{:S(2)}, u32[]{:S(2)}) %collective-permute-start.8) | collective-permute-done | bytes 98336 | tf_op jit(solution)/shard_map/ppermute | solution.py:487
  124.8 2.0 collective-permute-start.10
  126.8 1.3 collective-permute-start.11
  128.1 1.2 collective-permute-start.12
  130.2 10.8 %incoming_plan.1 = (bf16[8,2,704,128]{3,2,1,0:T(8,128)(2,1)S(1)}, s32[4,128]{1,0:T(4,128)S(1)}) custom-call(s32[8,5632]{1,0:T(8,128)S(1)} %copy-done.3, s32[8,768]{1,0:T(8,128)S(1)} %pad.13.wanted_ref), custom_call_target="tpu_custom_call" | custom-call | flops 230686720 | bytes 360448 | tf_op jit(solution)/shard_map/incoming_plan/pallas_call | solution.py:380
  141.0 6.1 %down.1.refs_0_ = f32[64,512]{1,0:T(8,128)S(1)} custom-call(s32[1]{0:T(128)} %bitcast.20.me_ref, s32[64,2]{1,0:T(8,128)S(1)} %bitcast.80, bf16[2,16,768]{2,1,0:T(8,128)(2,1)S(1)} %activate.1.refs_0_, bf16[2,16,768]{2,1,0:T(8,128)(2,1)S(1)} %collective-permute-done.10.refs_1_, bf16[2,16,768]{2,1,0:T(8,128)(2,1)S(1)} %collective-permute-done.11.refs_2_, ...), custom_call_target="tpu_custom_call" | custom-call | flops 369098752 | bytes 5767168 | tf_op jit(solution)/shard_map/down/pallas_call | solution.py:751
  147.8 10.9 %unpack_lines.2.refs_1_.rest_0_ = bf16[8,3,704,512]{3,2,1,0:T(8,128)(2,1)} custom-call(s32[4,128]{1,0:T(4,128)S(1)} %get-tuple-element.8.plan_ref, bf16[8,2,704,128]{3,2,1,0:T(8,128)(2,1)S(1)} %get-tuple-element.9.place_ref, bf16[8,1,704,512]{3,2,1,0:T(8,128)(2,1)} %all-to-all-done.block_ref), custom_call_target="tpu_custom_call" | custom-call | flops 5905580032 | bytes 11534336 | tf_op jit(solution)/shard_map/unpack_lines/pallas_call | solution.py:437
  159.6 1.3 collective-permute-done.13
  161.7 2.7 %collective-permute-start.16 = (f32[8,512]{1,0:T(8,128)S(1)}, f32[8,512]{1,0:T(8,128)S(1)}, u32[]{:S(2)}, u32[]{:S(2)}) collective-permute-start(f32[8,512]{1,0:T(8,128)S(1)} %get-tuple-element.23), channel_id=1, source_target_pairs={{0,24},{4,28},{8,16},{12,20},{16,8},{20,12},{24,0},{28,4},{1,25},{... | collective-permute-start | bytes 49160 | tf_op jit(solution)/shard_map/ppermute | solution.py:487
  165.3 62.7 %collective-permute-done.16 = f32[8,512]{1,0:T(8,128)S(1)} collective-permute-done((f32[8,512]{1,0:T(8,128)S(1)}, f32[8,512]{1,0:T(8,128)S(1)}, u32[]{:S(2)}, u32[]{:S(2)}) %collective-permute-start.16) | collective-permute-done | bytes 16416 | tf_op jit(solution)/shard_map/ppermute | solution.py:487
  228.6 17.8 %unpack_lines.3 = bf16[8,3,704,512]{3,2,1,0:T(8,128)(2,1)} custom-call(s32[4,128]{1,0:T(4,128)S(1)} %get-tuple-element.8.plan_ref, bf16[8,2,704,128]{3,2,1,0:T(8,128)(2,1)S(1)} %get-tuple-element.9.place_ref, bf16[8,2,704,512]{3,2,1,0:T(8,128)(2,1)} %all-to-all-done.1.block_ref, ...), custom_call_target="tpu_custom_call", output_to_operand_aliasing={{}: (3, {})} | custom-call | flops 11811160064 | bytes 23068672 | tf_op jit(solution)/shard_map/unpack_lines/pallas_call | solution.py:437
  (118 shorter events, 20.7 us)
Async XLA Ops:
  21.1 5.3 %copy-start.5 = (bf16[1,2,256,2048]{3,2,1,0:T(8,128)(2,1)S(1)}, bf16[1,2,256,2048]{3,2,1,0:T(8,128)(2,1)}, u32[]{:S(2)}) copy-start(bf16[1,2,256,2048]{3,2,1,0:T(8,128)(2,1)} %param.17) | copy-start | bytes 6291460
  21.1 73.2 %all-to-all-start = ((bf16[8,1,704,512]{3,2,1,0:T(8,128)(2,1)}), bf16[8,1,704,512]{3,2,1,0:T(8,128)(2,1)}, u32[]{:S(2)}, u32[]{:S(2)}) async-start(bf16[8,1,704,512]{3,2,1,0:T(8,128)(2,1)} %pack_lines.2.refs_1_), calls=%async_computation | async-start | bytes 11534336 | tf_op jit(solution)/shard_map/all_to_all | solution.py:525
  28.8 5.4 %copy-start.18 = (s32[8]{0:T(128)S(1)}, s32[8]{0:T(128)}, u32[]{:S(2)}) copy-start(s32[8]{0:T(128)} %param.19) | copy-start | bytes 100
  32.9 10.1 %copy-start.7 = (bf16[1,1,256,2048]{2,3,1,0:T(8,128)(2,1)S(1)}, bf16[1,1,256,2048]{2,3,1,0:T(8,128)(2,1)}, u32[]{:S(2)}) copy-start(bf16[1,1,256,2048]{2,3,1,0:T(8,128)(2,1)} %copy.144) | copy-start | bytes 3145732
  34.1 7.8 %copy-start.8 = (bf16[32,8,16,128]{3,2,1,0:T(8,128)(2,1)S(1)}, bf16[32,8,16,128]{3,2,1,0:T(8,128)(2,1)}, u32[]{:S(2)}) copy-start(bf16[32,8,16,128]{3,2,1,0:T(8,128)(2,1)} %copy.146) | copy-start | bytes 3145732
  34.4 2.8 %copy-start.15 = (pred[8,32]{1,0:T(8,128)(4,1)}, pred[8,32]{1,0:T(8,128)(4,1)S(1)}, u32[]{:S(2)}) copy-start(pred[8,32]{1,0:T(8,128)(4,1)S(1)} %broadcast_compare_fusion) | copy-start | bytes 772
  43.5 27.2 %copy-start.13 = (bf16[8,512]{1,0:T(8,128)(2,1)S(1)}, bf16[8,512]{1,0:T(8,128)(2,1)}, u32[]{:S(2)}) copy-start(bf16[8,512]{1,0:T(8,128)(2,1)} %param.14) | copy-start | bytes 24580
  43.5 26.7 %collective-permute-start.2 = (f32[8,4224]{1,0:T(8,128)S(1)}, f32[8,4224]{1,0:T(8,128)S(1)}, u32[]{:S(2)}, u32[]{:S(2)}) collective-permute-start(f32[8,4224]{1,0:T(8,128)S(1)} %concatenate.10), channel_id=1, source_target_pairs={{0,3},{1,2},{2,1},{3,0},{4,7},{5,6},{6,5},{7,4},{8,11},{9,10},{10,... | collective-permute-start | bytes 405512 | tf_op jit(solution)/shard_map/ppermute | solution.py:487
  48.3 21.9 %collective-permute-start.1 = (f32[8,4224]{1,0:T(8,128)S(1)}, f32[8,4224]{1,0:T(8,128)S(1)}, u32[]{:S(2)}, u32[]{:S(2)}) collective-permute-start(f32[8,4224]{1,0:T(8,128)S(1)} %concatenate.10), channel_id=1, source_target_pairs={{0,2},{1,3},{2,0},{3,1},{4,6},{5,7},{6,4},{7,5},{8,10},{9,11},{10,... | collective-permute-start | bytes 405512 | tf_op jit(solution)/shard_map/ppermute | solution.py:487
  48.3 21.9 %collective-permute-start = (f32[8,4224]{1,0:T(8,128)S(1)}, f32[8,4224]{1,0:T(8,128)S(1)}, u32[]{:S(2)}, u32[]{:S(2)}) collective-permute-start(f32[8,4224]{1,0:T(8,128)S(1)} %concatenate.10), channel_id=1, source_target_pairs={{0,1},{1,0},{2,3},{3,2},{4,5},{5,4},{6,7},{7,6},{8,9},{9,8},{10,11... | collective-permute-start | bytes 405512 | tf_op jit(solution)/shard_map/ppermute | solution.py:487
  74.2 17.8 %collective-permute-start.3 = (bf16[8,512]{1,0:T(8,128)(2,1)}, bf16[8,512]{1,0:T(8,128)(2,1)S(1)}, u32[]{:S(2)}, u32[]{:S(2)}) collective-permute-start(bf16[8,512]{1,0:T(8,128)(2,1)} %after.3), channel_id=1, source_target_pairs={{0,8},{4,12},{8,0},{12,4},{16,24},{20,28},{24,16},{28,20},{1,9},{5... | collective-permute-start | bytes 24584 | tf_op jit(solution)/shard_map/ppermute | solution.py:487
  75.9 16.5 %collective-permute-start.4 = (bf16[8,512]{1,0:T(8,128)(2,1)}, bf16[8,512]{1,0:T(8,128)(2,1)S(1)}, u32[]{:S(2)}, u32[]{:S(2)}) collective-permute-start(bf16[8,512]{1,0:T(8,128)(2,1)} %after.3), channel_id=1, source_target_pairs={{0,16},{4,20},{8,24},{12,28},{16,0},{20,4},{24,8},{28,12},{1,17},{... | collective-permute-start | bytes 24584 | tf_op jit(solution)/shard_map/ppermute | solution.py:487
  77.4 15.6 %collective-permute-start.5 = (bf16[8,512]{1,0:T(8,128)(2,1)}, bf16[8,512]{1,0:T(8,128)(2,1)S(1)}, u32[]{:S(2)}, u32[]{:S(2)}) collective-permute-start(bf16[8,512]{1,0:T(8,128)(2,1)} %after.3), channel_id=1, source_target_pairs={{0,24},{4,28},{8,16},{12,20},{16,8},{20,12},{24,0},{28,4},{1,25},{... | collective-permute-start | bytes 24584 | tf_op jit(solution)/shard_map/ppermute | solution.py:487
  94.3 5.7 %copy-start.16 = (s32[64,2]{0,1:T(2,128)S(1)}, s32[64,2]{0,1:T(2,128)}, u32[]{:S(2)}) copy-start(s32[64,2]{0,1:T(2,128)} %param.26) | copy-start | bytes 1540
  94.3 5.8 %copy-start.19 = (s32[8]{0:T(128)S(1)}, s32[8]{0:T(128)}, u32[]{:S(2)}) copy-start(s32[8]{0:T(128)} %constant.41.clone) | copy-start | bytes 100
  94.3 6.5 %copy-start.17 = (bf16[512]{0:T(512)(128)(2,1)S(1)}, bf16[512]{0:T(512)(128)(2,1)}, u32[]{:S(2)}) copy-start(bf16[512]{0:T(512)(128)(2,1)} %param.21) | copy-start | bytes 3076
  94.3 6.5 %copy-start.14 = (bf16[512,8]{0,1:T(8,128)(2,1)S(1)}, bf16[512,8]{0,1:T(8,128)(2,1)}, u32[]{:S(2)}) copy-start(bf16[512,8]{0,1:T(8,128)(2,1)} %param.22) | copy-start | bytes 24580
  94.3 6.8 %copy-start.9 = (bf16[8,512]{1,0:T(8,128)(2,1)S(1)}, bf16[8,512]{1,0:T(8,128)(2,1)}, u32[]{:S(2)}) copy-start(bf16[8,512]{1,0:T(8,128)(2,1)} %after.3) | copy-start | bytes 24580
  94.3 6.8 %copy-start.10 = (bf16[32,512]{1,0:T(8,128)(2,1)S(1)}, bf16[32,512]{1,0:T(8,128)(2,1)}, u32[]{:S(2)}) copy-start(bf16[32,512]{1,0:T(8,128)(2,1)} %pad_maximum_fusion.1.refs_1_) | copy-start | bytes 98308
  94.4 134.2 %all-to-all-start.1 = ((bf16[8,2,704,512]{3,2,1,0:T(8,128)(2,1)}), bf16[8,2,704,512]{3,2,1,0:T(8,128)(2,1)}, u32[]{:S(2)}, u32[]{:S(2)}) async-start(bf16[8,2,704,512]{3,2,1,0:T(8,128)(2,1)} %after.5), calls=%async_computation.1 | async-start | bytes 23068672 | tf_op jit(solution)/shard_map/all_to_all | solution.py:525
  101.1 1.8 collective-permute-start.6
  102.9 27.3 %copy-start.3 = (s32[8,5632]{1,0:T(8,128)S(1)}, s32[8,5632]{1,0:T(8,128)}, u32[]{:S(2)}) copy-start(s32[8,5632]{1,0:T(8,128)} %old_ref.1) | copy-start | bytes 540676
  111.7 5.5 %collective-permute-start.7 = (bf16[4,16,768]{2,1,0:T(8,128)(2,1)S(1)}, bf16[4,16,768]{2,1,0:T(8,128)(2,1)S(1)}, u32[]{:S(2)}, u32[]{:S(2)}) collective-permute-start(bf16[4,16,768]{2,1,0:T(8,128)(2,1)S(1)} %get-tuple-element.20), channel_id=1, source_target_pairs={{0,1},{1,0},{2,3},{3,2},{4,5},{5,4},{6,7},{7,6},{8,9},{9,8},{10,11... | collective-permute-start | bytes 294920 | tf_op jit(solution)/shard_map/ppermute | solution.py:487
  114.0 10.6 %collective-permute-start.8 = (bf16[4,16,768]{2,1,0:T(8,128)(2,1)S(1)}, bf16[4,16,768]{2,1,0:T(8,128)(2,1)S(1)}, u32[]{:S(2)}, u32[]{:S(2)}) collective-permute-start(bf16[4,16,768]{2,1,0:T(8,128)(2,1)S(1)} %get-tuple-element.19), channel_id=1, source_target_pairs={{0,2},{1,3},{2,0},{3,1},{4,6},{5,7},{6,4},{7,5},{8,10},{9,11},{10,... | collective-permute-start | bytes 294920 | tf_op jit(solution)/shard_map/ppermute | solution.py:487
  116.6 8.0 %collective-permute-start.9 = (bf16[4,16,768]{2,1,0:T(8,128)(2,1)S(1)}, bf16[4,16,768]{2,1,0:T(8,128)(2,1)S(1)}, u32[]{:S(2)}, u32[]{:S(2)}) collective-permute-start(bf16[4,16,768]{2,1,0:T(8,128)(2,1)S(1)} %get-tuple-element.18), channel_id=1, source_target_pairs={{0,3},{1,2},{2,1},{3,0},{4,7},{5,6},{6,5},{7,4},{8,11},{9,10},{10,... | collective-permute-start | bytes 294920 | tf_op jit(solution)/shard_map/ppermute | solution.py:487
  124.8 16.2 %collective-permute-start.10 = (bf16[2,16,768]{2,1,0:T(8,128)(2,1)S(1)}, bf16[2,16,768]{2,1,0:T(8,128)(2,1)S(1)}, u32[]{:S(2)}, u32[]{:S(2)}) collective-permute-start(bf16[2,16,768]{2,1,0:T(8,128)(2,1)S(1)} %activate.1.refs_0_), channel_id=1, source_target_pairs={{0,1},{1,0},{2,3},{3,2},{4,5},{5,4},{6,7},{7,6},{8,9},{9,8},{10,11... | collective-permute-start | bytes 147464 | tf_op jit(solution)/shard_map/ppermute | solution.py:487
  126.8 14.2 %collective-permute-start.11 = (bf16[2,16,768]{2,1,0:T(8,128)(2,1)S(1)}, bf16[2,16,768]{2,1,0:T(8,128)(2,1)S(1)}, u32[]{:S(2)}, u32[]{:S(2)}) collective-permute-start(bf16[2,16,768]{2,1,0:T(8,128)(2,1)S(1)} %activate.1.refs_0_), channel_id=1, source_target_pairs={{0,2},{1,3},{2,0},{3,1},{4,6},{5,7},{6,4},{7,5},{8,10},{9,11},{10,... | collective-permute-start | bytes 147464 | tf_op jit(solution)/shard_map/ppermute | solution.py:487
  128.1 12.9 %collective-permute-start.12 = (bf16[2,16,768]{2,1,0:T(8,128)(2,1)S(1)}, bf16[2,16,768]{2,1,0:T(8,128)(2,1)S(1)}, u32[]{:S(2)}, u32[]{:S(2)}) collective-permute-start(bf16[2,16,768]{2,1,0:T(8,128)(2,1)S(1)} %activate.1.refs_0_), channel_id=1, source_target_pairs={{0,3},{1,2},{2,1},{3,0},{4,7},{5,6},{6,5},{7,4},{8,11},{9,10},{10,... | collective-permute-start | bytes 147464 | tf_op jit(solution)/shard_map/ppermute | solution.py:487
  159.6 1.3 collective-permute-start.13
  161.7 66.2 %collective-permute-start.16 = (f32[8,512]{1,0:T(8,128)S(1)}, f32[8,512]{1,0:T(8,128)S(1)}, u32[]{:S(2)}, u32[]{:S(2)}) collective-permute-start(f32[8,512]{1,0:T(8,128)S(1)} %get-tuple-element.23), channel_id=1, source_target_pairs={{0,24},{4,28},{8,16},{12,20},{16,8},{20,12},{24,0},{28,4},{1,25},{... | collective-permute-start | bytes 49160 | tf_op jit(solution)/shard_map/ppermute | solution.py:487
  164.4 63.5 %collective-permute-start.15 = (f32[8,512]{1,0:T(8,128)S(1)}, f32[8,512]{1,0:T(8,128)S(1)}, u32[]{:S(2)}, u32[]{:S(2)}) collective-permute-start(f32[8,512]{1,0:T(8,128)S(1)} %get-tuple-element.24), channel_id=1, source_target_pairs={{0,16},{4,20},{8,24},{12,28},{16,0},{20,4},{24,8},{28,12},{1,17},{... | collective-permute-start | bytes 49160 | tf_op jit(solution)/shard_map/ppermute | solution.py:487
  165.0 63.0 %collective-permute-start.14 = (f32[8,512]{1,0:T(8,128)S(1)}, f32[8,512]{1,0:T(8,128)S(1)}, u32[]{:S(2)}, u32[]{:S(2)}) collective-permute-start(f32[8,512]{1,0:T(8,128)S(1)} %get-tuple-element.22), channel_id=1, source_target_pairs={{0,8},{4,12},{8,0},{12,4},{16,24},{20,28},{24,16},{28,20},{1,9},{5... | collective-permute-start | bytes 49160 | tf_op jit(solution)/shard_map/ppermute | solution.py:487
  (7 other events, 8.9 us)

commit v7 on v6

--- a/solution.py
+++ b/solution.py
@@ -219,7 +219,7 @@
     return pl.ds(pl.multiple_of(index * TILE, TILE), TILE)
 
 
-def pack_kernel(rows, span, plan_ref, place_ref, lines_ref, out_ref, packed_ref, number_ref, sems, *stages):
+def pack_kernel(rows, span, steps, plan_ref, place_ref, lines_ref, out_ref, packed_ref, number_ref, sems, *stages):
     part = pl.program_id(0)
     step = pl.program_id(1)
     deep = stages[0].shape[0] - STRAIGHT * TILE
@@ -283,18 +283,47 @@
 
             lax.fori_loop(0, rows, long_peer, 0)
 
-    @pl.when(step == pl.num_programs(1) - 1)
+    block_rows = out_ref.shape[2]
+    chunks = []
+    begin = 0
+    for after_step in range(steps):
+        end = block_rows
+        if after_step < steps - 1:
+            end = max(begin, block_rows * (after_step + 1) // steps // TILE * TILE - 2 * TILE)
+        if end > begin:
+            chunks.append((after_step, begin, end))
+        begin = end
+
+    def chunk_copy(n):
+        _, begin, end = chunks[n]
+        here = pl.ds(begin, end - begin)
+        return pltpu.make_async_copy(
+            packed_ref.at[:, here], out_ref.at[:, part, here], sems.at[n]
+        )
+
+    def final_by(n):
+        after_step, _, end = chunks[n]
+        first = (after_step + 1) * span * rows
+        least = functools.reduce(jnp.minimum, [plan_ref[0, first + d] for d in range(rows)])
+        return least * TILE >= end
+
+    for n in range(len(chunks) - 1):
+
+        @pl.when((step == chunks[n][0]) & final_by(n))
+        def _(n=n):
+            chunk_copy(n).start()
+
+    @pl.when(step == steps - 1)
     def _():
-        copies = [
-            pltpu.make_async_copy(
-                packed_ref.at[d, pl.ds(0, out_ref.shape[2])], out_ref.at[d, part], sems.at[d]
-            )
-            for d in range(rows)
-        ]
-        for copy in copies:
-            copy.start()
-        for copy in copies:
-            copy.wait()
+        for n in range(len(chunks) - 1):
+
+            @pl.when(jnp.logical_not(final_by(n)))
+            def _(n=n):
+                chunk_copy(n).start()
+
+        chunk_copy(len(chunks) - 1).start()
+        for n in range(len(chunks)):
+            chunk_copy(n).wait()
 
 
 def unpack_kernel(slot, span, plan_ref, place_ref, block_ref, *rest):
@@ -329,23 +358,47 @@
 
     @pl.when(step == 0)
     def _():
-        stage_ref[...] = jnp.zeros_like(stage_ref)
         begin(step)
 
     @pl.when(step + 1 < steps)
     def _():
         begin(step + 1)
 
+    lane = counting((lines, LANES), 1)
+
+    def multiply(j, depth):
+        within_block, block = place_ref[j, 0], place_ref[j, 1]
+        pieces = []
+        for first in range(0, depth, LANES):
+            away = jnp.abs(block - jnp.asarray(first // 256, jnp.bfloat16))
+            place = within_block + away * jnp.asarray(512, jnp.bfloat16)
+            pieces.append(equal_ones(lane + jnp.asarray(first % 256, jnp.bfloat16), place))
+        onehot = jnp.concatenate(pieces, axis=1)
+        for part in range(count):
+            out_ref[j, part] = jnp.dot(
+                onehot, stage_ref[buffer, j, part, :depth], preferred_element_type=jnp.float32
+            ).astype(jnp.bfloat16)
+
     for j in range(span):
         e = step * span + j
+        staged = rows * slot * TILE
 
         @pl.when(slotted(e))
         def _(j=j):
-            all_slots = stage_ref.at[buffer, j, :, pl.ds(0, rows * slot * TILE)]
+            all_slots = stage_ref.at[buffer, j, :, pl.ds(0, staged)]
             pltpu.make_async_copy(all_slots, all_slots, sems.at[buffer, j]).wait()
+            if staged % LANES:
+                stage_ref[buffer, j, :, staged:] = jnp.zeros(
+                    (count, deep - staged, width), jnp.bfloat16
+                )
+                multiply(j, deep)
+            else:
+                multiply(j, staged)
 
         @pl.when(jnp.logical_not(slotted(e)))
         def _(e=e, j=j):
+            stage_ref[buffer, j] = jnp.zeros((count, deep, width), jnp.bfloat16)
+
             def one_peer(s, carry):
                 def put(t, c):
                     copy = pltpu.make_async_copy(
@@ -360,20 +413,7 @@
                 return lax.fori_loop(0, entry(1, e, s), put, carry)
 
             lax.fori_loop(0, rows, one_peer, 0)
-
-    lane = counting((lines, LANES), 1)
-    for j in range(span):
-        within_block, block = place_ref[j, 0], place_ref[j, 1]
-        pieces = []
-        for first in range(0, deep, LANES):
-            away = jnp.abs(block - jnp.asarray(first // 256, jnp.bfloat16))
-            place = within_block + away * jnp.asarray(512, jnp.bfloat16)
-            pieces.append(equal_ones(lane + jnp.asarray(first % 256, jnp.bfloat16), place))
-        onehot = jnp.concatenate(pieces, axis=1)
-        for part in range(count):
-            out_ref[j, part] = jnp.dot(
-                onehot, stage_ref[buffer, j, part], preferred_element_type=jnp.float32
-            ).astype(jnp.bfloat16)
+            multiply(j, deep)
 
 
 def call_plan(kernel, name, table, ids, pairs, place):
@@ -393,7 +433,7 @@
     first, count = piece
     span = 2 - experts % 2
     return pl.pallas_call(
-        functools.partial(pack_kernel, rows, span),
+        functools.partial(pack_kernel, rows, span, experts // span),
         grid_spec=pltpu.PrefetchScalarGridSpec(
             num_scalar_prefetch=1,
             grid=(count, experts // span),
@@ -405,7 +445,7 @@
             scratch_shapes=[
                 pltpu.VMEM((rows, block_rows + STRAIGHT * TILE, width), jnp.bfloat16),
                 pltpu.VMEM((256, lines), jnp.bfloat16),
-                pltpu.SemaphoreType.DMA((rows,)),
+                pltpu.SemaphoreType.DMA((experts // span,)),
             ]
             + [pltpu.VMEM((deep + STRAIGHT * TILE, width), jnp.bfloat16)] * span,
         ),

time: 248 us -> 246 us (level)
  Pallas kernels: 93.4 us -> 89.7 us
    pallas_call x2, Pallas kernels: 33 us -> 29.5 us  [pack(): pl.pallas_call(functools.partial(pack_kernel, rows, span, experts // span...]
  transfers between devices with their start and end apart: 19 -> 19, of which waited for: 8 -> 7; matrix products, arithmetic and copies ran while one was open for 10% -> 10% of each run, Pallas kernels for 24% -> 23%
where the time goes in v7:
time: 246 us; the launch traced here: 245 us
  waiting for transfers between devices  90.9 us (37%)
  Pallas kernels  89.7 us (36%)
  starting transfers between devices  33 us (13%)
  local copies, waits for them, and re-layouts  15.4 us (6%)
  matrix products  8.49 us (3%)
  other arithmetic  6.18 us (3%)
    ppermute x17, waiting for transfers between devices, from_peer(): return lax.ppermute(block, axis, [(i, i ^ offset) for i in range(size)])  90.9 us
    pallas_call x2, Pallas kernels, pack(): pl.pallas_call(functools.partial(pack_kernel, rows, span, experts // span...  29.5 us
    pallas_call x2, Pallas kernels, unpack(): pl.pallas_call(functools.partial(unpack_kernel, slot, span), grid_spec=pl...  28.5 us
    ppermute x17, starting transfers between devices, from_peer(): return lax.ppermute(block, axis, [(i, i ^ offset) for i in range(size)])  22 us
    pallas_call x2, Pallas kernels, call_plan(): pl.pallas_call(kernel, out_shape=(place, jax.ShapeDtypeStruct((4, up_to(p...  16.6 us
    all_to_all x2, starting transfers between devices, send(): lax.all_to_all(block, 'row', split_axis=0, concat_axis=0, tiled=True)  10.9 us
    unnamed x49, local copies, waits for them, and re-layouts  8.98 us
    pallas_call x1, Pallas kernels, experts_part(): pl.pallas_call(gate_up_kernel, grid_spec=pltpu.PrefetchScalarGridSpec(num...  8.79 us
  transfers between devices with their start and end apart: 19, of which 7 were waited for; matrix products, arithmetic and copies ran while one was open for 10% of the time, Pallas kernels for 23%

profile of v7, /device:TPU:0, one launch (start us, length us, event | category | flops | bytes accessed | tf_op | source)
XLA Modules:
  0.0 245.0 jit_solution(14896087697899664584)
XLA Ops:
  2.4 5.7 %outgoing_plan.1 = (s32[8,1,768]{2,1,0:T(1,128)S(1)}, s32[4,128]{1,0:T(4,128)S(1)}) custom-call(s32[8,5632]{1,0:T(8,128)S(1)} %copy-done.2, s32[8,768]{1,0:T(8,128)S(1)} %pad.11.held_ref), custom_call_target="tpu_custom_call" | custom-call | flops 230686720 | bytes 360448 | tf_op jit(solution)/shard_map/outgoing_plan/pallas_call | solution.py:420
  9.3 10.6 %pack_lines.2.refs_1_ = bf16[8,1,704,512]{3,2,1,0:T(8,128)(2,1)} custom-call(s32[4,128]{1,0:T(4,128)} %copy-done.4, s32[8,1,768]{2,1,0:T(1,128)} %copy-done.1, bf16[8,3,704,512]{3,2,1,0:T(8,128)(2,1)} %bitcast.81), custom_call_target="tpu_custom_call" | custom-call | flops 5444206592 | bytes 11534336 | tf_op jit(solution)/shard_map/pack_lines/pallas_call | solution.py:435
  19.9 5.3 %all-to-all-start = ((bf16[8,1,704,512]{3,2,1,0:T(8,128)(2,1)}), bf16[8,1,704,512]{3,2,1,0:T(8,128)(2,1)}, u32[]{:S(2)}, u32[]{:S(2)}) async-start(bf16[8,1,704,512]{3,2,1,0:T(8,128)(2,1)} %pack_lines.2.refs_1_), calls=%async_computation | async-start | bytes 11534336 | tf_op jit(solution)/shard_map/all_to_all | solution.py:565
  27.7 1.3 copy.144
  29.0 1.5 copy.143
  30.5 1.2 copy.146
  31.7 1.2 copy.145
  33.2 2.0 fusion.33
  36.0 1.2 fusion.32
  42.3 4.8 %collective-permute-start.2 = (f32[8,4224]{1,0:T(8,128)S(1)}, f32[8,4224]{1,0:T(8,128)S(1)}, u32[]{:S(2)}, u32[]{:S(2)}) collective-permute-start(f32[8,4224]{1,0:T(8,128)S(1)} %concatenate.10), channel_id=1, source_target_pairs={{0,3},{1,2},{2,1},{3,0},{4,7},{5,6},{6,5},{7,4},{8,11},{9,10},{10,... | collective-permute-start | bytes 405512 | tf_op jit(solution)/shard_map/ppermute | solution.py:527
  47.8 18.9 %pack_lines.3.refs_2_.refs_0_ = bf16[8,2,704,512]{3,2,1,0:T(8,128)(2,1)} custom-call(s32[4,128]{1,0:T(4,128)} %copy-done.4, s32[8,1,768]{2,1,0:T(1,128)} %copy-done.1, bf16[8,3,704,512]{3,2,1,0:T(8,128)(2,1)} %bitcast.82), custom_call_target="tpu_custom_call" | custom-call | flops 10888413184 | bytes 23068672 | tf_op jit(solution)/shard_map/pack_lines/pallas_call | solution.py:435
  67.3 3.5 %fusion.4.refs_0_ = bf16[8,512]{1,0:T(8,128)(2,1)} fusion(bf16[4096,512]{1,0:T(8,128)(2,1)} %param.20, f32[8,4096]{1,0:T(8,128)S(1)} %fusion.8, f32[8,32]{0,1:T(8,128)S(1)} %copy.126, bf16[8,512]{1,0:T(8,128)(2,1)S(1)} %copy-done.13), kind=kOutput, calls=%fused_computation.9 | convolution fusion | flops 33632256 | bytes 4342784 | tf_op jit(solution)/shard_map/dot_general | solution.py:839
  70.7 1.7 collective-permute-start.3
  72.5 1.5 collective-permute-start.4
  74.2 16.6 %collective-permute-done.3 = bf16[8,512]{1,0:T(8,128)(2,1)S(1)} collective-permute-done((bf16[8,512]{1,0:T(8,128)(2,1)}, bf16[8,512]{1,0:T(8,128)(2,1)S(1)}, u32[]{:S(2)}, u32[]{:S(2)}) %collective-permute-start.3) | collective-permute-done | bytes 8224 | tf_op jit(solution)/shard_map/ppermute | solution.py:527
  91.8 1.3 pad_maximum_fusion.1.refs_1_
  93.1 5.6 %all-to-all-start.1 = ((bf16[8,2,704,512]{3,2,1,0:T(8,128)(2,1)}), bf16[8,2,704,512]{3,2,1,0:T(8,128)(2,1)}, u32[]{:S(2)}, u32[]{:S(2)}) async-start(bf16[8,2,704,512]{3,2,1,0:T(8,128)(2,1)} %after.5), calls=%async_computation.1 | async-start | bytes 23068672 | tf_op jit(solution)/shard_map/all_to_all | solution.py:565
  100.1 1.5 collective-permute-done.6
  101.7 8.8 %gate_up.1 = bf16[4,4,16,768]{3,2,1,0:T(8,128)(2,1)S(1)} custom-call(s32[1]{0:T(128)} %bitcast.20.me_ref, bf16[64,512]{1,0:T(8,128)(2,1)S(1)} %constant_dynamic-update-slice_fusion.h_ref, bf16[1,512]{1,0:T(2,128)(2,1)S(1)} %reshape.90.gain_ref, bf16[512,128]{1,0:T(8,128)(2,1)S(1)} %pad.12.router_ref, s32[64,2]{1,0:T(8,128)S(1)} %bitcast.78, ...), custom_call_target="tpu_custom_call" | custom-call | flops 738197504 | bytes 11534336 | tf_op jit(solution)/shard_map/gate_up/pallas_call | solution.py:764
  110.5 2.3 collective-permute-start.7
  112.8 2.6 %collective-permute-start.8 = (bf16[4,16,768]{2,1,0:T(8,128)(2,1)S(1)}, bf16[4,16,768]{2,1,0:T(8,128)(2,1)S(1)}, u32[]{:S(2)}, u32[]{:S(2)}) collective-permute-start(bf16[4,16,768]{2,1,0:T(8,128)(2,1)S(1)} %get-tuple-element.19), channel_id=1, source_target_pairs={{0,2},{1,3},{2,0},{3,1},{4,6},{5,7},{6,4},{7,5},{8,10},{9,11},{10,... | collective-permute-start | bytes 294920 | tf_op jit(solution)/shard_map/ppermute | solution.py:527
  116.1 7.4 %collective-permute-done.8.refs_2_ = bf16[4,16,768]{2,1,0:T(8,128)(2,1)S(1)} collective-permute-done((bf16[4,16,768]{2,1,0:T(8,128)(2,1)S(1)}, bf16[4,16,768]{2,1,0:T(8,128)(2,1)S(1)}, u32[]{:S(2)}, u32[]{:S(2)}) %collective-permute-start.8) | collective-permute-done | bytes 98336 | tf_op jit(solution)/shard_map/ppermute | solution.py:527
  123.6 1.9 collective-permute-start.10
  125.6 1.3 collective-permute-start.11
  126.9 1.2 collective-permute-start.12
  128.9 10.8 %incoming_plan.1 = (bf16[8,2,704,128]{3,2,1,0:T(8,128)(2,1)S(1)}, s32[4,128]{1,0:T(4,128)S(1)}) custom-call(s32[8,5632]{1,0:T(8,128)S(1)} %copy-done.3, s32[8,768]{1,0:T(8,128)S(1)} %pad.13.wanted_ref), custom_call_target="tpu_custom_call" | custom-call | flops 230686720 | bytes 360448 | tf_op jit(solution)/shard_map/incoming_plan/pallas_call | solution.py:420
  139.8 6.1 %down.1.refs_0_ = f32[64,512]{1,0:T(8,128)S(1)} custom-call(s32[1]{0:T(128)} %bitcast.20.me_ref, s32[64,2]{1,0:T(8,128)S(1)} %bitcast.80, bf16[2,16,768]{2,1,0:T(8,128)(2,1)S(1)} %activate.1.refs_0_, bf16[2,16,768]{2,1,0:T(8,128)(2,1)S(1)} %collective-permute-done.10.refs_1_, bf16[2,16,768]{2,1,0:T(8,128)(2,1)S(1)} %collective-permute-done.11.refs_2_, ...), custom_call_target="tpu_custom_call" | custom-call | flops 369098752 | bytes 5767168 | tf_op jit(solution)/shard_map/down/pallas_call | solution.py:791
  146.6 11.1 %unpack_lines.2.refs_1_.rest_0_ = bf16[8,3,704,512]{3,2,1,0:T(8,128)(2,1)} custom-call(s32[4,128]{1,0:T(4,128)S(1)} %get-tuple-element.8.plan_ref, bf16[8,2,704,128]{3,2,1,0:T(8,128)(2,1)S(1)} %get-tuple-element.9.place_ref, bf16[8,1,704,512]{3,2,1,0:T(8,128)(2,1)} %all-to-all-done.block_ref), custom_call_target="tpu_custom_call" | custom-call | flops 5905580032 | bytes 11534336 | tf_op jit(solution)/shard_map/unpack_lines/pallas_call | solution.py:477
  158.6 1.3 collective-permute-done.13
  160.7 2.7 %collective-permute-start.16 = (f32[8,512]{1,0:T(8,128)S(1)}, f32[8,512]{1,0:T(8,128)S(1)}, u32[]{:S(2)}, u32[]{:S(2)}) collective-permute-start(f32[8,512]{1,0:T(8,128)S(1)} %get-tuple-element.23), channel_id=1, source_target_pairs={{0,24},{4,28},{8,16},{12,20},{16,8},{20,12},{24,0},{28,4},{1,25},{... | collective-permute-start | bytes 49160 | tf_op jit(solution)/shard_map/ppermute | solution.py:527
  164.2 62.5 %collective-permute-done.16 = f32[8,512]{1,0:T(8,128)S(1)} collective-permute-done((f32[8,512]{1,0:T(8,128)S(1)}, f32[8,512]{1,0:T(8,128)S(1)}, u32[]{:S(2)}, u32[]{:S(2)}) %collective-permute-start.16) | collective-permute-done | bytes 16416 | tf_op jit(solution)/shard_map/ppermute | solution.py:527
  227.4 17.4 %unpack_lines.3 = bf16[8,3,704,512]{3,2,1,0:T(8,128)(2,1)} custom-call(s32[4,128]{1,0:T(4,128)S(1)} %get-tuple-element.8.plan_ref, bf16[8,2,704,128]{3,2,1,0:T(8,128)(2,1)S(1)} %get-tuple-element.9.place_ref, bf16[8,2,704,512]{3,2,1,0:T(8,128)(2,1)} %all-to-all-done.1.block_ref, ...), custom_call_target="tpu_custom_call", output_to_operand_aliasing={{}: (3, {})} | custom-call | flops 11811160064 | bytes 23068672 | tf_op jit(solution)/shard_map/unpack_lines/pallas_call | solution.py:477
  (118 shorter events, 20.7 us)
Async XLA Ops:
  19.9 5.3 %copy-start.5 = (bf16[1,2,256,2048]{3,2,1,0:T(8,128)(2,1)S(1)}, bf16[1,2,256,2048]{3,2,1,0:T(8,128)(2,1)}, u32[]{:S(2)}) copy-start(bf16[1,2,256,2048]{3,2,1,0:T(8,128)(2,1)} %param.17) | copy-start | bytes 6291460
  19.9 73.2 %all-to-all-start = ((bf16[8,1,704,512]{3,2,1,0:T(8,128)(2,1)}), bf16[8,1,704,512]{3,2,1,0:T(8,128)(2,1)}, u32[]{:S(2)}, u32[]{:S(2)}) async-start(bf16[8,1,704,512]{3,2,1,0:T(8,128)(2,1)} %pack_lines.2.refs_1_), calls=%async_computation | async-start | bytes 11534336 | tf_op jit(solution)/shard_map/all_to_all | solution.py:565
  27.7 5.4 %copy-start.18 = (s32[8]{0:T(128)S(1)}, s32[8]{0:T(128)}, u32[]{:S(2)}) copy-start(s32[8]{0:T(128)} %param.19) | copy-start | bytes 100
  31.7 10.1 %copy-start.7 = (bf16[1,1,256,2048]{2,3,1,0:T(8,128)(2,1)S(1)}, bf16[1,1,256,2048]{2,3,1,0:T(8,128)(2,1)}, u32[]{:S(2)}) copy-start(bf16[1,1,256,2048]{2,3,1,0:T(8,128)(2,1)} %copy.144) | copy-start | bytes 3145732
  32.9 7.8 %copy-start.8 = (bf16[32,8,16,128]{3,2,1,0:T(8,128)(2,1)S(1)}, bf16[32,8,16,128]{3,2,1,0:T(8,128)(2,1)}, u32[]{:S(2)}) copy-start(bf16[32,8,16,128]{3,2,1,0:T(8,128)(2,1)} %copy.146) | copy-start | bytes 3145732
  33.2 2.8 %copy-start.15 = (pred[8,32]{1,0:T(8,128)(4,1)}, pred[8,32]{1,0:T(8,128)(4,1)S(1)}, u32[]{:S(2)}) copy-start(pred[8,32]{1,0:T(8,128)(4,1)S(1)} %broadcast_compare_fusion) | copy-start | bytes 772
  42.3 24.9 %copy-start.13 = (bf16[8,512]{1,0:T(8,128)(2,1)S(1)}, bf16[8,512]{1,0:T(8,128)(2,1)}, u32[]{:S(2)}) copy-start(bf16[8,512]{1,0:T(8,128)(2,1)} %param.14) | copy-start | bytes 24580
  42.3 24.4 %collective-permute-start.2 = (f32[8,4224]{1,0:T(8,128)S(1)}, f32[8,4224]{1,0:T(8,128)S(1)}, u32[]{:S(2)}, u32[]{:S(2)}) collective-permute-start(f32[8,4224]{1,0:T(8,128)S(1)} %concatenate.10), channel_id=1, source_target_pairs={{0,3},{1,2},{2,1},{3,0},{4,7},{5,6},{6,5},{7,4},{8,11},{9,10},{10,... | collective-permute-start | bytes 405512 | tf_op jit(solution)/shard_map/ppermute | solution.py:527
  47.1 19.6 %collective-permute-start.1 = (f32[8,4224]{1,0:T(8,128)S(1)}, f32[8,4224]{1,0:T(8,128)S(1)}, u32[]{:S(2)}, u32[]{:S(2)}) collective-permute-start(f32[8,4224]{1,0:T(8,128)S(1)} %concatenate.10), channel_id=1, source_target_pairs={{0,2},{1,3},{2,0},{3,1},{4,6},{5,7},{6,4},{7,5},{8,10},{9,11},{10,... | collective-permute-start | bytes 405512 | tf_op jit(solution)/shard_map/ppermute | solution.py:527
  47.1 19.6 %collective-permute-start = (f32[8,4224]{1,0:T(8,128)S(1)}, f32[8,4224]{1,0:T(8,128)S(1)}, u32[]{:S(2)}, u32[]{:S(2)}) collective-permute-start(f32[8,4224]{1,0:T(8,128)S(1)} %concatenate.10), channel_id=1, source_target_pairs={{0,1},{1,0},{2,3},{3,2},{4,5},{5,4},{6,7},{7,6},{8,9},{9,8},{10,11... | collective-permute-start | bytes 405512 | tf_op jit(solution)/shard_map/ppermute | solution.py:527
  70.7 20.1 %collective-permute-start.3 = (bf16[8,512]{1,0:T(8,128)(2,1)}, bf16[8,512]{1,0:T(8,128)(2,1)S(1)}, u32[]{:S(2)}, u32[]{:S(2)}) collective-permute-start(bf16[8,512]{1,0:T(8,128)(2,1)} %after.3), channel_id=1, source_target_pairs={{0,8},{4,12},{8,0},{12,4},{16,24},{20,28},{24,16},{28,20},{1,9},{5... | collective-permute-start | bytes 24584 | tf_op jit(solution)/shard_map/ppermute | solution.py:527
  72.5 18.4 %collective-permute-start.4 = (bf16[8,512]{1,0:T(8,128)(2,1)}, bf16[8,512]{1,0:T(8,128)(2,1)S(1)}, u32[]{:S(2)}, u32[]{:S(2)}) collective-permute-start(bf16[8,512]{1,0:T(8,128)(2,1)} %after.3), channel_id=1, source_target_pairs={{0,16},{4,20},{8,24},{12,28},{16,0},{20,4},{24,8},{28,12},{1,17},{... | collective-permute-start | bytes 24584 | tf_op jit(solution)/shard_map/ppermute | solution.py:527
  74.0 17.8 %collective-permute-start.5 = (bf16[8,512]{1,0:T(8,128)(2,1)}, bf16[8,512]{1,0:T(8,128)(2,1)S(1)}, u32[]{:S(2)}, u32[]{:S(2)}) collective-permute-start(bf16[8,512]{1,0:T(8,128)(2,1)} %after.3), channel_id=1, source_target_pairs={{0,24},{4,28},{8,16},{12,20},{16,8},{20,12},{24,0},{28,4},{1,25},{... | collective-permute-start | bytes 24584 | tf_op jit(solution)/shard_map/ppermute | solution.py:527
  93.1 5.7 %copy-start.16 = (s32[64,2]{0,1:T(2,128)S(1)}, s32[64,2]{0,1:T(2,128)}, u32[]{:S(2)}) copy-start(s32[64,2]{0,1:T(2,128)} %param.26) | copy-start | bytes 1540
  93.1 5.8 %copy-start.19 = (s32[8]{0:T(128)S(1)}, s32[8]{0:T(128)}, u32[]{:S(2)}) copy-start(s32[8]{0:T(128)} %constant.41.clone) | copy-start | bytes 100
  93.1 6.5 %copy-start.17 = (bf16[512]{0:T(512)(128)(2,1)S(1)}, bf16[512]{0:T(512)(128)(2,1)}, u32[]{:S(2)}) copy-start(bf16[512]{0:T(512)(128)(2,1)} %param.21) | copy-start | bytes 3076
  93.1 6.5 %copy-start.14 = (bf16[512,8]{0,1:T(8,128)(2,1)S(1)}, bf16[512,8]{0,1:T(8,128)(2,1)}, u32[]{:S(2)}) copy-start(bf16[512,8]{0,1:T(8,128)(2,1)} %param.22) | copy-start | bytes 24580
  93.1 6.8 %copy-start.9 = (bf16[8,512]{1,0:T(8,128)(2,1)S(1)}, bf16[8,512]{1,0:T(8,128)(2,1)}, u32[]{:S(2)}) copy-start(bf16[8,512]{1,0:T(8,128)(2,1)} %after.3) | copy-start | bytes 24580
  93.1 6.8 %copy-start.10 = (bf16[32,512]{1,0:T(8,128)(2,1)S(1)}, bf16[32,512]{1,0:T(8,128)(2,1)}, u32[]{:S(2)}) copy-start(bf16[32,512]{1,0:T(8,128)(2,1)} %pad_maximum_fusion.1.refs_1_) | copy-start | bytes 98308
  93.1 134.2 %all-to-all-start.1 = ((bf16[8,2,704,512]{3,2,1,0:T(8,128)(2,1)}), bf16[8,2,704,512]{3,2,1,0:T(8,128)(2,1)}, u32[]{:S(2)}, u32[]{:S(2)}) async-start(bf16[8,2,704,512]{3,2,1,0:T(8,128)(2,1)} %after.5), calls=%async_computation.1 | async-start | bytes 23068672 | tf_op jit(solution)/shard_map/all_to_all | solution.py:565
  99.9 1.8 collective-permute-start.6
  101.7 27.2 %copy-start.3 = (s32[8,5632]{1,0:T(8,128)S(1)}, s32[8,5632]{1,0:T(8,128)}, u32[]{:S(2)}) copy-start(s32[8,5632]{1,0:T(8,128)} %old_ref.1) | copy-start | bytes 540676
  110.5 5.6 %collective-permute-start.7 = (bf16[4,16,768]{2,1,0:T(8,128)(2,1)S(1)}, bf16[4,16,768]{2,1,0:T(8,128)(2,1)S(1)}, u32[]{:S(2)}, u32[]{:S(2)}) collective-permute-start(bf16[4,16,768]{2,1,0:T(8,128)(2,1)S(1)} %get-tuple-element.20), channel_id=1, source_target_pairs={{0,1},{1,0},{2,3},{3,2},{4,5},{5,4},{6,7},{7,6},{8,9},{9,8},{10,11... | collective-permute-start | bytes 294920 | tf_op jit(solution)/shard_map/ppermute | solution.py:527
  112.8 10.7 %collective-permute-start.8 = (bf16[4,16,768]{2,1,0:T(8,128)(2,1)S(1)}, bf16[4,16,768]{2,1,0:T(8,128)(2,1)S(1)}, u32[]{:S(2)}, u32[]{:S(2)}) collective-permute-start(bf16[4,16,768]{2,1,0:T(8,128)(2,1)S(1)} %get-tuple-element.19), channel_id=1, source_target_pairs={{0,2},{1,3},{2,0},{3,1},{4,6},{5,7},{6,4},{7,5},{8,10},{9,11},{10,... | collective-permute-start | bytes 294920 | tf_op jit(solution)/shard_map/ppermute | solution.py:527
  115.4 8.1 %collective-permute-start.9 = (bf16[4,16,768]{2,1,0:T(8,128)(2,1)S(1)}, bf16[4,16,768]{2,1,0:T(8,128)(2,1)S(1)}, u32[]{:S(2)}, u32[]{:S(2)}) collective-permute-start(bf16[4,16,768]{2,1,0:T(8,128)(2,1)S(1)} %get-tuple-element.18), channel_id=1, source_target_pairs={{0,3},{1,2},{2,1},{3,0},{4,7},{5,6},{6,5},{7,4},{8,11},{9,10},{10,... | collective-permute-start | bytes 294920 | tf_op jit(solution)/shard_map/ppermute | solution.py:527
  123.6 16.1 %collective-permute-start.10 = (bf16[2,16,768]{2,1,0:T(8,128)(2,1)S(1)}, bf16[2,16,768]{2,1,0:T(8,128)(2,1)S(1)}, u32[]{:S(2)}, u32[]{:S(2)}) collective-permute-start(bf16[2,16,768]{2,1,0:T(8,128)(2,1)S(1)} %activate.1.refs_0_), channel_id=1, source_target_pairs={{0,1},{1,0},{2,3},{3,2},{4,5},{5,4},{6,7},{7,6},{8,9},{9,8},{10,11... | collective-permute-start | bytes 147464 | tf_op jit(solution)/shard_map/ppermute | solution.py:527
  125.6 14.2 %collective-permute-start.11 = (bf16[2,16,768]{2,1,0:T(8,128)(2,1)S(1)}, bf16[2,16,768]{2,1,0:T(8,128)(2,1)S(1)}, u32[]{:S(2)}, u32[]{:S(2)}) collective-permute-start(bf16[2,16,768]{2,1,0:T(8,128)(2,1)S(1)} %activate.1.refs_0_), channel_id=1, source_target_pairs={{0,2},{1,3},{2,0},{3,1},{4,6},{5,7},{6,4},{7,5},{8,10},{9,11},{10,... | collective-permute-start | bytes 147464 | tf_op jit(solution)/shard_map/ppermute | solution.py:527
  126.9 12.9 %collective-permute-start.12 = (bf16[2,16,768]{2,1,0:T(8,128)(2,1)S(1)}, bf16[2,16,768]{2,1,0:T(8,128)(2,1)S(1)}, u32[]{:S(2)}, u32[]{:S(2)}) collective-permute-start(bf16[2,16,768]{2,1,0:T(8,128)(2,1)S(1)} %activate.1.refs_0_), channel_id=1, source_target_pairs={{0,3},{1,2},{2,1},{3,0},{4,7},{5,6},{6,5},{7,4},{8,11},{9,10},{10,... | collective-permute-start | bytes 147464 | tf_op jit(solution)/shard_map/ppermute | solution.py:527
  158.6 1.3 collective-permute-start.13
  160.7 66.0 %collective-permute-start.16 = (f32[8,512]{1,0:T(8,128)S(1)}, f32[8,512]{1,0:T(8,128)S(1)}, u32[]{:S(2)}, u32[]{:S(2)}) collective-permute-start(f32[8,512]{1,0:T(8,128)S(1)} %get-tuple-element.23), channel_id=1, source_target_pairs={{0,24},{4,28},{8,16},{12,20},{16,8},{20,12},{24,0},{28,4},{1,25},{... | collective-permute-start | bytes 49160 | tf_op jit(solution)/shard_map/ppermute | solution.py:527
  163.4 63.4 %collective-permute-start.15 = (f32[8,512]{1,0:T(8,128)S(1)}, f32[8,512]{1,0:T(8,128)S(1)}, u32[]{:S(2)}, u32[]{:S(2)}) collective-permute-start(f32[8,512]{1,0:T(8,128)S(1)} %get-tuple-element.24), channel_id=1, source_target_pairs={{0,16},{4,20},{8,24},{12,28},{16,0},{20,4},{24,8},{28,12},{1,17},{... | collective-permute-start | bytes 49160 | tf_op jit(solution)/shard_map/ppermute | solution.py:527
  163.9 62.8 %collective-permute-start.14 = (f32[8,512]{1,0:T(8,128)S(1)}, f32[8,512]{1,0:T(8,128)S(1)}, u32[]{:S(2)}, u32[]{:S(2)}) collective-permute-start(f32[8,512]{1,0:T(8,128)S(1)} %get-tuple-element.22), channel_id=1, source_target_pairs={{0,8},{4,12},{8,0},{12,4},{16,24},{20,28},{24,16},{28,20},{1,9},{5... | collective-permute-start | bytes 49160 | tf_op jit(solution)/shard_map/ppermute | solution.py:527
  (7 other events, 8.9 us)

commit v8 on v7

--- a/solution.py
+++ b/solution.py
@@ -16,7 +16,7 @@
 norm_eps = 1e-06
 neg_big = -1e30
 VMEM_LIMIT = 48 * 1024 * 1024
-PACK_LIMIT = 61 * 1024 * 1024
+PACK_LIMIT = 59 * 1024 * 1024
 
 
 def up_to(value, unit):
@@ -341,28 +341,24 @@
     def slotted(e):
         return entry(3, e, 0) > 0
 
-    def begin(step):
-        for j in range(span):
-            e = step * span + j
-
-            @pl.when(slotted(e))
-            def _(e=e, j=j):
-                for s in range(rows):
-                    there = pl.ds(pl.multiple_of(entry(0, e, s) * TILE, TILE), slot * TILE)
-                    here = pl.ds(s * slot * TILE, slot * TILE)
-                    pltpu.make_async_copy(
-                        block_ref.at[s, :, there],
-                        stage_ref.at[step % 2, j, :, here],
-                        sems.at[step % 2, j],
-                    ).start()
+    def begin(step, j):
+        e = step * span + j
+
+        @pl.when(slotted(e))
+        def _():
+            for s in range(rows):
+                there = pl.ds(pl.multiple_of(entry(0, e, s) * TILE, TILE), slot * TILE)
+                here = pl.ds(s * slot * TILE, slot * TILE)
+                pltpu.make_async_copy(
+                    block_ref.at[s, :, there],
+                    stage_ref.at[step % 2, j, :, here],
+                    sems.at[step % 2, j],
+                ).start()
 
     @pl.when(step == 0)
     def _():
-        begin(step)
-
-    @pl.when(step + 1 < steps)
-    def _():
-        begin(step + 1)
+        for j in range(span):
+            begin(step, j)
 
     lane = counting((lines, LANES), 1)
 
@@ -387,6 +383,13 @@
         def _(j=j):
             all_slots = stage_ref.at[buffer, j, :, pl.ds(0, staged)]
             pltpu.make_async_copy(all_slots, all_slots, sems.at[buffer, j]).wait()
+
+        @pl.when(step + 1 < steps)
+        def _(j=j):
+            begin(step + 1, j)
+
+        @pl.when(slotted(e))
+        def _(j=j):
             if staged % LANES:
                 stage_ref[buffer, j, :, staged:] = jnp.zeros(
                     (count, deep - staged, width), jnp.bfloat16
@@ -753,11 +756,10 @@
     routes = routes.reshape(rows, own, topk)[order].reshape(tokens, topk)
     my_routes = lax.dynamic_slice_in_dim(routes, col_index * share, share, 0)
     router = jnp.pad(w_router, ((0, 0), (shift, LANES - shift - experts)))
-    same_core = jnp.concatenate(
-        [h_mid] + [from_peer(h_mid, "row", o) for o in range(2, rows, 2)], axis=0
-    )
+    across = [from_peer(h_mid, "row", o) for o in range(2, rows, 2)]
+    same_core = jnp.concatenate([h_mid] + across, axis=0)
     every_h = jnp.concatenate([same_core, from_peer(same_core, "row", 1)], axis=0)
-    migration.send([same_core])
+    migration.send(across)
     part_spec = lambda part: pl.BlockSpec((1, 1, lines, width), lambda e, me: (e, part, 0, 0))
     whole = lambda a: pl.BlockSpec(a.shape, lambda e, me: (0,) * a.ndim)
     gain = moe_gain.reshape(1, width)

time: 246 us -> 246 us (level)
    unnamed x49 -> x59, local copies, waits for them, and re-layouts: 8.98 us -> 9.6 us
where the time goes in v8:
time: 246 us; the launch traced here: 244 us
  waiting for transfers between devices  90.7 us (37%)
  Pallas kernels  89.9 us (37%)
  starting transfers between devices  33 us (13%)
  local copies, waits for them, and re-layouts  16 us (7%)
  matrix products  8.49 us (3%)
  other arithmetic  4.88 us (2%)
    ppermute x17, waiting for transfers between devices, from_peer(): return lax.ppermute(block, axis, [(i, i ^ offset) for i in range(size)])  90.7 us
    pallas_call x2, Pallas kernels, pack(): pl.pallas_call(functools.partial(pack_kernel, rows, span, experts // span...  29.5 us
    pallas_call x2, Pallas kernels, unpack(): pl.pallas_call(functools.partial(unpack_kernel, slot, span), grid_spec=pl...  28.7 us
    ppermute x17, starting transfers between devices, from_peer(): return lax.ppermute(block, axis, [(i, i ^ offset) for i in range(size)])  22.1 us
    pallas_call x2, Pallas kernels, call_plan(): pl.pallas_call(kernel, out_shape=(place, jax.ShapeDtypeStruct((4, up_to(p...  16.6 us
    all_to_all x2, starting transfers between devices, send(): lax.all_to_all(block, 'row', split_axis=0, concat_axis=0, tiled=True)  10.9 us
    unnamed x59, local copies, waits for them, and re-layouts  9.6 us
    pallas_call x1, Pallas kernels, experts_part(): pl.pallas_call(gate_up_kernel, grid_spec=pltpu.PrefetchScalarGridSpec(num...  8.79 us
  transfers between devices with their start and end apart: 19, of which 7 were waited for; matrix products, arithmetic and copies ran while one was open for 10% of the time, Pallas kernels for 23%

profile of v8, /device:TPU:0, one launch (start us, length us, event | category | flops | bytes accessed | tf_op | source)
XLA Modules:
  0.0 244.5 jit_solution(6541336257286136680)
XLA Ops:
  2.4 5.7 %outgoing_plan.1 = (s32[8,1,768]{2,1,0:T(1,128)S(1)}, s32[4,128]{1,0:T(4,128)S(1)}) custom-call(s32[8,5632]{1,0:T(8,128)S(1)} %copy-done.2, s32[8,768]{1,0:T(8,128)S(1)} %pad.11.held_ref), custom_call_target="tpu_custom_call" | custom-call | flops 230686720 | bytes 360448 | tf_op jit(solution)/shard_map/outgoing_plan/pallas_call | solution.py:423
  9.4 10.5 %pack_lines.2.refs_1_ = bf16[8,1,704,512]{3,2,1,0:T(8,128)(2,1)} custom-call(s32[4,128]{1,0:T(4,128)} %copy-done.4, s32[8,1,768]{2,1,0:T(1,128)} %copy-done.1, bf16[8,3,704,512]{3,2,1,0:T(8,128)(2,1)} %bitcast.81), custom_call_target="tpu_custom_call" | custom-call | flops 5444206592 | bytes 11534336 | tf_op jit(solution)/shard_map/pack_lines/pallas_call | solution.py:438
  19.9 5.3 %all-to-all-start = ((bf16[8,1,704,512]{3,2,1,0:T(8,128)(2,1)}), bf16[8,1,704,512]{3,2,1,0:T(8,128)(2,1)}, u32[]{:S(2)}, u32[]{:S(2)}) async-start(bf16[8,1,704,512]{3,2,1,0:T(8,128)(2,1)} %pack_lines.2.refs_1_), calls=%async_computation | async-start | bytes 11534336 | tf_op jit(solution)/shard_map/all_to_all | solution.py:568
  25.3 1.1 fusion.30
  27.7 1.3 copy.144
  29.0 1.5 copy.143
  30.5 1.2 copy.146
  31.7 1.2 copy.145
  33.1 2.0 fusion.33
  35.9 1.2 fusion.32
  42.3 4.8 %collective-permute-start.2 = (f32[8,4224]{1,0:T(8,128)S(1)}, f32[8,4224]{1,0:T(8,128)S(1)}, u32[]{:S(2)}, u32[]{:S(2)}) collective-permute-start(f32[8,4224]{1,0:T(8,128)S(1)} %concatenate.10), channel_id=1, source_target_pairs={{0,3},{1,2},{2,1},{3,0},{4,7},{5,6},{6,5},{7,4},{8,11},{9,10},{10,... | collective-permute-start | bytes 405512 | tf_op jit(solution)/shard_map/ppermute | solution.py:530
  47.7 19.0 %pack_lines.3.refs_2_.refs_0_ = bf16[8,2,704,512]{3,2,1,0:T(8,128)(2,1)} custom-call(s32[4,128]{1,0:T(4,128)} %copy-done.4, s32[8,1,768]{2,1,0:T(1,128)} %copy-done.1, bf16[8,3,704,512]{3,2,1,0:T(8,128)(2,1)} %bitcast.82), custom_call_target="tpu_custom_call" | custom-call | flops 10888413184 | bytes 23068672 | tf_op jit(solution)/shard_map/pack_lines/pallas_call | solution.py:438
  67.3 3.5 %fusion.4.refs_0_ = bf16[8,512]{1,0:T(8,128)(2,1)} fusion(bf16[4096,512]{1,0:T(8,128)(2,1)} %param.20, f32[8,4096]{1,0:T(8,128)S(1)} %fusion.8, f32[8,32]{0,1:T(8,128)S(1)} %copy.126, bf16[8,512]{1,0:T(8,128)(2,1)S(1)} %copy-done.18), kind=kOutput, calls=%fused_computation.9 | convolution fusion | flops 33632256 | bytes 4342784 | tf_op jit(solution)/shard_map/dot_general | solution.py:841
  70.8 1.7 collective-permute-start.3
  72.5 1.5 collective-permute-start.4
  74.3 16.6 %collective-permute-done.3.refs_1_ = bf16[8,512]{1,0:T(8,128)(2,1)S(1)} collective-permute-done((bf16[8,512]{1,0:T(8,128)(2,1)}, bf16[8,512]{1,0:T(8,128)(2,1)S(1)}, u32[]{:S(2)}, u32[]{:S(2)}) %collective-permute-start.3) | collective-permute-done | bytes 8224 | tf_op jit(solution)/shard_map/ppermute | solution.py:530
  92.5 5.6 %all-to-all-start.1 = ((bf16[8,2,704,512]{3,2,1,0:T(8,128)(2,1)}), bf16[8,2,704,512]{3,2,1,0:T(8,128)(2,1)}, u32[]{:S(2)}, u32[]{:S(2)}) async-start(bf16[8,2,704,512]{3,2,1,0:T(8,128)(2,1)} %after.5), calls=%async_computation.1 | async-start | bytes 23068672 | tf_op jit(solution)/shard_map/all_to_all | solution.py:568
  99.5 1.5 collective-permute-done.6
  101.0 8.8 %gate_up.1 = bf16[4,4,16,768]{3,2,1,0:T(8,128)(2,1)S(1)} custom-call(s32[1]{0:T(128)} %bitcast.20.me_ref, bf16[64,512]{1,0:T(8,128)(2,1)S(1)} %constant_dynamic-update-slice_fusion.h_ref, bf16[1,512]{1,0:T(2,128)(2,1)S(1)} %reshape.90.gain_ref, bf16[512,128]{1,0:T(8,128)(2,1)S(1)} %pad.12.router_ref, s32[64,2]{1,0:T(8,128)S(1)} %bitcast.78, ...), custom_call_target="tpu_custom_call" | custom-call | flops 738197504 | bytes 11534336 | tf_op jit(solution)/shard_map/gate_up/pallas_call | solution.py:766
  109.9 2.3 collective-permute-start.7
  112.1 2.6 %collective-permute-start.8 = (bf16[4,16,768]{2,1,0:T(8,128)(2,1)S(1)}, bf16[4,16,768]{2,1,0:T(8,128)(2,1)S(1)}, u32[]{:S(2)}, u32[]{:S(2)}) collective-permute-start(bf16[4,16,768]{2,1,0:T(8,128)(2,1)S(1)} %get-tuple-element.19), channel_id=1, source_target_pairs={{0,2},{1,3},{2,0},{3,1},{4,6},{5,7},{6,4},{7,5},{8,10},{9,11},{10,... | collective-permute-start | bytes 294920 | tf_op jit(solution)/shard_map/ppermute | solution.py:530
  115.4 7.4 %collective-permute-done.8.refs_2_ = bf16[4,16,768]{2,1,0:T(8,128)(2,1)S(1)} collective-permute-done((bf16[4,16,768]{2,1,0:T(8,128)(2,1)S(1)}, bf16[4,16,768]{2,1,0:T(8,128)(2,1)S(1)}, u32[]{:S(2)}, u32[]{:S(2)}) %collective-permute-start.8) | collective-permute-done | bytes 98336 | tf_op jit(solution)/shard_map/ppermute | solution.py:530
  123.0 1.9 collective-permute-start.10
  124.9 1.3 collective-permute-start.11
  126.2 1.2 collective-permute-start.12
  128.3 10.8 %incoming_plan.1 = (bf16[8,2,704,128]{3,2,1,0:T(8,128)(2,1)S(1)}, s32[4,128]{1,0:T(4,128)S(1)}) custom-call(s32[8,5632]{1,0:T(8,128)S(1)} %copy-done.3, s32[8,768]{1,0:T(8,128)S(1)} %pad.13.wanted_ref), custom_call_target="tpu_custom_call" | custom-call | flops 230686720 | bytes 360448 | tf_op jit(solution)/shard_map/incoming_plan/pallas_call | solution.py:423
  139.2 6.1 %down.1.refs_0_ = f32[64,512]{1,0:T(8,128)S(1)} custom-call(s32[1]{0:T(128)} %bitcast.20.me_ref, s32[64,2]{1,0:T(8,128)S(1)} %bitcast.80, bf16[2,16,768]{2,1,0:T(8,128)(2,1)S(1)} %activate.1.refs_0_, bf16[2,16,768]{2,1,0:T(8,128)(2,1)S(1)} %collective-permute-done.10.refs_1_, bf16[2,16,768]{2,1,0:T(8,128)(2,1)S(1)} %collective-permute-done.11.refs_2_, ...), custom_call_target="tpu_custom_call" | custom-call | flops 369098752 | bytes 5767168 | tf_op jit(solution)/shard_map/down/pallas_call | solution.py:793
  146.0 11.2 %unpack_lines.2.refs_1_.rest_0_ = bf16[8,3,704,512]{3,2,1,0:T(8,128)(2,1)} custom-call(s32[4,128]{1,0:T(4,128)S(1)} %get-tuple-element.8.plan_ref, bf16[8,2,704,128]{3,2,1,0:T(8,128)(2,1)S(1)} %get-tuple-element.9.place_ref, bf16[8,1,704,512]{3,2,1,0:T(8,128)(2,1)} %all-to-all-done.block_ref), custom_call_target="tpu_custom_call" | custom-call | flops 5905580032 | bytes 11534336 | tf_op jit(solution)/shard_map/unpack_lines/pallas_call | solution.py:480
  158.0 1.3 collective-permute-done.13
  160.1 2.7 %collective-permute-start.16 = (f32[8,512]{1,0:T(8,128)S(1)}, f32[8,512]{1,0:T(8,128)S(1)}, u32[]{:S(2)}, u32[]{:S(2)}) collective-permute-start(f32[8,512]{1,0:T(8,128)S(1)} %get-tuple-element.23), channel_id=1, source_target_pairs={{0,24},{4,28},{8,16},{12,20},{16,8},{20,12},{24,0},{28,4},{1,25},{... | collective-permute-start | bytes 49160 | tf_op jit(solution)/shard_map/ppermute | solution.py:530
  163.7 62.4 %collective-permute-done.16 = f32[8,512]{1,0:T(8,128)S(1)} collective-permute-done((f32[8,512]{1,0:T(8,128)S(1)}, f32[8,512]{1,0:T(8,128)S(1)}, u32[]{:S(2)}, u32[]{:S(2)}) %collective-permute-start.16) | collective-permute-done | bytes 16416 | tf_op jit(solution)/shard_map/ppermute | solution.py:530
  226.7 17.5 %unpack_lines.3 = bf16[8,3,704,512]{3,2,1,0:T(8,128)(2,1)} custom-call(s32[4,128]{1,0:T(4,128)S(1)} %get-tuple-element.8.plan_ref, bf16[8,2,704,128]{3,2,1,0:T(8,128)(2,1)S(1)} %get-tuple-element.9.place_ref, bf16[8,2,704,512]{3,2,1,0:T(8,128)(2,1)} %all-to-all-done.1.block_ref, ...), custom_call_target="tpu_custom_call", output_to_operand_aliasing={{}: (3, {})} | custom-call | flops 11811160064 | bytes 23068672 | tf_op jit(solution)/shard_map/unpack_lines/pallas_call | solution.py:480
  (128 shorter events, 20.2 us)
Async XLA Ops:
  19.9 72.6 %all-to-all-start = ((bf16[8,1,704,512]{3,2,1,0:T(8,128)(2,1)}), bf16[8,1,704,512]{3,2,1,0:T(8,128)(2,1)}, u32[]{:S(2)}, u32[]{:S(2)}) async-start(bf16[8,1,704,512]{3,2,1,0:T(8,128)(2,1)} %pack_lines.2.refs_1_), calls=%async_computation | async-start | bytes 11534336 | tf_op jit(solution)/shard_map/all_to_all | solution.py:568
  27.6 5.4 %copy-start.23 = (s32[8]{0:T(128)S(1)}, s32[8]{0:T(128)}, u32[]{:S(2)}) copy-start(s32[8]{0:T(128)} %param.19) | copy-start | bytes 100
  31.6 10.1 %copy-start.7 = (bf16[1,1,256,2048]{2,3,1,0:T(8,128)(2,1)S(1)}, bf16[1,1,256,2048]{2,3,1,0:T(8,128)(2,1)}, u32[]{:S(2)}) copy-start(bf16[1,1,256,2048]{2,3,1,0:T(8,128)(2,1)} %copy.144) | copy-start | bytes 3145732
  32.9 7.8 %copy-start.8 = (bf16[32,8,16,128]{3,2,1,0:T(8,128)(2,1)S(1)}, bf16[32,8,16,128]{3,2,1,0:T(8,128)(2,1)}, u32[]{:S(2)}) copy-start(bf16[32,8,16,128]{3,2,1,0:T(8,128)(2,1)} %copy.146) | copy-start | bytes 3145732
  42.3 25.0 %copy-start.18 = (bf16[8,512]{1,0:T(8,128)(2,1)S(1)}, bf16[8,512]{1,0:T(8,128)(2,1)}, u32[]{:S(2)}) copy-start(bf16[8,512]{1,0:T(8,128)(2,1)} %param.14) | copy-start | bytes 24580
  42.3 24.5 %collective-permute-start.2 = (f32[8,4224]{1,0:T(8,128)S(1)}, f32[8,4224]{1,0:T(8,128)S(1)}, u32[]{:S(2)}, u32[]{:S(2)}) collective-permute-start(f32[8,4224]{1,0:T(8,128)S(1)} %concatenate.10), channel_id=1, source_target_pairs={{0,3},{1,2},{2,1},{3,0},{4,7},{5,6},{6,5},{7,4},{8,11},{9,10},{10,... | collective-permute-start | bytes 405512 | tf_op jit(solution)/shard_map/ppermute | solution.py:530
  47.1 19.7 %collective-permute-start.1 = (f32[8,4224]{1,0:T(8,128)S(1)}, f32[8,4224]{1,0:T(8,128)S(1)}, u32[]{:S(2)}, u32[]{:S(2)}) collective-permute-start(f32[8,4224]{1,0:T(8,128)S(1)} %concatenate.10), channel_id=1, source_target_pairs={{0,2},{1,3},{2,0},{3,1},{4,6},{5,7},{6,4},{7,5},{8,10},{9,11},{10,... | collective-permute-start | bytes 405512 | tf_op jit(solution)/shard_map/ppermute | solution.py:530
  47.1 19.7 %collective-permute-start = (f32[8,4224]{1,0:T(8,128)S(1)}, f32[8,4224]{1,0:T(8,128)S(1)}, u32[]{:S(2)}, u32[]{:S(2)}) collective-permute-start(f32[8,4224]{1,0:T(8,128)S(1)} %concatenate.10), channel_id=1, source_target_pairs={{0,1},{1,0},{2,3},{3,2},{4,5},{5,4},{6,7},{7,6},{8,9},{9,8},{10,11... | collective-permute-start | bytes 405512 | tf_op jit(solution)/shard_map/ppermute | solution.py:530
  70.8 20.1 %collective-permute-start.3 = (bf16[8,512]{1,0:T(8,128)(2,1)}, bf16[8,512]{1,0:T(8,128)(2,1)S(1)}, u32[]{:S(2)}, u32[]{:S(2)}) collective-permute-start(bf16[8,512]{1,0:T(8,128)(2,1)} %after.3), channel_id=1, source_target_pairs={{0,8},{4,12},{8,0},{12,4},{16,24},{20,28},{24,16},{28,20},{1,9},{5... | collective-permute-start | bytes 24584 | tf_op jit(solution)/shard_map/ppermute | solution.py:530
  72.5 18.4 %collective-permute-start.4 = (bf16[8,512]{1,0:T(8,128)(2,1)}, bf16[8,512]{1,0:T(8,128)(2,1)S(1)}, u32[]{:S(2)}, u32[]{:S(2)}) collective-permute-start(bf16[8,512]{1,0:T(8,128)(2,1)} %after.3), channel_id=1, source_target_pairs={{0,16},{4,20},{8,24},{12,28},{16,0},{20,4},{24,8},{28,12},{1,17},{... | collective-permute-start | bytes 24584 | tf_op jit(solution)/shard_map/ppermute | solution.py:530
  74.0 17.8 %collective-permute-start.5 = (bf16[8,512]{1,0:T(8,128)(2,1)}, bf16[8,512]{1,0:T(8,128)(2,1)S(1)}, u32[]{:S(2)}, u32[]{:S(2)}) collective-permute-start(bf16[8,512]{1,0:T(8,128)(2,1)} %after.3), channel_id=1, source_target_pairs={{0,24},{4,28},{8,16},{12,20},{16,8},{20,12},{24,0},{28,4},{1,25},{... | collective-permute-start | bytes 24584 | tf_op jit(solution)/shard_map/ppermute | solution.py:530
  92.4 5.7 %copy-start.21 = (s32[64,2]{0,1:T(2,128)S(1)}, s32[64,2]{0,1:T(2,128)}, u32[]{:S(2)}) copy-start(s32[64,2]{0,1:T(2,128)} %param.26) | copy-start | bytes 1540
  92.4 5.8 %copy-start.24 = (s32[8]{0:T(128)S(1)}, s32[8]{0:T(128)}, u32[]{:S(2)}) copy-start(s32[8]{0:T(128)} %constant.41.clone) | copy-start | bytes 100
  92.4 6.5 %copy-start.22 = (bf16[512]{0:T(512)(128)(2,1)S(1)}, bf16[512]{0:T(512)(128)(2,1)}, u32[]{:S(2)}) copy-start(bf16[512]{0:T(512)(128)(2,1)} %param.21) | copy-start | bytes 3076
  92.4 6.5 %copy-start.19 = (bf16[512,8]{0,1:T(8,128)(2,1)S(1)}, bf16[512,8]{0,1:T(8,128)(2,1)}, u32[]{:S(2)}) copy-start(bf16[512,8]{0,1:T(8,128)(2,1)} %param.22) | copy-start | bytes 24580
  92.4 6.8 %copy-start.9 = (bf16[8,512]{1,0:T(8,128)(2,1)S(1)}, bf16[8,512]{1,0:T(8,128)(2,1)}, u32[]{:S(2)}) copy-start(bf16[8,512]{1,0:T(8,128)(2,1)} %after.3) | copy-start | bytes 24580
  92.4 6.8 %copy-start.11 = (bf16[8,512]{1,0:T(8,128)(2,1)S(1)}, bf16[8,512]{1,0:T(8,128)(2,1)}, u32[]{:S(2)}) copy-start(bf16[8,512]{1,0:T(8,128)(2,1)} %copy-done.10) | copy-start | bytes 24580
  92.4 6.8 %copy-start.13 = (bf16[8,512]{1,0:T(8,128)(2,1)S(1)}, bf16[8,512]{1,0:T(8,128)(2,1)}, u32[]{:S(2)}) copy-start(bf16[8,512]{1,0:T(8,128)(2,1)} %copy-done.12) | copy-start | bytes 24580
  92.5 6.8 %copy-start.15 = (bf16[8,512]{1,0:T(8,128)(2,1)S(1)}, bf16[8,512]{1,0:T(8,128)(2,1)}, u32[]{:S(2)}) copy-start(bf16[8,512]{1,0:T(8,128)(2,1)} %copy-done.14) | copy-start | bytes 24580
  92.5 134.2 %all-to-all-start.1 = ((bf16[8,2,704,512]{3,2,1,0:T(8,128)(2,1)}), bf16[8,2,704,512]{3,2,1,0:T(8,128)(2,1)}, u32[]{:S(2)}, u32[]{:S(2)}) async-start(bf16[8,2,704,512]{3,2,1,0:T(8,128)(2,1)} %after.5), calls=%async_computation.1 | async-start | bytes 23068672 | tf_op jit(solution)/shard_map/all_to_all | solution.py:568
  99.3 1.7 collective-permute-start.6
  101.0 27.3 %copy-start.3 = (s32[8,5632]{1,0:T(8,128)S(1)}, s32[8,5632]{1,0:T(8,128)}, u32[]{:S(2)}) copy-start(s32[8,5632]{1,0:T(8,128)} %old_ref.1) | copy-start | bytes 540676
  109.9 5.6 %collective-permute-start.7 = (bf16[4,16,768]{2,1,0:T(8,128)(2,1)S(1)}, bf16[4,16,768]{2,1,0:T(8,128)(2,1)S(1)}, u32[]{:S(2)}, u32[]{:S(2)}) collective-permute-start(bf16[4,16,768]{2,1,0:T(8,128)(2,1)S(1)} %get-tuple-element.20), channel_id=1, source_target_pairs={{0,1},{1,0},{2,3},{3,2},{4,5},{5,4},{6,7},{7,6},{8,9},{9,8},{10,11... | collective-permute-start | bytes 294920 | tf_op jit(solution)/shard_map/ppermute | solution.py:530
  112.1 10.7 %collective-permute-start.8 = (bf16[4,16,768]{2,1,0:T(8,128)(2,1)S(1)}, bf16[4,16,768]{2,1,0:T(8,128)(2,1)S(1)}, u32[]{:S(2)}, u32[]{:S(2)}) collective-permute-start(bf16[4,16,768]{2,1,0:T(8,128)(2,1)S(1)} %get-tuple-element.19), channel_id=1, source_target_pairs={{0,2},{1,3},{2,0},{3,1},{4,6},{5,7},{6,4},{7,5},{8,10},{9,11},{10,... | collective-permute-start | bytes 294920 | tf_op jit(solution)/shard_map/ppermute | solution.py:530
  114.7 8.0 %collective-permute-start.9 = (bf16[4,16,768]{2,1,0:T(8,128)(2,1)S(1)}, bf16[4,16,768]{2,1,0:T(8,128)(2,1)S(1)}, u32[]{:S(2)}, u32[]{:S(2)}) collective-permute-start(bf16[4,16,768]{2,1,0:T(8,128)(2,1)S(1)} %get-tuple-element.18), channel_id=1, source_target_pairs={{0,3},{1,2},{2,1},{3,0},{4,7},{5,6},{6,5},{7,4},{8,11},{9,10},{10,... | collective-permute-start | bytes 294920 | tf_op jit(solution)/shard_map/ppermute | solution.py:530
  123.0 16.2 %collective-permute-start.10 = (bf16[2,16,768]{2,1,0:T(8,128)(2,1)S(1)}, bf16[2,16,768]{2,1,0:T(8,128)(2,1)S(1)}, u32[]{:S(2)}, u32[]{:S(2)}) collective-permute-start(bf16[2,16,768]{2,1,0:T(8,128)(2,1)S(1)} %activate.1.refs_0_), channel_id=1, source_target_pairs={{0,1},{1,0},{2,3},{3,2},{4,5},{5,4},{6,7},{7,6},{8,9},{9,8},{10,11... | collective-permute-start | bytes 147464 | tf_op jit(solution)/shard_map/ppermute | solution.py:530
  124.9 14.2 %collective-permute-start.11 = (bf16[2,16,768]{2,1,0:T(8,128)(2,1)S(1)}, bf16[2,16,768]{2,1,0:T(8,128)(2,1)S(1)}, u32[]{:S(2)}, u32[]{:S(2)}) collective-permute-start(bf16[2,16,768]{2,1,0:T(8,128)(2,1)S(1)} %activate.1.refs_0_), channel_id=1, source_target_pairs={{0,2},{1,3},{2,0},{3,1},{4,6},{5,7},{6,4},{7,5},{8,10},{9,11},{10,... | collective-permute-start | bytes 147464 | tf_op jit(solution)/shard_map/ppermute | solution.py:530
  126.2 12.9 %collective-permute-start.12 = (bf16[2,16,768]{2,1,0:T(8,128)(2,1)S(1)}, bf16[2,16,768]{2,1,0:T(8,128)(2,1)S(1)}, u32[]{:S(2)}, u32[]{:S(2)}) collective-permute-start(bf16[2,16,768]{2,1,0:T(8,128)(2,1)S(1)} %activate.1.refs_0_), channel_id=1, source_target_pairs={{0,3},{1,2},{2,1},{3,0},{4,7},{5,6},{6,5},{7,4},{8,11},{9,10},{10,... | collective-permute-start | bytes 147464 | tf_op jit(solution)/shard_map/ppermute | solution.py:530
  158.0 1.3 collective-permute-start.13
  160.1 65.9 %collective-permute-start.16 = (f32[8,512]{1,0:T(8,128)S(1)}, f32[8,512]{1,0:T(8,128)S(1)}, u32[]{:S(2)}, u32[]{:S(2)}) collective-permute-start(f32[8,512]{1,0:T(8,128)S(1)} %get-tuple-element.23), channel_id=1, source_target_pairs={{0,24},{4,28},{8,16},{12,20},{16,8},{20,12},{24,0},{28,4},{1,25},{... | collective-permute-start | bytes 49160 | tf_op jit(solution)/shard_map/ppermute | solution.py:530
  162.8 63.3 %collective-permute-start.15 = (f32[8,512]{1,0:T(8,128)S(1)}, f32[8,512]{1,0:T(8,128)S(1)}, u32[]{:S(2)}, u32[]{:S(2)}) collective-permute-start(f32[8,512]{1,0:T(8,128)S(1)} %get-tuple-element.24), channel_id=1, source_target_pairs={{0,16},{4,20},{8,24},{12,28},{16,0},{20,4},{24,8},{28,12},{1,17},{... | collective-permute-start | bytes 49160 | tf_op jit(solution)/shard_map/ppermute | solution.py:530
  163.4 62.7 %collective-permute-start.14 = (f32[8,512]{1,0:T(8,128)S(1)}, f32[8,512]{1,0:T(8,128)S(1)}, u32[]{:S(2)}, u32[]{:S(2)}) collective-permute-start(f32[8,512]{1,0:T(8,128)S(1)} %get-tuple-element.22), channel_id=1, source_target_pairs={{0,8},{4,12},{8,0},{12,4},{16,24},{20,28},{24,16},{28,20},{1,9},{5... | collective-permute-start | bytes 49160 | tf_op jit(solution)/shard_map/ppermute | solution.py:530
  (12 other events, 19.5 us)

commit v9 on v8

--- a/solution.py
+++ b/solution.py
@@ -134,28 +134,32 @@
 
 
 def outgoing_kernel(lines, rows, new_ref, held_ref, stack_ref, plan_ref):
-    experts = new_ref.shape[0]
     width = held_ref.shape[1]
-    real = iota((1, width), 1) < lines
-    hits = []
     full = new_ref.shape[1]
     numbers = numbers_for(full)
     slot = iota((64, full), 1).astype(jnp.float32)
     values = (jnp.floor((slot + 0.5) * (1.0 / lines)).astype(jnp.bfloat16),)
+    hits = []
+    reals = []
     for (peer,) in look_up_all(new_ref, held_ref, numbers, values):
         peer = peer.astype(jnp.int32)
-        hits.append(jnp.where((iota((rows, width), 0) == peer) & real, 1.0, 0.0))
+        for first in range(0, width, BLOCK):
+            real = iota((1, BLOCK), 1) < lines - first
+            here = peer[:, first : first + BLOCK]
+            hits.append(jnp.where((iota((rows, BLOCK), 0) == here) & real, 1.0, 0.0))
+            reals.append(real)
+    blocks = len(hits)
     hits = jnp.concatenate(hits, axis=0)
-    until = ones_where(iota((width, width), 0) <= iota((width, width), 1))
+    until = ones_where(iota((BLOCK, BLOCK), 0) <= iota((BLOCK, BLOCK), 1))
     ranks = jnp.dot(hits.astype(jnp.bfloat16), until, preferred_element_type=jnp.float32)
-    counts = jnp.broadcast_to(jnp.sum(hits, axis=1, keepdims=True), (experts * rows, LANES))
-    start, lead, tiles, base = segment_plan(counts, experts, rows)
+    counts = jnp.broadcast_to(jnp.sum(hits, axis=1, keepdims=True), (blocks * rows, LANES))
+    start, lead, tiles, base = segment_plan(counts, blocks, rows)
     write_plan(plan_ref, (lead, tiles, base, start - lead * TILE))
     offset = (base * TILE + start - lead * TILE - 1.0)[:, :1]
     placed = hits * (ranks + offset)
-    for e in range(experts):
-        row = jnp.sum(placed[e * rows : (e + 1) * rows], axis=0, keepdims=True)
-        stack_ref[e] = jnp.where(real, row, -1.0).astype(jnp.int32)
+    for n, real in enumerate(reals):
+        row = jnp.sum(placed[n * rows : (n + 1) * rows], axis=0, keepdims=True)
+        stack_ref[n] = jnp.where(real, row, -1.0).astype(jnp.int32)
 
 
 def incoming_kernel(lines, rows, block_tiles, slot, old_ref, wanted_ref, stack_ref, plan_ref):
@@ -211,7 +215,8 @@
         stack_ref[e, 1] = block.astype(jnp.bfloat16)
 
 
-STRAIGHT = 8
+BLOCK = 256
+STRAIGHT = 4
 SLOT = 7
 
 
@@ -229,25 +234,34 @@
     def _():
         number_ref[...] = counting(number_ref.shape, 0)
 
+    blocks = len(stages) // span
+
     def entry(n, j, d):
-        return plan_ref[n, (step * span + j) * rows + d]
-
-    usual = min(deep, up_to(lines + rows * TILE, TILE))
+        return plan_ref[n, (step * len(stages) + j) * rows + d]
+
+    usual = min(deep, up_to(min(lines, BLOCK) + rows * TILE, TILE))
 
     def move(j, begin, end):
-        place = place_ref[j][:, :lines]
+        first = j % blocks * BLOCK
+        last = min(first + BLOCK, lines)
+        place = place_ref[j][:, : last - first]
         onehot = [
-            equal_ones(number_ref[: min(256, end - row)], within(place - begin, (row - begin) // 256))
+            equal_ones(
+                number_ref[: min(256, end - row), : last - first],
+                within(place - begin, (row - begin) // 256),
+            )
             for row in range(begin, end, 256)
         ]
         stages[j][begin:end] = jnp.dot(
-            jnp.concatenate(onehot, axis=0), lines_ref[j, 0], preferred_element_type=jnp.float32
+            jnp.concatenate(onehot, axis=0),
+            lines_ref[j // blocks, 0, first:last],
+            preferred_element_type=jnp.float32,
         ).astype(jnp.bfloat16)
 
-    for j in range(span):
+    for j in range(len(stages)):
         move(j, 0, usual)
     if usual < deep:
-        for j in range(span):
+        for j in range(len(stages)):
             used = entry(1, j, rows - 1) + entry(2, j, rows - 1)
 
             @pl.when(used * TILE > usual)
@@ -303,7 +317,7 @@
 
     def final_by(n):
         after_step, _, end = chunks[n]
-        first = (after_step + 1) * span * rows
+        first = (after_step + 1) * len(stages) * rows
         least = functools.reduce(jnp.minimum, [plan_ref[0, first + d] for d in range(rows)])
         return least * TILE >= end
 
@@ -435,22 +449,23 @@
     experts, _, lines, width = expert_lines.shape
     first, count = piece
     span = 2 - experts % 2
+    stages = span * place.shape[0] // experts
     return pl.pallas_call(
         functools.partial(pack_kernel, rows, span, experts // span),
         grid_spec=pltpu.PrefetchScalarGridSpec(
             num_scalar_prefetch=1,
             grid=(count, experts // span),
             in_specs=[
-                pl.BlockSpec((span, 1, place.shape[2]), lambda p, e, plan: (e, 0, 0)),
+                pl.BlockSpec((stages, 1, BLOCK), lambda p, e, plan: (e, 0, 0)),
                 pl.BlockSpec((span, 1, lines, width), lambda p, e, plan: (e, first + p, 0, 0)),
             ],
             out_specs=pl.BlockSpec(memory_space=pltpu.HBM),
             scratch_shapes=[
                 pltpu.VMEM((rows, block_rows + STRAIGHT * TILE, width), jnp.bfloat16),
-                pltpu.VMEM((256, lines), jnp.bfloat16),
+                pltpu.VMEM((256, BLOCK), jnp.bfloat16),
                 pltpu.SemaphoreType.DMA((experts // span,)),
             ]
-            + [pltpu.VMEM((deep + STRAIGHT * TILE, width), jnp.bfloat16)] * span,
+            + [pltpu.VMEM((deep + STRAIGHT * TILE, width), jnp.bfloat16)] * stages,
         ),
         out_shape=jax.ShapeDtypeStruct((rows, count, block_rows, width), jnp.bfloat16),
         compiler_params=pltpu.CompilerParams(vmem_limit_bytes=PACK_LIMIT),
@@ -534,18 +549,20 @@
     def __init__(self, expert_lines, old_lines, new_lines):
         rows = lax.axis_size("row")
         experts, parts, lines, width = expert_lines.shape
-        padded = up_to(lines, LANES)
+        padded = up_to(lines, BLOCK)
+        blocks = experts * (padded // BLOCK)
         block_rows = up_to(experts * lines // rows, TILE)
         pairs = experts * rows
         compact = up_to(lines + 2 * (TILE - 1) * rows, TILE)
+        deep = up_to(min(lines, BLOCK) + 2 * (TILE - 1) * rows, TILE)
         self.slot = min(SLOT, block_rows // TILE)
         self.deep = up_to(max(compact, rows * self.slot * TILE), 256)
         self.shape = expert_lines.shape
         self.pieces = [(parts - 1, 1), (0, parts - 1)]
         out_place, out_plan = call_plan(
             functools.partial(outgoing_kernel, lines, rows), "outgoing_plan",
-            new_lines, own_ids(old_lines, lines, padded), pairs,
-            jax.ShapeDtypeStruct((experts, 1, padded), jnp.int32),
+            new_lines, own_ids(old_lines, lines, padded), blocks * rows,
+            jax.ShapeDtypeStruct((blocks, 1, BLOCK), jnp.int32),
         )
         self.in_place, self.in_plan = call_plan(
             functools.partial(incoming_kernel, lines, rows, block_rows // TILE, self.slot),
@@ -554,7 +571,7 @@
             jax.ShapeDtypeStruct((experts, 2, lines, LANES), jnp.bfloat16),
         )
         self.packed = [
-            pack(expert_lines, out_place, out_plan, piece, rows, block_rows, compact)
+            pack(expert_lines, out_place, out_plan, piece, rows, block_rows, deep)
             for piece in self.pieces
         ]
         self.arrived = []

time: 246 us -> 245 us (level)
  waiting for transfers between devices: 90.7 us -> 93.9 us
  Pallas kernels: 89.9 us -> 87.4 us
    unnamed x59 -> x51, local copies, waits for them, and re-layouts: 9.6 us -> 6.1 us
    ppermute x17, waiting for transfers between devices: 90.7 us -> 93.9 us  [from_peer(): return lax.ppermute(block, axis, [(i, i ^ offset) for i in range(size)])]
    pallas_call x2, Pallas kernels: 29.5 us -> 27 us  [pack(): pl.pallas_call(functools.partial(pack_kernel, rows, span, experts // span...]
  transfers between devices with their start and end apart: 19 -> 19, of which waited for: 7 -> 7; matrix products, arithmetic and copies ran while one was open for 10% -> 10% of each run, Pallas kernels for 23% -> 22%
where the time goes in v9:
time: 245 us; the launch traced here: 243 us
  waiting for transfers between devices  93.9 us (38%)
  Pallas kernels  87.4 us (36%)
  starting transfers between devices  32.8 us (13%)
  local copies, waits for them, and re-layouts  14.7 us (6%)
  matrix products  8.46 us (3%)
  other arithmetic  4.9 us (2%)
    ppermute x17, waiting for transfers between devices, from_peer(): return lax.ppermute(block, axis, [(i, i ^ offset) for i in range(size)])  93.9 us
    pallas_call x2, Pallas kernels, unpack(): pl.pallas_call(functools.partial(unpack_kernel, slot, span), grid_spec=pl...  28.7 us
    pallas_call x2, Pallas kernels, pack(): pl.pallas_call(functools.partial(pack_kernel, rows, span, experts // span...  27 us
    ppermute x17, starting transfers between devices, from_peer(): return lax.ppermute(block, axis, [(i, i ^ offset) for i in range(size)])  22.2 us
    pallas_call x2, Pallas kernels, call_plan(): pl.pallas_call(kernel, out_shape=(place, jax.ShapeDtypeStruct((4, up_to(p...  16.6 us
    all_to_all x2, starting transfers between devices, send(): lax.all_to_all(block, 'row', split_axis=0, concat_axis=0, tiled=True)  10.6 us
    pallas_call x1, Pallas kernels, experts_part(): pl.pallas_call(gate_up_kernel, grid_spec=pltpu.PrefetchScalarGridSpec(num...  8.79 us
    pallas_call x1, Pallas kernels, experts_part(): pl.pallas_call(down_kernel, grid_spec=pltpu.PrefetchScalarGridSpec(num_sc...  6.14 us
  transfers between devices with their start and end apart: 19, of which 7 were waited for; matrix products, arithmetic and copies ran while one was open for 10% of the time, Pallas kernels for 22%

profile of v9, /device:TPU:0, one launch (start us, length us, event | category | flops | bytes accessed | tf_op | source)
XLA Modules:
  0.0 243.5 jit_solution(8228898119068370636)
XLA Ops:
  2.4 5.8 %outgoing_plan.1 = (s32[24,1,256]{2,1,0:T(1,128)S(1)}, s32[4,256]{1,0:T(4,128)S(1)}) custom-call(s32[8,5632]{1,0:T(8,128)S(1)} %copy-done.3, s32[8,768]{1,0:T(8,128)S(1)} %pad.11.held_ref), custom_call_target="tpu_custom_call" | custom-call | flops 230686720 | bytes 360448 | tf_op jit(solution)/shard_map/outgoing_plan/pallas_call | solution.py:437
  9.4 9.7 %pack_lines.2.refs_1_ = bf16[8,1,704,512]{3,2,1,0:T(8,128)(2,1)} custom-call(s32[4,256]{1,0:T(4,128)} %copy-done.2, s32[24,1,256]{2,1,0:T(1,128)} %copy-done.1, bf16[8,3,704,512]{3,2,1,0:T(8,128)(2,1)} %bitcast.81), custom_call_target="tpu_custom_call" | custom-call | flops 2860515328 | bytes 11534336 | tf_op jit(solution)/shard_map/pack_lines/pallas_call | solution.py:453
  19.1 5.0 %all-to-all-start = ((bf16[8,1,704,512]{3,2,1,0:T(8,128)(2,1)}), bf16[8,1,704,512]{3,2,1,0:T(8,128)(2,1)}, u32[]{:S(2)}, u32[]{:S(2)}) async-start(bf16[8,1,704,512]{3,2,1,0:T(8,128)(2,1)} %pack_lines.2.refs_1_), calls=%async_computation | async-start | bytes 11534336 | tf_op jit(solution)/shard_map/all_to_all | solution.py:585
  24.1 1.7 fusion.30
  26.9 1.7 fusion.29
  28.8 1.2 copy.145
  30.6 2.0 fusion.33
  33.4 1.2 fusion.32
  36.5 1.1 fusion.25
  38.1 1.1 fusion.5
  39.8 5.0 %collective-permute-start.2 = (f32[8,4224]{1,0:T(8,128)S(1)}, f32[8,4224]{1,0:T(8,128)S(1)}, u32[]{:S(2)}, u32[]{:S(2)}) collective-permute-start(f32[8,4224]{1,0:T(8,128)S(1)} %concatenate.10), channel_id=1, source_target_pairs={{0,3},{1,2},{2,1},{3,0},{4,7},{5,6},{6,5},{7,4},{8,11},{9,10},{10,... | collective-permute-start | bytes 405512 | tf_op jit(solution)/shard_map/ppermute | solution.py:545
  45.4 17.3 %pack_lines.3.refs_2_.refs_0_ = bf16[8,2,704,512]{3,2,1,0:T(8,128)(2,1)} custom-call(s32[4,256]{1,0:T(4,128)} %copy-done.2, s32[24,1,256]{2,1,0:T(1,128)} %copy-done.1, bf16[8,3,704,512]{3,2,1,0:T(8,128)(2,1)} %bitcast.82), custom_call_target="tpu_custom_call" | custom-call | flops 5721030656 | bytes 23068672 | tf_op jit(solution)/shard_map/pack_lines/pallas_call | solution.py:453
  63.2 3.5 %fusion.4.refs_0_ = bf16[8,512]{1,0:T(8,128)(2,1)} fusion(bf16[4096,512]{1,0:T(8,128)(2,1)} %param.20, f32[8,4096]{1,0:T(8,128)S(1)} %fusion.8, f32[8,32]{0,1:T(8,128)S(1)} %copy.126, bf16[8,512]{1,0:T(8,128)(2,1)S(1)} %copy-done.14), kind=kOutput, calls=%fused_computation.9 | convolution fusion | flops 33632256 | bytes 4342784 | tf_op jit(solution)/shard_map/dot_general | solution.py:858
  66.7 1.7 collective-permute-start.3
  68.4 1.1 collective-permute-start.4
  70.2 19.8 %collective-permute-done.3.refs_1_ = bf16[8,512]{1,0:T(8,128)(2,1)S(1)} collective-permute-done((bf16[8,512]{1,0:T(8,128)(2,1)}, bf16[8,512]{1,0:T(8,128)(2,1)S(1)}, u32[]{:S(2)}, u32[]{:S(2)}) %collective-permute-start.3) | collective-permute-done | bytes 8224 | tf_op jit(solution)/shard_map/ppermute | solution.py:545
  91.5 5.6 %all-to-all-start.1 = ((bf16[8,2,704,512]{3,2,1,0:T(8,128)(2,1)}), bf16[8,2,704,512]{3,2,1,0:T(8,128)(2,1)}, u32[]{:S(2)}, u32[]{:S(2)}) async-start(bf16[8,2,704,512]{3,2,1,0:T(8,128)(2,1)} %after.5), calls=%async_computation.1 | async-start | bytes 23068672 | tf_op jit(solution)/shard_map/all_to_all | solution.py:585
  98.5 1.5 collective-permute-done.6
  100.0 8.8 %gate_up.1 = bf16[4,4,16,768]{3,2,1,0:T(8,128)(2,1)S(1)} custom-call(s32[1]{0:T(128)} %bitcast.20.me_ref, bf16[64,512]{1,0:T(8,128)(2,1)S(1)} %constant_dynamic-update-slice_fusion.h_ref, bf16[1,512]{1,0:T(2,128)(2,1)S(1)} %reshape.90.gain_ref, bf16[512,128]{1,0:T(8,128)(2,1)S(1)} %pad.12.router_ref, s32[64,2]{1,0:T(8,128)S(1)} %bitcast.78, ...), custom_call_target="tpu_custom_call" | custom-call | flops 738197504 | bytes 11534336 | tf_op jit(solution)/shard_map/gate_up/pallas_call | solution.py:783
  108.9 2.3 collective-permute-start.7
  111.2 2.6 %collective-permute-start.8 = (bf16[4,16,768]{2,1,0:T(8,128)(2,1)S(1)}, bf16[4,16,768]{2,1,0:T(8,128)(2,1)S(1)}, u32[]{:S(2)}, u32[]{:S(2)}) collective-permute-start(bf16[4,16,768]{2,1,0:T(8,128)(2,1)S(1)} %get-tuple-element.19), channel_id=1, source_target_pairs={{0,2},{1,3},{2,0},{3,1},{4,6},{5,7},{6,4},{7,5},{8,10},{9,11},{10,... | collective-permute-start | bytes 294920 | tf_op jit(solution)/shard_map/ppermute | solution.py:545
  114.5 7.4 %collective-permute-done.8.refs_2_ = bf16[4,16,768]{2,1,0:T(8,128)(2,1)S(1)} collective-permute-done((bf16[4,16,768]{2,1,0:T(8,128)(2,1)S(1)}, bf16[4,16,768]{2,1,0:T(8,128)(2,1)S(1)}, u32[]{:S(2)}, u32[]{:S(2)}) %collective-permute-start.8) | collective-permute-done | bytes 98336 | tf_op jit(solution)/shard_map/ppermute | solution.py:545
  122.0 1.9 collective-permute-start.10
  124.0 1.3 collective-permute-start.11
  125.3 1.2 collective-permute-start.12
  127.3 10.8 %incoming_plan.1 = (bf16[8,2,704,128]{3,2,1,0:T(8,128)(2,1)S(1)}, s32[4,128]{1,0:T(4,128)S(1)}) custom-call(s32[8,5632]{1,0:T(8,128)S(1)} %copy-done.4, s32[8,768]{1,0:T(8,128)S(1)} %pad.13.wanted_ref), custom_call_target="tpu_custom_call" | custom-call | flops 230686720 | bytes 360448 | tf_op jit(solution)/shard_map/incoming_plan/pallas_call | solution.py:437
  138.2 6.1 %down.1.refs_0_ = f32[64,512]{1,0:T(8,128)S(1)} custom-call(s32[1]{0:T(128)} %bitcast.20.me_ref, s32[64,2]{1,0:T(8,128)S(1)} %bitcast.80, bf16[2,16,768]{2,1,0:T(8,128)(2,1)S(1)} %activate.1.refs_0_, bf16[2,16,768]{2,1,0:T(8,128)(2,1)S(1)} %collective-permute-done.10.refs_1_, bf16[2,16,768]{2,1,0:T(8,128)(2,1)S(1)} %collective-permute-done.11.refs_2_, ...), custom_call_target="tpu_custom_call" | custom-call | flops 369098752 | bytes 5767168 | tf_op jit(solution)/shard_map/down/pallas_call | solution.py:810
  145.0 11.2 %unpack_lines.2.refs_1_.rest_0_ = bf16[8,3,704,512]{3,2,1,0:T(8,128)(2,1)} custom-call(s32[4,128]{1,0:T(4,128)S(1)} %get-tuple-element.8.plan_ref, bf16[8,2,704,128]{3,2,1,0:T(8,128)(2,1)S(1)} %get-tuple-element.9.place_ref, bf16[8,1,704,512]{3,2,1,0:T(8,128)(2,1)} %all-to-all-done.block_ref), custom_call_target="tpu_custom_call" | custom-call | flops 5905580032 | bytes 11534336 | tf_op jit(solution)/shard_map/unpack_lines/pallas_call | solution.py:495
  157.1 1.3 collective-permute-done.13
  159.2 2.7 %collective-permute-start.16 = (f32[8,512]{1,0:T(8,128)S(1)}, f32[8,512]{1,0:T(8,128)S(1)}, u32[]{:S(2)}, u32[]{:S(2)}) collective-permute-start(f32[8,512]{1,0:T(8,128)S(1)} %get-tuple-element.23), channel_id=1, source_target_pairs={{0,24},{4,28},{8,16},{12,20},{16,8},{20,12},{24,0},{28,4},{1,25},{... | collective-permute-start | bytes 49160 | tf_op jit(solution)/shard_map/ppermute | solution.py:545
  162.7 62.4 %collective-permute-done.16 = f32[8,512]{1,0:T(8,128)S(1)} collective-permute-done((f32[8,512]{1,0:T(8,128)S(1)}, f32[8,512]{1,0:T(8,128)S(1)}, u32[]{:S(2)}, u32[]{:S(2)}) %collective-permute-start.16) | collective-permute-done | bytes 16416 | tf_op jit(solution)/shard_map/ppermute | solution.py:545
  225.7 17.5 %unpack_lines.3 = bf16[8,3,704,512]{3,2,1,0:T(8,128)(2,1)} custom-call(s32[4,128]{1,0:T(4,128)S(1)} %get-tuple-element.8.plan_ref, bf16[8,2,704,128]{3,2,1,0:T(8,128)(2,1)S(1)} %get-tuple-element.9.place_ref, bf16[8,2,704,512]{3,2,1,0:T(8,128)(2,1)} %all-to-all-done.1.block_ref, ...), custom_call_target="tpu_custom_call", output_to_operand_aliasing={{}: (3, {})} | custom-call | flops 11811160064 | bytes 23068672 | tf_op jit(solution)/shard_map/unpack_lines/pallas_call | solution.py:495
  (120 shorter events, 18.7 us)
Async XLA Ops:
  19.1 72.4 %all-to-all-start = ((bf16[8,1,704,512]{3,2,1,0:T(8,128)(2,1)}), bf16[8,1,704,512]{3,2,1,0:T(8,128)(2,1)}, u32[]{:S(2)}, u32[]{:S(2)}) async-start(bf16[8,1,704,512]{3,2,1,0:T(8,128)(2,1)} %pack_lines.2.refs_1_), calls=%async_computation | async-start | bytes 11534336 | tf_op jit(solution)/shard_map/all_to_all | solution.py:585
  26.8 3.2 %copy-start.12 = (bf16[8,4096]{1,0:T(8,128)(2,1)S(1)}, bf16[8,4096]{1,0:T(8,128)(2,1)}, u32[]{:S(2)}) copy-start(bf16[8,4096]{1,0:T(8,128)(2,1)} %param.15) | copy-start | bytes 196612
  26.9 3.2 %copy-start.13 = (bf16[8,2,2048]{2,1,0:T(2,128)(2,1)S(1)}, bf16[8,2,2048]{2,1,0:T(2,128)(2,1)}, u32[]{:S(2)}) copy-start(bf16[8,2,2048]{2,1,0:T(2,128)(2,1)} %param.16) | copy-start | bytes 196612
  26.9 3.7 %copy-start.19 = (s32[8]{0:T(128)S(1)}, s32[8]{0:T(128)}, u32[]{:S(2)}) copy-start(s32[8]{0:T(128)} %param.19) | copy-start | bytes 100
  39.7 23.4 %copy-start.14 = (bf16[8,512]{1,0:T(8,128)(2,1)S(1)}, bf16[8,512]{1,0:T(8,128)(2,1)}, u32[]{:S(2)}) copy-start(bf16[8,512]{1,0:T(8,128)(2,1)} %param.14) | copy-start | bytes 24580
  39.8 22.9 %collective-permute-start.2 = (f32[8,4224]{1,0:T(8,128)S(1)}, f32[8,4224]{1,0:T(8,128)S(1)}, u32[]{:S(2)}, u32[]{:S(2)}) collective-permute-start(f32[8,4224]{1,0:T(8,128)S(1)} %concatenate.10), channel_id=1, source_target_pairs={{0,3},{1,2},{2,1},{3,0},{4,7},{5,6},{6,5},{7,4},{8,11},{9,10},{10,... | collective-permute-start | bytes 405512 | tf_op jit(solution)/shard_map/ppermute | solution.py:545
  44.7 17.9 %collective-permute-start.1 = (f32[8,4224]{1,0:T(8,128)S(1)}, f32[8,4224]{1,0:T(8,128)S(1)}, u32[]{:S(2)}, u32[]{:S(2)}) collective-permute-start(f32[8,4224]{1,0:T(8,128)S(1)} %concatenate.10), channel_id=1, source_target_pairs={{0,2},{1,3},{2,0},{3,1},{4,6},{5,7},{6,4},{7,5},{8,10},{9,11},{10,... | collective-permute-start | bytes 405512 | tf_op jit(solution)/shard_map/ppermute | solution.py:545
  44.7 17.9 %collective-permute-start = (f32[8,4224]{1,0:T(8,128)S(1)}, f32[8,4224]{1,0:T(8,128)S(1)}, u32[]{:S(2)}, u32[]{:S(2)}) collective-permute-start(f32[8,4224]{1,0:T(8,128)S(1)} %concatenate.10), channel_id=1, source_target_pairs={{0,1},{1,0},{2,3},{3,2},{4,5},{5,4},{6,7},{7,6},{8,9},{9,8},{10,11... | collective-permute-start | bytes 405512 | tf_op jit(solution)/shard_map/ppermute | solution.py:545
  66.7 23.3 %collective-permute-start.3 = (bf16[8,512]{1,0:T(8,128)(2,1)}, bf16[8,512]{1,0:T(8,128)(2,1)S(1)}, u32[]{:S(2)}, u32[]{:S(2)}) collective-permute-start(bf16[8,512]{1,0:T(8,128)(2,1)} %after.3), channel_id=1, source_target_pairs={{0,8},{4,12},{8,0},{12,4},{16,24},{20,28},{24,16},{28,20},{1,9},{5... | collective-permute-start | bytes 24584 | tf_op jit(solution)/shard_map/ppermute | solution.py:545
  68.4 21.6 %collective-permute-start.4 = (bf16[8,512]{1,0:T(8,128)(2,1)}, bf16[8,512]{1,0:T(8,128)(2,1)S(1)}, u32[]{:S(2)}, u32[]{:S(2)}) collective-permute-start(bf16[8,512]{1,0:T(8,128)(2,1)} %after.3), channel_id=1, source_target_pairs={{0,16},{4,20},{8,24},{12,28},{16,0},{20,4},{24,8},{28,12},{1,17},{... | collective-permute-start | bytes 24584 | tf_op jit(solution)/shard_map/ppermute | solution.py:545
  69.5 21.3 %collective-permute-start.5 = (bf16[8,512]{1,0:T(8,128)(2,1)}, bf16[8,512]{1,0:T(8,128)(2,1)S(1)}, u32[]{:S(2)}, u32[]{:S(2)}) collective-permute-start(bf16[8,512]{1,0:T(8,128)(2,1)} %after.3), channel_id=1, source_target_pairs={{0,24},{4,28},{8,16},{12,20},{16,8},{20,12},{24,0},{28,4},{1,25},{... | collective-permute-start | bytes 24584 | tf_op jit(solution)/shard_map/ppermute | solution.py:545
  91.4 5.7 %copy-start.17 = (s32[64,2]{0,1:T(2,128)S(1)}, s32[64,2]{0,1:T(2,128)}, u32[]{:S(2)}) copy-start(s32[64,2]{0,1:T(2,128)} %param.26) | copy-start | bytes 1540
  91.4 5.8 %copy-start.20 = (s32[8]{0:T(128)S(1)}, s32[8]{0:T(128)}, u32[]{:S(2)}) copy-start(s32[8]{0:T(128)} %constant.41.clone) | copy-start | bytes 100
  91.4 6.5 %copy-start.18 = (bf16[512]{0:T(512)(128)(2,1)S(1)}, bf16[512]{0:T(512)(128)(2,1)}, u32[]{:S(2)}) copy-start(bf16[512]{0:T(512)(128)(2,1)} %param.21) | copy-start | bytes 3076
  91.4 6.5 %copy-start.15 = (bf16[512,8]{0,1:T(8,128)(2,1)S(1)}, bf16[512,8]{0,1:T(8,128)(2,1)}, u32[]{:S(2)}) copy-start(bf16[512,8]{0,1:T(8,128)(2,1)} %param.22) | copy-start | bytes 24580
  91.4 6.8 %copy-start.5 = (bf16[8,512]{1,0:T(8,128)(2,1)S(1)}, bf16[8,512]{1,0:T(8,128)(2,1)}, u32[]{:S(2)}) copy-start(bf16[8,512]{1,0:T(8,128)(2,1)} %after.3) | copy-start | bytes 24580
  91.5 6.8 %copy-start.7 = (bf16[8,512]{1,0:T(8,128)(2,1)S(1)}, bf16[8,512]{1,0:T(8,128)(2,1)}, u32[]{:S(2)}) copy-start(bf16[8,512]{1,0:T(8,128)(2,1)} %copy-done.6) | copy-start | bytes 24580
  91.5 6.8 %copy-start.9 = (bf16[8,512]{1,0:T(8,128)(2,1)S(1)}, bf16[8,512]{1,0:T(8,128)(2,1)}, u32[]{:S(2)}) copy-start(bf16[8,512]{1,0:T(8,128)(2,1)} %copy-done.8) | copy-start | bytes 24580
  91.5 6.8 %copy-start.11 = (bf16[8,512]{1,0:T(8,128)(2,1)S(1)}, bf16[8,512]{1,0:T(8,128)(2,1)}, u32[]{:S(2)}) copy-start(bf16[8,512]{1,0:T(8,128)(2,1)} %copy-done.10) | copy-start | bytes 24580
  91.5 134.2 %all-to-all-start.1 = ((bf16[8,2,704,512]{3,2,1,0:T(8,128)(2,1)}), bf16[8,2,704,512]{3,2,1,0:T(8,128)(2,1)}, u32[]{:S(2)}, u32[]{:S(2)}) async-start(bf16[8,2,704,512]{3,2,1,0:T(8,128)(2,1)} %after.5), calls=%async_computation.1 | async-start | bytes 23068672 | tf_op jit(solution)/shard_map/all_to_all | solution.py:585
  98.3 1.7 collective-permute-start.6
  100.0 27.3 %copy-start.4 = (s32[8,5632]{1,0:T(8,128)S(1)}, s32[8,5632]{1,0:T(8,128)}, u32[]{:S(2)}) copy-start(s32[8,5632]{1,0:T(8,128)} %old_ref.1) | copy-start | bytes 540676
  108.9 5.6 %collective-permute-start.7 = (bf16[4,16,768]{2,1,0:T(8,128)(2,1)S(1)}, bf16[4,16,768]{2,1,0:T(8,128)(2,1)S(1)}, u32[]{:S(2)}, u32[]{:S(2)}) collective-permute-start(bf16[4,16,768]{2,1,0:T(8,128)(2,1)S(1)} %get-tuple-element.20), channel_id=1, source_target_pairs={{0,1},{1,0},{2,3},{3,2},{4,5},{5,4},{6,7},{7,6},{8,9},{9,8},{10,11... | collective-permute-start | bytes 294920 | tf_op jit(solution)/shard_map/ppermute | solution.py:545
  111.2 10.7 %collective-permute-start.8 = (bf16[4,16,768]{2,1,0:T(8,128)(2,1)S(1)}, bf16[4,16,768]{2,1,0:T(8,128)(2,1)S(1)}, u32[]{:S(2)}, u32[]{:S(2)}) collective-permute-start(bf16[4,16,768]{2,1,0:T(8,128)(2,1)S(1)} %get-tuple-element.19), channel_id=1, source_target_pairs={{0,2},{1,3},{2,0},{3,1},{4,6},{5,7},{6,4},{7,5},{8,10},{9,11},{10,... | collective-permute-start | bytes 294920 | tf_op jit(solution)/shard_map/ppermute | solution.py:545
  113.8 8.1 %collective-permute-start.9 = (bf16[4,16,768]{2,1,0:T(8,128)(2,1)S(1)}, bf16[4,16,768]{2,1,0:T(8,128)(2,1)S(1)}, u32[]{:S(2)}, u32[]{:S(2)}) collective-permute-start(bf16[4,16,768]{2,1,0:T(8,128)(2,1)S(1)} %get-tuple-element.18), channel_id=1, source_target_pairs={{0,3},{1,2},{2,1},{3,0},{4,7},{5,6},{6,5},{7,4},{8,11},{9,10},{10,... | collective-permute-start | bytes 294920 | tf_op jit(solution)/shard_map/ppermute | solution.py:545
  122.0 16.1 %collective-permute-start.10 = (bf16[2,16,768]{2,1,0:T(8,128)(2,1)S(1)}, bf16[2,16,768]{2,1,0:T(8,128)(2,1)S(1)}, u32[]{:S(2)}, u32[]{:S(2)}) collective-permute-start(bf16[2,16,768]{2,1,0:T(8,128)(2,1)S(1)} %activate.1.refs_0_), channel_id=1, source_target_pairs={{0,1},{1,0},{2,3},{3,2},{4,5},{5,4},{6,7},{7,6},{8,9},{9,8},{10,11... | collective-permute-start | bytes 147464 | tf_op jit(solution)/shard_map/ppermute | solution.py:545
  124.0 14.2 %collective-permute-start.11 = (bf16[2,16,768]{2,1,0:T(8,128)(2,1)S(1)}, bf16[2,16,768]{2,1,0:T(8,128)(2,1)S(1)}, u32[]{:S(2)}, u32[]{:S(2)}) collective-permute-start(bf16[2,16,768]{2,1,0:T(8,128)(2,1)S(1)} %activate.1.refs_0_), channel_id=1, source_target_pairs={{0,2},{1,3},{2,0},{3,1},{4,6},{5,7},{6,4},{7,5},{8,10},{9,11},{10,... | collective-permute-start | bytes 147464 | tf_op jit(solution)/shard_map/ppermute | solution.py:545
  125.3 12.9 %collective-permute-start.12 = (bf16[2,16,768]{2,1,0:T(8,128)(2,1)S(1)}, bf16[2,16,768]{2,1,0:T(8,128)(2,1)S(1)}, u32[]{:S(2)}, u32[]{:S(2)}) collective-permute-start(bf16[2,16,768]{2,1,0:T(8,128)(2,1)S(1)} %activate.1.refs_0_), channel_id=1, source_target_pairs={{0,3},{1,2},{2,1},{3,0},{4,7},{5,6},{6,5},{7,4},{8,11},{9,10},{10,... | collective-permute-start | bytes 147464 | tf_op jit(solution)/shard_map/ppermute | solution.py:545
  157.1 1.3 collective-permute-start.13
  159.2 65.9 %collective-permute-start.16 = (f32[8,512]{1,0:T(8,128)S(1)}, f32[8,512]{1,0:T(8,128)S(1)}, u32[]{:S(2)}, u32[]{:S(2)}) collective-permute-start(f32[8,512]{1,0:T(8,128)S(1)} %get-tuple-element.23), channel_id=1, source_target_pairs={{0,24},{4,28},{8,16},{12,20},{16,8},{20,12},{24,0},{28,4},{1,25},{... | collective-permute-start | bytes 49160 | tf_op jit(solution)/shard_map/ppermute | solution.py:545
  161.9 63.2 %collective-permute-start.15 = (f32[8,512]{1,0:T(8,128)S(1)}, f32[8,512]{1,0:T(8,128)S(1)}, u32[]{:S(2)}, u32[]{:S(2)}) collective-permute-start(f32[8,512]{1,0:T(8,128)S(1)} %get-tuple-element.24), channel_id=1, source_target_pairs={{0,16},{4,20},{8,24},{12,28},{16,0},{20,4},{24,8},{28,12},{1,17},{... | collective-permute-start | bytes 49160 | tf_op jit(solution)/shard_map/ppermute | solution.py:545
  162.4 62.7 %collective-permute-start.14 = (f32[8,512]{1,0:T(8,128)S(1)}, f32[8,512]{1,0:T(8,128)S(1)}, u32[]{:S(2)}, u32[]{:S(2)}) collective-permute-start(f32[8,512]{1,0:T(8,128)S(1)} %get-tuple-element.22), channel_id=1, source_target_pairs={{0,8},{4,12},{8,0},{12,4},{16,24},{20,28},{24,16},{28,20},{1,9},{5... | collective-permute-start | bytes 49160 | tf_op jit(solution)/shard_map/ppermute | solution.py:545
  (8 other events, 7.8 us)

commit v10 on v9

--- a/solution.py
+++ b/solution.py
@@ -239,7 +239,9 @@
     def entry(n, j, d):
         return plan_ref[n, (step * len(stages) + j) * rows + d]
 
-    usual = min(deep, up_to(min(lines, BLOCK) + rows * TILE, TILE))
+    def usual(j):
+        held = min(BLOCK, lines - j % blocks * BLOCK)
+        return min(deep, up_to(held + (rows + 3) * TILE, TILE))
 
     def move(j, begin, end):
         first = j % blocks * BLOCK
@@ -259,14 +261,14 @@
         ).astype(jnp.bfloat16)
 
     for j in range(len(stages)):
-        move(j, 0, usual)
-    if usual < deep:
-        for j in range(len(stages)):
+        move(j, 0, usual(j))
+    for j in range(len(stages)):
+        if usual(j) < deep:
             used = entry(1, j, rows - 1) + entry(2, j, rows - 1)
 
-            @pl.when(used * TILE > usual)
+            @pl.when(used * TILE > usual(j))
             def _(j=j):
-                move(j, usual, deep)
+                move(j, usual(j), deep)
 
     for j, stage_ref in enumerate(stages):
 
@@ -433,11 +435,11 @@
             multiply(j, deep)
 
 
-def call_plan(kernel, name, table, ids, pairs, place):
+def call_plan(kernel, name, table, ids, pairs, place, limit):
     return pl.pallas_call(
         kernel,
         out_shape=(place, jax.ShapeDtypeStruct((4, up_to(pairs, LANES)), jnp.int32)),
-        compiler_params=params(),
+        compiler_params=pltpu.CompilerParams(vmem_limit_bytes=limit),
         cost_estimate=pl.CostEstimate(
             flops=20 * table.size * 256, bytes_accessed=8 * table.size, transcendentals=0
         ),
@@ -562,13 +564,13 @@
         out_place, out_plan = call_plan(
             functools.partial(outgoing_kernel, lines, rows), "outgoing_plan",
             new_lines, own_ids(old_lines, lines, padded), blocks * rows,
-            jax.ShapeDtypeStruct((blocks, 1, BLOCK), jnp.int32),
+            jax.ShapeDtypeStruct((blocks, 1, BLOCK), jnp.int32), PACK_LIMIT,
         )
         self.in_place, self.in_plan = call_plan(
             functools.partial(incoming_kernel, lines, rows, block_rows // TILE, self.slot),
             "incoming_plan",
             old_lines, own_ids(new_lines, lines, padded), pairs,
-            jax.ShapeDtypeStruct((experts, 2, lines, LANES), jnp.bfloat16),
+            jax.ShapeDtypeStruct((experts, 2, lines, LANES), jnp.bfloat16), VMEM_LIMIT,
         )
         self.packed = [
             pack(expert_lines, out_place, out_plan, piece, rows, block_rows, deep)

time: 245 us -> 245 us (level)
    unnamed x51 -> x45, local copies, waits for them, and re-layouts: 6.1 us -> 3.98 us
where the time goes in v10:
time: 245 us; the launch traced here: 243 us
  waiting for transfers between devices  94.1 us (38%)
  Pallas kernels  88.8 us (36%)
  starting transfers between devices  32.8 us (13%)
  local copies, waits for them, and re-layouts  13.1 us (5%)
  matrix products  8.46 us (3%)
  other arithmetic  4.89 us (2%)
    ppermute x17, waiting for transfers between devices, from_peer(): return lax.ppermute(block, axis, [(i, i ^ offset) for i in range(size)])  94 us
    pallas_call x2, Pallas kernels, unpack(): pl.pallas_call(functools.partial(unpack_kernel, slot, span), grid_spec=pl...  28.7 us
    pallas_call x2, Pallas kernels, pack(): pl.pallas_call(functools.partial(pack_kernel, rows, span, experts // span...  26.8 us
    ppermute x17, starting transfers between devices, from_peer(): return lax.ppermute(block, axis, [(i, i ^ offset) for i in range(size)])  22 us
    pallas_call x2, Pallas kernels, call_plan(): pl.pallas_call(kernel, out_shape=(place, jax.ShapeDtypeStruct((4, up_to(p...  18.1 us
    all_to_all x2, starting transfers between devices, send(): lax.all_to_all(block, 'row', split_axis=0, concat_axis=0, tiled=True)  10.8 us
    pallas_call x1, Pallas kernels, experts_part(): pl.pallas_call(gate_up_kernel, grid_spec=pltpu.PrefetchScalarGridSpec(num...  8.79 us
    pallas_call x1, Pallas kernels, experts_part(): pl.pallas_call(down_kernel, grid_spec=pltpu.PrefetchScalarGridSpec(num_sc...  6.14 us
  transfers between devices with their start and end apart: 19, of which 7 were waited for; matrix products, arithmetic and copies ran while one was open for 10% of the time, Pallas kernels for 22%

profile of v10, /device:TPU:0, one launch (start us, length us, event | category | flops | bytes accessed | tf_op | source)
XLA Modules:
  0.0 243.5 jit_solution(10153108791725950844)
XLA Ops:
  2.1 7.3 %outgoing_plan.1 = (s32[24,1,256]{2,1,0:T(1,128)}, s32[4,256]{1,0:T(4,128)}) custom-call(s32[8,5632]{1,0:T(8,128)} %new_ref.1, s32[8,768]{1,0:T(8,128)} %pad.11.held_ref), custom_call_target="tpu_custom_call" | custom-call | flops 230686720 | bytes 360448 | tf_op jit(solution)/shard_map/outgoing_plan/pallas_call | solution.py:439
  9.4 9.7 %pack_lines.2.refs_1_ = bf16[8,1,704,512]{3,2,1,0:T(8,128)(2,1)} custom-call(s32[4,256]{1,0:T(4,128)} %get-tuple-element.6.plan_ref, s32[24,1,256]{2,1,0:T(1,128)} %get-tuple-element.7.place_ref, bf16[8,3,704,512]{3,2,1,0:T(8,128)(2,1)} %bitcast.81), custom_call_target="tpu_custom_call" | custom-call | flops 2860515328 | bytes 11534336 | tf_op jit(solution)/shard_map/pack_lines/pallas_call | solution.py:455
  19.1 5.2 %all-to-all-start = ((bf16[8,1,704,512]{3,2,1,0:T(8,128)(2,1)}), bf16[8,1,704,512]{3,2,1,0:T(8,128)(2,1)}, u32[]{:S(2)}, u32[]{:S(2)}) async-start(bf16[8,1,704,512]{3,2,1,0:T(8,128)(2,1)} %pack_lines.2.refs_1_), calls=%async_computation | async-start | bytes 11534336 | tf_op jit(solution)/shard_map/all_to_all | solution.py:587
  24.2 1.7 fusion.30
  27.0 1.7 fusion.29
  29.0 1.2 copy.145
  30.8 2.0 fusion.33
  33.5 1.2 fusion.32
  36.6 1.1 fusion.25
  38.2 1.1 fusion.5
  39.9 4.8 %collective-permute-start.2 = (f32[8,4224]{1,0:T(8,128)S(1)}, f32[8,4224]{1,0:T(8,128)S(1)}, u32[]{:S(2)}, u32[]{:S(2)}) collective-permute-start(f32[8,4224]{1,0:T(8,128)S(1)} %concatenate.10), channel_id=1, source_target_pairs={{0,3},{1,2},{2,1},{3,0},{4,7},{5,6},{6,5},{7,4},{8,11},{9,10},{10,... | collective-permute-start | bytes 405512 | tf_op jit(solution)/shard_map/ppermute | solution.py:547
  45.3 17.2 %pack_lines.3.refs_2_.refs_0_ = bf16[8,2,704,512]{3,2,1,0:T(8,128)(2,1)} custom-call(s32[4,256]{1,0:T(4,128)} %get-tuple-element.6.plan_ref, s32[24,1,256]{2,1,0:T(1,128)} %get-tuple-element.7.place_ref, bf16[8,3,704,512]{3,2,1,0:T(8,128)(2,1)} %bitcast.82), custom_call_target="tpu_custom_call" | custom-call | flops 5721030656 | bytes 23068672 | tf_op jit(solution)/shard_map/pack_lines/pallas_call | solution.py:455
  63.1 3.5 %fusion.4.refs_0_ = bf16[8,512]{1,0:T(8,128)(2,1)} fusion(bf16[4096,512]{1,0:T(8,128)(2,1)} %param.20, f32[8,4096]{1,0:T(8,128)S(1)} %fusion.8, f32[8,32]{0,1:T(8,128)S(1)} %copy.126, bf16[8,512]{1,0:T(8,128)(2,1)S(1)} %copy-done.11), kind=kOutput, calls=%fused_computation.9 | convolution fusion | flops 33632256 | bytes 4342784 | tf_op jit(solution)/shard_map/dot_general | solution.py:860
  66.6 1.7 collective-permute-start.3
  68.3 1.5 collective-permute-start.4
  70.1 19.8 %collective-permute-done.3.refs_1_ = bf16[8,512]{1,0:T(8,128)(2,1)S(1)} collective-permute-done((bf16[8,512]{1,0:T(8,128)(2,1)}, bf16[8,512]{1,0:T(8,128)(2,1)S(1)}, u32[]{:S(2)}, u32[]{:S(2)}) %collective-permute-start.3) | collective-permute-done | bytes 8224 | tf_op jit(solution)/shard_map/ppermute | solution.py:547
  91.5 5.6 %all-to-all-start.1 = ((bf16[8,2,704,512]{3,2,1,0:T(8,128)(2,1)}), bf16[8,2,704,512]{3,2,1,0:T(8,128)(2,1)}, u32[]{:S(2)}, u32[]{:S(2)}) async-start(bf16[8,2,704,512]{3,2,1,0:T(8,128)(2,1)} %after.5), calls=%async_computation.1 | async-start | bytes 23068672 | tf_op jit(solution)/shard_map/all_to_all | solution.py:587
  98.5 1.5 collective-permute-done.6
  100.0 8.8 %gate_up.1 = bf16[4,4,16,768]{3,2,1,0:T(8,128)(2,1)S(1)} custom-call(s32[1]{0:T(128)} %bitcast.20.me_ref, bf16[64,512]{1,0:T(8,128)(2,1)S(1)} %constant_dynamic-update-slice_fusion.h_ref, bf16[1,512]{1,0:T(2,128)(2,1)S(1)} %reshape.90.gain_ref, bf16[512,128]{1,0:T(8,128)(2,1)S(1)} %pad.12.router_ref, s32[64,2]{1,0:T(8,128)S(1)} %bitcast.78, ...), custom_call_target="tpu_custom_call" | custom-call | flops 738197504 | bytes 11534336 | tf_op jit(solution)/shard_map/gate_up/pallas_call | solution.py:785
  108.9 2.3 collective-permute-start.7
  111.1 2.6 %collective-permute-start.8 = (bf16[4,16,768]{2,1,0:T(8,128)(2,1)S(1)}, bf16[4,16,768]{2,1,0:T(8,128)(2,1)S(1)}, u32[]{:S(2)}, u32[]{:S(2)}) collective-permute-start(bf16[4,16,768]{2,1,0:T(8,128)(2,1)S(1)} %get-tuple-element.19), channel_id=1, source_target_pairs={{0,2},{1,3},{2,0},{3,1},{4,6},{5,7},{6,4},{7,5},{8,10},{9,11},{10,... | collective-permute-start | bytes 294920 | tf_op jit(solution)/shard_map/ppermute | solution.py:547
  114.4 7.4 %collective-permute-done.8.refs_2_ = bf16[4,16,768]{2,1,0:T(8,128)(2,1)S(1)} collective-permute-done((bf16[4,16,768]{2,1,0:T(8,128)(2,1)S(1)}, bf16[4,16,768]{2,1,0:T(8,128)(2,1)S(1)}, u32[]{:S(2)}, u32[]{:S(2)}) %collective-permute-start.8) | collective-permute-done | bytes 98336 | tf_op jit(solution)/shard_map/ppermute | solution.py:547
  122.0 1.9 collective-permute-start.10
  123.9 1.3 collective-permute-start.11
  125.2 1.2 collective-permute-start.12
  127.3 10.8 %incoming_plan.1 = (bf16[8,2,704,128]{3,2,1,0:T(8,128)(2,1)S(1)}, s32[4,128]{1,0:T(4,128)S(1)}) custom-call(s32[8,5632]{1,0:T(8,128)S(1)} %copy-done.1, s32[8,768]{1,0:T(8,128)S(1)} %pad.13.wanted_ref), custom_call_target="tpu_custom_call" | custom-call | flops 230686720 | bytes 360448 | tf_op jit(solution)/shard_map/incoming_plan/pallas_call | solution.py:439
  138.1 6.1 %down.1.refs_0_ = f32[64,512]{1,0:T(8,128)S(1)} custom-call(s32[1]{0:T(128)} %bitcast.20.me_ref, s32[64,2]{1,0:T(8,128)S(1)} %bitcast.80, bf16[2,16,768]{2,1,0:T(8,128)(2,1)S(1)} %activate.1.refs_0_, bf16[2,16,768]{2,1,0:T(8,128)(2,1)S(1)} %collective-permute-done.10.refs_1_, bf16[2,16,768]{2,1,0:T(8,128)(2,1)S(1)} %collective-permute-done.11.refs_2_, ...), custom_call_target="tpu_custom_call" | custom-call | flops 369098752 | bytes 5767168 | tf_op jit(solution)/shard_map/down/pallas_call | solution.py:812
  144.9 11.2 %unpack_lines.2.refs_1_.rest_0_ = bf16[8,3,704,512]{3,2,1,0:T(8,128)(2,1)} custom-call(s32[4,128]{1,0:T(4,128)S(1)} %get-tuple-element.8.plan_ref, bf16[8,2,704,128]{3,2,1,0:T(8,128)(2,1)S(1)} %get-tuple-element.9.place_ref, bf16[8,1,704,512]{3,2,1,0:T(8,128)(2,1)} %all-to-all-done.block_ref), custom_call_target="tpu_custom_call" | custom-call | flops 5905580032 | bytes 11534336 | tf_op jit(solution)/shard_map/unpack_lines/pallas_call | solution.py:497
  157.0 1.3 collective-permute-done.13
  159.1 2.7 %collective-permute-start.16 = (f32[8,512]{1,0:T(8,128)S(1)}, f32[8,512]{1,0:T(8,128)S(1)}, u32[]{:S(2)}, u32[]{:S(2)}) collective-permute-start(f32[8,512]{1,0:T(8,128)S(1)} %get-tuple-element.23), channel_id=1, source_target_pairs={{0,24},{4,28},{8,16},{12,20},{16,8},{20,12},{24,0},{28,4},{1,25},{... | collective-permute-start | bytes 49160 | tf_op jit(solution)/shard_map/ppermute | solution.py:547
  162.7 62.4 %collective-permute-done.16 = f32[8,512]{1,0:T(8,128)S(1)} collective-permute-done((f32[8,512]{1,0:T(8,128)S(1)}, f32[8,512]{1,0:T(8,128)S(1)}, u32[]{:S(2)}, u32[]{:S(2)}) %collective-permute-start.16) | collective-permute-done | bytes 16416 | tf_op jit(solution)/shard_map/ppermute | solution.py:547
  225.7 17.5 %unpack_lines.3 = bf16[8,3,704,512]{3,2,1,0:T(8,128)(2,1)} custom-call(s32[4,128]{1,0:T(4,128)S(1)} %get-tuple-element.8.plan_ref, bf16[8,2,704,128]{3,2,1,0:T(8,128)(2,1)S(1)} %get-tuple-element.9.place_ref, bf16[8,2,704,512]{3,2,1,0:T(8,128)(2,1)} %all-to-all-done.1.block_ref, ...), custom_call_target="tpu_custom_call", output_to_operand_aliasing={{}: (3, {})} | custom-call | flops 11811160064 | bytes 23068672 | tf_op jit(solution)/shard_map/unpack_lines/pallas_call | solution.py:497
  (114 shorter events, 16.9 us)
Async XLA Ops:
  19.1 72.4 %all-to-all-start = ((bf16[8,1,704,512]{3,2,1,0:T(8,128)(2,1)}), bf16[8,1,704,512]{3,2,1,0:T(8,128)(2,1)}, u32[]{:S(2)}, u32[]{:S(2)}) async-start(bf16[8,1,704,512]{3,2,1,0:T(8,128)(2,1)} %pack_lines.2.refs_1_), calls=%async_computation | async-start | bytes 11534336 | tf_op jit(solution)/shard_map/all_to_all | solution.py:587
  27.0 3.2 %copy-start.9 = (bf16[8,4096]{1,0:T(8,128)(2,1)S(1)}, bf16[8,4096]{1,0:T(8,128)(2,1)}, u32[]{:S(2)}) copy-start(bf16[8,4096]{1,0:T(8,128)(2,1)} %param.15) | copy-start | bytes 196612
  27.0 3.2 %copy-start.10 = (bf16[8,2,2048]{2,1,0:T(2,128)(2,1)S(1)}, bf16[8,2,2048]{2,1,0:T(2,128)(2,1)}, u32[]{:S(2)}) copy-start(bf16[8,2,2048]{2,1,0:T(2,128)(2,1)} %param.16) | copy-start | bytes 196612
  27.0 3.7 %copy-start.16 = (s32[8]{0:T(128)S(1)}, s32[8]{0:T(128)}, u32[]{:S(2)}) copy-start(s32[8]{0:T(128)} %param.19) | copy-start | bytes 100
  39.9 23.2 %copy-start.11 = (bf16[8,512]{1,0:T(8,128)(2,1)S(1)}, bf16[8,512]{1,0:T(8,128)(2,1)}, u32[]{:S(2)}) copy-start(bf16[8,512]{1,0:T(8,128)(2,1)} %param.14) | copy-start | bytes 24580
  39.9 22.6 %collective-permute-start.2 = (f32[8,4224]{1,0:T(8,128)S(1)}, f32[8,4224]{1,0:T(8,128)S(1)}, u32[]{:S(2)}, u32[]{:S(2)}) collective-permute-start(f32[8,4224]{1,0:T(8,128)S(1)} %concatenate.10), channel_id=1, source_target_pairs={{0,3},{1,2},{2,1},{3,0},{4,7},{5,6},{6,5},{7,4},{8,11},{9,10},{10,... | collective-permute-start | bytes 405512 | tf_op jit(solution)/shard_map/ppermute | solution.py:547
  44.7 17.9 %collective-permute-start.1 = (f32[8,4224]{1,0:T(8,128)S(1)}, f32[8,4224]{1,0:T(8,128)S(1)}, u32[]{:S(2)}, u32[]{:S(2)}) collective-permute-start(f32[8,4224]{1,0:T(8,128)S(1)} %concatenate.10), channel_id=1, source_target_pairs={{0,2},{1,3},{2,0},{3,1},{4,6},{5,7},{6,4},{7,5},{8,10},{9,11},{10,... | collective-permute-start | bytes 405512 | tf_op jit(solution)/shard_map/ppermute | solution.py:547
  44.7 17.9 %collective-permute-start = (f32[8,4224]{1,0:T(8,128)S(1)}, f32[8,4224]{1,0:T(8,128)S(1)}, u32[]{:S(2)}, u32[]{:S(2)}) collective-permute-start(f32[8,4224]{1,0:T(8,128)S(1)} %concatenate.10), channel_id=1, source_target_pairs={{0,1},{1,0},{2,3},{3,2},{4,5},{5,4},{6,7},{7,6},{8,9},{9,8},{10,11... | collective-permute-start | bytes 405512 | tf_op jit(solution)/shard_map/ppermute | solution.py:547
  66.6 23.3 %collective-permute-start.3 = (bf16[8,512]{1,0:T(8,128)(2,1)}, bf16[8,512]{1,0:T(8,128)(2,1)S(1)}, u32[]{:S(2)}, u32[]{:S(2)}) collective-permute-start(bf16[8,512]{1,0:T(8,128)(2,1)} %after.3), channel_id=1, source_target_pairs={{0,8},{4,12},{8,0},{12,4},{16,24},{20,28},{24,16},{28,20},{1,9},{5... | collective-permute-start | bytes 24584 | tf_op jit(solution)/shard_map/ppermute | solution.py:547
  68.3 21.6 %collective-permute-start.4 = (bf16[8,512]{1,0:T(8,128)(2,1)}, bf16[8,512]{1,0:T(8,128)(2,1)S(1)}, u32[]{:S(2)}, u32[]{:S(2)}) collective-permute-start(bf16[8,512]{1,0:T(8,128)(2,1)} %after.3), channel_id=1, source_target_pairs={{0,16},{4,20},{8,24},{12,28},{16,0},{20,4},{24,8},{28,12},{1,17},{... | collective-permute-start | bytes 24584 | tf_op jit(solution)/shard_map/ppermute | solution.py:547
  69.8 21.1 %collective-permute-start.5 = (bf16[8,512]{1,0:T(8,128)(2,1)}, bf16[8,512]{1,0:T(8,128)(2,1)S(1)}, u32[]{:S(2)}, u32[]{:S(2)}) collective-permute-start(bf16[8,512]{1,0:T(8,128)(2,1)} %after.3), channel_id=1, source_target_pairs={{0,24},{4,28},{8,16},{12,20},{16,8},{20,12},{24,0},{28,4},{1,25},{... | collective-permute-start | bytes 24584 | tf_op jit(solution)/shard_map/ppermute | solution.py:547
  91.4 5.7 %copy-start.14 = (s32[64,2]{0,1:T(2,128)S(1)}, s32[64,2]{0,1:T(2,128)}, u32[]{:S(2)}) copy-start(s32[64,2]{0,1:T(2,128)} %param.26) | copy-start | bytes 1540
  91.4 5.8 %copy-start.17 = (s32[8]{0:T(128)S(1)}, s32[8]{0:T(128)}, u32[]{:S(2)}) copy-start(s32[8]{0:T(128)} %constant.41.clone) | copy-start | bytes 100
  91.4 6.5 %copy-start.15 = (bf16[512]{0:T(512)(128)(2,1)S(1)}, bf16[512]{0:T(512)(128)(2,1)}, u32[]{:S(2)}) copy-start(bf16[512]{0:T(512)(128)(2,1)} %param.21) | copy-start | bytes 3076
  91.4 6.5 %copy-start.12 = (bf16[512,8]{0,1:T(8,128)(2,1)S(1)}, bf16[512,8]{0,1:T(8,128)(2,1)}, u32[]{:S(2)}) copy-start(bf16[512,8]{0,1:T(8,128)(2,1)} %param.22) | copy-start | bytes 24580
  91.5 6.8 %copy-start.2 = (bf16[8,512]{1,0:T(8,128)(2,1)S(1)}, bf16[8,512]{1,0:T(8,128)(2,1)}, u32[]{:S(2)}) copy-start(bf16[8,512]{1,0:T(8,128)(2,1)} %after.3) | copy-start | bytes 24580
  91.5 6.8 %copy-start.4 = (bf16[8,512]{1,0:T(8,128)(2,1)S(1)}, bf16[8,512]{1,0:T(8,128)(2,1)}, u32[]{:S(2)}) copy-start(bf16[8,512]{1,0:T(8,128)(2,1)} %copy-done.3) | copy-start | bytes 24580
  91.5 6.8 %copy-start.6 = (bf16[8,512]{1,0:T(8,128)(2,1)S(1)}, bf16[8,512]{1,0:T(8,128)(2,1)}, u32[]{:S(2)}) copy-start(bf16[8,512]{1,0:T(8,128)(2,1)} %copy-done.5) | copy-start | bytes 24580
  91.5 6.8 %copy-start.8 = (bf16[8,512]{1,0:T(8,128)(2,1)S(1)}, bf16[8,512]{1,0:T(8,128)(2,1)}, u32[]{:S(2)}) copy-start(bf16[8,512]{1,0:T(8,128)(2,1)} %copy-done.7) | copy-start | bytes 24580
  91.5 134.2 %all-to-all-start.1 = ((bf16[8,2,704,512]{3,2,1,0:T(8,128)(2,1)}), bf16[8,2,704,512]{3,2,1,0:T(8,128)(2,1)}, u32[]{:S(2)}, u32[]{:S(2)}) async-start(bf16[8,2,704,512]{3,2,1,0:T(8,128)(2,1)} %after.5), calls=%async_computation.1 | async-start | bytes 23068672 | tf_op jit(solution)/shard_map/all_to_all | solution.py:587
  98.3 1.7 collective-permute-start.6
  100.0 27.2 %copy-start.1 = (s32[8,5632]{1,0:T(8,128)S(1)}, s32[8,5632]{1,0:T(8,128)}, u32[]{:S(2)}) copy-start(s32[8,5632]{1,0:T(8,128)} %old_ref.1) | copy-start | bytes 540676
  108.9 5.5 %collective-permute-start.7 = (bf16[4,16,768]{2,1,0:T(8,128)(2,1)S(1)}, bf16[4,16,768]{2,1,0:T(8,128)(2,1)S(1)}, u32[]{:S(2)}, u32[]{:S(2)}) collective-permute-start(bf16[4,16,768]{2,1,0:T(8,128)(2,1)S(1)} %get-tuple-element.20), channel_id=1, source_target_pairs={{0,1},{1,0},{2,3},{3,2},{4,5},{5,4},{6,7},{7,6},{8,9},{9,8},{10,11... | collective-permute-start | bytes 294920 | tf_op jit(solution)/shard_map/ppermute | solution.py:547
  111.1 10.7 %collective-permute-start.8 = (bf16[4,16,768]{2,1,0:T(8,128)(2,1)S(1)}, bf16[4,16,768]{2,1,0:T(8,128)(2,1)S(1)}, u32[]{:S(2)}, u32[]{:S(2)}) collective-permute-start(bf16[4,16,768]{2,1,0:T(8,128)(2,1)S(1)} %get-tuple-element.19), channel_id=1, source_target_pairs={{0,2},{1,3},{2,0},{3,1},{4,6},{5,7},{6,4},{7,5},{8,10},{9,11},{10,... | collective-permute-start | bytes 294920 | tf_op jit(solution)/shard_map/ppermute | solution.py:547
  113.7 8.1 %collective-permute-start.9 = (bf16[4,16,768]{2,1,0:T(8,128)(2,1)S(1)}, bf16[4,16,768]{2,1,0:T(8,128)(2,1)S(1)}, u32[]{:S(2)}, u32[]{:S(2)}) collective-permute-start(bf16[4,16,768]{2,1,0:T(8,128)(2,1)S(1)} %get-tuple-element.18), channel_id=1, source_target_pairs={{0,3},{1,2},{2,1},{3,0},{4,7},{5,6},{6,5},{7,4},{8,11},{9,10},{10,... | collective-permute-start | bytes 294920 | tf_op jit(solution)/shard_map/ppermute | solution.py:547
  122.0 16.1 %collective-permute-start.10 = (bf16[2,16,768]{2,1,0:T(8,128)(2,1)S(1)}, bf16[2,16,768]{2,1,0:T(8,128)(2,1)S(1)}, u32[]{:S(2)}, u32[]{:S(2)}) collective-permute-start(bf16[2,16,768]{2,1,0:T(8,128)(2,1)S(1)} %activate.1.refs_0_), channel_id=1, source_target_pairs={{0,1},{1,0},{2,3},{3,2},{4,5},{5,4},{6,7},{7,6},{8,9},{9,8},{10,11... | collective-permute-start | bytes 147464 | tf_op jit(solution)/shard_map/ppermute | solution.py:547
  123.9 14.2 %collective-permute-start.11 = (bf16[2,16,768]{2,1,0:T(8,128)(2,1)S(1)}, bf16[2,16,768]{2,1,0:T(8,128)(2,1)S(1)}, u32[]{:S(2)}, u32[]{:S(2)}) collective-permute-start(bf16[2,16,768]{2,1,0:T(8,128)(2,1)S(1)} %activate.1.refs_0_), channel_id=1, source_target_pairs={{0,2},{1,3},{2,0},{3,1},{4,6},{5,7},{6,4},{7,5},{8,10},{9,11},{10,... | collective-permute-start | bytes 147464 | tf_op jit(solution)/shard_map/ppermute | solution.py:547
  125.2 12.9 %collective-permute-start.12 = (bf16[2,16,768]{2,1,0:T(8,128)(2,1)S(1)}, bf16[2,16,768]{2,1,0:T(8,128)(2,1)S(1)}, u32[]{:S(2)}, u32[]{:S(2)}) collective-permute-start(bf16[2,16,768]{2,1,0:T(8,128)(2,1)S(1)} %activate.1.refs_0_), channel_id=1, source_target_pairs={{0,3},{1,2},{2,1},{3,0},{4,7},{5,6},{6,5},{7,4},{8,11},{9,10},{10,... | collective-permute-start | bytes 147464 | tf_op jit(solution)/shard_map/ppermute | solution.py:547
  157.0 1.3 collective-permute-start.13
  159.1 66.0 %collective-permute-start.16 = (f32[8,512]{1,0:T(8,128)S(1)}, f32[8,512]{1,0:T(8,128)S(1)}, u32[]{:S(2)}, u32[]{:S(2)}) collective-permute-start(f32[8,512]{1,0:T(8,128)S(1)} %get-tuple-element.23), channel_id=1, source_target_pairs={{0,24},{4,28},{8,16},{12,20},{16,8},{20,12},{24,0},{28,4},{1,25},{... | collective-permute-start | bytes 49160 | tf_op jit(solution)/shard_map/ppermute | solution.py:547
  161.8 63.3 %collective-permute-start.15 = (f32[8,512]{1,0:T(8,128)S(1)}, f32[8,512]{1,0:T(8,128)S(1)}, u32[]{:S(2)}, u32[]{:S(2)}) collective-permute-start(f32[8,512]{1,0:T(8,128)S(1)} %get-tuple-element.24), channel_id=1, source_target_pairs={{0,16},{4,20},{8,24},{12,28},{16,0},{20,4},{24,8},{28,12},{1,17},{... | collective-permute-start | bytes 49160 | tf_op jit(solution)/shard_map/ppermute | solution.py:547
  162.3 62.8 %collective-permute-start.14 = (f32[8,512]{1,0:T(8,128)S(1)}, f32[8,512]{1,0:T(8,128)S(1)}, u32[]{:S(2)}, u32[]{:S(2)}) collective-permute-start(f32[8,512]{1,0:T(8,128)S(1)} %get-tuple-element.22), channel_id=1, source_target_pairs={{0,8},{4,12},{8,0},{12,4},{16,24},{20,28},{24,16},{28,20},{1,9},{5... | collective-permute-start | bytes 49160 | tf_op jit(solution)/shard_map/ppermute | solution.py:547
  (5 other events, 6.0 us)
